TPU v7x, 32 devices: a whole 2x2x4 slice. The times are simulated.
32 devices in a mesh: rep: 16 (over z, y, x), tp: 2 (over core).
Axes of the slice: x: 2, y: 2, z: 4, core: 2. Of those that a mesh axis runs over, the one named last changes fastest.
Arguments:
- tokens: bfloat16 [16384, 4096], P('rep', 'tp'), may hold values from -6 to 6
- norm_gain: bfloat16 [4096], P('tp'), may hold values from 0.099609375 to 1.8984375
- local_weights: bfloat16 [65536, 256], P('rep', 'tp'), may hold values from -6 to 6
- anchor: float32 [4096, 256], P('rep', 'tp'), may hold values from -6 to 6
- momentum: float32 [4096, 256], P('rep', 'tp'), may hold values from -3 to 3
- key_grad: bfloat16 [16384, 256], P('rep', 'tp'), may hold values from -6 to 6
Outputs:
- new_keys: bfloat16 [16384, 256], P('rep', 'tp')
- weight_grad: bfloat16 [65536, 256], P('rep', 'tp')
- merged: bfloat16 [65536, 256], P('rep', 'tp')
- new_anchor: float32 [4096, 256], P('rep', 'tp')
- new_momentum: float32 [4096, 256], P('rep', 'tp')
All inputs are finite; a program needn't handle non-finite values.
Results may differ from a plain program's by a relative error of at most 0.0058.
Values may be sent and summed in bfloat16 or wider, within the bound.
No kernel may reach another device: no remote copies, remote signals or barrier semaphores. Data moves between devices by JAX's collectives and lax.ppermute only.
A program may use at most 64 MiB of HBM per device.

v0:
```python
import math

import jax
import jax.numpy as jnp
from jax import lax
from jax.sharding import PartitionSpec as P

HD = 128


momentum_rate = 0.9
outer_rate = 0.7
mix_rate = 0.5
rope_base = 500000.0
norm_eps = 1e-05


def angles(row_count):
    positions = jnp.arange(row_count, dtype=jnp.float32)
    freq_table = jnp.exp(-(jnp.arange(HD // 2, dtype=jnp.float32) * 2.0 / HD) * math.log(rope_base))
    turned = positions[:, None] * freq_table[None, :]
    return (jnp.cos(turned), jnp.sin(turned))


def rotate(values, cosine, sine_vals):
    row_count = values.shape[0]
    by_head = values.reshape(row_count, -1, HD)
    lower_half = by_head[..., : HD // 2]
    upper_half = by_head[..., HD // 2 :]
    cos_part = cosine[:, None, :]
    sin_part = sine_vals[:, None, :]
    turned = jnp.concatenate(
        [
            lower_half * cos_part - upper_half * sin_part,
            upper_half * cos_part + lower_half * sin_part,
        ],
        axis=-1,
    )
    return turned.reshape(row_count, -1)


def normalize(hidden, norm_gain):
    widened = hidden.astype(jnp.float32)
    mean_square = jnp.mean(widened * widened, axis=-1, keepdims=True)
    return (widened * lax.rsqrt(mean_square + norm_eps) * norm_gain.astype(jnp.float32)).astype(
        jnp.bfloat16
    )


def key_layer(tokens, norm_gain, local_weights, key_grad):
    all_features, all_gain = (
        lax.all_gather(tokens, "tp", axis=1, tiled=True),
        lax.all_gather(norm_gain, "tp", axis=0, tiled=True),
    )
    row_count = tokens.shape[0]
    inv_width = 1.0 / math.sqrt(all_features.shape[1])
    cosine, sine_vals = angles(row_count)
    normed = normalize(all_features, all_gain)
    raw_keys = jnp.dot(normed, local_weights, preferred_element_type=jnp.float32) * inv_width
    key_rows = rotate(raw_keys, cosine, sine_vals).astype(jnp.bfloat16)
    raw_grad = rotate(key_grad.astype(jnp.float32), cosine, -sine_vals).astype(jnp.bfloat16)
    contracted = lax.dot_general(
        normed, raw_grad, (((0,), (0,)), ((), ())), preferred_element_type=jnp.float32
    )
    weight_grad = (contracted * inv_width).astype(jnp.bfloat16)
    return (key_rows, weight_grad)


def outer_step(local_weights, anchor, momentum):
    replicas = lax.axis_size("rep")
    widened = local_weights.astype(jnp.float32)
    summed = lax.psum_scatter(widened, "rep", scatter_dimension=0, tiled=True)
    mean_weights = summed / replicas
    change = anchor - mean_weights
    new_momentum = momentum_rate * momentum + change
    new_anchor = anchor - outer_rate * (change + momentum_rate * new_momentum)
    outgoing = new_anchor.astype(jnp.bfloat16)
    global_rows = lax.all_gather(outgoing, "rep", axis=0, tiled=True).astype(jnp.float32)
    merged = (widened + mix_rate * (global_rows - widened)).astype(jnp.bfloat16)
    return (merged, new_anchor, new_momentum)


def body(tokens, norm_gain, local_weights, anchor, momentum, key_grad):
    key_rows, weight_grad = key_layer(tokens, norm_gain, local_weights, key_grad)
    merged, new_anchor, new_momentum = outer_step(local_weights, anchor, momentum)
    return (key_rows, weight_grad, merged, new_anchor, new_momentum)


def solution(mesh):
    in_specs = (
        P("rep", "tp"),
        P("tp"),
        P("rep", "tp"),
        P("rep", "tp"),
        P("rep", "tp"),
        P("rep", "tp"),
    )
    out_specs = (P("rep", "tp"), P("rep", "tp"), P("rep", "tp"), P("rep", "tp"), P("rep", "tp"))
    return jax.shard_map(body, mesh=mesh, in_specs=in_specs, out_specs=out_specs, check_vma=False)
```

profile of v0, /device:TPU:0, one launch (start us, length us, event | category | flops | bytes accessed | tf_op | source)
XLA Modules:
  0.0 194.3 jit_solution(4774823189702922459)
XLA Ops:
  7.2 0.0 copy-start.1
  7.2 0.0 copy-start.3
  7.2 0.0 copy-start.2
  7.2 0.0 reduce-scatter.2.cloned.1.call-start
  7.2 2.8 %convert_element_type.39 = f32[4096,128]{1,0:T(8,128)} convert(bf16[4096,128]{1,0:T(8,128)(2,1)} %param.8) | non-fusion elementwise | flops 524288 | bytes 3145728 | tf_op jit(solution)/shard_map/convert_element_type | solution.py:71
  10.0 0.0 reduce-scatter.2.cloned.1.call-update
  10.1 0.0 all-gather.5.cloned.1.call-start
  10.1 83.5 %reduce-scatter.2.cloned.1.call-done = f32[256,128]{1,0:T(8,128)} async-done(((f32[4096,128]{1,0:T(8,128)}), f32[256,128]{1,0:T(8,128)}) %reduce-scatter.2.cloned.1.call-update) | async-done | bytes 131088 | tf_op jit(solution)/shard_map/reduce_scatter | solution.py:72
  93.7 1.8 fusion.19
  95.4 0.0 all-gather.5.cloned.1.call-update
  95.5 0.0 all-gather.3.cloned.1.call-start
  95.5 0.7 all-gather.3.cloned.1.call-update
  96.2 0.0 copy-done.3
  96.2 1.8 all_gather.10
  98.0 0.1 copy.13
  98.2 51.3 %all-gather.5.cloned.1.call-done = bf16[4096,128]{1,0:T(8,128)(2,1)} async-done(((bf16[256,128]{1,0:T(8,128)(2,1)}), bf16[4096,128]{1,0:T(8,128)(2,1)}) %all-gather.5.cloned.1.call-update) | async-done | bytes 1048592 | tf_op jit(solution)/shard_map/all_gather | solution.py:78
  149.5 2.6 %add_convert_fusion = bf16[4096,128]{1,0:T(8,128)(2,1)} fusion(bf16[4096,128]{1,0:T(8,128)(2,1)} %all-gather.5.cloned.1.call-done, bf16[4096,128]{1,0:T(8,128)(2,1)S(1)} %copy-done.1), kind=kLoop, calls=%fused_computation.8 | loop fusion | flops 3145728 | bytes 3145728 | tf_op jit(solution)/shard_map/convert_element_type | solution.py:79
  152.1 17.6 %all-gather.3.cloned.1.call-done = bf16[1024,4096]{1,0:T(8,128)(2,1)} async-done(((bf16[1024,2048]{1,0:T(8,128)(2,1)}), bf16[1024,4096]{1,0:T(8,128)(2,1)}) %all-gather.3.cloned.1.call-update) | async-done | bytes 8388624 | tf_op jit(solution)/shard_map/all_gather | solution.py:52
  169.8 5.2 %fusion = f32[1024]{0:T(1024)S(1)} fusion(bf16[1024,4096]{1,0:T(8,128)(2,1)} %all-gather.3.cloned.1.call-done), kind=kLoop, calls=%fused_computation.2 | loop fusion | flops 12581888 | bytes 8392704 | tf_op jit(solution)/shard_map/reduce_sum | solution.py:44
  175.0 0.5 copy-done
  175.5 2.9 %fusion.10 = f32[1024,1,128]{0,2,1:T(8,128)S(1)} fusion(bf16[4096,128]{1,0:T(8,128)(2,1)S(1)} %copy-done.1, bf16[1024,4096]{1,0:T(8,128)(2,1)S(1)} %copy-done, f32[4096]{0:T(1024)S(1)} %convert_element_type.34, f32[1024]{0:T(1024)S(1)} %add_rsqrt_fusion), kind=kOutput, calls=%fused_computation.10 | convolution fusion | flops 1090650112 | bytes 9981952 | tf_op jit(solution)/shard_map/dot_general | solution.py:59
  178.4 1.2 subtract_convert_fusion
  179.7 0.8 copy.14
  180.6 7.2 %fusion.3 = bf16[4096,128]{1,0:T(8,128)(2,1)} fusion(bf16[1024,4096]{1,0:T(8,128)(2,1)} %all-gather.3.cloned.1.call-done, f32[4096]{0:T(1024)S(1)} %convert_element_type.34, f32[1024]{0:T(1024)S(1)} %add_rsqrt_fusion, bf16[1024,1,64]{0,2,1:T(8,128)(2,1)S(1)} %get-tuple-element.19, bf16[1024,1,64]{0,2,1:T(8,128)(2,1)S(1)} %get-tuple-element.18), kind=kOutput, calls=%fused_computation.6 | convolution fusion | flops 1092091904 | bytes 9719808 | tf_op jit(solution)/shard_map/dot_general | solution.py:62
  (8 shorter events, 0.1 us)
Async XLA Ops:
  7.2 142.4 %copy-start.1 = (bf16[4096,128]{1,0:T(8,128)(2,1)S(1)}, bf16[4096,128]{1,0:T(8,128)(2,1)}, u32[]{:S(2)}) copy-start(bf16[4096,128]{1,0:T(8,128)(2,1)} %param.8) | copy-start | bytes 3145732
  7.2 89.0 %copy-start.3 = (bf16[2048]{0:T(1024)(128)(2,1)S(1)}, bf16[2048]{0:T(1024)(128)(2,1)}, u32[]{:S(2)}) copy-start(bf16[2048]{0:T(1024)(128)(2,1)} %param.7) | copy-start | bytes 12292
  7.2 90.8 %copy-start.2 = (bf16[1024,128]{1,0:T(8,128)(2,1)S(1)}, bf16[1024,128]{1,0:T(8,128)(2,1)}, u32[]{:S(2)}) copy-start(bf16[1024,128]{1,0:T(8,128)(2,1)} %param.11) | copy-start | bytes 786436
  7.2 86.5 %reduce-scatter.2.cloned.1.call-start = ((), (), s32[]{:S(2)}) async-start(), calls=%async_computation.2 | async-start | bytes 2228224 | tf_op jit(solution)/shard_map/reduce_scatter | solution.py:72
  10.1 139.5 %all-gather.5.cloned.1.call-start = ((), (), s32[]{:S(2)}) async-start(), calls=%async_computation.3 | async-start | bytes 1114112 | tf_op jit(solution)/shard_map/all_gather | solution.py:78
  95.5 74.3 %all-gather.3.cloned.1.call-start = ((), (), s32[]{:S(2)}) async-start(), calls=%async_computation.1 | async-start | bytes 12582912 | tf_op jit(solution)/shard_map/all_gather | solution.py:52
  169.8 5.8 %copy-start = (bf16[1024,4096]{1,0:T(8,128)(2,1)S(1)}, bf16[1024,4096]{1,0:T(8,128)(2,1)}, u32[]{:S(2)}) copy-start(bf16[1024,4096]{1,0:T(8,128)(2,1)} %all-gather.3.cloned.1.call-done) | copy-start | bytes 25165828
Sparse Core Ops, SparseCore 0:
  10.3 83.3 reduce-scatter.1
  97.0 52.5 all-gather.4
  151.1 18.6 all-gather.2
where the time goes:
time: 195 us; the launch traced here: 194 us
  waiting for transfers between devices  153 us (78%)
  between operations  13.8 us (7%)
  other arithmetic  13.7 us (7%)
  matrix products  10.1 us (5%)
    reduce_scatter x1, waiting for transfers between devices, outer_step(): summed = lax.psum_scatter(widened, 'rep', scatter_dimension=0, tiled=True)  83.5 us
    all_gather x1, waiting for transfers between devices, outer_step(): lax.all_gather(outgoing, 'rep', axis=0, tiled=True).astype(jnp.float32)  51.3 us
    all_gather x1, waiting for transfers between devices, key_layer(): lax.all_gather(tokens, 'tp', axis=1, tiled=True)  17.6 us
    dot_general x1, matrix products, key_layer(): lax.dot_general(normed, raw_grad, (((0,), (0,)), ((), ())), preferred_ele...  7.18 us
    reduce_sum x1, other arithmetic, normalize(): mean_square = jnp.mean(widened * widened, axis=-1, keepdims=True)  5.22 us
  transfers between devices with their start and end apart: 3, of which 3 were waited for; matrix products, arithmetic and copies ran while one was open for 1% of the time, Pallas kernels for 0%

commit v1 on v0

v1 whole, which is shorter than its diff:
```python
import functools
import math

import jax
import jax.numpy as jnp
from jax import lax
from jax.experimental import pallas as pl
from jax.experimental.pallas import tpu as pltpu
from jax.sharding import PartitionSpec as P

HD = 128


momentum_rate = 0.9
outer_rate = 0.7
mix_rate = 0.5
rope_base = 500000.0
norm_eps = 1e-05


def angles(row_count):
    positions = jnp.arange(row_count, dtype=jnp.float32)
    freq_table = jnp.exp(-(jnp.arange(HD // 2, dtype=jnp.float32) * 2.0 / HD) * math.log(rope_base))
    turned = positions[:, None] * freq_table[None, :]
    return (jnp.cos(turned), jnp.sin(turned))


def rotate(values, cosine, sine_vals):
    lower_half = values[:, : HD // 2]
    upper_half = values[:, HD // 2 :]
    return jnp.concatenate(
        [
            lower_half * cosine - upper_half * sine_vals,
            upper_half * cosine + lower_half * sine_vals,
        ],
        axis=-1,
    )


def swap(value, axis, offset):
    size = lax.axis_size(axis)
    return lax.ppermute(value, axis, [(i, i ^ offset) for i in range(size)])


def key_layer(tokens, norm_gain, local_weights, key_grad):
    cores = lax.axis_size("tp")
    me = lax.axis_index("tp")
    rows, part = tokens.shape
    features = part * cores
    inv_width = 1.0 / math.sqrt(features)
    cosine, sine_vals = angles(rows)

    widened = tokens.astype(jnp.float32)
    squares = jnp.sum(widened * widened, axis=-1)
    blocks = local_weights.reshape(cores, part, HD)
    weights = [lax.dynamic_index_in_dim(blocks, me, 0, keepdims=False)]
    for k in range(1, cores):
        weights.append(swap(lax.dynamic_index_in_dim(blocks, me ^ k, 0, keepdims=False), "tp", k))
    weights = jnp.concatenate(weights, axis=1)

    raw_grad = rotate(key_grad.astype(jnp.float32), cosine, -sine_vals).astype(jnp.bfloat16)
    grads = jnp.concatenate([raw_grad] + [swap(raw_grad, "tp", k) for k in range(1, cores)], axis=1)
    total = squares
    for k in range(1, cores):
        total = total + swap(squares, "tp", k)
    scale = lax.rsqrt(total / features + norm_eps)[:, None]
    normed = (widened * scale * norm_gain.astype(jnp.float32)).astype(jnp.bfloat16)

    partial = jnp.dot(normed, weights, preferred_element_type=jnp.float32)
    raw_keys = partial[:, :HD]
    for k in range(1, cores):
        raw_keys = raw_keys + swap(partial[:, k * HD : (k + 1) * HD], "tp", k)
    key_rows = rotate(raw_keys * inv_width, cosine, sine_vals).astype(jnp.bfloat16)

    contracted = lax.dot_general(
        normed, grads, (((0,), (0,)), ((), ())), preferred_element_type=jnp.float32
    )
    contracted = (contracted * inv_width).astype(jnp.bfloat16)
    weight_grad = jnp.zeros((features, HD), jnp.bfloat16)
    for k in range(cores):
        block = contracted[:, k * HD : (k + 1) * HD]
        if k:
            block = swap(block, "tp", k)
        weight_grad = lax.dynamic_update_slice(weight_grad, block, ((me ^ k) * part, 0))
    return (key_rows, weight_grad)


def merge_kernel(plane, w_ref, *refs):
    *g_refs, out_ref = refs
    me = lax.axis_index("rep")
    far = g_refs[0].shape[0]
    rows = g_refs[0].shape[1]
    for p in range(plane):
        for z in range(far):
            k = p + z * plane
            place = pl.ds(pl.multiple_of((me ^ k) * rows, rows), rows)
            w = w_ref[place, :].astype(jnp.float32)
            g = g_refs[p][z].astype(jnp.float32)
            out_ref[place, :] = (w + mix_rate * (g - w)).astype(jnp.bfloat16)


def merge(local_weights, gathered):
    vmem = pl.BlockSpec(memory_space=pltpu.VMEM)
    return pl.pallas_call(
        functools.partial(merge_kernel, len(gathered)),
        out_shape=jax.ShapeDtypeStruct(local_weights.shape, jnp.bfloat16),
        in_specs=[vmem] * (1 + len(gathered)),
        out_specs=vmem,
        compiler_params=pltpu.CompilerParams(vmem_limit_bytes=32 * 2**20),
    )(local_weights, *gathered)


def outer_step(local_weights, anchor, momentum):
    replicas = lax.axis_size("rep")
    rows = anchor.shape[0]
    chunks = local_weights.reshape(replicas, rows, HD)
    received = lax.all_to_all(chunks, "rep", 0, 0)
    mean_weights = jnp.sum(received.astype(jnp.float32), axis=0) / replicas
    change = anchor - mean_weights
    new_momentum = momentum_rate * momentum + change
    new_anchor = anchor - outer_rate * (change + momentum_rate * new_momentum)
    outgoing = new_anchor.astype(jnp.bfloat16)

    plane = 4
    far = replicas // plane
    column = jnp.stack([outgoing] + [swap(outgoing, "rep", z * plane) for z in range(1, far)])
    gathered = [column] + [swap(column, "rep", p) for p in range(1, plane)]
    merged = merge(local_weights, gathered)
    return (merged, new_anchor, new_momentum)


def body(tokens, norm_gain, local_weights, anchor, momentum, key_grad):
    key_rows, weight_grad = key_layer(tokens, norm_gain, local_weights, key_grad)
    merged, new_anchor, new_momentum = outer_step(local_weights, anchor, momentum)
    return (key_rows, weight_grad, merged, new_anchor, new_momentum)


def solution(mesh):
    split = P("rep", "tp")
    return jax.shard_map(
        body,
        mesh=mesh,
        in_specs=(split, P("tp"), split, split, split, split),
        out_specs=(split,) * 5,
        check_vma=False,
    )
```

time: 195 us -> 68.5 us (0.35)
  waiting for transfers between devices: 153 us -> 31.6 us
  starting transfers between devices: 0.12 us -> 17.5 us
  between operations: 13.8 us -> 0.83 us
  other arithmetic: 13.7 us -> 5.41 us
  matrix products: 10.1 us -> 5.35 us
  local copies, waits for them, and re-layouts: 1.53 us -> 4.78 us
  Pallas kernels: 0 us -> 2.7 us
    reduce_scatter x1 -> x0, waiting for transfers between devices: 83.5 us -> none  [outer_step(): summed = lax.psum_scatter(widened, 'rep', scatter_dimension=0, tiled=True)]
    all_gather x2 -> x0, waiting for transfers between devices: 68.9 us -> none  [the longest x1 51.3 us: outer_step(): lax.all_gather(outgoing, 'rep', axis=0, tiled=True).astype(jnp.float32)]
    all_to_all x0 -> x1, waiting for transfers between devices: none -> 16.1 us  [outer_step(): received = lax.all_to_all(chunks, 'rep', 0, 0)]
    ppermute x0 -> x11, waiting for transfers between devices: none -> 15.5 us  [swap(): return lax.ppermute(value, axis, [(i, i ^ offset) for i in range(size)])]
    ppermute x0 -> x11, starting transfers between devices: none -> 9.26 us  [swap(): return lax.ppermute(value, axis, [(i, i ^ offset) for i in range(size)])]
    all_to_all x0 -> x1, starting transfers between devices: none -> 8.2 us  [outer_step(): received = lax.all_to_all(chunks, 'rep', 0, 0)]
    convert_element_type x4 -> x2, other arithmetic: 5.41 us -> 0.05 us  [the longest x1 0.04 us: key_layer(): key_grad.astype(jnp.float32)]
    dot_general x2, matrix products: 10.1 us -> 5.35 us  [the longest x1 3.83 us: key_layer(): lax.dot_general(normed, grads, (((0,), (0,)), ((), ())), preferred_elemen...]
  transfers between devices with their start and end apart: 3 -> 12, of which waited for: 3 -> 9; matrix products, arithmetic and copies ran while one was open for 1% -> 18% of each run, Pallas kernels for 0% -> 0%
where the time goes in v1:
time: 68.5 us; the launch traced here: 68.1 us
  waiting for transfers between devices  31.6 us (46%)
  starting transfers between devices  17.5 us (26%)
  other arithmetic  5.41 us (8%)
  matrix products  5.35 us (8%)
  local copies, waits for them, and re-layouts  4.78 us (7%)
  Pallas kernels  2.7 us (4%)
  between operations  0.83 us (1%)
    all_to_all x1, waiting for transfers between devices, outer_step(): received = lax.all_to_all(chunks, 'rep', 0, 0)  16.1 us
    ppermute x11, waiting for transfers between devices, swap(): return lax.ppermute(value, axis, [(i, i ^ offset) for i in range(size)])  15.5 us
    ppermute x11, starting transfers between devices, swap(): return lax.ppermute(value, axis, [(i, i ^ offset) for i in range(size)])  9.26 us
    all_to_all x1, starting transfers between devices, outer_step(): received = lax.all_to_all(chunks, 'rep', 0, 0)  8.2 us
    dot_general x1, matrix products, key_layer(): lax.dot_general(normed, grads, (((0,), (0,)), ((), ())), preferred_elemen...  3.83 us
    reduce_sum x1, other arithmetic, key_layer(): squares = jnp.sum(widened * widened, axis=-1)  3.07 us
    pallas_call x1, Pallas kernels, merge(): pl.pallas_call(functools.partial(merge_kernel, len(gathered)), out_shape=...  2.7 us
    unnamed x12, local copies, waits for them, and re-layouts  1.96 us
  transfers between devices with their start and end apart: 12, of which 9 were waited for; matrix products, arithmetic and copies ran while one was open for 18% of the time, Pallas kernels for 0%

profile of v1, /device:TPU:0, one launch (start us, length us, event | category | flops | bytes accessed | tf_op | source)
XLA Modules:
  0.0 68.1 jit_solution(4434718552204259192)
XLA Ops:
  0.7 1.4 %dynamic-slice_bitcast_fusion.1 = (bf16[2048,128]{1,0:T(8,128)(2,1)S(1)}, bf16[2048,128]{1,0:T(8,128)(2,1)S(1)}) fusion(bf16[2,2048,128]{2,1,0:T(8,128)(2,1)} %bitcast, s32[]{:T(128)S(6)} %select_n.13, s32[]{:T(128)S(6)} %select_n.14), kind=kLoop, calls=%fused_computation.21 | loop fusion | bytes 2097160 | tf_op jit(solution)/shard_map/jit(dynamic_index_in_dim)/squeeze | solution.py:56
  2.6 3.1 %fusion = f32[1024]{0:T(1024)S(1)} fusion(bf16[1024,2048]{1,0:T(8,128)(2,1)} %param.6), kind=kLoop, calls=%fused_computation.2 | loop fusion | flops 6290432 | bytes 4198400 | tf_op jit(solution)/shard_map/reduce_sum | solution.py:54
  5.8 1.1 %collective-permute-done = f32[1024]{0:T(1024)S(1)} collective-permute-done((f32[1024]{0:T(1024)S(1)}, f32[1024]{0:T(1024)S(1)}, u32[]{:S(2)}, u32[]{:S(2)}) %collective-permute-start) | collective-permute-done | bytes 4128 | tf_op jit(solution)/shard_map/ppermute | solution.py:42
  6.9 1.5 %fusion.5 = f32[1024,256]{0,1:T(8,128)S(1)} fusion(bf16[1024,2048]{1,0:T(8,128)(2,1)S(1)} %copy-done, f32[2048]{0:T(1024)S(1)} %convert_element_type.24, f32[1024]{0:T(1024)S(1)} %add_rsqrt_fusion, bf16[2048,128]{1,0:T(8,128)(2,1)S(1)} %collective-permute-done.1, bf16[2048,128]{1,0:T(8,128)(2,1)S(1)} %get-tuple-element.15), kind=kOutput, calls=%fused_computation.8 | convolution fusion | flops 1084227584 | bytes 6303744 | tf_op jit(solution)/shard_map/dot_general | solution.py:69
  8.7 8.2 %all-to-all-start = ((bf16[16,256,128]{2,1,0:T(8,128)(2,1)}), bf16[16,256,128]{2,1,0:T(8,128)(2,1)S(1)}, u32[]{:S(2)}, u32[]{:S(2)}) async-start(bf16[16,256,128]{2,1,0:T(8,128)(2,1)} %bitcast.3), calls=%async_computation | async-start | bytes 2097152 | tf_op jit(solution)/shard_map/all_to_all | solution.py:117
  17.0 1.1 %copy.11 = bf16[1024,128]{0,1:T(8,128)(2,1)S(1)} copy(bf16[1024,128]{1,0:T(8,128)(2,1)} %param.11) | data formatting | bytes 524288 | tf_op args[5]
  18.2 1.2 %subtract_convert_fusion = (bf16[1024,64]{0,1:T(8,128)(2,1)S(1)}, bf16[1024,64]{0,1:T(8,128)(2,1)S(1)}, bf16[1024,64]{0,1:T(8,128)(2,1)S(1)}, bf16[1024,64]{0,1:T(8,128)(2,1)S(1)}) fusion(f32[1024,128]{0,1:T(8,128)S(1)} %convert_element_type.26, f32[64]{0:T(128)S(1)} %multiply_exponential_fusion, f32[1024,128]{0,1:T(8,128)S(1)} %fusion.10), kind=kLoop, calls=%fused_computation.26 | loop fusion | flops 1179648 | bytes 1573120 | tf_op jit(solution)/shard_map/convert
  19.6 1.5 %collective-permute-done.3 = bf16[1024,128]{0,1:T(8,128)(2,1)S(1)} collective-permute-done((bf16[1024,128]{0,1:T(8,128)(2,1)S(1)}, bf16[1024,128]{0,1:T(8,128)(2,1)S(1)}, u32[]{:S(2)}, u32[]{:S(2)}) %collective-permute-start.3) | collective-permute-done | bytes 262176 | tf_op jit(solution)/shard_map/ppermute | solution.py:42
  21.1 3.8 %fusion.3 = bf16[2048,256]{1,0:T(8,128)(2,1)S(1)} fusion(bf16[1024,2048]{1,0:T(8,128)(2,1)} %param.6, f32[2048]{0:T(1024)S(1)} %convert_element_type.24, f32[1024]{0:T(1024)S(1)} %add_rsqrt_fusion, bf16[1024,128]{0,1:T(8,128)(2,1)S(1)} %collective-permute-done.3, bf16[1024,64]{0,1:T(8,128)(2,1)S(1)} %get-tuple-element.18, ...), kind=kOutput, calls=%fused_computation.6 | convolution fusion | flops 1084751872 | bytes 5779456 | tf_op jit(solution)/shard_map/dot_general | solution.py:75
  25.4 16.1 %all-to-all-done = bf16[16,256,128]{2,1,0:T(8,128)(2,1)S(1)} async-done(((bf16[16,256,128]{2,1,0:T(8,128)(2,1)}), bf16[16,256,128]{2,1,0:T(8,128)(2,1)S(1)}, u32[]{:S(2)}, u32[]{:S(2)}) %all-to-all-start) | async-done | bytes 1048608 | tf_op jit(solution)/shard_map/all_to_all | solution.py:117
  41.7 0.7 %fusion.21 = (bf16[256,128]{1,0:T(8,128)(2,1)S(1)}, f32[256,128]{1,0:T(8,128)}, f32[256,128]{1,0:T(8,128)}) fusion(f32[256,128]{1,0:T(8,128)S(1)} %copy-done.2, f32[256,128]{1,0:T(8,128)S(1)} %convert_reduce_fusion, f32[256,128]{1,0:T(8,128)S(1)} %copy-done.3), kind=kLoop, calls=%fused_computation.41 | loop fusion | flops 294912 | bytes 720896 | tf_op jit(solution)/shard_map/convert_element_type | solution.py:122
  42.5 3.0 %collective-permute-start.7 = (bf16[256,128]{1,0:T(8,128)(2,1)S(1)}, bf16[256,128]{1,0:T(8,128)(2,1)S(1)}, u32[]{:S(2)}, u32[]{:S(2)}) collective-permute-start(bf16[256,128]{1,0:T(8,128)(2,1)S(1)} %get-tuple-element.10), channel_id=1, source_target_pairs={{0,24},{2,26},{4,28},{6,30},{8,16},{10,18},{12,20},{14,22},{16,8},... | collective-permute-start | bytes 196616 | tf_op jit(solution)/shard_map/ppermute | solution.py:42
  45.5 1.5 %collective-permute-start.6 = (bf16[256,128]{1,0:T(8,128)(2,1)S(1)}, bf16[256,128]{1,0:T(8,128)(2,1)S(1)}, u32[]{:S(2)}, u32[]{:S(2)}) collective-permute-start(bf16[256,128]{1,0:T(8,128)(2,1)S(1)} %get-tuple-element.10), channel_id=1, source_target_pairs={{0,16},{2,18},{4,20},{6,22},{8,24},{10,26},{12,28},{14,30},{16,0},... | collective-permute-start | bytes 196616 | tf_op jit(solution)/shard_map/ppermute | solution.py:42
  47.0 2.2 %collective-permute-done.7 = bf16[256,128]{1,0:T(8,128)(2,1)S(1)} collective-permute-done((bf16[256,128]{1,0:T(8,128)(2,1)S(1)}, bf16[256,128]{1,0:T(8,128)(2,1)S(1)}, u32[]{:S(2)}, u32[]{:S(2)}) %collective-permute-start.7) | collective-permute-done | bytes 65568 | tf_op jit(solution)/shard_map/ppermute | solution.py:42
  49.2 2.0 %collective-permute-done.6 = bf16[256,128]{1,0:T(8,128)(2,1)S(1)} collective-permute-done((bf16[256,128]{1,0:T(8,128)(2,1)S(1)}, bf16[256,128]{1,0:T(8,128)(2,1)S(1)}, u32[]{:S(2)}, u32[]{:S(2)}) %collective-permute-start.6) | collective-permute-done | bytes 65568 | tf_op jit(solution)/shard_map/ppermute | solution.py:42
  51.3 0.6 collective-permute-done.5
  52.2 2.0 %collective-permute-start.9 = (bf16[4,256,128]{2,1,0:T(8,128)(2,1)S(1)}, bf16[4,256,128]{2,1,0:T(8,128)(2,1)S(1)}, u32[]{:S(2)}, u32[]{:S(2)}) collective-permute-start(bf16[4,256,128]{2,1,0:T(8,128)(2,1)S(1)} %pad_maximum_fusion.2.refs_0_), channel_id=1, source_target_pairs={{0,4},{2,6},{4,0},{6,2},{8,12},{10,14},{12,8},{14,10},{16,20},{18,... | collective-permute-start | bytes 786440 | tf_op jit(solution)/shard_map/ppermute | solution.py:42
  54.2 1.3 %collective-permute-start.10 = (bf16[4,256,128]{2,1,0:T(8,128)(2,1)S(1)}, bf16[4,256,128]{2,1,0:T(8,128)(2,1)S(1)}, u32[]{:S(2)}, u32[]{:S(2)}) collective-permute-start(bf16[4,256,128]{2,1,0:T(8,128)(2,1)S(1)} %pad_maximum_fusion.2.refs_0_), channel_id=1, source_target_pairs={{0,6},{2,4},{4,2},{6,0},{8,14},{10,12},{12,10},{14,8},{16,22},{18,... | collective-permute-start | bytes 786440 | tf_op jit(solution)/shard_map/ppermute | solution.py:42
  55.5 0.8 %copy.12 = bf16[1024,128]{1,0:T(8,128)(2,1)} copy(bf16[1024,128]{0,1:T(8,128)(2,1)S(1)} %pad_maximum_fusion) | data formatting | bytes 524288
  56.4 1.1 %constant_dynamic-update-slice_fusion = bf16[4096,128]{1,0:T(8,128)(2,1)S(1)} fusion(bf16[4096,128]{1,0:T(8,128)(2,1)S(1)} %get-tuple-element.14, bf16[2048,128]{1,0:T(8,128)(2,1)} %collective-permute-done.4, s32[]{:T(128)S(6)} %select_n.16), kind=kLoop, calls=%fused_computation.37 | loop fusion | bytes 1048580 | tf_op jit(solution)/shard_map/dynamic_update_slice | solution.py:84
  57.5 2.8 %collective-permute-done.8.refs_1_ = bf16[4,256,128]{2,1,0:T(8,128)(2,1)S(1)} collective-permute-done((bf16[4,256,128]{2,1,0:T(8,128)(2,1)S(1)}, bf16[4,256,128]{2,1,0:T(8,128)(2,1)S(1)}, u32[]{:S(2)}, u32[]{:S(2)}) %collective-permute-start.8) | collective-permute-done | bytes 262176 | tf_op jit(solution)/shard_map/ppermute | solution.py:42
  60.3 3.7 %collective-permute-done.9.refs_2_ = bf16[4,256,128]{2,1,0:T(8,128)(2,1)S(1)} collective-permute-done((bf16[4,256,128]{2,1,0:T(8,128)(2,1)S(1)}, bf16[4,256,128]{2,1,0:T(8,128)(2,1)S(1)}, u32[]{:S(2)}, u32[]{:S(2)}) %collective-permute-start.9) | collective-permute-done | bytes 262176 | tf_op jit(solution)/shard_map/ppermute | solution.py:42
  64.0 1.5 %collective-permute-done.10.refs_3_ = bf16[4,256,128]{2,1,0:T(8,128)(2,1)S(1)} collective-permute-done((bf16[4,256,128]{2,1,0:T(8,128)(2,1)S(1)}, bf16[4,256,128]{2,1,0:T(8,128)(2,1)S(1)}, u32[]{:S(2)}, u32[]{:S(2)}) %collective-permute-start.10) | collective-permute-done | bytes 262176 | tf_op jit(solution)/shard_map/ppermute | solution.py:42
  65.4 2.7 %shard_map.101 = bf16[4096,128]{1,0:T(8,128)(2,1)} custom-call(bf16[4096,128]{1,0:T(8,128)(2,1)} %w_ref.1, bf16[4,256,128]{2,1,0:T(8,128)(2,1)S(1)} %pad_maximum_fusion.2.refs_0_, bf16[4,256,128]{2,1,0:T(8,128)(2,1)S(1)} %collective-permute-done.8.refs_1_, bf16[4,256,128]{2,1,0:T(8,128)(2,1)S(1)} %collective-permute-done.9.refs_2_, ...), custom_call_target="tpu_custom_call" | custom-call | tf_op jit(solution)/shard_map/pallas_call | solution.py:104
  (32 shorter events, 2.1 us)
Async XLA Ops:
  0.6 5.2 %copy-start.4 = (bf16[2048]{0:T(1024)(128)(2,1)S(1)}, bf16[2048]{0:T(1024)(128)(2,1)}, u32[]{:S(2)}) copy-start(bf16[2048]{0:T(1024)(128)(2,1)} %param.7) | copy-start | bytes 12292
  0.7 6.3 %copy-start = (bf16[1024,2048]{1,0:T(8,128)(2,1)S(1)}, bf16[1024,2048]{1,0:T(8,128)(2,1)}, u32[]{:S(2)}) copy-start(bf16[1024,2048]{1,0:T(8,128)(2,1)} %param.6) | copy-start | bytes 12582916
  2.1 4.8 %collective-permute-start.1 = (bf16[2048,128]{1,0:T(8,128)(2,1)S(1)}, bf16[2048,128]{1,0:T(8,128)(2,1)S(1)}, u32[]{:S(2)}, u32[]{:S(2)}) collective-permute-start(bf16[2048,128]{1,0:T(8,128)(2,1)S(1)} %get-tuple-element.16), channel_id=1, source_target_pairs={{0,1},{1,0},{2,3},{3,2},{4,5},{5,4},{6,7},{7,6},{8,9},{9,8},{10,11... | collective-permute-start | bytes 1572872 | tf_op jit(solution)/shard_map/ppermute | solution.py:42
  5.7 1.2 %collective-permute-start = (f32[1024]{0:T(1024)S(1)}, f32[1024]{0:T(1024)S(1)}, u32[]{:S(2)}, u32[]{:S(2)}) collective-permute-start(f32[1024]{0:T(1024)S(1)} %fusion), channel_id=1, source_target_pairs={{0,1},{1,0},{2,3},{3,2},{4,5},{5,4},{6,7},{7,6},{8,9},{9,8},{10,11... | collective-permute-start | bytes 12296 | tf_op jit(solution)/shard_map/ppermute | solution.py:42
  8.5 9.6 %collective-permute-start.2 = (f32[1024,128]{0,1:T(8,128)S(1)}, f32[1024,128]{0,1:T(8,128)S(1)}, u32[]{:S(2)}, u32[]{:S(2)}) collective-permute-start(f32[1024,128]{0,1:T(8,128)S(1)} %slice.33), channel_id=1, source_target_pairs={{0,1},{1,0},{2,3},{3,2},{4,5},{5,4},{6,7},{7,6},{8,9},{9,8},{10,11... | collective-permute-start | bytes 1572872 | tf_op jit(solution)/shard_map/ppermute | solution.py:42
  8.7 32.8 %all-to-all-start = ((bf16[16,256,128]{2,1,0:T(8,128)(2,1)}), bf16[16,256,128]{2,1,0:T(8,128)(2,1)S(1)}, u32[]{:S(2)}, u32[]{:S(2)}) async-start(bf16[16,256,128]{2,1,0:T(8,128)(2,1)} %bitcast.3), calls=%async_computation | async-start | bytes 2097152 | tf_op jit(solution)/shard_map/all_to_all | solution.py:117
  19.5 1.6 %collective-permute-start.3 = (bf16[1024,128]{0,1:T(8,128)(2,1)S(1)}, bf16[1024,128]{0,1:T(8,128)(2,1)S(1)}, u32[]{:S(2)}, u32[]{:S(2)}) collective-permute-start(bf16[1024,128]{0,1:T(8,128)(2,1)S(1)} %pad_maximum_fusion.1), channel_id=1, source_target_pairs={{0,1},{1,0},{2,3},{3,2},{4,5},{5,4},{6,7},{7,6},{8,9},{9,8},{10,11... | collective-permute-start | bytes 786440 | tf_op jit(solution)/shard_map/ppermute | solution.py:42
  24.9 16.8 %copy-start.2 = (f32[256,128]{1,0:T(8,128)S(1)}, f32[256,128]{1,0:T(8,128)}, u32[]{:S(2)}) copy-start(f32[256,128]{1,0:T(8,128)} %param.9) | copy-start | bytes 393220
  24.9 16.8 %copy-start.3 = (f32[256,128]{1,0:T(8,128)S(1)}, f32[256,128]{1,0:T(8,128)}, u32[]{:S(2)}) copy-start(f32[256,128]{1,0:T(8,128)} %param.10) | copy-start | bytes 393220
  25.2 31.2 %collective-permute-start.4 = (bf16[2048,128]{1,0:T(8,128)(2,1)S(1)}, bf16[2048,128]{1,0:T(8,128)(2,1)}, u32[]{:S(2)}, u32[]{:S(2)}) collective-permute-start(bf16[2048,128]{1,0:T(8,128)(2,1)S(1)} %get-tuple-element.13), channel_id=1, source_target_pairs={{0,1},{1,0},{2,3},{3,2},{4,5},{5,4},{6,7},{7,6},{8,9},{9,8},{10,11... | collective-permute-start | bytes 1572872 | tf_op jit(solution)/shard_map/ppermute | solution.py:42
  42.5 6.8 %collective-permute-start.7 = (bf16[256,128]{1,0:T(8,128)(2,1)S(1)}, bf16[256,128]{1,0:T(8,128)(2,1)S(1)}, u32[]{:S(2)}, u32[]{:S(2)}) collective-permute-start(bf16[256,128]{1,0:T(8,128)(2,1)S(1)} %get-tuple-element.10), channel_id=1, source_target_pairs={{0,24},{2,26},{4,28},{6,30},{8,16},{10,18},{12,20},{14,22},{16,8},... | collective-permute-start | bytes 196616 | tf_op jit(solution)/shard_map/ppermute | solution.py:42
  45.5 5.7 %collective-permute-start.6 = (bf16[256,128]{1,0:T(8,128)(2,1)S(1)}, bf16[256,128]{1,0:T(8,128)(2,1)S(1)}, u32[]{:S(2)}, u32[]{:S(2)}) collective-permute-start(bf16[256,128]{1,0:T(8,128)(2,1)S(1)} %get-tuple-element.10), channel_id=1, source_target_pairs={{0,16},{2,18},{4,20},{6,22},{8,24},{10,26},{12,28},{14,30},{16,0},... | collective-permute-start | bytes 196616 | tf_op jit(solution)/shard_map/ppermute | solution.py:42
  47.0 4.9 %collective-permute-start.5 = (bf16[256,128]{1,0:T(8,128)(2,1)S(1)}, bf16[256,128]{1,0:T(8,128)(2,1)S(1)}, u32[]{:S(2)}, u32[]{:S(2)}) collective-permute-start(bf16[256,128]{1,0:T(8,128)(2,1)S(1)} %get-tuple-element.10), channel_id=1, source_target_pairs={{0,8},{2,10},{4,12},{6,14},{8,0},{10,2},{12,4},{14,6},{16,24},{18,... | collective-permute-start | bytes 196616 | tf_op jit(solution)/shard_map/ppermute | solution.py:42
  51.9 8.3 %collective-permute-start.8 = (bf16[4,256,128]{2,1,0:T(8,128)(2,1)S(1)}, bf16[4,256,128]{2,1,0:T(8,128)(2,1)S(1)}, u32[]{:S(2)}, u32[]{:S(2)}) collective-permute-start(bf16[4,256,128]{2,1,0:T(8,128)(2,1)S(1)} %pad_maximum_fusion.2.refs_0_), channel_id=1, source_target_pairs={{0,2},{2,0},{4,6},{6,4},{8,10},{10,8},{12,14},{14,12},{16,18},{18,... | collective-permute-start | bytes 786440 | tf_op jit(solution)/shard_map/ppermute | solution.py:42
  52.2 11.8 %collective-permute-start.9 = (bf16[4,256,128]{2,1,0:T(8,128)(2,1)S(1)}, bf16[4,256,128]{2,1,0:T(8,128)(2,1)S(1)}, u32[]{:S(2)}, u32[]{:S(2)}) collective-permute-start(bf16[4,256,128]{2,1,0:T(8,128)(2,1)S(1)} %pad_maximum_fusion.2.refs_0_), channel_id=1, source_target_pairs={{0,4},{2,6},{4,0},{6,2},{8,12},{10,14},{12,8},{14,10},{16,20},{18,... | collective-permute-start | bytes 786440 | tf_op jit(solution)/shard_map/ppermute | solution.py:42
  54.2 11.2 %collective-permute-start.10 = (bf16[4,256,128]{2,1,0:T(8,128)(2,1)S(1)}, bf16[4,256,128]{2,1,0:T(8,128)(2,1)S(1)}, u32[]{:S(2)}, u32[]{:S(2)}) collective-permute-start(bf16[4,256,128]{2,1,0:T(8,128)(2,1)S(1)} %pad_maximum_fusion.2.refs_0_), channel_id=1, source_target_pairs={{0,6},{2,4},{4,2},{6,0},{8,14},{10,12},{12,10},{14,8},{16,22},{18,... | collective-permute-start | bytes 786440 | tf_op jit(solution)/shard_map/ppermute | solution.py:42
  57.5 10.7 %copy-start.1 = (bf16[4096,128]{1,0:T(8,128)(2,1)}, bf16[4096,128]{1,0:T(8,128)(2,1)S(1)}, u32[]{:S(2)}) copy-start(bf16[4096,128]{1,0:T(8,128)(2,1)S(1)} %constant_dynamic-update-slice_fusion) | copy-start | bytes 3145732

commit v2 on v1

v2 whole, which is shorter than its diff:
```python
import functools
import math

import jax
import jax.numpy as jnp
from jax import lax
from jax.experimental import pallas as pl
from jax.experimental.pallas import tpu as pltpu
from jax.sharding import PartitionSpec as P

HD = 128
PLANE = 4


momentum_rate = 0.9
outer_rate = 0.7
mix_rate = 0.5
rope_base = 500000.0
norm_eps = 1e-05


def angles(row_count):
    positions = jnp.arange(row_count, dtype=jnp.float32)
    freq_table = jnp.exp(-(jnp.arange(HD // 2, dtype=jnp.float32) * 2.0 / HD) * math.log(rope_base))
    turned = positions[:, None] * freq_table[None, :]
    return (jnp.cos(turned), jnp.sin(turned))


def rotate(values, cosine, sine_vals):
    lower_half = values[:, : HD // 2]
    upper_half = values[:, HD // 2 :]
    return jnp.concatenate(
        [
            lower_half * cosine - upper_half * sine_vals,
            upper_half * cosine + lower_half * sine_vals,
        ],
        axis=-1,
    )


def swap(value, axis, offset):
    size = lax.axis_size(axis)
    return lax.ppermute(value, axis, [(i, i ^ offset) for i in range(size)])


def share_weights(local_weights):
    cores = lax.axis_size("tp")
    me = lax.axis_index("tp")
    blocks = local_weights.reshape(cores, -1, HD)
    weights = [lax.dynamic_index_in_dim(blocks, me, 0, keepdims=False)]
    for k in range(1, cores):
        weights.append(swap(lax.dynamic_index_in_dim(blocks, me ^ k, 0, keepdims=False), "tp", k))
    return weights


def normalize(tokens, total, norm_gain):
    features = tokens.shape[1] * lax.axis_size("tp")
    scale = lax.rsqrt(total / features + norm_eps)[:, None]
    return (tokens.astype(jnp.float32) * scale * norm_gain.astype(jnp.float32)).astype(jnp.bfloat16)


def place_blocks(blocks):
    me = lax.axis_index("tp")
    part = blocks[0].shape[0]
    whole = jnp.zeros((len(blocks) * part, HD), blocks[0].dtype)
    for k, block in enumerate(blocks):
        whole = lax.dynamic_update_slice(whole, block, ((me ^ k) * part, 0))
    return whole


def pick_kernel(groups, w_ref, *refs):
    *out_refs, sems = refs
    me = lax.axis_index("rep")
    rows = out_refs[0].shape[1]
    copies = []
    for g, group in enumerate(groups):
        for p in range(PLANE):
            for i, z in enumerate(group):
                place = pl.ds(pl.multiple_of((me ^ (z * PLANE + p)) * rows, rows), rows)
                out = out_refs[g * PLANE + p].at[i]
                copies.append(pltpu.make_async_copy(w_ref.at[place, :], out, sems.at[len(copies)]))
    for copy in copies:
        copy.start()
    for copy in copies:
        copy.wait()


def pick(local_weights, rows, groups):
    shapes = [
        jax.ShapeDtypeStruct((len(group), rows, HD), local_weights.dtype)
        for group in groups
        for _ in range(PLANE)
    ]
    out = pl.pallas_call(
        functools.partial(pick_kernel, groups),
        out_shape=shapes,
        in_specs=[pl.BlockSpec(memory_space=pl.ANY)],
        out_specs=[pl.BlockSpec(memory_space=pltpu.VMEM)] * len(shapes),
        scratch_shapes=[pltpu.SemaphoreType.DMA((PLANE * sum(map(len, groups)),))],
    )(local_weights)
    return [out[g * PLANE : (g + 1) * PLANE] for g in range(len(groups))]


def merge_kernel(order, w_ref, *refs):
    out_ref, w_buf, out_buf, in_sems, out_sems = refs[-5:]
    me = lax.axis_index("rep")
    rows = refs[0].shape[0]
    places = [pl.ds(pl.multiple_of((me ^ k) * rows, rows), rows) for k in order]
    loads = [
        pltpu.make_async_copy(w_ref.at[place, :], w_buf.at[i], in_sems.at[i])
        for i, place in enumerate(places)
    ]
    stores = [
        pltpu.make_async_copy(out_buf.at[i], out_ref.at[place, :], out_sems.at[i])
        for i, place in enumerate(places)
    ]
    for load in loads:
        load.start()
    for i, (load, store) in enumerate(zip(loads, stores)):
        load.wait()
        w = w_buf[i].astype(jnp.float32)
        g = refs[i][...].astype(jnp.float32)
        out_buf[i] = (w + mix_rate * (g - w)).astype(jnp.bfloat16)
        store.start()
    for store in stores:
        store.wait()


def merge(local_weights, chunks, base=None):
    order = tuple(chunks)
    rows = chunks[order[0]].shape[0]
    anywhere = pl.BlockSpec(memory_space=pl.ANY)
    vmem = pl.BlockSpec(memory_space=pltpu.VMEM)
    args = [local_weights, *chunks.values()]
    specs = [anywhere] + [vmem] * len(order)
    aliases = {}
    if base is not None:
        aliases = {len(args): 0}
        args.append(base)
        specs.append(anywhere)
    count = len(order)
    return pl.pallas_call(
        functools.partial(merge_kernel, order),
        out_shape=jax.ShapeDtypeStruct(local_weights.shape, jnp.bfloat16),
        in_specs=specs,
        out_specs=anywhere,
        scratch_shapes=[
            pltpu.VMEM((count, rows, HD), jnp.bfloat16),
            pltpu.VMEM((count, rows, HD), jnp.bfloat16),
            pltpu.SemaphoreType.DMA((count,)),
            pltpu.SemaphoreType.DMA((count,)),
        ],
        input_output_aliases=aliases,
    )(*args)


def after(*values):
    return lax.optimization_barrier(values)


def body(tokens, norm_gain, local_weights, anchor, momentum, key_grad):
    cores = lax.axis_size("tp")
    replicas = lax.axis_size("rep")
    far = replicas // PLANE
    inv_width = 1.0 / math.sqrt(tokens.shape[1] * cores)
    step = max(far // 4, 1)
    zs = list(range(far - 1, -1, -1))
    groups = [zs[:step], zs[step : 2 * step], zs[2 * step :]]

    picked = pick(local_weights, anchor.shape[0], groups)
    picked, tokens, local_weights_tp = after(picked, tokens, local_weights)
    plane = [[swap(group[p], "rep", p) for p in (3, 1, 2)] for group in picked]

    def sum_plane(own, parts):
        total = own.astype(jnp.float32)
        for part in parts:
            total = total + part.astype(jnp.float32)
        return total

    def send_far(group, total):
        return [swap(total[i], "rep", z * PLANE) if z else total[i] for i, z in enumerate(group)]

    weights = share_weights(local_weights_tp)
    widened = tokens.astype(jnp.float32)
    squares = jnp.sum(widened * widened, axis=-1)

    squares, plane[0], key_grad = after(squares, plane[0], key_grad)
    sums = send_far(groups[0], sum_plane(picked[0][0], plane[0]))
    total = squares
    for k in range(1, cores):
        total = total + swap(squares, "tp", k)
    cosine, sine_vals = angles(tokens.shape[0])
    raw_grad = rotate(key_grad.astype(jnp.float32), cosine, -sine_vals).astype(jnp.bfloat16)

    raw_grad, plane[1], total, tokens = after(raw_grad, plane[1], total, tokens)
    sums += send_far(groups[1], sum_plane(picked[1][0], plane[1]))
    grads = jnp.concatenate([raw_grad] + [swap(raw_grad, "tp", k) for k in range(1, cores)], axis=1)
    normed = normalize(tokens, total, norm_gain)
    partial = jnp.dot(normed, jnp.concatenate(weights, axis=1), preferred_element_type=jnp.float32)

    partial, plane[2], tokens, grads = after(partial, plane[2], tokens, grads)
    sums += send_far(groups[2], sum_plane(picked[2][0], plane[2]))
    raw_keys = partial[:, :HD]
    for k in range(1, cores):
        raw_keys = raw_keys + swap(partial[:, k * HD : (k + 1) * HD], "tp", k)
    normed = normalize(tokens, total, norm_gain)
    contracted = lax.dot_general(
        normed, grads, (((0,), (0,)), ((), ())), preferred_element_type=jnp.float32
    )
    contracted = (contracted * inv_width).astype(jnp.bfloat16)

    contracted, sums, raw_keys = after(contracted, sums, raw_keys)
    mean_weights = sum(sums) / replicas
    change = anchor - mean_weights
    new_momentum = momentum_rate * momentum + change
    new_anchor = anchor - outer_rate * (change + momentum_rate * new_momentum)
    outgoing = new_anchor.astype(jnp.bfloat16)

    near = [outgoing] + [swap(outgoing, "rep", p) for p in range(1, PLANE)]
    columns = [swap(outgoing, "rep", z * PLANE) for z in range(1, far)]
    key_rows = rotate(raw_keys * inv_width, cosine, sine_vals).astype(jnp.bfloat16)
    blocks = [contracted[:, :HD]]
    for k in range(1, cores):
        blocks.append(swap(contracted[:, k * HD : (k + 1) * HD], "tp", k))
    weight_grad = place_blocks(blocks)

    gathered = dict(enumerate(near))
    late = {}
    split = far // 4
    for part, start in ((columns[:split], 1), (columns[split:], 1 + split)):
        block = jnp.stack(part)
        late = {}
        for p in range(PLANE):
            moved = swap(block, "rep", p) if p else block
            for i in range(len(part)):
                late[(start + i) * PLANE + p] = moved[i]
        if start == 1:
            gathered.update(late)
    merged = merge(local_weights, gathered)
    merged = merge(local_weights, late, merged)
    return (key_rows, weight_grad, merged, new_anchor, new_momentum)


def solution(mesh):
    split = P("rep", "tp")
    return jax.shard_map(
        body,
        mesh=mesh,
        in_specs=(split, P("tp"), split, split, split, split),
        out_specs=(split,) * 5,
        check_vma=False,
    )
```

time: 68.5 us -> 70.1 us (1.023)
  waiting for transfers between devices: 31.6 us -> 12.5 us
  starting transfers between devices: 17.5 us -> 30.9 us
  Pallas kernels: 2.7 us -> 8.27 us
  other arithmetic: 5.41 us -> 9.66 us
  matrix products: 5.35 us -> 3.17 us
    ppermute x11 -> x29, starting transfers between devices: 9.26 us -> 30.9 us  [swap(): return lax.ppermute(value, axis, [(i, i ^ offset) for i in range(size)])]
    all_to_all x1 -> x0, waiting for transfers between devices: 16.1 us -> none  [outer_step(): received = lax.all_to_all(chunks, 'rep', 0, 0)]
    all_to_all x1 -> x0, starting transfers between devices: 8.2 us -> none  [outer_step(): received = lax.all_to_all(chunks, 'rep', 0, 0)]
    pallas_call x1 -> x3, Pallas kernels: 2.7 us -> 8.27 us  [the longest x2 5.83 us: merge(): pl.pallas_call(functools.partial(merge_kernel, order), out_shape=jax.Shap...]
    another operation x2 -> x3, other arithmetic: 1.28 us -> 4.43 us
    ppermute x11 -> x29, waiting for transfers between devices: 15.5 us -> 12.5 us  [swap(): return lax.ppermute(value, axis, [(i, i ^ offset) for i in range(size)])]
    dot_general x2, matrix products: 5.35 us -> 3.17 us  [the longest x1 1.85 us: body(): lax.dot_general(normed, grads, (((0,), (0,)), ((), ())), preferred_elemen...]
    dynamic_update_slice x1, local copies, waits for them, and re-layouts: 1.11 us -> 0.07 us  [place_blocks(): whole = lax.dynamic_update_slice(whole, block, ((me ^ k) * part, 0))]
  transfers between devices with their start and end apart: 12 -> 29, of which waited for: 9 -> 7; matrix products, arithmetic and copies ran while one was open for 18% -> 21% of each run, Pallas kernels for 0% -> 8%
where the time goes in v2:
time: 70.1 us; the launch traced here: 69.7 us
  starting transfers between devices  30.9 us (44%)
  waiting for transfers between devices  12.5 us (18%)
  other arithmetic  9.66 us (14%)
  Pallas kernels  8.27 us (12%)
  local copies, waits for them, and re-layouts  4.09 us (6%)
  matrix products  3.17 us (5%)
  between operations  1.11 us (2%)
    ppermute x29, starting transfers between devices, swap(): return lax.ppermute(value, axis, [(i, i ^ offset) for i in range(size)])  30.9 us
    ppermute x29, waiting for transfers between devices, swap(): return lax.ppermute(value, axis, [(i, i ^ offset) for i in range(size)])  12.5 us
    pallas_call x2, Pallas kernels, merge(): pl.pallas_call(functools.partial(merge_kernel, order), out_shape=jax.Shap...  5.83 us
    another operation x2, other arithmetic  4.42 us
    reduce_sum x1, other arithmetic, body(): squares = jnp.sum(widened * widened, axis=-1)  3.13 us
    pallas_call x1, Pallas kernels, pick(): pl.pallas_call(functools.partial(pick_kernel, groups), out_shape=shapes,...  2.44 us
    squeeze x3, local copies, waits for them, and re-layouts, body(): late[(start + i) * PLANE + p] = moved[i]  2 us
    dot_general x1, matrix products, body(): lax.dot_general(normed, grads, (((0,), (0,)), ((), ())), preferred_elemen...  1.85 us
  transfers between devices with their start and end apart: 29, of which 7 were waited for; matrix products, arithmetic and copies ran while one was open for 21% of the time, Pallas kernels for 8%

profile of v2, /device:TPU:0, one launch (start us, length us, event | category | flops | bytes accessed | tf_op | source)
XLA Modules:
  0.0 69.7 jit_solution(17841872516749314298)
XLA Ops:
  0.7 2.4 %shard_map.101 = (bf16[1,256,128]{2,1,0:T(8,128)(2,1)}, bf16[1,256,128]{2,1,0:T(8,128)(2,1)}, bf16[1,256,128]{2,1,0:T(8,128)(2,1)}, bf16[1,256,128]{2,1,0:T(8,12...) custom-call(bf16[4096,128]{1,0:T(8,128)(2,1)} %w_ref.5), custom_call_target="tpu_custom_call" | custom-call | tf_op jit(solution)/shard_map/pallas_call | solution.py:94
  3.1 4.0 %collective-permute-start = (bf16[1,256,128]{2,1,0:T(8,128)(2,1)}, bf16[1,256,128]{2,1,0:T(8,128)(2,1)S(1)}, u32[]{:S(2)}, u32[]{:S(2)}) collective-permute-start(bf16[1,256,128]{2,1,0:T(8,128)(2,1)} %get-tuple-element.67), channel_id=1, source_target_pairs={{0,6},{2,4},{4,2},{6,0},{8,14},{10,12},{12,10},{14,8},{16,22},{18,... | collective-permute-start | bytes 196616 | tf_op jit(solution)/shard_map/ppermute | solution.py:43
  7.7 2.8 %collective-permute-start.3 = (bf16[1,256,128]{2,1,0:T(8,128)(2,1)}, bf16[1,256,128]{2,1,0:T(8,128)(2,1)S(1)}, u32[]{:S(2)}, u32[]{:S(2)}) collective-permute-start(bf16[1,256,128]{2,1,0:T(8,128)(2,1)} %get-tuple-element.71), channel_id=1, source_target_pairs={{0,6},{2,4},{4,2},{6,0},{8,14},{10,12},{12,10},{14,8},{16,22},{18,... | collective-permute-start | bytes 196616 | tf_op jit(solution)/shard_map/ppermute | solution.py:43
  11.1 3.1 %multiply_reduce_fusion = f32[1024]{0:T(1024)S(1)} fusion(bf16[1024,2048]{1,0:T(8,128)(2,1)} %param.6), kind=kLoop, calls=%fused_computation.2 | loop fusion | flops 6290432 | bytes 4198400 | tf_op jit(solution)/shard_map/reduce_sum | solution.py:185
  15.2 2.2 %subtract_convert_fusion.1 = (bf16[1024,64]{1,0:T(8,128)(2,1)S(1)}, bf16[1024,64]{1,0:T(8,128)(2,1)S(1)}) fusion(f32[1024,128]{1,0:T(8,128)S(1)} %convert_element_type.67, f32[64]{0:T(128)S(1)} %multiply_exponential_fusion), kind=kLoop, calls=%fused_computation.22 | loop fusion | flops 655360 | bytes 786688 | tf_op jit(solution)/shard_map/convert.2
  17.7 2.9 %collective-permute-start.8 = (bf16[2,256,128]{2,1,0:T(8,128)(2,1)S(1)}, bf16[2,256,128]{2,1,0:T(8,128)(2,1)S(1)}, u32[]{:S(2)}, u32[]{:S(2)}) collective-permute-start(bf16[2,256,128]{2,1,0:T(8,128)(2,1)S(1)} %copy-done.22), channel_id=1, source_target_pairs={{0,6},{2,4},{4,2},{6,0},{8,14},{10,12},{12,10},{14,8},{16,22},{18,... | collective-permute-start | bytes 393224 | tf_op jit(solution)/shard_map/ppermute | solution.py:43
  21.4 1.5 %collective-permute-done.11 = bf16[1024,128]{1,0:T(8,128)(2,1)S(1)} collective-permute-done((bf16[1024,128]{1,0:T(8,128)(2,1)S(1)}, bf16[1024,128]{1,0:T(8,128)(2,1)S(1)}, u32[]{:S(2)}, u32[]{:S(2)}) %collective-permute-start.11) | collective-permute-done | bytes 262176 | tf_op jit(solution)/shard_map/ppermute | solution.py:43
  22.9 4.0 %collective-permute-start.12 = (f32[256,128]{1,0:T(8,128)S(1)}, f32[256,128]{1,0:T(8,128)S(1)}, u32[]{:S(2)}, u32[]{:S(2)}) collective-permute-start(f32[256,128]{1,0:T(8,128)S(1)} %add_bitcast_fusion.1), channel_id=1, source_target_pairs={{0,24},{2,26},{4,28},{6,30},{8,16},{10,18},{12,20},{14,22},{16,8},... | collective-permute-start | bytes 393224 | tf_op jit(solution)/shard_map/ppermute | solution.py:43
  27.1 1.3 %fusion = f32[1024,256]{1,0:T(8,128)S(1)} fusion(bf16[1024,2048]{1,0:T(8,128)(2,1)S(1)} %copy-done.1, f32[2048]{0:T(1024)S(1)} %convert_element_type.69, f32[1024]{0:T(1024)S(1)} %add_rsqrt_fusion, bf16[2048,128]{1,0:T(8,128)(2,1)S(1)} %collective-permute-done.7, bf16[2048,128]{1,0:T(8,128)(2,1)S(1)} %get-tuple-element.108), kind=kOutput, calls=%fused_computation.3 | convolution fusion | flops 1084227584 | bytes 6303744 | tf_op jit(solution)/shard_map/dot_general | solution.py:199
  29.3 1.9 %fusion.7 = bf16[2048,256]{1,0:T(8,128)(2,1)S(1)} fusion(bf16[1024,256]{1,0:T(8,128)(2,1)S(1)} %pad_maximum_fusion, bf16[1024,2048]{1,0:T(8,128)(2,1)S(1)} %copy-done.1, f32[2048]{0:T(1024)S(1)} %convert_element_type.69, f32[1024]{0:T(1024)S(1)} %add_rsqrt_fusion), kind=kOutput, calls=%fused_computation.10 | convolution fusion | flops 1083179008 | bytes 5779456 | tf_op jit(solution)/shard_map/dot_general | solution.py:207
  31.3 7.0 %collective-permute-done.13 = f32[256,128]{1,0:T(8,128)S(1)} collective-permute-done((f32[256,128]{1,0:T(8,128)S(1)}, f32[256,128]{1,0:T(8,128)S(1)}, u32[]{:S(2)}, u32[]{:S(2)}) %collective-permute-start.13) | collective-permute-done | bytes 131104 | tf_op jit(solution)/shard_map/ppermute | solution.py:43
  39.0 2.5 %collective-permute-start.18 = (bf16[256,128]{1,0:T(8,128)(2,1)S(1)}, bf16[256,128]{1,0:T(8,128)(2,1)S(1)}, u32[]{:S(2)}, u32[]{:S(2)}) collective-permute-start(bf16[256,128]{1,0:T(8,128)(2,1)S(1)} %get-tuple-element.103.refs_0_), channel_id=1, source_target_pairs={{0,24},{2,26},{4,28},{6,30},{8,16},{10,18},{12,20},{14,22},{16,8},... | collective-permute-start | bytes 196616 | tf_op jit(solution)/shard_map/ppermute | solution.py:43
  41.5 1.5 %collective-permute-start.22 = (bf16[256,128]{1,0:T(8,128)(2,1)S(1)}, bf16[256,128]{1,0:T(8,128)(2,1)S(1)}, u32[]{:S(2)}, u32[]{:S(2)}) collective-permute-start(bf16[256,128]{1,0:T(8,128)(2,1)S(1)} %get-tuple-element.103.refs_0_), channel_id=1, source_target_pairs={{0,2},{2,0},{4,6},{6,4},{8,10},{10,8},{12,14},{14,12},{16,18},{18,... | collective-permute-start | bytes 196616 | tf_op jit(solution)/shard_map/ppermute | solution.py:43
  43.0 1.5 %collective-permute-start.23 = (bf16[256,128]{1,0:T(8,128)(2,1)S(1)}, bf16[256,128]{1,0:T(8,128)(2,1)S(1)}, u32[]{:S(2)}, u32[]{:S(2)}) collective-permute-start(bf16[256,128]{1,0:T(8,128)(2,1)S(1)} %get-tuple-element.103.refs_0_), channel_id=1, source_target_pairs={{0,4},{2,6},{4,0},{6,2},{8,12},{10,14},{12,8},{14,10},{16,20},{18,... | collective-permute-start | bytes 196616 | tf_op jit(solution)/shard_map/ppermute | solution.py:43
  45.3 1.0 %collective-permute-done.17.refs_0_ = bf16[256,128]{1,0:T(8,128)(2,1)S(1)} collective-permute-done((bf16[256,128]{1,0:T(8,128)(2,1)S(1)}, bf16[256,128]{1,0:T(8,128)(2,1)S(1)}, u32[]{:S(2)}, u32[]{:S(2)}) %collective-permute-start.17) | collective-permute-done | bytes 65568 | tf_op jit(solution)/shard_map/ppermute | solution.py:43
  46.4 1.6 %collective-permute-start.19 = (bf16[2,256,128]{2,1,0:T(8,128)(2,1)S(1)}, bf16[2,256,128]{2,1,0:T(8,128)(2,1)S(1)}, u32[]{:S(2)}, u32[]{:S(2)}) collective-permute-start(bf16[2,256,128]{2,1,0:T(8,128)(2,1)S(1)} %pad_maximum_fusion.3), channel_id=1, source_target_pairs={{0,2},{2,0},{4,6},{6,4},{8,10},{10,8},{12,14},{14,12},{16,18},{18,... | collective-permute-start | bytes 393224 | tf_op jit(solution)/shard_map/ppermute | solution.py:43
  48.0 2.2 %subtract_convert_fusion = (bf16[1024,64]{1,0:T(8,128)(2,1)S(1)}, bf16[1024,64]{1,0:T(8,128)(2,1)S(1)}) fusion(f32[1024,128]{1,0:T(8,128)S(1)} %broadcast_multiply_fusion, f32[64]{0:T(128)S(1)} %multiply_exponential_fusion), kind=kLoop, calls=%fused_computation.17 | loop fusion | flops 589824 | bytes 786688 | tf_op jit(solution)/shard_map/convert
  50.6 1.5 %collective-permute-start.26 = (bf16[1,256,128]{2,1,0:T(8,128)(2,1)S(1)}, bf16[1,256,128]{2,1,0:T(8,128)(2,1)S(1)}, u32[]{:S(2)}, u32[]{:S(2)}) collective-permute-start(bf16[1,256,128]{2,1,0:T(8,128)(2,1)S(1)} %bitcast.35), channel_id=1, source_target_pairs={{0,2},{2,0},{4,6},{6,4},{8,10},{10,8},{12,14},{14,12},{16,18},{18,... | collective-permute-start | bytes 196616 | tf_op jit(solution)/shard_map/ppermute | solution.py:43
  52.1 1.5 %collective-permute-start.27 = (bf16[1,256,128]{2,1,0:T(8,128)(2,1)S(1)}, bf16[1,256,128]{2,1,0:T(8,128)(2,1)S(1)}, u32[]{:S(2)}, u32[]{:S(2)}) collective-permute-start(bf16[1,256,128]{2,1,0:T(8,128)(2,1)S(1)} %bitcast.36), channel_id=1, source_target_pairs={{0,4},{2,6},{4,0},{6,2},{8,12},{10,14},{12,8},{14,10},{16,20},{18,... | collective-permute-start | bytes 196616 | tf_op jit(solution)/shard_map/ppermute | solution.py:43
  55.2 1.4 %collective-permute-start.20 = (bf16[2,256,128]{2,1,0:T(8,128)(2,1)S(1)}, bf16[2,256,128]{2,1,0:T(8,128)(2,1)S(1)}, u32[]{:S(2)}, u32[]{:S(2)}) collective-permute-start(bf16[2,256,128]{2,1,0:T(8,128)(2,1)S(1)} %pad_maximum_fusion.3), channel_id=1, source_target_pairs={{0,4},{2,6},{4,0},{6,2},{8,12},{10,14},{12,8},{14,10},{16,20},{18,... | collective-permute-start | bytes 393224 | tf_op jit(solution)/shard_map/ppermute | solution.py:43
  56.6 1.4 %collective-permute-start.21 = (bf16[2,256,128]{2,1,0:T(8,128)(2,1)S(1)}, bf16[2,256,128]{2,1,0:T(8,128)(2,1)S(1)}, u32[]{:S(2)}, u32[]{:S(2)}) collective-permute-start(bf16[2,256,128]{2,1,0:T(8,128)(2,1)S(1)} %pad_maximum_fusion.3), channel_id=1, source_target_pairs={{0,6},{2,4},{4,2},{6,0},{8,14},{10,12},{12,10},{14,8},{16,22},{18,... | collective-permute-start | bytes 393224 | tf_op jit(solution)/shard_map/ppermute | solution.py:43
  59.5 2.9 %shard_map.102.refs_8_ = bf16[4096,128]{1,0:T(8,128)(2,1)} custom-call(bf16[4096,128]{1,0:T(8,128)(2,1)} %w_ref.5, bf16[256,128]{1,0:T(8,128)(2,1)} %copy-done.6, bf16[256,128]{1,0:T(8,128)(2,1)} %copy-done.10, bf16[256,128]{1,0:T(8,128)(2,1)} %copy-done.11, bf16[256,128]{1,0:T(8,128)(2,1)} %copy-done.12, bf16[256,128]{1,0:T(8,128)(2,1)} %copy-done.13, ...), custom_call_target="tpu_custom_call" | custom-call | tf_op jit(solution)/shard_map/pallas_call | solution.py:142
  63.1 1.3 %collective-permute-done.20 = bf16[2,256,128]{2,1,0:T(8,128)(2,1)S(1)} collective-permute-done((bf16[2,256,128]{2,1,0:T(8,128)(2,1)S(1)}, bf16[2,256,128]{2,1,0:T(8,128)(2,1)S(1)}, u32[]{:S(2)}, u32[]{:S(2)}) %collective-permute-start.20) | collective-permute-done | bytes 131104 | tf_op jit(solution)/shard_map/ppermute | solution.py:43
  65.7 2.9 %shard_map.103 = bf16[4096,128]{1,0:T(8,128)(2,1)} custom-call(bf16[4096,128]{1,0:T(8,128)(2,1)} %w_ref.5, bf16[256,128]{1,0:T(8,128)(2,1)} %copy-done.3, bf16[256,128]{1,0:T(8,128)(2,1)} %copy-done.4, bf16[256,128]{1,0:T(8,128)(2,1)} %get-tuple-element.121.refs_2_, bf16[256,128]{1,0:T(8,128)(2,1)} %get-tuple-element.120.refs_3_, ...), custom_call_target="tpu_custom_call", output_to_operand_aliasing={{}: (9, {})} | custom-call | tf_op jit(solution)/shard_map/pallas_call | solution.py:142
  (114 shorter events, 12.4 us)
Async XLA Ops:
  3.1 11.3 %collective-permute-start = (bf16[1,256,128]{2,1,0:T(8,128)(2,1)}, bf16[1,256,128]{2,1,0:T(8,128)(2,1)S(1)}, u32[]{:S(2)}, u32[]{:S(2)}) collective-permute-start(bf16[1,256,128]{2,1,0:T(8,128)(2,1)} %get-tuple-element.67), channel_id=1, source_target_pairs={{0,6},{2,4},{4,2},{6,0},{8,14},{10,12},{12,10},{14,8},{16,22},{18,... | collective-permute-start | bytes 196616 | tf_op jit(solution)/shard_map/ppermute | solution.py:43
  7.1 7.5 %collective-permute-start.1 = (bf16[1,256,128]{2,1,0:T(8,128)(2,1)}, bf16[1,256,128]{2,1,0:T(8,128)(2,1)S(1)}, u32[]{:S(2)}, u32[]{:S(2)}) collective-permute-start(bf16[1,256,128]{2,1,0:T(8,128)(2,1)} %get-tuple-element.68), channel_id=1, source_target_pairs={{0,2},{2,0},{4,6},{6,4},{8,10},{10,8},{12,14},{14,12},{16,18},{18,... | collective-permute-start | bytes 196616 | tf_op jit(solution)/shard_map/ppermute | solution.py:43
  7.6 7.0 %collective-permute-start.2 = (bf16[1,256,128]{2,1,0:T(8,128)(2,1)}, bf16[1,256,128]{2,1,0:T(8,128)(2,1)S(1)}, u32[]{:S(2)}, u32[]{:S(2)}) collective-permute-start(bf16[1,256,128]{2,1,0:T(8,128)(2,1)} %get-tuple-element.69), channel_id=1, source_target_pairs={{0,4},{2,6},{4,0},{6,2},{8,12},{10,14},{12,8},{14,10},{16,20},{18,... | collective-permute-start | bytes 196616 | tf_op jit(solution)/shard_map/ppermute | solution.py:43
  7.7 12.9 %collective-permute-start.3 = (bf16[1,256,128]{2,1,0:T(8,128)(2,1)}, bf16[1,256,128]{2,1,0:T(8,128)(2,1)S(1)}, u32[]{:S(2)}, u32[]{:S(2)}) collective-permute-start(bf16[1,256,128]{2,1,0:T(8,128)(2,1)} %get-tuple-element.71), channel_id=1, source_target_pairs={{0,6},{2,4},{4,2},{6,0},{8,14},{10,12},{12,10},{14,8},{16,22},{18,... | collective-permute-start | bytes 196616 | tf_op jit(solution)/shard_map/ppermute | solution.py:43
  10.6 10.7 %collective-permute-start.4 = (bf16[1,256,128]{2,1,0:T(8,128)(2,1)}, bf16[1,256,128]{2,1,0:T(8,128)(2,1)S(1)}, u32[]{:S(2)}, u32[]{:S(2)}) collective-permute-start(bf16[1,256,128]{2,1,0:T(8,128)(2,1)} %get-tuple-element.72), channel_id=1, source_target_pairs={{0,2},{2,0},{4,6},{6,4},{8,10},{10,8},{12,14},{14,12},{16,18},{18,... | collective-permute-start | bytes 196616 | tf_op jit(solution)/shard_map/ppermute | solution.py:43
  14.4 6.9 %collective-permute-start.5 = (bf16[1,256,128]{2,1,0:T(8,128)(2,1)S(1)}, bf16[1,256,128]{2,1,0:T(8,128)(2,1)S(1)}, u32[]{:S(2)}, u32[]{:S(2)}) collective-permute-start(bf16[1,256,128]{2,1,0:T(8,128)(2,1)S(1)} %copy-done.23), channel_id=1, source_target_pairs={{0,4},{2,6},{4,0},{6,2},{8,12},{10,14},{12,8},{14,10},{16,20},{18,... | collective-permute-start | bytes 196616 | tf_op jit(solution)/shard_map/ppermute | solution.py:43
  14.6 12.3 %collective-permute-start.7 = (bf16[2048,128]{1,0:T(8,128)(2,1)S(1)}, bf16[2048,128]{1,0:T(8,128)(2,1)S(1)}, u32[]{:S(2)}, u32[]{:S(2)}) collective-permute-start(bf16[2048,128]{1,0:T(8,128)(2,1)S(1)} %get-tuple-element.109), channel_id=1, source_target_pairs={{0,1},{1,0},{2,3},{3,2},{4,5},{5,4},{6,7},{7,6},{8,9},{9,8},{10,11... | collective-permute-start | bytes 1572872 | tf_op jit(solution)/shard_map/ppermute | solution.py:43
  17.7 10.7 %collective-permute-start.8 = (bf16[2,256,128]{2,1,0:T(8,128)(2,1)S(1)}, bf16[2,256,128]{2,1,0:T(8,128)(2,1)S(1)}, u32[]{:S(2)}, u32[]{:S(2)}) collective-permute-start(bf16[2,256,128]{2,1,0:T(8,128)(2,1)S(1)} %copy-done.22), channel_id=1, source_target_pairs={{0,6},{2,4},{4,2},{6,0},{8,14},{10,12},{12,10},{14,8},{16,22},{18,... | collective-permute-start | bytes 393224 | tf_op jit(solution)/shard_map/ppermute | solution.py:43
  20.6 7.8 %collective-permute-start.9 = (bf16[2,256,128]{2,1,0:T(8,128)(2,1)S(1)}, bf16[2,256,128]{2,1,0:T(8,128)(2,1)S(1)}, u32[]{:S(2)}, u32[]{:S(2)}) collective-permute-start(bf16[2,256,128]{2,1,0:T(8,128)(2,1)S(1)} %copy-done.21), channel_id=1, source_target_pairs={{0,2},{2,0},{4,6},{6,4},{8,10},{10,8},{12,14},{14,12},{16,18},{18,... | collective-permute-start | bytes 393224 | tf_op jit(solution)/shard_map/ppermute | solution.py:43
  21.2 7.2 %collective-permute-start.10 = (bf16[2,256,128]{2,1,0:T(8,128)(2,1)S(1)}, bf16[2,256,128]{2,1,0:T(8,128)(2,1)S(1)}, u32[]{:S(2)}, u32[]{:S(2)}) collective-permute-start(bf16[2,256,128]{2,1,0:T(8,128)(2,1)S(1)} %copy-done.20), channel_id=1, source_target_pairs={{0,4},{2,6},{4,0},{6,2},{8,12},{10,14},{12,8},{14,10},{16,20},{18,... | collective-permute-start | bytes 393224 | tf_op jit(solution)/shard_map/ppermute | solution.py:43
  22.9 8.4 %collective-permute-start.12 = (f32[256,128]{1,0:T(8,128)S(1)}, f32[256,128]{1,0:T(8,128)S(1)}, u32[]{:S(2)}, u32[]{:S(2)}) collective-permute-start(f32[256,128]{1,0:T(8,128)S(1)} %add_bitcast_fusion.1), channel_id=1, source_target_pairs={{0,24},{2,26},{4,28},{6,30},{8,16},{10,18},{12,20},{14,22},{16,8},... | collective-permute-start | bytes 393224 | tf_op jit(solution)/shard_map/ppermute | solution.py:43
  27.0 11.3 %collective-permute-start.13 = (f32[256,128]{1,0:T(8,128)S(1)}, f32[256,128]{1,0:T(8,128)S(1)}, u32[]{:S(2)}, u32[]{:S(2)}) collective-permute-start(f32[256,128]{1,0:T(8,128)S(1)} %add_bitcast_fusion), channel_id=1, source_target_pairs={{0,16},{2,18},{4,20},{6,22},{8,24},{10,26},{12,28},{14,30},{16,0},... | collective-permute-start | bytes 393224 | tf_op jit(solution)/shard_map/ppermute | solution.py:43
  28.5 9.7 %collective-permute-start.14 = (f32[256,128]{1,0:T(8,128)S(1)}, f32[256,128]{1,0:T(8,128)S(1)}, u32[]{:S(2)}, u32[]{:S(2)}) collective-permute-start(f32[256,128]{1,0:T(8,128)S(1)} %get-tuple-element.115), channel_id=1, source_target_pairs={{0,8},{2,10},{4,12},{6,14},{8,0},{10,2},{12,4},{14,6},{16,24},{18,... | collective-permute-start | bytes 393224 | tf_op jit(solution)/shard_map/ppermute | solution.py:43
  39.0 7.3 %collective-permute-start.17 = (bf16[256,128]{1,0:T(8,128)(2,1)S(1)}, bf16[256,128]{1,0:T(8,128)(2,1)S(1)}, u32[]{:S(2)}, u32[]{:S(2)}) collective-permute-start(bf16[256,128]{1,0:T(8,128)(2,1)S(1)} %get-tuple-element.103.refs_0_), channel_id=1, source_target_pairs={{0,16},{2,18},{4,20},{6,22},{8,24},{10,26},{12,28},{14,30},{16,0},... | collective-permute-start | bytes 196616 | tf_op jit(solution)/shard_map/ppermute | solution.py:43
  39.0 7.4 %collective-permute-start.18 = (bf16[256,128]{1,0:T(8,128)(2,1)S(1)}, bf16[256,128]{1,0:T(8,128)(2,1)S(1)}, u32[]{:S(2)}, u32[]{:S(2)}) collective-permute-start(bf16[256,128]{1,0:T(8,128)(2,1)S(1)} %get-tuple-element.103.refs_0_), channel_id=1, source_target_pairs={{0,24},{2,26},{4,28},{6,30},{8,16},{10,18},{12,20},{14,22},{16,8},... | collective-permute-start | bytes 196616 | tf_op jit(solution)/shard_map/ppermute | solution.py:43
  41.5 10.6 %collective-permute-start.22 = (bf16[256,128]{1,0:T(8,128)(2,1)S(1)}, bf16[256,128]{1,0:T(8,128)(2,1)S(1)}, u32[]{:S(2)}, u32[]{:S(2)}) collective-permute-start(bf16[256,128]{1,0:T(8,128)(2,1)S(1)} %get-tuple-element.103.refs_0_), channel_id=1, source_target_pairs={{0,2},{2,0},{4,6},{6,4},{8,10},{10,8},{12,14},{14,12},{16,18},{18,... | collective-permute-start | bytes 196616 | tf_op jit(solution)/shard_map/ppermute | solution.py:43
  43.0 10.6 %collective-permute-start.23 = (bf16[256,128]{1,0:T(8,128)(2,1)S(1)}, bf16[256,128]{1,0:T(8,128)(2,1)S(1)}, u32[]{:S(2)}, u32[]{:S(2)}) collective-permute-start(bf16[256,128]{1,0:T(8,128)(2,1)S(1)} %get-tuple-element.103.refs_0_), channel_id=1, source_target_pairs={{0,4},{2,6},{4,0},{6,2},{8,12},{10,14},{12,8},{14,10},{16,20},{18,... | collective-permute-start | bytes 196616 | tf_op jit(solution)/shard_map/ppermute | solution.py:43
  44.5 10.4 %collective-permute-start.24 = (bf16[256,128]{1,0:T(8,128)(2,1)S(1)}, bf16[256,128]{1,0:T(8,128)(2,1)S(1)}, u32[]{:S(2)}, u32[]{:S(2)}) collective-permute-start(bf16[256,128]{1,0:T(8,128)(2,1)S(1)} %get-tuple-element.103.refs_0_), channel_id=1, source_target_pairs={{0,6},{2,4},{4,2},{6,0},{8,14},{10,12},{12,10},{14,8},{16,22},{18,... | collective-permute-start | bytes 196616 | tf_op jit(solution)/shard_map/ppermute | solution.py:43
  46.4 16.0 %collective-permute-start.19 = (bf16[2,256,128]{2,1,0:T(8,128)(2,1)S(1)}, bf16[2,256,128]{2,1,0:T(8,128)(2,1)S(1)}, u32[]{:S(2)}, u32[]{:S(2)}) collective-permute-start(bf16[2,256,128]{2,1,0:T(8,128)(2,1)S(1)} %pad_maximum_fusion.3), channel_id=1, source_target_pairs={{0,2},{2,0},{4,6},{6,4},{8,10},{10,8},{12,14},{14,12},{16,18},{18,... | collective-permute-start | bytes 393224 | tf_op jit(solution)/shard_map/ppermute | solution.py:43
  50.6 4.7 %collective-permute-start.26 = (bf16[1,256,128]{2,1,0:T(8,128)(2,1)S(1)}, bf16[1,256,128]{2,1,0:T(8,128)(2,1)S(1)}, u32[]{:S(2)}, u32[]{:S(2)}) collective-permute-start(bf16[1,256,128]{2,1,0:T(8,128)(2,1)S(1)} %bitcast.35), channel_id=1, source_target_pairs={{0,2},{2,0},{4,6},{6,4},{8,10},{10,8},{12,14},{14,12},{16,18},{18,... | collective-permute-start | bytes 196616 | tf_op jit(solution)/shard_map/ppermute | solution.py:43
  53.6 5.3 %collective-permute-start.28 = (bf16[1,256,128]{2,1,0:T(8,128)(2,1)S(1)}, bf16[1,256,128]{2,1,0:T(8,128)(2,1)S(1)}, u32[]{:S(2)}, u32[]{:S(2)}) collective-permute-start(bf16[1,256,128]{2,1,0:T(8,128)(2,1)S(1)} %bitcast.37), channel_id=1, source_target_pairs={{0,6},{2,4},{4,2},{6,0},{8,14},{10,12},{12,10},{14,8},{16,22},{18,... | collective-permute-start | bytes 196616 | tf_op jit(solution)/shard_map/ppermute | solution.py:43
  54.9 13.7 %collective-permute-start.16 = (bf16[2048,128]{1,0:T(8,128)(2,1)S(1)}, bf16[2048,128]{1,0:T(8,128)(2,1)S(1)}, u32[]{:S(2)}, u32[]{:S(2)}) collective-permute-start(bf16[2048,128]{1,0:T(8,128)(2,1)S(1)} %get-tuple-element.106), channel_id=1, source_target_pairs={{0,1},{1,0},{2,3},{3,2},{4,5},{5,4},{6,7},{7,6},{8,9},{9,8},{10,11... | collective-permute-start | bytes 1572872 | tf_op jit(solution)/shard_map/ppermute | solution.py:43
  55.2 9.1 %collective-permute-start.20 = (bf16[2,256,128]{2,1,0:T(8,128)(2,1)S(1)}, bf16[2,256,128]{2,1,0:T(8,128)(2,1)S(1)}, u32[]{:S(2)}, u32[]{:S(2)}) collective-permute-start(bf16[2,256,128]{2,1,0:T(8,128)(2,1)S(1)} %pad_maximum_fusion.3), channel_id=1, source_target_pairs={{0,4},{2,6},{4,0},{6,2},{8,12},{10,14},{12,8},{14,10},{16,20},{18,... | collective-permute-start | bytes 393224 | tf_op jit(solution)/shard_map/ppermute | solution.py:43
  56.6 8.4 %collective-permute-start.21 = (bf16[2,256,128]{2,1,0:T(8,128)(2,1)S(1)}, bf16[2,256,128]{2,1,0:T(8,128)(2,1)S(1)}, u32[]{:S(2)}, u32[]{:S(2)}) collective-permute-start(bf16[2,256,128]{2,1,0:T(8,128)(2,1)S(1)} %pad_maximum_fusion.3), channel_id=1, source_target_pairs={{0,6},{2,4},{4,2},{6,0},{8,14},{10,12},{12,10},{14,8},{16,22},{18,... | collective-permute-start | bytes 393224 | tf_op jit(solution)/shard_map/ppermute | solution.py:43
  (29 other events, 233.5 us)

commit v3 on v0

v3 whole, which is shorter than its diff:
```python
import functools
import math

import jax
import jax.numpy as jnp
from jax import lax
from jax.experimental import pallas as pl
from jax.experimental.pallas import tpu as pltpu
from jax.sharding import Mesh, PartitionSpec as P

HD = 128
CUBE = 8
SPAN = 32


momentum_rate = 0.9
outer_rate = 0.7
mix_rate = 0.5
rope_base = 500000.0
norm_eps = 1e-05

VMEM = pl.BlockSpec(memory_space=pltpu.VMEM)
LIGHT = pl.CostEstimate(flops=1, bytes_accessed=1, transcendentals=0)
PARAMS = pltpu.CompilerParams(vmem_limit_bytes=40 * 2**20)


def swap(value, axis, offset):
    size = lax.axis_size(axis)
    if not offset:
        return value
    return lax.ppermute(value, axis, [(i, i ^ offset) for i in range(size)])


def after(*values):
    return lax.optimization_barrier(values)


def rows_at(index, rows):
    return pl.ds(pl.multiple_of(index * rows, rows), rows)


def prepare_kernel(w_ref, grad_ref, cos_ref, sin_ref, *out_refs):
    me = lax.axis_index("tp")
    rows = grad_ref.shape[0]
    part = w_ref.shape[0] // (len(out_refs) + 1)
    lane = lax.broadcasted_iota(jnp.int32, (SPAN, HD), 1)
    lower = lane < HD // 2
    pair = jnp.where(lower, lane, lane - HD // 2).astype(jnp.float32)
    freq = jnp.exp(-(pair * 2.0 / HD) * math.log(rope_base))
    step = lax.broadcasted_iota(jnp.int32, (SPAN, HD), 0).astype(jnp.float32)
    near_cos, near_sin = jnp.cos(step * freq), jnp.sin(step * freq)
    near_sin = jnp.where(lower, -near_sin, near_sin)
    for block in range(0, rows // SPAN, SPAN):
        far = (step + block) * SPAN * freq
        far_cos, far_sin = jnp.cos(far), jnp.sin(far)
        far_sin = jnp.where(lower, -far_sin, far_sin)
        for i in range(min(SPAN, rows // SPAN - block)):
            place = pl.ds((block + i) * SPAN, SPAN)
            a_cos, a_sin = far_cos[i : i + 1], far_sin[i : i + 1]
            cosine = a_cos * near_cos - a_sin * near_sin
            signed = a_sin * near_cos + a_cos * near_sin
            cos_ref[place, :] = cosine
            sin_ref[place, :] = signed
            grad = grad_ref[place, :].astype(jnp.float32)
            turned = grad * cosine - pltpu.roll(grad, HD // 2, 1) * signed
            for out in out_refs:
                out[pl.ds(part + (block + i) * SPAN, SPAN), :] = turned.astype(jnp.bfloat16)
    for k, out in enumerate(out_refs):
        out[:part, :] = w_ref[rows_at(me ^ (k + 1), part), :]


def prepare(local_weights, key_grad):
    cores = lax.axis_size("tp")
    rows = key_grad.shape[0]
    table = jax.ShapeDtypeStruct((rows, HD), jnp.float32)
    packed = jax.ShapeDtypeStruct((local_weights.shape[0] // cores + rows, HD), jnp.bfloat16)
    cosine, signed, *packs = pl.pallas_call(
        prepare_kernel,
        out_shape=[table] * 2 + [packed] * (cores - 1),
        in_specs=[VMEM] * 2,
        out_specs=[VMEM] * (cores + 1),
        compiler_params=PARAMS,
        cost_estimate=LIGHT,
    )(local_weights, key_grad)
    return cosine, signed, packs


def squares_kernel(x_ref, out_ref):
    total = None
    for c in range(x_ref.shape[1] // HD):
        x = x_ref[:, c * HD : (c + 1) * HD].astype(jnp.float32)
        total = x * x if total is None else total + x * x
    out_ref[...] = jnp.sum(total.T, axis=0, keepdims=True)


def squares_of(tokens):
    rows, part = tokens.shape
    block = 256
    out = pl.pallas_call(
        squares_kernel,
        out_shape=jax.ShapeDtypeStruct((1, rows), jnp.float32),
        grid=(rows // block,),
        in_specs=[pl.BlockSpec((block, part), lambda i: (i, 0))],
        out_specs=pl.BlockSpec((1, block), lambda i: (0, i)),
        compiler_params=PARAMS,
        cost_estimate=LIGHT,
    )(tokens)
    return out.reshape(rows)


def turn_kernel(inv_width, own_ref, *refs):
    *other_refs, cos_ref, sin_ref, out_ref = refs
    total = own_ref[:, :HD]
    for other in other_refs:
        total = total + other[...]
    keys = total * inv_width
    turned = keys * cos_ref[...] + pltpu.roll(keys, HD // 2, 1) * sin_ref[...]
    out_ref[...] = turned.astype(jnp.bfloat16)


def turn(inv_width, partial, others, cosine, signed):
    rows = partial.shape[0]
    return pl.pallas_call(
        functools.partial(turn_kernel, inv_width),
        out_shape=jax.ShapeDtypeStruct((rows, HD), jnp.bfloat16),
        in_specs=[VMEM] * (3 + len(others)),
        out_specs=VMEM,
        compiler_params=PARAMS,
        cost_estimate=LIGHT,
    )(partial, *others, cosine, signed)


def normalize(tokens, total, norm_gain):
    features = tokens.shape[1] * lax.axis_size("tp")
    scale = lax.rsqrt(total / features + norm_eps)[:, None]
    return (tokens.astype(jnp.float32) * scale * norm_gain.astype(jnp.float32)).astype(jnp.bfloat16)


def place_kernel(own_ref, *refs):
    *other_refs, out_ref = refs
    me = lax.axis_index("tp")
    part = own_ref.shape[0]
    out_ref[rows_at(me, part), :] = own_ref[:, :HD]
    for k, other in enumerate(other_refs):
        out_ref[rows_at(me ^ (k + 1), part), :] = other[...]


def place_blocks(own, others):
    part = own.shape[0]
    return pl.pallas_call(
        place_kernel,
        out_shape=jax.ShapeDtypeStruct(((1 + len(others)) * part, HD), own.dtype),
        in_specs=[VMEM] * (1 + len(others)),
        out_specs=VMEM,
        compiler_params=PARAMS,
        cost_estimate=LIGHT,
    )(own, *others)


def merge_kernel(w_ref, near_ref, out_ref, out_buf, sems):
    me = lax.axis_index("hi")
    cube, far, rows, _ = near_ref.shape
    stores = []
    for c in range(cube):
        for h in range(far):
            place = rows_at((me ^ h) * cube + c, rows)
            i = len(stores)
            w = w_ref[place, :].astype(jnp.float32)
            g = near_ref[c, h].astype(jnp.float32)
            out_buf[i] = (w + mix_rate * (g - w)).astype(jnp.bfloat16)
            stores.append(pltpu.make_async_copy(out_buf.at[i], out_ref.at[place, :], sems.at[i]))
            stores[-1].start()
    for store in stores:
        store.wait()


def merge(local_weights, near):
    cube, far, rows, _ = near.shape
    return pl.pallas_call(
        merge_kernel,
        out_shape=jax.ShapeDtypeStruct(local_weights.shape, jnp.bfloat16),
        in_specs=[VMEM] * 2,
        out_specs=pl.BlockSpec(memory_space=pl.ANY),
        scratch_shapes=[
            pltpu.VMEM((cube * far, rows, HD), jnp.bfloat16),
            pltpu.SemaphoreType.DMA((cube * far,)),
        ],
        compiler_params=PARAMS,
        cost_estimate=LIGHT,
    )(local_weights, near)


def body(tokens, norm_gain, local_weights, anchor, momentum, key_grad):
    cores = lax.axis_size("tp")
    far = lax.axis_size("hi")
    me = lax.axis_index("hi")
    rows, part = tokens.shape
    own_rows = anchor.shape[0]
    inv_width = 1.0 / math.sqrt(part * cores)

    chunks = local_weights.reshape(far, CUBE, own_rows, HD).transpose(1, 0, 2, 3)
    chunks, tokens, w, key_grad = after(chunks, tokens, local_weights, key_grad)
    received = lax.all_to_all(chunks, "cube", 0, 0)
    squares = squares_of(tokens)
    cosine, signed, packs = prepare(w, key_grad)
    squares_in = [swap(squares, "tp", k) for k in range(1, cores)]
    packs_in = [swap(pack, "tp", k + 1) for k, pack in enumerate(packs)]
    own_weights = lax.dynamic_slice_in_dim(w, lax.axis_index("tp") * part, part, 0)
    weights = jnp.concatenate([own_weights] + [pack[:part] for pack in packs_in], axis=1)
    grads = jnp.concatenate([pack[part:] for pack in [packs[0]] + packs_in], axis=1)
    norm = normalize(tokens, sum(squares_in, squares), norm_gain)
    partial = jnp.dot(norm, weights, preferred_element_type=jnp.float32)

    received, partial, tokens, grads = after(received, partial, tokens, grads)
    summed = jnp.sum(received.astype(jnp.float32), axis=0)
    sums = [
        swap(lax.dynamic_index_in_dim(summed, me ^ h, 0, keepdims=False), "hi", h)
        for h in range(far)
    ]
    keys_in = [swap(partial[:, k * HD : (k + 1) * HD], "tp", k) for k in range(1, cores)]
    norm = normalize(tokens, sum(squares_in, squares), norm_gain)
    contracted = lax.dot_general(
        norm, grads, (((0,), (0,)), ((), ())), preferred_element_type=jnp.float32
    )
    contracted = (contracted * inv_width).astype(jnp.bfloat16)

    contracted, sums, keys_in = after(contracted, sums, keys_in)
    mean_weights = sum(sums) / (far * CUBE)
    change = anchor - mean_weights
    new_momentum = momentum_rate * momentum + change
    new_anchor = anchor - outer_rate * (change + momentum_rate * new_momentum)
    outgoing = new_anchor.astype(jnp.bfloat16)

    column = jnp.stack([swap(outgoing, "hi", h) for h in range(far)])
    grads_in = [swap(contracted[:, k * HD : (k + 1) * HD], "tp", k) for k in range(1, cores)]
    column, grads_in, partial = after(column, grads_in, partial)
    near = lax.all_to_all(jnp.broadcast_to(column, (CUBE, *column.shape)), "cube", 0, 0)
    key_rows = turn(inv_width, partial, keys_in, cosine, signed)
    weight_grad = place_blocks(contracted, grads_in)
    merged = merge(w, near)
    return (key_rows, weight_grad, merged, new_anchor, new_momentum)


def solution(mesh):
    replicas, cores = mesh.devices.shape
    cubes = Mesh(mesh.devices.reshape(replicas // CUBE, CUBE, cores), ("hi", "cube", "tp"))
    split = P(("hi", "cube"), "tp")
    return jax.shard_map(
        body,
        mesh=cubes,
        in_specs=(split, P("tp"), split, split, split, split),
        out_specs=(split,) * 5,
        check_vma=False,
    )
```

time: 195 us -> 62.6 us (0.32)
  waiting for transfers between devices: 153 us -> 16.7 us
  local copies, waits for them, and re-layouts: 1.53 us -> 16.6 us
  starting transfers between devices: 0.12 us -> 13.7 us
  between operations: 13.8 us -> 0.87 us
  other arithmetic: 13.7 us -> 1.78 us
  Pallas kernels: 0 us -> 4.71 us
  matrix products: 10.1 us -> 7.61 us
    reduce_scatter x1 -> x0, waiting for transfers between devices: 83.5 us -> none  [outer_step(): summed = lax.psum_scatter(widened, 'rep', scatter_dimension=0, tiled=True)]
    all_gather x2 -> x0, waiting for transfers between devices: 68.9 us -> none  [the longest x1 51.3 us: outer_step(): lax.all_gather(outgoing, 'rep', axis=0, tiled=True).astype(jnp.float32)]
    all_to_all x0 -> x2, starting transfers between devices: none -> 10.2 us  [the longest x1 6.31 us: body(): received = lax.all_to_all(chunks, 'cube', 0, 0)]
    unnamed x10 -> x32, local copies, waits for them, and re-layouts: 1.53 us -> 10 us
    all_to_all x0 -> x2, waiting for transfers between devices: none -> 8.4 us  [the longest x1 7.13 us: body(): lax.all_to_all(jnp.broadcast_to(column, (CUBE, *column.shape)), 'cube', 0...]
    ppermute x0 -> x6, waiting for transfers between devices: none -> 8.34 us  [swap(): return lax.ppermute(value, axis, [(i, i ^ offset) for i in range(size)])]
    convert_element_type x4 -> x1, other arithmetic: 7.19 us -> 0.76 us  [body(): outgoing = new_anchor.astype(jnp.bfloat16)]
    reduce_sum x1, other arithmetic: 5.22 us -> 0.14 us  [body(): summed = jnp.sum(received.astype(jnp.float32), axis=0)]
  transfers between devices with their start and end apart: 3 -> 8, of which waited for: 3 -> 4; matrix products, arithmetic and copies ran while one was open for 1% -> 20% of each run, Pallas kernels for 0% -> 6%
where the time goes in v3:
time: 62.6 us; the launch traced here: 62 us
  waiting for transfers between devices  16.7 us (27%)
  local copies, waits for them, and re-layouts  16.6 us (27%)
  starting transfers between devices  13.7 us (22%)
  matrix products  7.61 us (12%)
  Pallas kernels  4.71 us (8%)
  other arithmetic  1.78 us (3%)
  between operations  0.87 us (1%)
    unnamed x32, local copies, waits for them, and re-layouts  10 us
    ppermute x6, waiting for transfers between devices, swap(): return lax.ppermute(value, axis, [(i, i ^ offset) for i in range(size)])  8.34 us
    all_to_all x1, waiting for transfers between devices, body(): lax.all_to_all(jnp.broadcast_to(column, (CUBE, *column.shape)), 'cube', 0...  7.13 us
    all_to_all x1, starting transfers between devices, body(): received = lax.all_to_all(chunks, 'cube', 0, 0)  6.31 us
    dot_general x1, matrix products, body(): lax.dot_general(norm, grads, (((0,), (0,)), ((), ())), preferred_element_...  3.99 us
    all_to_all x1, starting transfers between devices, body(): lax.all_to_all(jnp.broadcast_to(column, (CUBE, *column.shape)), 'cube', 0...  3.9 us
    dot_general x1, matrix products, body(): partial = jnp.dot(norm, weights, preferred_element_type=jnp.float32)  3.62 us
    ppermute x6, starting transfers between devices, swap(): return lax.ppermute(value, axis, [(i, i ^ offset) for i in range(size)])  3.5 us
  transfers between devices with their start and end apart: 8, of which 4 were waited for; matrix products, arithmetic and copies ran while one was open for 20% of the time, Pallas kernels for 6%

profile of v3, /device:TPU:0, one launch (start us, length us, event | category | flops | bytes accessed | tf_op | source)
XLA Modules:
  0.0 62.0 jit_solution(5444662439605246678)
XLA Ops:
  0.7 2.4 %copy.11 = bf16[8,2,256,128]{3,2,1,0:T(8,128)(2,1)} copy(bf16[8,2,256,128]{3,2,0,1:T(8,128)(2,1)} %bitcast.11) | data formatting | bytes 2097152 | tf_op jit(solution)/shard_map/optimization_barrier | solution.py:35
  3.0 6.3 %all-to-all-start = ((bf16[8,2,256,128]{3,2,1,0:T(8,128)(2,1)}), bf16[8,2,256,128]{3,2,1,0:T(8,128)(2,1)S(1)}, u32[]{:S(2)}, u32[]{:S(2)}) async-start(bf16[8,2,256,128]{3,2,1,0:T(8,128)(2,1)} %copy.11), calls=%async_computation | async-start | bytes 2097152 | tf_op jit(solution)/shard_map/all_to_all | solution.py:203
  11.4 2.2 %copy-done.1 = bf16[1024,2048]{1,0:T(8,128)(2,1)S(1)} copy-done((bf16[1024,2048]{1,0:T(8,128)(2,1)S(1)}, bf16[1024,2048]{1,0:T(8,128)(2,1)}, u32[]{:S(2)}) %copy-start.1) | copy-done | bytes 4194328
  13.6 1.1 %shard_map.101 = f32[1,1024]{1,0:T(1,128)S(1)} custom-call(bf16[1024,2048]{1,0:T(8,128)(2,1)S(1)} %copy-done.1), custom_call_target="tpu_custom_call" | custom-call | flops 1 | bytes 1 | tf_op jit(solution)/shard_map/pallas_call | solution.py:99
  16.2 1.0 %slice.21 = bf16[1024,128]{1,0:T(8,128)(2,1)S(1)} slice(bf16[3072,128]{1,0:T(8,128)(2,1)} %collective-permute-done.1), slice={[2048:3072], [0:128]} | slice | bytes 524288 | tf_op jit(solution)/shard_map/slice | solution.py:210
  17.2 1.1 %slice.20 = bf16[2048,128]{1,0:T(8,128)(2,1)S(1)} slice(bf16[3072,128]{1,0:T(8,128)(2,1)} %collective-permute-done.1), slice={[0:2048], [0:128]} | slice | bytes 1048576 | tf_op jit(solution)/shard_map/slice | solution.py:209
  18.3 0.9 %pad_maximum_fusion = bf16[1024,256]{1,0:T(8,128)(2,1)} fusion(bf16[1024,128]{1,0:T(8,128)(2,1)S(1)} %slice.21, bf16[1024,128]{1,0:T(8,128)(2,1)S(1)} %slice.16), kind=kLoop, calls=%fused_computation.14 | loop fusion | flops 1048576 | bytes 1048576 | tf_op jit(solution)/shard_map/concatenate | solution.py:210
  19.1 3.6 %fusion.own_ref = f32[1024,256]{1,0:T(8,128)S(1)} fusion(bf16[1024,2048]{1,0:T(8,128)(2,1)} %x_ref, f32[2048]{0:T(1024)S(1)} %convert_element_type.26, f32[1024]{0:T(1024)S(1)} %add_rsqrt_fusion, bf16[2048,128]{1,0:T(8,128)(2,1)S(1)} %slice.20, bf16[2048,128]{1,0:T(8,128)(2,1)} %constant_dynamic-slice_fusion), kind=kOutput, calls=%fused_computation.2 | convolution fusion | flops 1084227584 | bytes 6303744 | tf_op jit(solution)/shard_map/dot_general | solution.py:212
  22.8 1.3 %all-to-all-done = bf16[8,2,256,128]{3,2,1,0:T(8,128)(2,1)S(1)} async-done(((bf16[8,2,256,128]{3,2,1,0:T(8,128)(2,1)}), bf16[8,2,256,128]{3,2,1,0:T(8,128)(2,1)S(1)}, u32[]{:S(2)}, u32[]{:S(2)}) %all-to-all-start) | async-done | bytes 1048608 | tf_op jit(solution)/shard_map/all_to_all | solution.py:203
  24.2 2.7 %collective-permute-start.2 = (f32[256,128]{1,0:T(8,128)S(1)}, f32[256,128]{1,0:T(8,128)S(1)}, u32[]{:S(2)}, u32[]{:S(2)}) collective-permute-start(f32[256,128]{1,0:T(8,128)S(1)} %get-tuple-element.44), channel_id=1, source_target_pairs={{0,16},{16,0},{1,17},{17,1},{2,18},{18,2},{3,19},{19,3},{4,20},{20... | collective-permute-start | bytes 393224 | tf_op jit(solution)/shard_map/ppermute | solution.py:31
  27.0 4.0 %fusion.7.own_ref = bf16[2048,256]{1,0:T(8,128)(2,1)S(1)} fusion(bf16[1024,256]{1,0:T(8,128)(2,1)} %pad_maximum_fusion, bf16[1024,2048]{1,0:T(8,128)(2,1)} %x_ref, f32[2048]{0:T(1024)S(1)} %convert_element_type.26, f32[1024]{0:T(1024)S(1)} %add_rsqrt_fusion), kind=kOutput, calls=%fused_computation.9 | convolution fusion | flops 1083179008 | bytes 5779456 | tf_op jit(solution)/shard_map/dot_general | solution.py:222
  31.0 1.7 %collective-permute-done.2 = f32[256,128]{1,0:T(8,128)S(1)} collective-permute-done((f32[256,128]{1,0:T(8,128)S(1)}, f32[256,128]{1,0:T(8,128)S(1)}, u32[]{:S(2)}, u32[]{:S(2)}) %collective-permute-start.2) | collective-permute-done | bytes 131104 | tf_op jit(solution)/shard_map/ppermute | solution.py:31
  33.7 6.6 %collective-permute-done.4 = bf16[256,128]{1,0:T(8,128)(2,1)S(1)} collective-permute-done((bf16[256,128]{1,0:T(8,128)(2,1)S(1)}, bf16[256,128]{1,0:T(8,128)(2,1)S(1)}, u32[]{:S(2)}, u32[]{:S(2)}) %collective-permute-start.4) | collective-permute-done | bytes 65568 | tf_op jit(solution)/shard_map/ppermute | solution.py:31
  41.2 1.2 %broadcast_in_dim.2 = bf16[8,2,256,128]{3,2,1,0:T(8,128)(2,1)} broadcast(bf16[2,256,128]{2,1,0:T(8,128)(2,1)S(1)} %pad_maximum_fusion.1), dimensions={1,2,3} | broadcast | bytes 1179648 | tf_op jit(solution)/shard_map/broadcast_in_dim | solution.py:237
  42.4 3.9 %all-to-all-start.1 = ((bf16[8,2,256,128]{3,2,1,0:T(8,128)(2,1)}), bf16[8,2,256,128]{3,2,1,0:T(8,128)(2,1)S(1)}, u32[]{:S(2)}, u32[]{:S(2)}) async-start(bf16[8,2,256,128]{3,2,1,0:T(8,128)(2,1)} %broadcast_in_dim.2), calls=%async_computation.1 | async-start | bytes 2097152 | tf_op jit(solution)/shard_map/all_to_all | solution.py:237
  46.3 1.0 %copy-done.5 = bf16[2048,128]{1,0:T(8,128)(2,1)S(1)} copy-done((bf16[2048,128]{1,0:T(8,128)(2,1)S(1)}, bf16[2048,128]{1,0:T(8,128)(2,1)}, u32[]{:S(2)}) %copy-start.5) | copy-done | bytes 524312
  47.4 1.1 %shard_map.104 = bf16[4096,128]{1,0:T(8,128)(2,1)} custom-call(bf16[2048,256]{1,0:T(8,128)(2,1)S(1)} %fusion.7.own_ref, bf16[2048,128]{1,0:T(8,128)(2,1)S(1)} %copy-done.5), custom_call_target="tpu_custom_call" | custom-call | flops 1 | bytes 1 | tf_op jit(solution)/shard_map/pallas_call | solution.py:150
  48.5 1.2 %copy-done.3 = f32[1024,256]{1,0:T(8,128)S(1)} copy-done((f32[1024,256]{1,0:T(8,128)S(1)}, f32[1024,256]{1,0:T(8,128)}, u32[]{:S(2)}) %copy-start.3) | copy-done | bytes 1048600
  49.7 1.0 %copy-done.7 = f32[1024,128]{1,0:T(8,128)S(1)} copy-done((f32[1024,128]{1,0:T(8,128)S(1)}, f32[1024,128]{1,0:T(8,128)}, u32[]{:S(2)}) %copy-start.7) | copy-done | bytes 524312
  50.7 1.0 %copy-done.9 = f32[1024,128]{1,0:T(8,128)S(1)} copy-done((f32[1024,128]{1,0:T(8,128)S(1)}, f32[1024,128]{1,0:T(8,128)}, u32[]{:S(2)}) %copy-start.9) | copy-done | bytes 524312
  51.8 1.0 %copy-done.11 = f32[1024,128]{1,0:T(8,128)S(1)} copy-done((f32[1024,128]{1,0:T(8,128)S(1)}, f32[1024,128]{1,0:T(8,128)}, u32[]{:S(2)}) %copy-start.11) | copy-done | bytes 524312
  52.8 0.9 %shard_map.103 = bf16[1024,128]{1,0:T(8,128)(2,1)} custom-call(f32[1024,256]{1,0:T(8,128)S(1)} %copy-done.3, f32[1024,128]{1,0:T(8,128)S(1)} %copy-done.11, f32[1024,128]{1,0:T(8,128)S(1)} %copy-done.7, f32[1024,128]{1,0:T(8,128)S(1)} %copy-done.9), custom_call_target="tpu_custom_call" | custom-call | flops 1 | bytes 1 | tf_op jit(solution)/shard_map/pallas_call | solution.py:123
  53.7 7.1 %all-to-all-done.1.near_ref = bf16[8,2,256,128]{3,2,1,0:T(8,128)(2,1)S(1)} async-done(((bf16[8,2,256,128]{3,2,1,0:T(8,128)(2,1)}), bf16[8,2,256,128]{3,2,1,0:T(8,128)(2,1)S(1)}, u32[]{:S(2)}, u32[]{:S(2)}) %all-to-all-start.1) | async-done | bytes 1048608 | tf_op jit(solution)/shard_map/all_to_all | solution.py:237
  60.9 1.2 %shard_map.105 = bf16[4096,128]{1,0:T(8,128)(2,1)} custom-call(bf16[4096,128]{1,0:T(8,128)(2,1)S(1)} %copy-done, bf16[8,2,256,128]{3,2,1,0:T(8,128)(2,1)S(1)} %all-to-all-done.1.near_ref), custom_call_target="tpu_custom_call" | custom-call | flops 1 | bytes 1 | tf_op jit(solution)/shard_map/pallas_call | solution.py:179
  (46 shorter events, 5.6 us)
Async XLA Ops:
  0.6 8.7 %copy-start = (bf16[4096,128]{1,0:T(8,128)(2,1)S(1)}, bf16[4096,128]{1,0:T(8,128)(2,1)}, u32[]{:S(2)}) copy-start(bf16[4096,128]{1,0:T(8,128)(2,1)} %w_ref.1) | copy-start | bytes 3145732
  0.6 8.7 %copy-start.12 = (bf16[1024,128]{1,0:T(8,128)(2,1)S(1)}, bf16[1024,128]{1,0:T(8,128)(2,1)}, u32[]{:S(2)}) copy-start(bf16[1024,128]{1,0:T(8,128)(2,1)} %grad_ref) | copy-start | bytes 786436
  3.0 13.1 %copy-start.15 = (bf16[2048]{0:T(1024)(128)(2,1)S(1)}, bf16[2048]{0:T(1024)(128)(2,1)}, u32[]{:S(2)}) copy-start(bf16[2048]{0:T(1024)(128)(2,1)} %param.7) | copy-start | bytes 12292
  3.0 21.0 %all-to-all-start = ((bf16[8,2,256,128]{3,2,1,0:T(8,128)(2,1)}), bf16[8,2,256,128]{3,2,1,0:T(8,128)(2,1)S(1)}, u32[]{:S(2)}, u32[]{:S(2)}) async-start(bf16[8,2,256,128]{3,2,1,0:T(8,128)(2,1)} %copy.11), calls=%async_computation | async-start | bytes 2097152 | tf_op jit(solution)/shard_map/all_to_all | solution.py:203
  9.8 0.8 %copy-start.6 = (f32[1024,128]{1,0:T(8,128)}, f32[1024,128]{1,0:T(8,128)S(1)}, u32[]{:S(2)}) copy-start(f32[1024,128]{1,0:T(8,128)S(1)} %get-tuple-element.37.refs_1_) | copy-start | bytes 1572868
  10.6 0.8 %copy-start.8 = (f32[1024,128]{1,0:T(8,128)}, f32[1024,128]{1,0:T(8,128)S(1)}, u32[]{:S(2)}) copy-start(f32[1024,128]{1,0:T(8,128)S(1)} %get-tuple-element.38.refs_2_) | copy-start | bytes 1572868
  11.4 4.8 %collective-permute-start.1 = (bf16[3072,128]{1,0:T(8,128)(2,1)S(1)}, bf16[3072,128]{1,0:T(8,128)(2,1)}, u32[]{:S(2)}, u32[]{:S(2)}) collective-permute-start(bf16[3072,128]{1,0:T(8,128)(2,1)S(1)} %get-tuple-element.27), channel_id=1, source_target_pairs={{0,1},{1,0},{2,3},{3,2},{4,5},{5,4},{6,7},{7,6},{8,9},{9,8},{10,11... | collective-permute-start | bytes 2359304 | tf_op jit(solution)/shard_map/ppermute | solution.py:31
  11.4 2.2 %copy-start.1 = (bf16[1024,2048]{1,0:T(8,128)(2,1)S(1)}, bf16[1024,2048]{1,0:T(8,128)(2,1)}, u32[]{:S(2)}) copy-start(bf16[1024,2048]{1,0:T(8,128)(2,1)} %x_ref) | copy-start | bytes 12582916
  14.7 1.5 %collective-permute-start = (f32[1024]{0:T(1024)S(1)}, f32[1024]{0:T(1024)S(1)}, u32[]{:S(2)}, u32[]{:S(2)}) collective-permute-start(f32[1024]{0:T(1024)S(1)} %bitcast.12), channel_id=1, source_target_pairs={{0,1},{1,0},{2,3},{3,2},{4,5},{5,4},{6,7},{7,6},{8,9},{9,8},{10,11... | collective-permute-start | bytes 12296 | tf_op jit(solution)/shard_map/ppermute | solution.py:31
  22.8 8.2 %copy-start.2 = (f32[1024,256]{1,0:T(8,128)}, f32[1024,256]{1,0:T(8,128)S(1)}, u32[]{:S(2)}) copy-start(f32[1024,256]{1,0:T(8,128)S(1)} %fusion.own_ref) | copy-start | bytes 3145732
  24.2 8.5 %collective-permute-start.2 = (f32[256,128]{1,0:T(8,128)S(1)}, f32[256,128]{1,0:T(8,128)S(1)}, u32[]{:S(2)}, u32[]{:S(2)}) collective-permute-start(f32[256,128]{1,0:T(8,128)S(1)} %get-tuple-element.44), channel_id=1, source_target_pairs={{0,16},{16,0},{1,17},{17,1},{2,18},{18,2},{3,19},{19,3},{4,20},{20... | collective-permute-start | bytes 393224 | tf_op jit(solution)/shard_map/ppermute | solution.py:31
  26.9 5.9 %copy-start.13 = (f32[256,128]{1,0:T(8,128)S(1)}, f32[256,128]{1,0:T(8,128)}, u32[]{:S(2)}) copy-start(f32[256,128]{1,0:T(8,128)} %param.9) | copy-start | bytes 393220
  26.9 5.9 %copy-start.14 = (f32[256,128]{1,0:T(8,128)S(1)}, f32[256,128]{1,0:T(8,128)}, u32[]{:S(2)}) copy-start(f32[256,128]{1,0:T(8,128)} %param.10) | copy-start | bytes 393220
  26.9 5.8 %collective-permute-start.3 = (f32[1024,128]{1,0:T(8,128)S(1)}, f32[1024,128]{1,0:T(8,128)S(1)}, u32[]{:S(2)}, u32[]{:S(2)}) collective-permute-start(f32[1024,128]{1,0:T(8,128)S(1)} %slice.18), channel_id=1, source_target_pairs={{0,1},{1,0},{2,3},{3,2},{4,5},{5,4},{6,7},{7,6},{8,9},{9,8},{10,11... | collective-permute-start | bytes 1572872 | tf_op jit(solution)/shard_map/ppermute | solution.py:31
  32.7 7.7 %copy-start.10 = (f32[1024,128]{1,0:T(8,128)}, f32[1024,128]{1,0:T(8,128)S(1)}, u32[]{:S(2)}) copy-start(f32[1024,128]{1,0:T(8,128)S(1)} %collective-permute-done.3.refs_0_) | copy-start | bytes 1572868
  32.8 7.6 %collective-permute-start.5 = (bf16[2048,128]{1,0:T(8,128)(2,1)S(1)}, bf16[2048,128]{1,0:T(8,128)(2,1)S(1)}, u32[]{:S(2)}, u32[]{:S(2)}) collective-permute-start(bf16[2048,128]{1,0:T(8,128)(2,1)S(1)} %slice.19), channel_id=1, source_target_pairs={{0,1},{1,0},{2,3},{3,2},{4,5},{5,4},{6,7},{7,6},{8,9},{9,8},{10,11... | collective-permute-start | bytes 1572872 | tf_op jit(solution)/shard_map/ppermute | solution.py:31
  33.6 6.8 %collective-permute-start.4 = (bf16[256,128]{1,0:T(8,128)(2,1)S(1)}, bf16[256,128]{1,0:T(8,128)(2,1)S(1)}, u32[]{:S(2)}, u32[]{:S(2)}) collective-permute-start(bf16[256,128]{1,0:T(8,128)(2,1)S(1)} %get-tuple-element.41), channel_id=1, source_target_pairs={{0,16},{16,0},{1,17},{17,1},{2,18},{18,2},{3,19},{19,3},{4,20},{20... | collective-permute-start | bytes 196616 | tf_op jit(solution)/shard_map/ppermute | solution.py:31
  40.4 0.8 %copy-start.4 = (bf16[2048,128]{1,0:T(8,128)(2,1)}, bf16[2048,128]{1,0:T(8,128)(2,1)S(1)}, u32[]{:S(2)}) copy-start(bf16[2048,128]{1,0:T(8,128)(2,1)S(1)} %collective-permute-done.5.refs_0_) | copy-start | bytes 1572868
  42.4 18.4 %all-to-all-start.1 = ((bf16[8,2,256,128]{3,2,1,0:T(8,128)(2,1)}), bf16[8,2,256,128]{3,2,1,0:T(8,128)(2,1)S(1)}, u32[]{:S(2)}, u32[]{:S(2)}) async-start(bf16[8,2,256,128]{3,2,1,0:T(8,128)(2,1)} %broadcast_in_dim.2), calls=%async_computation.1 | async-start | bytes 2097152 | tf_op jit(solution)/shard_map/all_to_all | solution.py:237
  46.3 1.0 %copy-start.5 = (bf16[2048,128]{1,0:T(8,128)(2,1)S(1)}, bf16[2048,128]{1,0:T(8,128)(2,1)}, u32[]{:S(2)}) copy-start(bf16[2048,128]{1,0:T(8,128)(2,1)} %copy-done.4) | copy-start | bytes 1572868
  48.5 1.2 %copy-start.3 = (f32[1024,256]{1,0:T(8,128)S(1)}, f32[1024,256]{1,0:T(8,128)}, u32[]{:S(2)}) copy-start(f32[1024,256]{1,0:T(8,128)} %copy-done.2) | copy-start | bytes 3145732
  49.7 1.0 %copy-start.7 = (f32[1024,128]{1,0:T(8,128)S(1)}, f32[1024,128]{1,0:T(8,128)}, u32[]{:S(2)}) copy-start(f32[1024,128]{1,0:T(8,128)} %copy-done.6) | copy-start | bytes 1572868
  50.7 1.0 %copy-start.9 = (f32[1024,128]{1,0:T(8,128)S(1)}, f32[1024,128]{1,0:T(8,128)}, u32[]{:S(2)}) copy-start(f32[1024,128]{1,0:T(8,128)} %copy-done.8) | copy-start | bytes 1572868
  51.8 1.0 %copy-start.11 = (f32[1024,128]{1,0:T(8,128)S(1)}, f32[1024,128]{1,0:T(8,128)}, u32[]{:S(2)}) copy-start(f32[1024,128]{1,0:T(8,128)} %copy-done.10) | copy-start | bytes 1572868

commit v4 on v3

--- a/solution.py
+++ b/solution.py
@@ -21,7 +21,7 @@
 
 VMEM = pl.BlockSpec(memory_space=pltpu.VMEM)
 LIGHT = pl.CostEstimate(flops=1, bytes_accessed=1, transcendentals=0)
-PARAMS = pltpu.CompilerParams(vmem_limit_bytes=40 * 2**20)
+PARAMS = pltpu.CompilerParams(vmem_limit_bytes=12 * 2**20)
 
 
 def swap(value, axis, offset):
@@ -157,16 +157,46 @@
     )(own, *others)
 
 
-def merge_kernel(w_ref, near_ref, out_ref, out_buf, sems):
+def pick_kernel(order, w_ref, out_ref, sems):
     me = lax.axis_index("hi")
-    cube, far, rows, _ = near_ref.shape
+    cube, _, rows, _ = out_ref.shape
+    copies = []
+    for i, h in enumerate(order):
+        for c in range(cube) if len(order) > 1 else [None]:
+            if c is None:
+                source, target = w_ref.at[rows_at(me ^ h, cube)], out_ref.at[:, 0]
+            else:
+                source, target = w_ref.at[(me ^ h) * cube + c], out_ref.at[c, i]
+            copies.append(pltpu.make_async_copy(source, target, sems.at[len(copies)]))
+            copies[-1].start()
+    for copy in copies:
+        copy.wait()
+
+
+def pick(chunks, order):
+    _, rows, _ = chunks.shape
+    return pl.pallas_call(
+        functools.partial(pick_kernel, order),
+        out_shape=jax.ShapeDtypeStruct((CUBE, len(order), rows, HD), chunks.dtype),
+        in_specs=[pl.BlockSpec(memory_space=pl.ANY)],
+        out_specs=VMEM,
+        scratch_shapes=[pltpu.SemaphoreType.DMA((CUBE * len(order),))],
+        compiler_params=PARAMS,
+        cost_estimate=LIGHT,
+    )(chunks)
+
+
+def merge_kernel(order, w_ref, near_ref, *refs):
+    out_ref, out_buf, sems = refs[-3:]
+    me = lax.axis_index("hi")
+    cube, _, rows, _ = near_ref.shape
     stores = []
     for c in range(cube):
-        for h in range(far):
+        for j, h in enumerate(order):
             place = rows_at((me ^ h) * cube + c, rows)
             i = len(stores)
             w = w_ref[place, :].astype(jnp.float32)
-            g = near_ref[c, h].astype(jnp.float32)
+            g = near_ref[c, j].astype(jnp.float32)
             out_buf[i] = (w + mix_rate * (g - w)).astype(jnp.bfloat16)
             stores.append(pltpu.make_async_copy(out_buf.at[i], out_ref.at[place, :], sems.at[i]))
             stores[-1].start()
@@ -174,70 +204,76 @@
         store.wait()
 
 
-def merge(local_weights, near):
-    cube, far, rows, _ = near.shape
-    return pl.pallas_call(
-        merge_kernel,
+def merge(local_weights, near, order, base=None):
+    cube, _, rows, _ = near.shape
+    anywhere = pl.BlockSpec(memory_space=pl.ANY)
+    return pl.pallas_call(
+        functools.partial(merge_kernel, order),
         out_shape=jax.ShapeDtypeStruct(local_weights.shape, jnp.bfloat16),
-        in_specs=[VMEM] * 2,
-        out_specs=pl.BlockSpec(memory_space=pl.ANY),
+        in_specs=[VMEM] * 2 + [anywhere] * (base is not None),
+        out_specs=anywhere,
         scratch_shapes=[
-            pltpu.VMEM((cube * far, rows, HD), jnp.bfloat16),
-            pltpu.SemaphoreType.DMA((cube * far,)),
+            pltpu.VMEM((cube * len(order), rows, HD), jnp.bfloat16),
+            pltpu.SemaphoreType.DMA((cube * len(order),)),
         ],
-        compiler_params=PARAMS,
-        cost_estimate=LIGHT,
-    )(local_weights, near)
+        input_output_aliases={} if base is None else {2: 0},
+        compiler_params=PARAMS,
+        cost_estimate=LIGHT,
+    )(local_weights, near, *([] if base is None else [base]))
 
 
 def body(tokens, norm_gain, local_weights, anchor, momentum, key_grad):
     cores = lax.axis_size("tp")
     far = lax.axis_size("hi")
-    me = lax.axis_index("hi")
     rows, part = tokens.shape
     own_rows = anchor.shape[0]
     inv_width = 1.0 / math.sqrt(part * cores)
-
-    chunks = local_weights.reshape(far, CUBE, own_rows, HD).transpose(1, 0, 2, 3)
-    chunks, tokens, w, key_grad = after(chunks, tokens, local_weights, key_grad)
-    received = lax.all_to_all(chunks, "cube", 0, 0)
+    others = list(range(1, far))
+
+    chunks = local_weights.reshape(far * CUBE, own_rows, HD)
+    sent = pick(chunks, others)
+    sent, tokens, w, key_grad, chunks = after(sent, tokens, local_weights, key_grad, chunks)
+    received = lax.all_to_all(sent, "cube", 0, 0)
+    kept = lax.all_to_all(pick(chunks, [0]), "cube", 0, 0)
     squares = squares_of(tokens)
+    squares_in = [swap(squares, "tp", k) for k in range(1, cores)]
     cosine, signed, packs = prepare(w, key_grad)
-    squares_in = [swap(squares, "tp", k) for k in range(1, cores)]
     packs_in = [swap(pack, "tp", k + 1) for k, pack in enumerate(packs)]
+
+    received, packs_in, tokens, squares_in = after(received, packs_in, tokens, squares_in)
+    summed = jnp.sum(received.astype(jnp.float32), axis=0)
+    sums = [swap(summed[i], "hi", h) for i, h in enumerate(others)]
     own_weights = lax.dynamic_slice_in_dim(w, lax.axis_index("tp") * part, part, 0)
     weights = jnp.concatenate([own_weights] + [pack[:part] for pack in packs_in], axis=1)
     grads = jnp.concatenate([pack[part:] for pack in [packs[0]] + packs_in], axis=1)
     norm = normalize(tokens, sum(squares_in, squares), norm_gain)
     partial = jnp.dot(norm, weights, preferred_element_type=jnp.float32)
-
-    received, partial, tokens, grads = after(received, partial, tokens, grads)
-    summed = jnp.sum(received.astype(jnp.float32), axis=0)
-    sums = [
-        swap(lax.dynamic_index_in_dim(summed, me ^ h, 0, keepdims=False), "hi", h)
-        for h in range(far)
-    ]
     keys_in = [swap(partial[:, k * HD : (k + 1) * HD], "tp", k) for k in range(1, cores)]
+
+    kept, sums, partial, tokens, grads = after(kept, sums, partial, tokens, grads)
+    mean_weights = sum(sums, jnp.sum(kept[:, 0].astype(jnp.float32), axis=0)) / (far * CUBE)
+    change = anchor - mean_weights
+    new_momentum = momentum_rate * momentum + change
+    new_anchor = anchor - outer_rate * (change + momentum_rate * new_momentum)
+    outgoing = new_anchor.astype(jnp.bfloat16)
+
+    column = [swap(outgoing, "hi", h) for h in others]
+    near = lax.all_to_all(jnp.broadcast_to(outgoing, (CUBE, 1, own_rows, HD)), "cube", 0, 0)
     norm = normalize(tokens, sum(squares_in, squares), norm_gain)
     contracted = lax.dot_general(
         norm, grads, (((0,), (0,)), ((), ())), preferred_element_type=jnp.float32
     )
     contracted = (contracted * inv_width).astype(jnp.bfloat16)
 
-    contracted, sums, keys_in = after(contracted, sums, keys_in)
-    mean_weights = sum(sums) / (far * CUBE)
-    change = anchor - mean_weights
-    new_momentum = momentum_rate * momentum + change
-    new_anchor = anchor - outer_rate * (change + momentum_rate * new_momentum)
-    outgoing = new_anchor.astype(jnp.bfloat16)
-
-    column = jnp.stack([swap(outgoing, "hi", h) for h in range(far)])
+    column, near, contracted, keys_in, partial = after(column, near, contracted, keys_in, partial)
+    column = jnp.broadcast_to(jnp.stack(column), (CUBE, len(others), own_rows, HD))
+    rest = lax.all_to_all(column, "cube", 0, 0)
     grads_in = [swap(contracted[:, k * HD : (k + 1) * HD], "tp", k) for k in range(1, cores)]
-    column, grads_in, partial = after(column, grads_in, partial)
-    near = lax.all_to_all(jnp.broadcast_to(column, (CUBE, *column.shape)), "cube", 0, 0)
     key_rows = turn(inv_width, partial, keys_in, cosine, signed)
     weight_grad = place_blocks(contracted, grads_in)
-    merged = merge(w, near)
+    merged = merge(w, near, [0])
+    rest, key_rows, weight_grad, merged = after(rest, key_rows, weight_grad, merged)
+    merged = merge(w, rest, others, merged)
     return (key_rows, weight_grad, merged, new_anchor, new_momentum)
 
 

time: 62.6 us -> 69.7 us (1.11)
  starting transfers between devices: 13.7 us -> 24 us
  waiting for transfers between devices: 16.7 us -> 8.9 us
  Pallas kernels: 4.71 us -> 9.22 us
  local copies, waits for them, and re-layouts: 16.6 us -> 14.4 us
  other arithmetic: 1.78 us -> 3.84 us
    all_to_all x2 -> x4, starting transfers between devices: 10.2 us -> 20.1 us  [the longest x1 6.2 us: body(): received = lax.all_to_all(sent, 'cube', 0, 0)]
    ppermute x6, waiting for transfers between devices: 8.34 us -> 1.55 us  [swap(): return lax.ppermute(value, axis, [(i, i ^ offset) for i in range(size)])]
    pallas_call x1 -> x4, Pallas kernels: 1.16 us -> 5.67 us  [the longest x2 3.87 us: merge(): pl.pallas_call(functools.partial(merge_kernel, order), out_shape=jax.Shap...]
    optimization_barrier x1 -> x0, local copies, waits for them, and re-layouts: 2.4 us -> none  [after(): return lax.optimization_barrier(values)]
    unnamed x32 -> x28, local copies, waits for them, and re-layouts: 10 us -> 11.7 us
    reduce_sum x0 -> x1, other arithmetic: none -> 1.12 us  [body(): jnp.sum(kept[:, 0].astype(jnp.float32), axis=0)]
    all_to_all x2 -> x4, waiting for transfers between devices: 8.4 us -> 7.34 us  [the longest x1 4.26 us: body(): kept = lax.all_to_all(pick(chunks, [0]), 'cube', 0, 0)]
    slice x1, local copies, waits for them, and re-layouts: 1.08 us -> 0.03 us  [body(): pack[:part]]
  transfers between devices with their start and end apart: 8 -> 10, of which waited for: 4 -> 4; matrix products, arithmetic and copies ran while one was open for 20% -> 14% of each run, Pallas kernels for 6% -> 9%
where the time goes in v4:
time: 69.7 us; the launch traced here: 68.8 us
  starting transfers between devices  24 us (34%)
  local copies, waits for them, and re-layouts  14.4 us (21%)
  Pallas kernels  9.22 us (13%)
  waiting for transfers between devices  8.9 us (13%)
  matrix products  7.58 us (11%)
  other arithmetic  3.84 us (6%)
  between operations  0.84 us (1%)
    unnamed x28, local copies, waits for them, and re-layouts  11.7 us
    all_to_all x1, starting transfers between devices, body(): received = lax.all_to_all(sent, 'cube', 0, 0)  6.2 us
    all_to_all x1, starting transfers between devices, body(): kept = lax.all_to_all(pick(chunks, [0]), 'cube', 0, 0)  5.11 us
    all_to_all x1, starting transfers between devices, body(): lax.all_to_all(jnp.broadcast_to(outgoing, (CUBE, 1, own_rows, HD)), 'cube...  4.61 us
    all_to_all x1, waiting for transfers between devices, body(): kept = lax.all_to_all(pick(chunks, [0]), 'cube', 0, 0)  4.26 us
    all_to_all x1, starting transfers between devices, body(): rest = lax.all_to_all(column, 'cube', 0, 0)  4.15 us
    dot_general x1, matrix products, body(): lax.dot_general(norm, grads, (((0,), (0,)), ((), ())), preferred_element_...  3.96 us
    ppermute x6, starting transfers between devices, swap(): return lax.ppermute(value, axis, [(i, i ^ offset) for i in range(size)])  3.95 us
  transfers between devices with their start and end apart: 10, of which 4 were waited for; matrix products, arithmetic and copies ran while one was open for 14% of the time, Pallas kernels for 9%

profile of v4, /device:TPU:0, one launch (start us, length us, event | category | flops | bytes accessed | tf_op | source)
XLA Modules:
  0.0 68.8 jit_solution(2523563604616500431)
XLA Ops:
  0.6 1.2 %copy-done = bf16[4096,128]{1,0:T(8,128)(2,1)S(1)} copy-done((bf16[4096,128]{1,0:T(8,128)(2,1)S(1)}, bf16[4096,128]{1,0:T(8,128)(2,1)}, u32[]{:S(2)}) %copy-start) | copy-done | bytes 1048600
  2.8 6.2 %all-to-all-start.1 = ((bf16[8,1,256,128]{3,2,1,0:T(8,128)(2,1)}), bf16[8,1,256,128]{3,2,1,0:T(8,128)(2,1)S(1)}, u32[]{:S(2)}, u32[]{:S(2)}) async-start(bf16[8,1,256,128]{3,2,1,0:T(8,128)(2,1)} %shard_map.101), calls=%async_computation.1 | async-start | bytes 1048576 | tf_op jit(solution)/shard_map/all_to_all | solution.py:236
  9.0 1.2 %copy-done.1 = bf16[4096,128]{1,0:T(8,128)(2,1)S(1)} copy-done((bf16[4096,128]{1,0:T(8,128)(2,1)S(1)}, bf16[4096,128]{1,0:T(8,128)(2,1)}, u32[]{:S(2)}) %copy-start.1) | copy-done | bytes 1048600
  10.2 0.9 %copy-done.10 = bf16[1024,128]{1,0:T(8,128)(2,1)S(1)} copy-done((bf16[1024,128]{1,0:T(8,128)(2,1)S(1)}, bf16[1024,128]{1,0:T(8,128)(2,1)}, u32[]{:S(2)}) %copy-start.10) | copy-done | bytes 262168
  13.2 2.2 %copy-done.3 = bf16[1024,2048]{1,0:T(8,128)(2,1)S(1)} copy-done((bf16[1024,2048]{1,0:T(8,128)(2,1)S(1)}, bf16[1024,2048]{1,0:T(8,128)(2,1)}, u32[]{:S(2)}) %copy-start.3) | copy-done | bytes 4194328
  15.4 1.1 %shard_map.104 = f32[1,1024]{1,0:T(1,128)S(1)} custom-call(bf16[1024,2048]{1,0:T(8,128)(2,1)S(1)} %copy-done.3), custom_call_target="tpu_custom_call" | custom-call | flops 1 | bytes 1 | tf_op jit(solution)/shard_map/pallas_call | solution.py:99
  18.9 5.1 %all-to-all-start = ((bf16[8,1,256,128]{3,2,1,0:T(8,128)(2,1)}), bf16[8,1,256,128]{3,2,1,0:T(8,128)(2,1)}, u32[]{:S(2)}, u32[]{:S(2)}) async-start(bf16[8,1,256,128]{3,2,1,0:T(8,128)(2,1)} %shard_map.102), calls=%async_computation | async-start | bytes 1048576 | tf_op jit(solution)/shard_map/all_to_all | solution.py:237
  24.1 2.7 %collective-permute-start.2 = (f32[256,128]{1,0:T(8,128)S(1)}, f32[256,128]{1,0:T(8,128)}, u32[]{:S(2)}, u32[]{:S(2)}) collective-permute-start(f32[256,128]{1,0:T(8,128)S(1)} %convert_reduce_fusion.1), channel_id=1, source_target_pairs={{0,16},{16,0},{1,17},{17,1},{2,18},{18,2},{3,19},{19,3},{4,20},{20... | collective-permute-start | bytes 393224 | tf_op jit(solution)/shard_map/ppermute | solution.py:31
  27.4 3.6 %fusion.own_ref = f32[1024,256]{1,0:T(8,128)S(1)} fusion(bf16[1024,2048]{1,0:T(8,128)(2,1)} %x_ref, f32[2048]{0:T(1024)S(1)} %convert_element_type.31, f32[1024]{0:T(1024)S(1)} %add_rsqrt_fusion, bf16[2048,128]{1,0:T(8,128)(2,1)S(1)} %slice.15, bf16[2048,128]{1,0:T(8,128)(2,1)} %constant_dynamic-slice_fusion), kind=kOutput, calls=%fused_computation.2 | convolution fusion | flops 1084227584 | bytes 6303744 | tf_op jit(solution)/shard_map/dot_general | solution.py:250
  31.9 4.3 %all-to-all-done = bf16[8,1,256,128]{3,2,1,0:T(8,128)(2,1)} async-done(((bf16[8,1,256,128]{3,2,1,0:T(8,128)(2,1)}), bf16[8,1,256,128]{3,2,1,0:T(8,128)(2,1)}, u32[]{:S(2)}, u32[]{:S(2)}) %all-to-all-start) | async-done | bytes 524320 | tf_op jit(solution)/shard_map/all_to_all | solution.py:237
  36.2 1.1 %convert_reduce_fusion = f32[256,128]{1,0:T(8,128)S(1)} fusion(bf16[8,1,256,128]{3,2,1,0:T(8,128)(2,1)} %all-to-all-done), kind=kLoop, calls=%fused_computation.13 | loop fusion | flops 491520 | bytes 655360 | tf_op jit(solution)/shard_map/reduce_sum | solution.py:254
  37.3 1.8 %fusion.12 = (bf16[256,128]{1,0:T(8,128)(2,1)S(1)}, f32[256,128]{1,0:T(8,128)}, f32[256,128]{1,0:T(8,128)}) fusion(f32[256,128]{1,0:T(8,128)} %param.9, f32[256,128]{1,0:T(8,128)S(1)} %convert_reduce_fusion, f32[256,128]{1,0:T(8,128)} %collective-permute-done.2, f32[256,128]{1,0:T(8,128)} %param.10), kind=kLoop, calls=%fused_computation.22 | loop fusion | flops 327680 | bytes 851968 | tf_op jit(solution)/shard_map/convert_element_type | solution.py:258
  39.9 4.6 %all-to-all-start.2 = ((bf16[8,1,256,128]{3,2,1,0:T(8,128)(2,1)}), bf16[8,1,256,128]{3,2,1,0:T(8,128)(2,1)}, u32[]{:S(2)}, u32[]{:S(2)}) async-start(bf16[8,1,256,128]{3,2,1,0:T(8,128)(2,1)} %broadcast_in_dim.4), calls=%async_computation.2 | async-start | bytes 1048576 | tf_op jit(solution)/shard_map/all_to_all | solution.py:261
  45.2 4.0 %fusion.7.own_ref = bf16[2048,256]{1,0:T(8,128)(2,1)S(1)} fusion(bf16[1024,256]{1,0:T(8,128)(2,1)} %pad_maximum_fusion, bf16[1024,2048]{1,0:T(8,128)(2,1)} %x_ref, f32[2048]{0:T(1024)S(1)} %convert_element_type.31, f32[1024]{0:T(1024)S(1)} %copy-done.13), kind=kOutput, calls=%fused_computation.9 | convolution fusion | flops 1083179008 | bytes 5779456 | tf_op jit(solution)/shard_map/dot_general | solution.py:263
  49.2 1.5 %collective-permute-done.3 = bf16[256,128]{1,0:T(8,128)(2,1)S(1)} collective-permute-done((bf16[256,128]{1,0:T(8,128)(2,1)S(1)}, bf16[256,128]{1,0:T(8,128)(2,1)S(1)}, u32[]{:S(2)}, u32[]{:S(2)}) %collective-permute-start.3) | collective-permute-done | bytes 65568 | tf_op jit(solution)/shard_map/ppermute | solution.py:31
  51.5 2.6 %all-to-all-done.2.near_ref = bf16[8,1,256,128]{3,2,1,0:T(8,128)(2,1)} async-done(((bf16[8,1,256,128]{3,2,1,0:T(8,128)(2,1)}), bf16[8,1,256,128]{3,2,1,0:T(8,128)(2,1)}, u32[]{:S(2)}, u32[]{:S(2)}) %all-to-all-start.2) | async-done | bytes 524320 | tf_op jit(solution)/shard_map/all_to_all | solution.py:261
  55.0 4.1 %all-to-all-start.3 = ((bf16[8,1,256,128]{3,2,1,0:T(8,128)(2,1)}), bf16[8,1,256,128]{3,2,1,0:T(8,128)(2,1)}, u32[]{:S(2)}, u32[]{:S(2)}) async-start(bf16[8,1,256,128]{3,2,1,0:T(8,128)(2,1)} %broadcast_in_dim.5), calls=%async_computation.3 | async-start | bytes 1048576 | tf_op jit(solution)/shard_map/all_to_all | solution.py:270
  59.3 1.9 %shard_map.107.refs_0_ = bf16[4096,128]{1,0:T(8,128)(2,1)} custom-call(bf16[4096,128]{1,0:T(8,128)(2,1)S(1)} %copy-done.2, bf16[8,1,256,128]{3,2,1,0:T(8,128)(2,1)} %all-to-all-done.2.near_ref), custom_call_target="tpu_custom_call" | custom-call | flops 1 | bytes 1 | tf_op jit(solution)/shard_map/pallas_call | solution.py:210
  61.3 1.0 %copy-done.5 = f32[1024,128]{1,0:T(8,128)S(1)} copy-done((f32[1024,128]{1,0:T(8,128)S(1)}, f32[1024,128]{1,0:T(8,128)}, u32[]{:S(2)}) %copy-start.5) | copy-done | bytes 524312
  62.3 1.0 %copy-done.7 = f32[1024,128]{1,0:T(8,128)S(1)} copy-done((f32[1024,128]{1,0:T(8,128)S(1)}, f32[1024,128]{1,0:T(8,128)}, u32[]{:S(2)}) %copy-start.7) | copy-done | bytes 524312
  63.3 1.0 %copy-done.9 = f32[1024,128]{1,0:T(8,128)S(1)} copy-done((f32[1024,128]{1,0:T(8,128)S(1)}, f32[1024,128]{1,0:T(8,128)}, u32[]{:S(2)}) %copy-start.9) | copy-done | bytes 524312
  64.4 0.9 %shard_map.105 = bf16[1024,128]{1,0:T(8,128)(2,1)} custom-call(f32[1024,256]{1,0:T(8,128)S(1)} %fusion.own_ref, f32[1024,128]{1,0:T(8,128)S(1)} %copy-done.9, f32[1024,128]{1,0:T(8,128)S(1)} %copy-done.5, f32[1024,128]{1,0:T(8,128)S(1)} %copy-done.7), custom_call_target="tpu_custom_call" | custom-call | flops 1 | bytes 1 | tf_op jit(solution)/shard_map/pallas_call | solution.py:123
  65.3 1.1 %shard_map.106 = bf16[4096,128]{1,0:T(8,128)(2,1)} custom-call(bf16[2048,256]{1,0:T(8,128)(2,1)S(1)} %fusion.7.own_ref, bf16[2048,128]{1,0:T(8,128)(2,1)S(1)} %collective-permute-done.5.refs_0_), custom_call_target="tpu_custom_call" | custom-call | flops 1 | bytes 1 | tf_op jit(solution)/shard_map/pallas_call | solution.py:150
  66.9 1.9 %shard_map.108 = bf16[4096,128]{1,0:T(8,128)(2,1)} custom-call(bf16[4096,128]{1,0:T(8,128)(2,1)S(1)} %copy-done.2, bf16[8,1,256,128]{3,2,1,0:T(8,128)(2,1)} %all-to-all-done.3.near_ref, bf16[4096,128]{1,0:T(8,128)(2,1)} %shard_map.107.refs_0_), custom_call_target="tpu_custom_call", output_to_operand_aliasing={{}: (2, {})} | custom-call | flops 1 | bytes 1 | tf_op jit(solution)/shard_map/pallas_call | solution.py:210
  (48 shorter events, 10.6 us)
Async XLA Ops:
  0.6 1.2 %copy-start = (bf16[4096,128]{1,0:T(8,128)(2,1)S(1)}, bf16[4096,128]{1,0:T(8,128)(2,1)}, u32[]{:S(2)}) copy-start(bf16[4096,128]{1,0:T(8,128)(2,1)} %w_ref.2) | copy-start | bytes 3145732
  1.9 15.2 %copy-start.2 = (bf16[4096,128]{1,0:T(8,128)(2,1)S(1)}, bf16[4096,128]{1,0:T(8,128)(2,1)}, u32[]{:S(2)}) copy-start(bf16[4096,128]{1,0:T(8,128)(2,1)} %w_ref.2) | copy-start | bytes 3145732
  2.8 16.1 %all-to-all-start.1 = ((bf16[8,1,256,128]{3,2,1,0:T(8,128)(2,1)}), bf16[8,1,256,128]{3,2,1,0:T(8,128)(2,1)S(1)}, u32[]{:S(2)}, u32[]{:S(2)}) async-start(bf16[8,1,256,128]{3,2,1,0:T(8,128)(2,1)} %shard_map.101), calls=%async_computation.1 | async-start | bytes 1048576 | tf_op jit(solution)/shard_map/all_to_all | solution.py:236
  9.0 1.2 %copy-start.1 = (bf16[4096,128]{1,0:T(8,128)(2,1)S(1)}, bf16[4096,128]{1,0:T(8,128)(2,1)}, u32[]{:S(2)}) copy-start(bf16[4096,128]{1,0:T(8,128)(2,1)} %w_ref.2) | copy-start | bytes 3145732
  10.2 0.9 %copy-start.10 = (bf16[1024,128]{1,0:T(8,128)(2,1)S(1)}, bf16[1024,128]{1,0:T(8,128)(2,1)}, u32[]{:S(2)}) copy-start(bf16[1024,128]{1,0:T(8,128)(2,1)} %grad_ref) | copy-start | bytes 786436
  11.1 7.7 %copy-start.11 = (bf16[2048]{0:T(1024)(128)(2,1)S(1)}, bf16[2048]{0:T(1024)(128)(2,1)}, u32[]{:S(2)}) copy-start(bf16[2048]{0:T(1024)(128)(2,1)} %param.7) | copy-start | bytes 12292
  11.5 0.8 %copy-start.4 = (f32[1024,128]{1,0:T(8,128)}, f32[1024,128]{1,0:T(8,128)S(1)}, u32[]{:S(2)}) copy-start(f32[1024,128]{1,0:T(8,128)S(1)} %get-tuple-element.49.refs_1_) | copy-start | bytes 1572868
  12.3 0.8 %copy-start.6 = (f32[1024,128]{1,0:T(8,128)}, f32[1024,128]{1,0:T(8,128)S(1)}, u32[]{:S(2)}) copy-start(f32[1024,128]{1,0:T(8,128)S(1)} %get-tuple-element.50.refs_2_) | copy-start | bytes 1572868
  13.2 10.8 %collective-permute-start = (bf16[3072,128]{1,0:T(8,128)(2,1)S(1)}, bf16[3072,128]{1,0:T(8,128)(2,1)S(1)}, u32[]{:S(2)}, u32[]{:S(2)}) collective-permute-start(bf16[3072,128]{1,0:T(8,128)(2,1)S(1)} %get-tuple-element.35), channel_id=1, source_target_pairs={{0,1},{1,0},{2,3},{3,2},{4,5},{5,4},{6,7},{7,6},{8,9},{9,8},{10,11... | collective-permute-start | bytes 2359304 | tf_op jit(solution)/shard_map/ppermute | solution.py:31
  13.2 2.2 %copy-start.3 = (bf16[1024,2048]{1,0:T(8,128)(2,1)S(1)}, bf16[1024,2048]{1,0:T(8,128)(2,1)}, u32[]{:S(2)}) copy-start(bf16[1024,2048]{1,0:T(8,128)(2,1)} %x_ref) | copy-start | bytes 12582916
  16.5 7.5 %collective-permute-start.1 = (f32[1024]{0:T(1024)S(1)}, f32[1024]{0:T(1024)S(1)}, u32[]{:S(2)}, u32[]{:S(2)}) collective-permute-start(f32[1024]{0:T(1024)S(1)} %bitcast.5), channel_id=1, source_target_pairs={{0,1},{1,0},{2,3},{3,2},{4,5},{5,4},{6,7},{7,6},{8,9},{9,8},{10,11... | collective-permute-start | bytes 12296 | tf_op jit(solution)/shard_map/ppermute | solution.py:31
  18.9 17.3 %all-to-all-start = ((bf16[8,1,256,128]{3,2,1,0:T(8,128)(2,1)}), bf16[8,1,256,128]{3,2,1,0:T(8,128)(2,1)}, u32[]{:S(2)}, u32[]{:S(2)}) async-start(bf16[8,1,256,128]{3,2,1,0:T(8,128)(2,1)} %shard_map.102), calls=%async_computation | async-start | bytes 1048576 | tf_op jit(solution)/shard_map/all_to_all | solution.py:237
  24.1 12.1 %collective-permute-start.2 = (f32[256,128]{1,0:T(8,128)S(1)}, f32[256,128]{1,0:T(8,128)}, u32[]{:S(2)}, u32[]{:S(2)}) collective-permute-start(f32[256,128]{1,0:T(8,128)S(1)} %convert_reduce_fusion.1), channel_id=1, source_target_pairs={{0,16},{16,0},{1,17},{17,1},{2,18},{18,2},{3,19},{19,3},{4,20},{20... | collective-permute-start | bytes 393224 | tf_op jit(solution)/shard_map/ppermute | solution.py:31
  26.8 0.6 copy-start.12
  31.0 14.2 %copy-start.13 = (f32[1024]{0:T(1024)S(1)}, f32[1024]{0:T(1024)}, u32[]{:S(2)}) copy-start(f32[1024]{0:T(1024)} %copy-done.12) | copy-start | bytes 12292
  39.9 14.2 %all-to-all-start.2 = ((bf16[8,1,256,128]{3,2,1,0:T(8,128)(2,1)}), bf16[8,1,256,128]{3,2,1,0:T(8,128)(2,1)}, u32[]{:S(2)}, u32[]{:S(2)}) async-start(bf16[8,1,256,128]{3,2,1,0:T(8,128)(2,1)} %broadcast_in_dim.4), calls=%async_computation.2 | async-start | bytes 1048576 | tf_op jit(solution)/shard_map/all_to_all | solution.py:261
  44.6 6.2 %collective-permute-start.4 = (f32[1024,128]{1,0:T(8,128)S(1)}, f32[1024,128]{1,0:T(8,128)S(1)}, u32[]{:S(2)}, u32[]{:S(2)}) collective-permute-start(f32[1024,128]{1,0:T(8,128)S(1)} %slice.20), channel_id=1, source_target_pairs={{0,1},{1,0},{2,3},{3,2},{4,5},{5,4},{6,7},{7,6},{8,9},{9,8},{10,11... | collective-permute-start | bytes 1572872 | tf_op jit(solution)/shard_map/ppermute | solution.py:31
  44.7 6.1 %collective-permute-start.3 = (bf16[256,128]{1,0:T(8,128)(2,1)S(1)}, bf16[256,128]{1,0:T(8,128)(2,1)S(1)}, u32[]{:S(2)}, u32[]{:S(2)}) collective-permute-start(bf16[256,128]{1,0:T(8,128)(2,1)S(1)} %get-tuple-element.57), channel_id=1, source_target_pairs={{0,16},{16,0},{1,17},{17,1},{2,18},{18,2},{3,19},{19,3},{4,20},{20... | collective-permute-start | bytes 196616 | tf_op jit(solution)/shard_map/ppermute | solution.py:31
  50.8 0.8 %copy-start.8 = (f32[1024,128]{1,0:T(8,128)}, f32[1024,128]{1,0:T(8,128)S(1)}, u32[]{:S(2)}) copy-start(f32[1024,128]{1,0:T(8,128)S(1)} %collective-permute-done.4.refs_0_) | copy-start | bytes 1572868
  55.0 11.8 %all-to-all-start.3 = ((bf16[8,1,256,128]{3,2,1,0:T(8,128)(2,1)}), bf16[8,1,256,128]{3,2,1,0:T(8,128)(2,1)}, u32[]{:S(2)}, u32[]{:S(2)}) async-start(bf16[8,1,256,128]{3,2,1,0:T(8,128)(2,1)} %broadcast_in_dim.5), calls=%async_computation.3 | async-start | bytes 1048576 | tf_op jit(solution)/shard_map/all_to_all | solution.py:270
  59.2 6.1 %collective-permute-start.5 = (bf16[2048,128]{1,0:T(8,128)(2,1)S(1)}, bf16[2048,128]{1,0:T(8,128)(2,1)S(1)}, u32[]{:S(2)}, u32[]{:S(2)}) collective-permute-start(bf16[2048,128]{1,0:T(8,128)(2,1)S(1)} %slice.19), channel_id=1, source_target_pairs={{0,1},{1,0},{2,3},{3,2},{4,5},{5,4},{6,7},{7,6},{8,9},{9,8},{10,11... | collective-permute-start | bytes 1572872 | tf_op jit(solution)/shard_map/ppermute | solution.py:31
  61.2 1.0 %copy-start.5 = (f32[1024,128]{1,0:T(8,128)S(1)}, f32[1024,128]{1,0:T(8,128)}, u32[]{:S(2)}) copy-start(f32[1024,128]{1,0:T(8,128)} %copy-done.4) | copy-start | bytes 1572868
  62.3 1.0 %copy-start.7 = (f32[1024,128]{1,0:T(8,128)S(1)}, f32[1024,128]{1,0:T(8,128)}, u32[]{:S(2)}) copy-start(f32[1024,128]{1,0:T(8,128)} %copy-done.6) | copy-start | bytes 1572868
  63.3 1.0 %copy-start.9 = (f32[1024,128]{1,0:T(8,128)S(1)}, f32[1024,128]{1,0:T(8,128)}, u32[]{:S(2)}) copy-start(f32[1024,128]{1,0:T(8,128)} %copy-done.8) | copy-start | bytes 1572868

commit v5 on v3

v5 whole, which is shorter than its diff:
```python
import functools
import math

import jax
import jax.numpy as jnp
from jax import lax
from jax.experimental import pallas as pl
from jax.experimental.pallas import tpu as pltpu
from jax.sharding import PartitionSpec as P

HD = 128
PLANE = 4
CUBE = 8
SPAN = 32


momentum_rate = 0.9
outer_rate = 0.7
mix_rate = 0.5
rope_base = 500000.0
norm_eps = 1e-05

VMEM = pl.BlockSpec(memory_space=pltpu.VMEM)
LIGHT = pl.CostEstimate(flops=1, bytes_accessed=1, transcendentals=0)
PARAMS = pltpu.CompilerParams(vmem_limit_bytes=12 * 2**20)


def swap(value, axis, offset):
    size = lax.axis_size(axis)
    if not offset:
        return value
    return lax.ppermute(value, axis, [(i, i ^ offset) for i in range(size)])


def after(*values):
    return lax.optimization_barrier(values)


def rows_at(index, rows):
    return pl.ds(pl.multiple_of(index * rows, rows), rows)


def pick_kernel(w_ref, *out_refs):
    me = lax.axis_index("rep")
    far, rows, _ = out_refs[0].shape
    for c, out in enumerate(out_refs):
        for h in range(far):
            out[h] = w_ref[rows_at(me ^ (h * CUBE + c), rows), :]


def pick(local_weights, rows):
    far = local_weights.shape[0] // (CUBE * rows)
    shape = jax.ShapeDtypeStruct((far, rows, HD), local_weights.dtype)
    return pl.pallas_call(
        pick_kernel,
        out_shape=[shape] * CUBE,
        in_specs=[VMEM],
        out_specs=[VMEM] * CUBE,
        compiler_params=PARAMS,
        cost_estimate=LIGHT,
    )(local_weights)


def prepare_kernel(grad_ref, cos_ref, sin_ref, out_ref):
    rows = grad_ref.shape[0]
    lane = lax.broadcasted_iota(jnp.int32, (SPAN, HD), 1)
    lower = lane < HD // 2
    pair = jnp.where(lower, lane, lane - HD // 2).astype(jnp.float32)
    freq = jnp.exp(-(pair * 2.0 / HD) * math.log(rope_base))
    step = lax.broadcasted_iota(jnp.int32, (SPAN, HD), 0).astype(jnp.float32)
    near_cos, near_sin = jnp.cos(step * freq), jnp.sin(step * freq)
    near_sin = jnp.where(lower, -near_sin, near_sin)
    for block in range(0, rows // SPAN, SPAN):
        far = (step + block) * SPAN * freq
        far_cos, far_sin = jnp.cos(far), jnp.sin(far)
        far_sin = jnp.where(lower, -far_sin, far_sin)
        for i in range(min(SPAN, rows // SPAN - block)):
            place = pl.ds((block + i) * SPAN, SPAN)
            a_cos, a_sin = far_cos[i : i + 1], far_sin[i : i + 1]
            cosine = a_cos * near_cos - a_sin * near_sin
            signed = a_sin * near_cos + a_cos * near_sin
            cos_ref[place, :] = cosine
            sin_ref[place, :] = signed
            grad = grad_ref[place, :].astype(jnp.float32)
            turned = grad * cosine - pltpu.roll(grad, HD // 2, 1) * signed
            out_ref[place, :] = turned.astype(jnp.bfloat16)


def prepare(key_grad):
    table = jax.ShapeDtypeStruct(key_grad.shape, jnp.float32)
    return pl.pallas_call(
        prepare_kernel,
        out_shape=[table, table, jax.ShapeDtypeStruct(key_grad.shape, jnp.bfloat16)],
        in_specs=[VMEM],
        out_specs=[VMEM] * 3,
        compiler_params=PARAMS,
        cost_estimate=LIGHT,
    )(key_grad)


def squares_kernel(x_ref, out_ref):
    total = None
    for c in range(x_ref.shape[1] // HD):
        x = x_ref[:, c * HD : (c + 1) * HD].astype(jnp.float32)
        total = x * x if total is None else total + x * x
    out_ref[...] = jnp.sum(total.T, axis=0, keepdims=True)


def squares_of(tokens):
    rows, part = tokens.shape
    block = 256
    out = pl.pallas_call(
        squares_kernel,
        out_shape=jax.ShapeDtypeStruct((1, rows), jnp.float32),
        grid=(rows // block,),
        in_specs=[pl.BlockSpec((block, part), lambda i: (i, 0))],
        out_specs=pl.BlockSpec((1, block), lambda i: (0, i)),
        compiler_params=PARAMS,
        cost_estimate=LIGHT,
    )(tokens)
    return out.reshape(rows)


def turn_kernel(inv_width, raw_ref, cos_ref, sin_ref, out_ref):
    keys = raw_ref[...] * inv_width
    turned = keys * cos_ref[...] + pltpu.roll(keys, HD // 2, 1) * sin_ref[...]
    out_ref[...] = turned.astype(jnp.bfloat16)


def turn(inv_width, raw_keys, cosine, signed):
    return pl.pallas_call(
        functools.partial(turn_kernel, inv_width),
        out_shape=jax.ShapeDtypeStruct(raw_keys.shape, jnp.bfloat16),
        in_specs=[VMEM] * 3,
        out_specs=VMEM,
        compiler_params=PARAMS,
        cost_estimate=LIGHT,
    )(raw_keys, cosine, signed)


def normalize(tokens, scale, norm_gain):
    return (tokens.astype(jnp.float32) * scale * norm_gain.astype(jnp.float32)).astype(jnp.bfloat16)


def place_kernel(*refs):
    *block_refs, out_ref = refs
    me = lax.axis_index("tp")
    part = block_refs[0].shape[0]
    for k, block in enumerate(block_refs):
        out_ref[rows_at(me ^ k, part), :] = block[...]


def place_blocks(blocks):
    part, _ = blocks[0].shape
    return pl.pallas_call(
        place_kernel,
        out_shape=jax.ShapeDtypeStruct((len(blocks) * part, HD), blocks[0].dtype),
        in_specs=[VMEM] * len(blocks),
        out_specs=VMEM,
        compiler_params=PARAMS,
        cost_estimate=LIGHT,
    )(*blocks)


def merge_kernel(offsets, w_ref, *refs):
    count = len(offsets)
    out_ref, out_buf, sems = refs[-3:]
    me = lax.axis_index("rep")
    rows = out_buf.shape[1]
    stores = []
    for chunk, ref in zip(offsets, refs):
        for j, k in enumerate(chunk):
            place = rows_at(me ^ k, rows)
            i = len(stores)
            w = w_ref[place, :].astype(jnp.float32)
            g = ref[j].astype(jnp.float32)
            out_buf[i] = (w + mix_rate * (g - w)).astype(jnp.bfloat16)
            stores.append(pltpu.make_async_copy(out_buf.at[i], out_ref.at[place, :], sems.at[i]))
            stores[-1].start()
    for store in stores:
        store.wait()


def merge(local_weights, chunks, offsets, base=None):
    rows = chunks[0].shape[1]
    anywhere = pl.BlockSpec(memory_space=pl.ANY)
    args = [local_weights, *chunks]
    specs = [VMEM] * len(args)
    aliases = {}
    if base is not None:
        aliases = {len(args): 0}
        args.append(base)
        specs.append(anywhere)
    count = sum(map(len, offsets))
    return pl.pallas_call(
        functools.partial(merge_kernel, offsets),
        out_shape=jax.ShapeDtypeStruct(local_weights.shape, jnp.bfloat16),
        in_specs=specs,
        out_specs=anywhere,
        scratch_shapes=[
            pltpu.VMEM((count, rows, HD), jnp.bfloat16),
            pltpu.SemaphoreType.DMA((count,)),
        ],
        input_output_aliases=aliases,
        compiler_params=PARAMS,
        cost_estimate=LIGHT,
    )(*args)


def body(tokens, norm_gain, local_weights, anchor, momentum, key_grad):
    cores = lax.axis_size("tp")
    replicas = lax.axis_size("rep")
    far = replicas // PLANE
    rows, part = tokens.shape
    inv_width = 1.0 / math.sqrt(part * cores)

    x = [swap(tokens, "tp", k) for k in range(cores)]
    gain = [swap(norm_gain, "tp", k) for k in range(cores)]
    picked = pick(local_weights, anchor.shape[0])
    picked, w, own, key_grad = after(picked, local_weights, tokens, key_grad)
    x[0] = own
    cube = [swap(picked[c], "rep", c) for c in (7, 3, 5, 6, 1, 2, 4)]
    squares = squares_of(own)
    cosine, signed, raw_grad = prepare(key_grad)

    cube, squares, raw_grad, x, gain = after(cube, squares, raw_grad, x, gain)
    total = picked[0].astype(jnp.float32)
    for block in cube:
        total = total + block.astype(jnp.float32)
    sums = [swap(total[h], "rep", h * CUBE) if h else total[h] for h in range(replicas // CUBE)]
    for k in range(1, cores):
        squares = squares + squares_of(x[k])
    scale = lax.rsqrt(squares / (part * cores) + norm_eps)[:, None]
    me = lax.axis_index("tp")
    raw_keys = 0.0
    for k in range(cores):
        block = lax.dynamic_slice_in_dim(w, (me ^ k) * part, part, 0)
        norm = normalize(x[k], scale, gain[k])
        raw_keys = raw_keys + jnp.dot(norm, block, preferred_element_type=jnp.float32)

    sums, raw_keys, x, scale = after(sums, raw_keys, x, scale)
    mean_weights = sum(sums) / replicas
    change = anchor - mean_weights
    new_momentum = momentum_rate * momentum + change
    new_anchor = anchor - outer_rate * (change + momentum_rate * new_momentum)
    outgoing = new_anchor.astype(jnp.bfloat16)[None]

    columns = [swap(outgoing, "rep", z * PLANE) for z in range(far - 1, 0, -1)]
    blocks = []
    for k in range(cores):
        norm = normalize(x[k], scale, gain[k])
        contracted = lax.dot_general(
            norm, raw_grad, (((0,), (0,)), ((), ())), preferred_element_type=jnp.float32
        )
        blocks.append((contracted * inv_width).astype(jnp.bfloat16))
    near = [outgoing] + [swap(outgoing, "rep", p) for p in range(1, PLANE)]
    blocks, near, raw_keys, columns = after(blocks, near, raw_keys, columns)
    block = jnp.concatenate(columns)
    rest = [block] + [swap(block, "rep", p) for p in range(1, PLANE)]
    key_rows = turn(inv_width, raw_keys, cosine, signed)
    weight_grad = place_blocks(blocks)

    zs = range(far - 1, 0, -1)
    early = near + rest[:1]
    merged = merge(w, early, [[p] for p in range(PLANE)] + [[z * PLANE for z in zs]])
    offsets = [[z * PLANE + p for z in zs] for p in range(1, PLANE)]
    key_rows, weight_grad, merged, *rest = after(key_rows, weight_grad, merged, *rest[1:])
    merged = merge(w, rest, offsets, merged)
    return (key_rows, weight_grad, merged, new_anchor, new_momentum)


def solution(mesh):
    split = P("rep", "tp")
    return jax.shard_map(
        body,
        mesh=mesh,
        in_specs=(split, P("tp"), split, split, split, split),
        out_specs=(split,) * 5,
        check_vma=False,
    )
```

time: 62.6 us -> 65.1 us (1.040)
  starting transfers between devices: 13.7 us -> 29.3 us
  local copies, waits for them, and re-layouts: 16.6 us -> 3.5 us
  waiting for transfers between devices: 16.7 us -> 9.73 us
  Pallas kernels: 4.71 us -> 8.8 us
  matrix products: 7.61 us -> 10.6 us
    ppermute x6 -> x19, starting transfers between devices: 3.5 us -> 29.3 us  [swap(): return lax.ppermute(value, axis, [(i, i ^ offset) for i in range(size)])]
    all_to_all x2 -> x0, starting transfers between devices: 10.2 us -> none  [the longest x1 6.31 us: body(): received = lax.all_to_all(chunks, 'cube', 0, 0)]
    all_to_all x2 -> x0, waiting for transfers between devices: 8.4 us -> none  [the longest x1 7.13 us: body(): lax.all_to_all(jnp.broadcast_to(column, (CUBE, *column.shape)), 'cube', 0...]
    unnamed x32 -> x18, local copies, waits for them, and re-layouts: 10 us -> 3.46 us
    pallas_call x1 -> x2, Pallas kernels: 1.15 us -> 4.58 us  [squares_of(): pl.pallas_call(squares_kernel, out_shape=jax.ShapeDtypeStruct((1, rows),...]
    dot_general x2 -> x4, matrix products: 7.61 us -> 10.6 us  [the longest x2 5.61 us: body(): lax.dot_general(norm, raw_grad, (((0,), (0,)), ((), ())), preferred_eleme...]
    optimization_barrier x1 -> x0, local copies, waits for them, and re-layouts: 2.4 us -> none  [after(): return lax.optimization_barrier(values)]
    slice x5 -> x0, local copies, waits for them, and re-layouts: 2.13 us -> none  [the longest x1 1.08 us: body(): pack[:part]]
  transfers between devices with their start and end apart: 8 -> 19, of which waited for: 4 -> 7; matrix products, arithmetic and copies ran while one was open for 20% -> 16% of each run, Pallas kernels for 6% -> 7%
where the time goes in v5:
time: 65.1 us; the launch traced here: 64.7 us
  starting transfers between devices  29.3 us (45%)
  matrix products  10.6 us (16%)
  waiting for transfers between devices  9.73 us (15%)
  Pallas kernels  8.8 us (14%)
  local copies, waits for them, and re-layouts  3.5 us (5%)
  other arithmetic  1.93 us (3%)
  between operations  0.88 us (1%)
    ppermute x19, starting transfers between devices, swap(): return lax.ppermute(value, axis, [(i, i ^ offset) for i in range(size)])  29.3 us
    ppermute x19, waiting for transfers between devices, swap(): return lax.ppermute(value, axis, [(i, i ^ offset) for i in range(size)])  9.73 us
    dot_general x2, matrix products, body(): lax.dot_general(norm, raw_grad, (((0,), (0,)), ((), ())), preferred_eleme...  5.61 us
    dot_general x2, matrix products, body(): jnp.dot(norm, block, preferred_element_type=jnp.float32)  5.03 us
    pallas_call x2, Pallas kernels, squares_of(): pl.pallas_call(squares_kernel, out_shape=jax.ShapeDtypeStruct((1, rows),...  4.58 us
    unnamed x18, local copies, waits for them, and re-layouts  3.46 us
    pallas_call x2, Pallas kernels, merge(): pl.pallas_call(functools.partial(merge_kernel, offsets), out_shape=jax.Sh...  1.8 us
  transfers between devices with their start and end apart: 19, of which 7 were waited for; matrix products, arithmetic and copies ran while one was open for 16% of the time, Pallas kernels for 7%

profile of v5, /device:TPU:0, one launch (start us, length us, event | category | flops | bytes accessed | tf_op | source)
XLA Modules:
  0.0 64.7 jit_solution(8140880618176493440)
XLA Ops:
  1.2 1.2 %copy-done = bf16[4096,128]{1,0:T(8,128)(2,1)S(1)} copy-done((bf16[4096,128]{1,0:T(8,128)(2,1)S(1)}, bf16[4096,128]{1,0:T(8,128)(2,1)}, u32[]{:S(2)}) %copy-start) | copy-done | bytes 1048600
  2.4 4.5 %collective-permute-start = (bf16[2,256,128]{2,1,0:T(8,128)(2,1)S(1)}, bf16[2,256,128]{2,1,0:T(8,128)(2,1)S(1)}, u32[]{:S(2)}, u32[]{:S(2)}) collective-permute-start(bf16[2,256,128]{2,1,0:T(8,128)(2,1)S(1)} %get-tuple-element.71), channel_id=1, source_target_pairs={{0,14},{2,12},{4,10},{6,8},{8,6},{10,4},{12,2},{14,0},{16,30},{18,... | collective-permute-start | bytes 393224 | tf_op jit(solution)/shard_map/ppermute | solution.py:32
  7.5 1.4 %collective-permute-start.2 = (bf16[2,256,128]{2,1,0:T(8,128)(2,1)S(1)}, bf16[2,256,128]{2,1,0:T(8,128)(2,1)S(1)}, u32[]{:S(2)}, u32[]{:S(2)}) collective-permute-start(bf16[2,256,128]{2,1,0:T(8,128)(2,1)S(1)} %get-tuple-element.73), channel_id=1, source_target_pairs={{0,10},{2,8},{4,14},{6,12},{8,2},{10,0},{12,6},{14,4},{16,26},{18,... | collective-permute-start | bytes 393224 | tf_op jit(solution)/shard_map/ppermute | solution.py:32
  8.8 1.4 %collective-permute-done.8 = bf16[2048]{0:T(1024)(128)(2,1)S(1)} collective-permute-done((bf16[2048]{0:T(1024)(128)(2,1)}, bf16[2048]{0:T(1024)(128)(2,1)S(1)}, u32[]{:S(2)}, u32[]{:S(2)}) %collective-permute-start.8) | collective-permute-done | bytes 4128 | tf_op jit(solution)/shard_map/ppermute | solution.py:32
  10.2 2.5 %collective-permute-start.3 = (bf16[2,256,128]{2,1,0:T(8,128)(2,1)S(1)}, bf16[2,256,128]{2,1,0:T(8,128)(2,1)S(1)}, u32[]{:S(2)}, u32[]{:S(2)}) collective-permute-start(bf16[2,256,128]{2,1,0:T(8,128)(2,1)S(1)} %get-tuple-element.74), channel_id=1, source_target_pairs={{0,12},{2,14},{4,8},{6,10},{8,4},{10,6},{12,0},{14,2},{16,28},{18,... | collective-permute-start | bytes 393224 | tf_op jit(solution)/shard_map/ppermute | solution.py:32
  13.5 4.5 %collective-permute-done.1 = bf16[2,256,128]{2,1,0:T(8,128)(2,1)S(1)} collective-permute-done((bf16[2,256,128]{2,1,0:T(8,128)(2,1)S(1)}, bf16[2,256,128]{2,1,0:T(8,128)(2,1)S(1)}, u32[]{:S(2)}, u32[]{:S(2)}) %collective-permute-start.1) | collective-permute-done | bytes 131104 | tf_op jit(solution)/shard_map/ppermute | solution.py:32
  18.1 2.9 %collective-permute-start.5 = (bf16[2,256,128]{2,1,0:T(8,128)(2,1)S(1)}, bf16[2,256,128]{2,1,0:T(8,128)(2,1)}, u32[]{:S(2)}, u32[]{:S(2)}) collective-permute-start(bf16[2,256,128]{2,1,0:T(8,128)(2,1)S(1)} %get-tuple-element.76), channel_id=1, source_target_pairs={{0,4},{2,6},{4,0},{6,2},{8,12},{10,14},{12,8},{14,10},{16,20},{18,... | collective-permute-start | bytes 393224 | tf_op jit(solution)/shard_map/ppermute | solution.py:32
  21.0 1.6 %collective-permute-start.6 = (bf16[2,256,128]{2,1,0:T(8,128)(2,1)S(1)}, bf16[2,256,128]{2,1,0:T(8,128)(2,1)}, u32[]{:S(2)}, u32[]{:S(2)}) collective-permute-start(bf16[2,256,128]{2,1,0:T(8,128)(2,1)S(1)} %get-tuple-element.77), channel_id=1, source_target_pairs={{0,8},{2,10},{4,12},{6,14},{8,0},{10,2},{12,4},{14,6},{16,24},{18,... | collective-permute-start | bytes 393224 | tf_op jit(solution)/shard_map/ppermute | solution.py:32
  22.6 2.2 %copy-done.2 = bf16[1024,2048]{1,0:T(8,128)(2,1)S(1)} copy-done((bf16[1024,2048]{1,0:T(8,128)(2,1)S(1)}, bf16[1024,2048]{1,0:T(8,128)(2,1)}, u32[]{:S(2)}) %copy-start.2) | copy-done | bytes 4194328
  24.8 1.1 %shard_map.102 = f32[1,1024]{1,0:T(1,128)S(1)} custom-call(bf16[1024,2048]{1,0:T(8,128)(2,1)S(1)} %copy-done.2), custom_call_target="tpu_custom_call" | custom-call | flops 1 | bytes 1 | tf_op jit(solution)/shard_map/pallas_call | solution.py:112
  26.4 1.2 %convert_add_fusion = f32[2,256,128]{2,1,0:T(8,128)S(1)} fusion(bf16[2,256,128]{2,1,0:T(8,128)(2,1)} %collective-permute-done.6, bf16[2,256,128]{2,1,0:T(8,128)(2,1)} %collective-permute-done.5, bf16[2,256,128]{2,1,0:T(8,128)(2,1)} %collective-permute-done.4, bf16[2,256,128]{2,1,0:T(8,128)(2,1)S(1)} %collective-permute-done.3, ...), kind=kLoop, calls=%fused_computation.23 | loop fusion | flops 983040 | bytes 1310720 | tf_op jit(solution)/shard_map/add | solution.py:229
  27.6 3.4 %shard_map.104 = f32[1,1024]{1,0:T(1,128)S(1)} custom-call(bf16[1024,2048]{1,0:T(8,128)(2,1)} %collective-permute-done.7.x_ref), custom_call_target="tpu_custom_call" | custom-call | flops 1 | bytes 1 | tf_op jit(solution)/shard_map/pallas_call | solution.py:112
  31.1 2.7 %collective-permute-start.9 = (f32[256,128]{1,0:T(8,128)S(1)}, f32[256,128]{1,0:T(8,128)S(1)}, u32[]{:S(2)}, u32[]{:S(2)}) collective-permute-start(f32[256,128]{1,0:T(8,128)S(1)} %get-tuple-element.122), channel_id=1, source_target_pairs={{0,16},{2,18},{4,20},{6,22},{8,24},{10,26},{12,28},{14,30},{16,0},... | collective-permute-start | bytes 393224 | tf_op jit(solution)/shard_map/ppermute | solution.py:32
  33.8 3.6 %fusion.1 = f32[1024,128]{1,0:T(8,128)S(1)} fusion(bf16[1024,2048]{1,0:T(8,128)(2,1)} %collective-permute-done.7.x_ref, f32[2048]{0:T(1024)S(1)} %convert_element_type.77, f32[1024]{0:T(1024)S(1)} %add_rsqrt_fusion, bf16[4096,128]{1,0:T(8,128)(2,1)S(1)} %copy-done.1, s32[]{:T(128)S(6)} %select_n.7), kind=kOutput, calls=%fused_computation.5 | convolution fusion | flops 545259520 | bytes 5255172 | tf_op jit(solution)/shard_map/dot_general | solution.py:239
  37.4 1.4 %fusion.16.raw_ref = f32[1024,128]{1,0:T(8,128)S(1)} fusion(f32[1024,128]{1,0:T(8,128)S(1)} %fusion.1, bf16[1024,2048]{1,0:T(8,128)(2,1)S(1)} %copy-done.3, f32[2048]{0:T(1024)S(1)} %convert_element_type.74, f32[1024]{0:T(1024)S(1)} %add_rsqrt_fusion, bf16[4096,128]{1,0:T(8,128)(2,1)S(1)} %copy-done.1, s32[]{:T(128)S(6)} %select_n.6), kind=kOutput, calls=%fused_computation.20 | convolution fusion | flops 545390592 | bytes 5779460 | tf_op jit(solution)/shard_map/dot_general | solution.py:239
  40.9 2.5 %collective-permute-start.14 = (bf16[1,256,128]{2,1,0:T(8,128)(2,1)S(1)}, bf16[1,256,128]{2,1,0:T(8,128)(2,1)S(1)}, u32[]{:S(2)}, u32[]{:S(2)}) collective-permute-start(bf16[1,256,128]{2,1,0:T(8,128)(2,1)S(1)} %get-tuple-element.106.refs_0_), channel_id=1, source_target_pairs={{0,16},{2,18},{4,20},{6,22},{8,24},{10,26},{12,28},{14,30},{16,0},... | collective-permute-start | bytes 196616 | tf_op jit(solution)/shard_map/ppermute | solution.py:32
  43.4 1.1 %collective-permute-start.13 = (bf16[1,256,128]{2,1,0:T(8,128)(2,1)S(1)}, bf16[1,256,128]{2,1,0:T(8,128)(2,1)S(1)}, u32[]{:S(2)}, u32[]{:S(2)}) collective-permute-start(bf16[1,256,128]{2,1,0:T(8,128)(2,1)S(1)} %get-tuple-element.106.refs_0_), channel_id=1, source_target_pairs={{0,24},{2,26},{4,28},{6,30},{8,16},{10,18},{12,20},{14,22},{16,8},... | collective-permute-start | bytes 196616 | tf_op jit(solution)/shard_map/ppermute | solution.py:32
  45.9 3.8 %fusion.15.refs_1_ = bf16[2048,128]{1,0:T(8,128)(2,1)S(1)} fusion(bf16[1024,128]{1,0:T(8,128)(2,1)S(1)} %get-tuple-element.96, bf16[1024,2048]{1,0:T(8,128)(2,1)} %collective-permute-done.7.x_ref, f32[1024]{0:T(1024)S(1)} %add_rsqrt_fusion, f32[2048]{0:T(1024)S(1)} %convert_element_type.77), kind=kOutput, calls=%fused_computation.19 | convolution fusion | flops 545783808 | bytes 4993024 | tf_op jit(solution)/shard_map/dot_general | solution.py:252
  49.7 2.2 %collective-permute-start.10 = (bf16[1,256,128]{2,1,0:T(8,128)(2,1)S(1)}, bf16[1,256,128]{2,1,0:T(8,128)(2,1)S(1)}, u32[]{:S(2)}, u32[]{:S(2)}) collective-permute-start(bf16[1,256,128]{2,1,0:T(8,128)(2,1)S(1)} %get-tuple-element.106.refs_0_), channel_id=1, source_target_pairs={{0,2},{2,0},{4,6},{6,4},{8,10},{10,8},{12,14},{14,12},{16,18},{18,... | collective-permute-start | bytes 196616 | tf_op jit(solution)/shard_map/ppermute | solution.py:32
  51.9 1.8 %fusion.14.refs_0_ = bf16[2048,128]{1,0:T(8,128)(2,1)S(1)} fusion(bf16[1024,128]{1,0:T(8,128)(2,1)S(1)} %get-tuple-element.96, bf16[1024,2048]{1,0:T(8,128)(2,1)S(1)} %copy-done.3, f32[1024]{0:T(1024)S(1)} %add_rsqrt_fusion, f32[2048]{0:T(1024)S(1)} %convert_element_type.74), kind=kOutput, calls=%fused_computation.18 | convolution fusion | flops 545783808 | bytes 4993024 | tf_op jit(solution)/shard_map/dot_general | solution.py:252
  54.2 2.0 %collective-permute-start.18 = (bf16[3,256,128]{2,1,0:T(8,128)(2,1)S(1)}, bf16[3,256,128]{2,1,0:T(8,128)(2,1)S(1)}, u32[]{:S(2)}, u32[]{:S(2)}) collective-permute-start(bf16[3,256,128]{2,1,0:T(8,128)(2,1)S(1)} %constant_dynamic-update-slice_fusion.refs_4_), channel_id=1, source_target_pairs={{0,6},{2,4},{4,2},{6,0},{8,14},{10,12},{12,10},{14,8},{16,22},{18,... | collective-permute-start | bytes 589832 | tf_op jit(solution)/shard_map/ppermute | solution.py:32
  56.2 1.9 %collective-permute-start.17 = (bf16[3,256,128]{2,1,0:T(8,128)(2,1)S(1)}, bf16[3,256,128]{2,1,0:T(8,128)(2,1)S(1)}, u32[]{:S(2)}, u32[]{:S(2)}) collective-permute-start(bf16[3,256,128]{2,1,0:T(8,128)(2,1)S(1)} %constant_dynamic-update-slice_fusion.refs_4_), channel_id=1, source_target_pairs={{0,4},{2,6},{4,0},{6,2},{8,12},{10,14},{12,8},{14,10},{16,20},{18,... | collective-permute-start | bytes 589832 | tf_op jit(solution)/shard_map/ppermute | solution.py:32
  58.1 1.0 %shard_map.106 = bf16[4096,128]{1,0:T(8,128)(2,1)} custom-call(bf16[2048,128]{1,0:T(8,128)(2,1)S(1)} %fusion.14.refs_0_, bf16[2048,128]{1,0:T(8,128)(2,1)S(1)} %fusion.15.refs_1_), custom_call_target="tpu_custom_call" | custom-call | flops 1 | bytes 1 | tf_op jit(solution)/shard_map/pallas_call | solution.py:155
  61.8 2.0 %collective-permute-done.17.refs_1_ = bf16[3,256,128]{2,1,0:T(8,128)(2,1)S(1)} collective-permute-done((bf16[3,256,128]{2,1,0:T(8,128)(2,1)S(1)}, bf16[3,256,128]{2,1,0:T(8,128)(2,1)S(1)}, u32[]{:S(2)}, u32[]{:S(2)}) %collective-permute-start.17) | collective-permute-done | bytes 196640 | tf_op jit(solution)/shard_map/ppermute | solution.py:32
  (51 shorter events, 9.7 us)
Async XLA Ops:
  0.6 25.8 %collective-permute-start.7 = (bf16[1024,2048]{1,0:T(8,128)(2,1)}, bf16[1024,2048]{1,0:T(8,128)(2,1)}, u32[]{:S(2)}, u32[]{:S(2)}) collective-permute-start(bf16[1024,2048]{1,0:T(8,128)(2,1)} %x_ref), channel_id=1, source_target_pairs={{0,1},{1,0},{2,3},{3,2},{4,5},{5,4},{6,7},{7,6},{8,9},{9,8},{10,11... | collective-permute-start | bytes 12582920 | tf_op jit(solution)/shard_map/ppermute | solution.py:32
  2.4 23.6 %copy-start.4 = (bf16[1024,128]{1,0:T(8,128)(2,1)S(1)}, bf16[1024,128]{1,0:T(8,128)(2,1)}, u32[]{:S(2)}) copy-start(bf16[1024,128]{1,0:T(8,128)(2,1)} %grad_ref) | copy-start | bytes 786436
  2.4 10.3 %collective-permute-start = (bf16[2,256,128]{2,1,0:T(8,128)(2,1)S(1)}, bf16[2,256,128]{2,1,0:T(8,128)(2,1)S(1)}, u32[]{:S(2)}, u32[]{:S(2)}) collective-permute-start(bf16[2,256,128]{2,1,0:T(8,128)(2,1)S(1)} %get-tuple-element.71), channel_id=1, source_target_pairs={{0,14},{2,12},{4,10},{6,8},{8,6},{10,4},{12,2},{14,0},{16,30},{18,... | collective-permute-start | bytes 393224 | tf_op jit(solution)/shard_map/ppermute | solution.py:32
  7.0 11.1 %collective-permute-start.1 = (bf16[2,256,128]{2,1,0:T(8,128)(2,1)S(1)}, bf16[2,256,128]{2,1,0:T(8,128)(2,1)S(1)}, u32[]{:S(2)}, u32[]{:S(2)}) collective-permute-start(bf16[2,256,128]{2,1,0:T(8,128)(2,1)S(1)} %get-tuple-element.72), channel_id=1, source_target_pairs={{0,6},{2,4},{4,2},{6,0},{8,14},{10,12},{12,10},{14,8},{16,22},{18,... | collective-permute-start | bytes 393224 | tf_op jit(solution)/shard_map/ppermute | solution.py:32
  7.5 13.5 %collective-permute-start.2 = (bf16[2,256,128]{2,1,0:T(8,128)(2,1)S(1)}, bf16[2,256,128]{2,1,0:T(8,128)(2,1)S(1)}, u32[]{:S(2)}, u32[]{:S(2)}) collective-permute-start(bf16[2,256,128]{2,1,0:T(8,128)(2,1)S(1)} %get-tuple-element.73), channel_id=1, source_target_pairs={{0,10},{2,8},{4,14},{6,12},{8,2},{10,0},{12,6},{14,4},{16,26},{18,... | collective-permute-start | bytes 393224 | tf_op jit(solution)/shard_map/ppermute | solution.py:32
  8.8 1.4 %collective-permute-start.8 = (bf16[2048]{0:T(1024)(128)(2,1)}, bf16[2048]{0:T(1024)(128)(2,1)S(1)}, u32[]{:S(2)}, u32[]{:S(2)}) collective-permute-start(bf16[2048]{0:T(1024)(128)(2,1)} %param.7), channel_id=1, source_target_pairs={{0,1},{1,0},{2,3},{3,2},{4,5},{5,4},{6,7},{7,6},{8,9},{9,8},{10,11... | collective-permute-start | bytes 12296 | tf_op jit(solution)/shard_map/ppermute | solution.py:32
  10.2 16.1 %collective-permute-start.3 = (bf16[2,256,128]{2,1,0:T(8,128)(2,1)S(1)}, bf16[2,256,128]{2,1,0:T(8,128)(2,1)S(1)}, u32[]{:S(2)}, u32[]{:S(2)}) collective-permute-start(bf16[2,256,128]{2,1,0:T(8,128)(2,1)S(1)} %get-tuple-element.74), channel_id=1, source_target_pairs={{0,12},{2,14},{4,8},{6,10},{8,4},{10,6},{12,0},{14,2},{16,28},{18,... | collective-permute-start | bytes 393224 | tf_op jit(solution)/shard_map/ppermute | solution.py:32
  12.8 13.6 %collective-permute-start.4 = (bf16[2,256,128]{2,1,0:T(8,128)(2,1)S(1)}, bf16[2,256,128]{2,1,0:T(8,128)(2,1)}, u32[]{:S(2)}, u32[]{:S(2)}) collective-permute-start(bf16[2,256,128]{2,1,0:T(8,128)(2,1)S(1)} %get-tuple-element.75), channel_id=1, source_target_pairs={{0,2},{2,0},{4,6},{6,4},{8,10},{10,8},{12,14},{14,12},{16,18},{18,... | collective-permute-start | bytes 393224 | tf_op jit(solution)/shard_map/ppermute | solution.py:32
  18.1 8.3 %collective-permute-start.5 = (bf16[2,256,128]{2,1,0:T(8,128)(2,1)S(1)}, bf16[2,256,128]{2,1,0:T(8,128)(2,1)}, u32[]{:S(2)}, u32[]{:S(2)}) collective-permute-start(bf16[2,256,128]{2,1,0:T(8,128)(2,1)S(1)} %get-tuple-element.76), channel_id=1, source_target_pairs={{0,4},{2,6},{4,0},{6,2},{8,12},{10,14},{12,8},{14,10},{16,20},{18,... | collective-permute-start | bytes 393224 | tf_op jit(solution)/shard_map/ppermute | solution.py:32
  21.0 5.4 %collective-permute-start.6 = (bf16[2,256,128]{2,1,0:T(8,128)(2,1)S(1)}, bf16[2,256,128]{2,1,0:T(8,128)(2,1)}, u32[]{:S(2)}, u32[]{:S(2)}) collective-permute-start(bf16[2,256,128]{2,1,0:T(8,128)(2,1)S(1)} %get-tuple-element.77), channel_id=1, source_target_pairs={{0,8},{2,10},{4,12},{6,14},{8,0},{10,2},{12,4},{14,6},{16,24},{18,... | collective-permute-start | bytes 393224 | tf_op jit(solution)/shard_map/ppermute | solution.py:32
  22.6 2.2 %copy-start.2 = (bf16[1024,2048]{1,0:T(8,128)(2,1)S(1)}, bf16[1024,2048]{1,0:T(8,128)(2,1)}, u32[]{:S(2)}) copy-start(bf16[1024,2048]{1,0:T(8,128)(2,1)} %x_ref) | copy-start | bytes 12582916
  25.9 5.1 %copy-start.7 = (bf16[2048]{0:T(1024)(128)(2,1)S(1)}, bf16[2048]{0:T(1024)(128)(2,1)}, u32[]{:S(2)}) copy-start(bf16[2048]{0:T(1024)(128)(2,1)} %param.7) | copy-start | bytes 12292
  25.9 7.8 %copy-start.1 = (bf16[4096,128]{1,0:T(8,128)(2,1)S(1)}, bf16[4096,128]{1,0:T(8,128)(2,1)}, u32[]{:S(2)}) copy-start(bf16[4096,128]{1,0:T(8,128)(2,1)} %w_ref.3) | copy-start | bytes 3145732
  31.1 8.3 %collective-permute-start.9 = (f32[256,128]{1,0:T(8,128)S(1)}, f32[256,128]{1,0:T(8,128)S(1)}, u32[]{:S(2)}, u32[]{:S(2)}) collective-permute-start(f32[256,128]{1,0:T(8,128)S(1)} %get-tuple-element.122), channel_id=1, source_target_pairs={{0,16},{2,18},{4,20},{6,22},{8,24},{10,26},{12,28},{14,30},{16,0},... | collective-permute-start | bytes 393224 | tf_op jit(solution)/shard_map/ppermute | solution.py:32
  33.8 3.7 %copy-start.3 = (bf16[1024,2048]{1,0:T(8,128)(2,1)S(1)}, bf16[1024,2048]{1,0:T(8,128)(2,1)}, u32[]{:S(2)}) copy-start(bf16[1024,2048]{1,0:T(8,128)(2,1)} %x_ref) | copy-start | bytes 12582916
  40.1 9.5 %collective-permute-start.15 = (bf16[1,256,128]{2,1,0:T(8,128)(2,1)S(1)}, bf16[1,256,128]{2,1,0:T(8,128)(2,1)S(1)}, u32[]{:S(2)}, u32[]{:S(2)}) collective-permute-start(bf16[1,256,128]{2,1,0:T(8,128)(2,1)S(1)} %get-tuple-element.106.refs_0_), channel_id=1, source_target_pairs={{0,8},{2,10},{4,12},{6,14},{8,0},{10,2},{12,4},{14,6},{16,24},{18,... | collective-permute-start | bytes 196616 | tf_op jit(solution)/shard_map/ppermute | solution.py:32
  40.9 12.9 %collective-permute-start.14 = (bf16[1,256,128]{2,1,0:T(8,128)(2,1)S(1)}, bf16[1,256,128]{2,1,0:T(8,128)(2,1)S(1)}, u32[]{:S(2)}, u32[]{:S(2)}) collective-permute-start(bf16[1,256,128]{2,1,0:T(8,128)(2,1)S(1)} %get-tuple-element.106.refs_0_), channel_id=1, source_target_pairs={{0,16},{2,18},{4,20},{6,22},{8,24},{10,26},{12,28},{14,30},{16,0},... | collective-permute-start | bytes 196616 | tf_op jit(solution)/shard_map/ppermute | solution.py:32
  43.4 10.3 %collective-permute-start.13 = (bf16[1,256,128]{2,1,0:T(8,128)(2,1)S(1)}, bf16[1,256,128]{2,1,0:T(8,128)(2,1)S(1)}, u32[]{:S(2)}, u32[]{:S(2)}) collective-permute-start(bf16[1,256,128]{2,1,0:T(8,128)(2,1)S(1)} %get-tuple-element.106.refs_0_), channel_id=1, source_target_pairs={{0,24},{2,26},{4,28},{6,30},{8,16},{10,18},{12,20},{14,22},{16,8},... | collective-permute-start | bytes 196616 | tf_op jit(solution)/shard_map/ppermute | solution.py:32
  44.5 9.2 %collective-permute-start.12 = (bf16[1,256,128]{2,1,0:T(8,128)(2,1)S(1)}, bf16[1,256,128]{2,1,0:T(8,128)(2,1)S(1)}, u32[]{:S(2)}, u32[]{:S(2)}) collective-permute-start(bf16[1,256,128]{2,1,0:T(8,128)(2,1)S(1)} %get-tuple-element.106.refs_0_), channel_id=1, source_target_pairs={{0,6},{2,4},{4,2},{6,0},{8,14},{10,12},{12,10},{14,8},{16,22},{18,... | collective-permute-start | bytes 196616 | tf_op jit(solution)/shard_map/ppermute | solution.py:32
  45.3 8.4 %collective-permute-start.11 = (bf16[1,256,128]{2,1,0:T(8,128)(2,1)S(1)}, bf16[1,256,128]{2,1,0:T(8,128)(2,1)S(1)}, u32[]{:S(2)}, u32[]{:S(2)}) collective-permute-start(bf16[1,256,128]{2,1,0:T(8,128)(2,1)S(1)} %get-tuple-element.106.refs_0_), channel_id=1, source_target_pairs={{0,4},{2,6},{4,0},{6,2},{8,12},{10,14},{12,8},{14,10},{16,20},{18,... | collective-permute-start | bytes 196616 | tf_op jit(solution)/shard_map/ppermute | solution.py:32
  49.7 4.5 %collective-permute-start.10 = (bf16[1,256,128]{2,1,0:T(8,128)(2,1)S(1)}, bf16[1,256,128]{2,1,0:T(8,128)(2,1)S(1)}, u32[]{:S(2)}, u32[]{:S(2)}) collective-permute-start(bf16[1,256,128]{2,1,0:T(8,128)(2,1)S(1)} %get-tuple-element.106.refs_0_), channel_id=1, source_target_pairs={{0,2},{2,0},{4,6},{6,4},{8,10},{10,8},{12,14},{14,12},{16,18},{18,... | collective-permute-start | bytes 196616 | tf_op jit(solution)/shard_map/ppermute | solution.py:32
  54.2 7.6 %collective-permute-start.18 = (bf16[3,256,128]{2,1,0:T(8,128)(2,1)S(1)}, bf16[3,256,128]{2,1,0:T(8,128)(2,1)S(1)}, u32[]{:S(2)}, u32[]{:S(2)}) collective-permute-start(bf16[3,256,128]{2,1,0:T(8,128)(2,1)S(1)} %constant_dynamic-update-slice_fusion.refs_4_), channel_id=1, source_target_pairs={{0,6},{2,4},{4,2},{6,0},{8,14},{10,12},{12,10},{14,8},{16,22},{18,... | collective-permute-start | bytes 589832 | tf_op jit(solution)/shard_map/ppermute | solution.py:32
  56.2 7.5 %collective-permute-start.17 = (bf16[3,256,128]{2,1,0:T(8,128)(2,1)S(1)}, bf16[3,256,128]{2,1,0:T(8,128)(2,1)S(1)}, u32[]{:S(2)}, u32[]{:S(2)}) collective-permute-start(bf16[3,256,128]{2,1,0:T(8,128)(2,1)S(1)} %constant_dynamic-update-slice_fusion.refs_4_), channel_id=1, source_target_pairs={{0,4},{2,6},{4,0},{6,2},{8,12},{10,14},{12,8},{14,10},{16,20},{18,... | collective-permute-start | bytes 589832 | tf_op jit(solution)/shard_map/ppermute | solution.py:32
  58.1 5.7 %collective-permute-start.16 = (bf16[3,256,128]{2,1,0:T(8,128)(2,1)S(1)}, bf16[3,256,128]{2,1,0:T(8,128)(2,1)S(1)}, u32[]{:S(2)}, u32[]{:S(2)}) collective-permute-start(bf16[3,256,128]{2,1,0:T(8,128)(2,1)S(1)} %constant_dynamic-update-slice_fusion.refs_4_), channel_id=1, source_target_pairs={{0,2},{2,0},{4,6},{6,4},{8,10},{10,8},{12,14},{14,12},{16,18},{18,... | collective-permute-start | bytes 589832 | tf_op jit(solution)/shard_map/ppermute | solution.py:32
  (3 other events, 5.1 us)

commit v6 on v5

--- a/solution.py
+++ b/solution.py
@@ -40,25 +40,31 @@
     return pl.ds(pl.multiple_of(index * rows, rows), rows)
 
 
-def pick_kernel(w_ref, *out_refs):
-    me = lax.axis_index("rep")
+def pick_kernel(cores, w_ref, *out_refs):
+    me, core = lax.axis_index("rep"), lax.axis_index("tp")
     far, rows, _ = out_refs[0].shape
-    for c, out in enumerate(out_refs):
+    for c in range(CUBE):
         for h in range(far):
-            out[h] = w_ref[rows_at(me ^ (h * CUBE + c), rows), :]
+            out_refs[c][h] = w_ref[rows_at(me ^ (h * CUBE + c), rows), :]
+    for k, out in enumerate(out_refs[CUBE:]):
+        out[...] = w_ref[rows_at(core ^ k, out.shape[0]), :]
 
 
 def pick(local_weights, rows):
-    far = local_weights.shape[0] // (CUBE * rows)
-    shape = jax.ShapeDtypeStruct((far, rows, HD), local_weights.dtype)
-    return pl.pallas_call(
-        pick_kernel,
-        out_shape=[shape] * CUBE,
+    cores = lax.axis_size("tp")
+    features = local_weights.shape[0]
+    kind = local_weights.dtype
+    shapes = [jax.ShapeDtypeStruct((features // (CUBE * rows), rows, HD), kind)] * CUBE
+    shapes += [jax.ShapeDtypeStruct((features // cores, HD), kind)] * cores
+    out = pl.pallas_call(
+        functools.partial(pick_kernel, cores),
+        out_shape=shapes,
         in_specs=[VMEM],
-        out_specs=[VMEM] * CUBE,
+        out_specs=[VMEM] * len(shapes),
         compiler_params=PARAMS,
         cost_estimate=LIGHT,
     )(local_weights)
+    return out[:CUBE], out[CUBE:]
 
 
 def prepare_kernel(grad_ref, cos_ref, sin_ref, out_ref):
@@ -216,29 +222,34 @@
 
     x = [swap(tokens, "tp", k) for k in range(cores)]
     gain = [swap(norm_gain, "tp", k) for k in range(cores)]
-    picked = pick(local_weights, anchor.shape[0])
-    picked, w, own, key_grad = after(picked, local_weights, tokens, key_grad)
+    picked, halves = pick(local_weights, anchor.shape[0])
+    picked, halves, w, own, key_grad = after(picked, halves, local_weights, tokens, key_grad)
     x[0] = own
-    cube = [swap(picked[c], "rep", c) for c in (7, 3, 5, 6, 1, 2, 4)]
-    squares = squares_of(own)
+    cube = [swap(picked[c], "rep", c) for c in (1, 2, 4, 7, 3, 5, 6)]
     cosine, signed, raw_grad = prepare(key_grad)
+    squares = sum(squares_of(block) for block in x)
 
     cube, squares, raw_grad, x, gain = after(cube, squares, raw_grad, x, gain)
     total = picked[0].astype(jnp.float32)
     for block in cube:
         total = total + block.astype(jnp.float32)
     sums = [swap(total[h], "rep", h * CUBE) if h else total[h] for h in range(replicas // CUBE)]
-    for k in range(1, cores):
-        squares = squares + squares_of(x[k])
     scale = lax.rsqrt(squares / (part * cores) + norm_eps)[:, None]
-    me = lax.axis_index("tp")
     raw_keys = 0.0
     for k in range(cores):
-        block = lax.dynamic_slice_in_dim(w, (me ^ k) * part, part, 0)
         norm = normalize(x[k], scale, gain[k])
-        raw_keys = raw_keys + jnp.dot(norm, block, preferred_element_type=jnp.float32)
-
-    sums, raw_keys, x, scale = after(sums, raw_keys, x, scale)
+        raw_keys = raw_keys + jnp.dot(norm, halves[k], preferred_element_type=jnp.float32)
+
+    def weight_rows(k):
+        norm = normalize(x[k], scale, gain[k])
+        contracted = lax.dot_general(
+            norm, raw_grad, (((0,), (0,)), ((), ())), preferred_element_type=jnp.float32
+        )
+        return (contracted * inv_width).astype(jnp.bfloat16)
+
+    blocks = [weight_rows(0)]
+
+    sums, raw_keys, blocks, x, scale = after(sums, raw_keys, blocks, x, scale)
     mean_weights = sum(sums) / replicas
     change = anchor - mean_weights
     new_momentum = momentum_rate * momentum + change
@@ -246,15 +257,9 @@
     outgoing = new_anchor.astype(jnp.bfloat16)[None]
 
     columns = [swap(outgoing, "rep", z * PLANE) for z in range(far - 1, 0, -1)]
-    blocks = []
-    for k in range(cores):
-        norm = normalize(x[k], scale, gain[k])
-        contracted = lax.dot_general(
-            norm, raw_grad, (((0,), (0,)), ((), ())), preferred_element_type=jnp.float32
-        )
-        blocks.append((contracted * inv_width).astype(jnp.bfloat16))
     near = [outgoing] + [swap(outgoing, "rep", p) for p in range(1, PLANE)]
-    blocks, near, raw_keys, columns = after(blocks, near, raw_keys, columns)
+    near, raw_keys, x, columns = after(near, raw_keys, x, columns)
+    blocks += [weight_rows(k) for k in range(1, cores)]
     block = jnp.concatenate(columns)
     rest = [block] + [swap(block, "rep", p) for p in range(1, PLANE)]
     key_rows = turn(inv_width, raw_keys, cosine, signed)

time: 65.1 us -> 55.9 us (0.86)
  matrix products: 10.6 us -> 6.29 us
  Pallas kernels: 8.8 us -> 6.6 us
  waiting for transfers between devices: 9.73 us -> 8.02 us
  other arithmetic: 1.93 us -> 0.91 us
    dot_general x4, matrix products: 10.6 us -> 6.29 us  [the longest x2 3.58 us: weight_rows(): lax.dot_general(norm, raw_grad, (((0,), (0,)), ((), ())), preferred_eleme...]
    pallas_call x2, Pallas kernels: 4.58 us -> 2.31 us  [squares_of(): pl.pallas_call(squares_kernel, out_shape=jax.ShapeDtypeStruct((1, rows),...]
    ppermute x19, waiting for transfers between devices: 9.73 us -> 8.02 us  [swap(): return lax.ppermute(value, axis, [(i, i ^ offset) for i in range(size)])]
    add x1, other arithmetic: 1.17 us -> 0.14 us  [body(): total = total + block.astype(jnp.float32)]
  transfers between devices with their start and end apart: 19 -> 19, of which waited for: 7 -> 9; matrix products, arithmetic and copies ran while one was open for 16% -> 11% of each run, Pallas kernels for 7% -> 10%
where the time goes in v6:
time: 55.9 us; the launch traced here: 55.7 us
  starting transfers between devices  29.5 us (53%)
  waiting for transfers between devices  8.02 us (14%)
  Pallas kernels  6.6 us (12%)
  matrix products  6.29 us (11%)
  local copies, waits for them, and re-layouts  3.5 us (6%)
  other arithmetic  0.91 us (2%)
  between operations  0.84 us (2%)
    ppermute x19, starting transfers between devices, swap(): return lax.ppermute(value, axis, [(i, i ^ offset) for i in range(size)])  29.5 us
    ppermute x19, waiting for transfers between devices, swap(): return lax.ppermute(value, axis, [(i, i ^ offset) for i in range(size)])  8.02 us
    dot_general x2, matrix products, weight_rows(): lax.dot_general(norm, raw_grad, (((0,), (0,)), ((), ())), preferred_eleme...  3.58 us
    unnamed x18, local copies, waits for them, and re-layouts  3.46 us
    dot_general x2, matrix products, body(): jnp.dot(norm, halves[k], preferred_element_type=jnp.float32)  2.71 us
    pallas_call x2, Pallas kernels, squares_of(): pl.pallas_call(squares_kernel, out_shape=jax.ShapeDtypeStruct((1, rows),...  2.31 us
    pallas_call x2, Pallas kernels, merge(): pl.pallas_call(functools.partial(merge_kernel, offsets), out_shape=jax.Sh...  1.8 us
  transfers between devices with their start and end apart: 19, of which 9 were waited for; matrix products, arithmetic and copies ran while one was open for 11% of the time, Pallas kernels for 10%

profile of v6, /device:TPU:0, one launch (start us, length us, event | category | flops | bytes accessed | tf_op | source)
XLA Modules:
  0.0 55.7 jit_solution(11936350907199241054)
XLA Ops:
  1.2 1.2 %copy-done = bf16[4096,128]{1,0:T(8,128)(2,1)S(1)} copy-done((bf16[4096,128]{1,0:T(8,128)(2,1)S(1)}, bf16[4096,128]{1,0:T(8,128)(2,1)}, u32[]{:S(2)}) %copy-start) | copy-done | bytes 1048600
  2.5 2.6 %collective-permute-start = (bf16[2,256,128]{2,1,0:T(8,128)(2,1)S(1)}, bf16[2,256,128]{2,1,0:T(8,128)(2,1)S(1)}, u32[]{:S(2)}, u32[]{:S(2)}) collective-permute-start(bf16[2,256,128]{2,1,0:T(8,128)(2,1)S(1)} %get-tuple-element.76), channel_id=1, source_target_pairs={{0,2},{2,0},{4,6},{6,4},{8,10},{10,8},{12,14},{14,12},{16,18},{18,... | collective-permute-start | bytes 393224 | tf_op jit(solution)/shard_map/ppermute | solution.py:32
  5.1 1.5 %collective-permute-start.1 = (bf16[2,256,128]{2,1,0:T(8,128)(2,1)S(1)}, bf16[2,256,128]{2,1,0:T(8,128)(2,1)S(1)}, u32[]{:S(2)}, u32[]{:S(2)}) collective-permute-start(bf16[2,256,128]{2,1,0:T(8,128)(2,1)S(1)} %get-tuple-element.77), channel_id=1, source_target_pairs={{0,4},{2,6},{4,0},{6,2},{8,12},{10,14},{12,8},{14,10},{16,20},{18,... | collective-permute-start | bytes 393224 | tf_op jit(solution)/shard_map/ppermute | solution.py:32
  6.6 1.6 %collective-permute-start.2 = (bf16[2,256,128]{2,1,0:T(8,128)(2,1)S(1)}, bf16[2,256,128]{2,1,0:T(8,128)(2,1)S(1)}, u32[]{:S(2)}, u32[]{:S(2)}) collective-permute-start(bf16[2,256,128]{2,1,0:T(8,128)(2,1)S(1)} %get-tuple-element.78), channel_id=1, source_target_pairs={{0,8},{2,10},{4,12},{6,14},{8,0},{10,2},{12,4},{14,6},{16,24},{18,... | collective-permute-start | bytes 393224 | tf_op jit(solution)/shard_map/ppermute | solution.py:32
  8.2 4.8 %collective-permute-start.3 = (bf16[2,256,128]{2,1,0:T(8,128)(2,1)S(1)}, bf16[2,256,128]{2,1,0:T(8,128)(2,1)S(1)}, u32[]{:S(2)}, u32[]{:S(2)}) collective-permute-start(bf16[2,256,128]{2,1,0:T(8,128)(2,1)S(1)} %get-tuple-element.79), channel_id=1, source_target_pairs={{0,14},{2,12},{4,10},{6,8},{8,6},{10,4},{12,2},{14,0},{16,30},{18,... | collective-permute-start | bytes 393224 | tf_op jit(solution)/shard_map/ppermute | solution.py:32
  13.5 1.4 %collective-permute-start.5 = (bf16[2,256,128]{2,1,0:T(8,128)(2,1)S(1)}, bf16[2,256,128]{2,1,0:T(8,128)(2,1)S(1)}, u32[]{:S(2)}, u32[]{:S(2)}) collective-permute-start(bf16[2,256,128]{2,1,0:T(8,128)(2,1)S(1)} %get-tuple-element.81), channel_id=1, source_target_pairs={{0,10},{2,8},{4,14},{6,12},{8,2},{10,0},{12,6},{14,4},{16,26},{18,... | collective-permute-start | bytes 393224 | tf_op jit(solution)/shard_map/ppermute | solution.py:32
  14.8 2.5 %collective-permute-start.6 = (bf16[2,256,128]{2,1,0:T(8,128)(2,1)S(1)}, bf16[2,256,128]{2,1,0:T(8,128)(2,1)S(1)}, u32[]{:S(2)}, u32[]{:S(2)}) collective-permute-start(bf16[2,256,128]{2,1,0:T(8,128)(2,1)S(1)} %get-tuple-element.82), channel_id=1, source_target_pairs={{0,12},{2,14},{4,8},{6,10},{8,4},{10,6},{12,0},{14,2},{16,28},{18,... | collective-permute-start | bytes 393224 | tf_op jit(solution)/shard_map/ppermute | solution.py:32
  17.4 2.2 %copy-done.2 = bf16[1024,2048]{1,0:T(8,128)(2,1)S(1)} copy-done((bf16[1024,2048]{1,0:T(8,128)(2,1)S(1)}, bf16[1024,2048]{1,0:T(8,128)(2,1)}, u32[]{:S(2)}) %copy-start.2) | copy-done | bytes 4194328
  19.6 1.1 %shard_map.102 = f32[1,1024]{1,0:T(1,128)S(1)} custom-call(bf16[1024,2048]{1,0:T(8,128)(2,1)S(1)} %copy-done.2), custom_call_target="tpu_custom_call" | custom-call | flops 1 | bytes 1 | tf_op jit(solution)/shard_map/pallas_call | solution.py:118
  21.1 1.2 %shard_map.103 = f32[1,1024]{1,0:T(1,128)S(1)} custom-call(bf16[1024,2048]{1,0:T(8,128)(2,1)S(1)} %collective-permute-done.7.x_ref), custom_call_target="tpu_custom_call" | custom-call | flops 1 | bytes 1 | tf_op jit(solution)/shard_map/pallas_call | solution.py:118
  24.0 2.7 %collective-permute-start.9 = (f32[256,128]{1,0:T(8,128)S(1)}, f32[256,128]{1,0:T(8,128)S(1)}, u32[]{:S(2)}, u32[]{:S(2)}) collective-permute-start(f32[256,128]{1,0:T(8,128)S(1)} %get-tuple-element.128), channel_id=1, source_target_pairs={{0,16},{2,18},{4,20},{6,22},{8,24},{10,26},{12,28},{14,30},{16,0},... | collective-permute-start | bytes 393224 | tf_op jit(solution)/shard_map/ppermute | solution.py:32
  26.8 1.3 %fusion = f32[1024,128]{1,0:T(8,128)S(1)} fusion(bf16[2048,128]{1,0:T(8,128)(2,1)S(1)} %get-tuple-element.99, bf16[1024,2048]{1,0:T(8,128)(2,1)S(1)} %collective-permute-done.7.x_ref, f32[2048]{0:T(1024)S(1)} %convert_element_type.73, f32[1024]{0:T(1024)S(1)} %add_rsqrt_fusion), kind=kOutput, calls=%fused_computation.3 | convolution fusion | flops 545259520 | bytes 5255168 | tf_op jit(solution)/shard_map/dot_general | solution.py:241
  28.1 1.4 %convolution_add_fusion.raw_ref = f32[1024,128]{1,0:T(8,128)S(1)} fusion(f32[1024,128]{1,0:T(8,128)S(1)} %fusion, bf16[2048,128]{1,0:T(8,128)(2,1)S(1)} %get-tuple-element.96, bf16[1024,2048]{1,0:T(8,128)(2,1)S(1)} %copy-done.3, f32[2048]{0:T(1024)S(1)} %convert_element_type.70, f32[1024]{0:T(1024)S(1)} %add_rsqrt_fusion), kind=kOutput, calls=%fused_computation.13 | convolution fusion | flops 545390592 | bytes 5779456 | tf_op jit(solution)/shard_map/dot_general | solution.py:241
  29.5 1.8 %fusion.8.refs_0_ = bf16[2048,128]{1,0:T(8,128)(2,1)S(1)} fusion(bf16[1024,128]{1,0:T(8,128)(2,1)S(1)} %get-tuple-element.100, bf16[1024,2048]{1,0:T(8,128)(2,1)S(1)} %copy-done.3, f32[2048]{0:T(1024)S(1)} %convert_element_type.70, f32[1024]{0:T(1024)S(1)} %add_rsqrt_fusion), kind=kOutput, calls=%fused_computation.12 | convolution fusion | flops 545783808 | bytes 4993024 | tf_op jit(solution)/shard_map/dot_general | solution.py:245
  31.3 1.5 %collective-permute-done.9 = f32[256,128]{1,0:T(8,128)S(1)} collective-permute-done((f32[256,128]{1,0:T(8,128)S(1)}, f32[256,128]{1,0:T(8,128)S(1)}, u32[]{:S(2)}, u32[]{:S(2)}) %collective-permute-start.9) | collective-permute-done | bytes 131104 | tf_op jit(solution)/shard_map/ppermute | solution.py:32
  34.2 2.7 %collective-permute-start.14 = (bf16[1,256,128]{2,1,0:T(8,128)(2,1)S(1)}, bf16[1,256,128]{2,1,0:T(8,128)(2,1)S(1)}, u32[]{:S(2)}, u32[]{:S(2)}) collective-permute-start(bf16[1,256,128]{2,1,0:T(8,128)(2,1)S(1)} %get-tuple-element.112.refs_0_), channel_id=1, source_target_pairs={{0,16},{2,18},{4,20},{6,22},{8,24},{10,26},{12,28},{14,30},{16,0},... | collective-permute-start | bytes 196616 | tf_op jit(solution)/shard_map/ppermute | solution.py:32
  36.9 1.1 %collective-permute-start.13 = (bf16[1,256,128]{2,1,0:T(8,128)(2,1)S(1)}, bf16[1,256,128]{2,1,0:T(8,128)(2,1)S(1)}, u32[]{:S(2)}, u32[]{:S(2)}) collective-permute-start(bf16[1,256,128]{2,1,0:T(8,128)(2,1)S(1)} %get-tuple-element.112.refs_0_), channel_id=1, source_target_pairs={{0,24},{2,26},{4,28},{6,30},{8,16},{10,18},{12,20},{14,22},{16,8},... | collective-permute-start | bytes 196616 | tf_op jit(solution)/shard_map/ppermute | solution.py:32
  37.9 1.5 %collective-permute-start.12 = (bf16[1,256,128]{2,1,0:T(8,128)(2,1)S(1)}, bf16[1,256,128]{2,1,0:T(8,128)(2,1)S(1)}, u32[]{:S(2)}, u32[]{:S(2)}) collective-permute-start(bf16[1,256,128]{2,1,0:T(8,128)(2,1)S(1)} %get-tuple-element.112.refs_0_), channel_id=1, source_target_pairs={{0,6},{2,4},{4,2},{6,0},{8,14},{10,12},{12,10},{14,8},{16,22},{18,... | collective-permute-start | bytes 196616 | tf_op jit(solution)/shard_map/ppermute | solution.py:32
  39.4 1.2 %collective-permute-start.11 = (bf16[1,256,128]{2,1,0:T(8,128)(2,1)S(1)}, bf16[1,256,128]{2,1,0:T(8,128)(2,1)S(1)}, u32[]{:S(2)}, u32[]{:S(2)}) collective-permute-start(bf16[1,256,128]{2,1,0:T(8,128)(2,1)S(1)} %get-tuple-element.112.refs_0_), channel_id=1, source_target_pairs={{0,4},{2,6},{4,0},{6,2},{8,12},{10,14},{12,8},{14,10},{16,20},{18,... | collective-permute-start | bytes 196616 | tf_op jit(solution)/shard_map/ppermute | solution.py:32
  41.4 1.5 %collective-permute-done.13 = bf16[1,256,128]{2,1,0:T(8,128)(2,1)S(1)} collective-permute-done((bf16[1,256,128]{2,1,0:T(8,128)(2,1)S(1)}, bf16[1,256,128]{2,1,0:T(8,128)(2,1)S(1)}, u32[]{:S(2)}, u32[]{:S(2)}) %collective-permute-start.13) | collective-permute-done | bytes 65568 | tf_op jit(solution)/shard_map/ppermute | solution.py:32
  44.9 2.2 %collective-permute-start.18 = (bf16[3,256,128]{2,1,0:T(8,128)(2,1)S(1)}, bf16[3,256,128]{2,1,0:T(8,128)(2,1)S(1)}, u32[]{:S(2)}, u32[]{:S(2)}) collective-permute-start(bf16[3,256,128]{2,1,0:T(8,128)(2,1)S(1)} %constant_dynamic-update-slice_fusion.refs_4_), channel_id=1, source_target_pairs={{0,6},{2,4},{4,2},{6,0},{8,14},{10,12},{12,10},{14,8},{16,22},{18,... | collective-permute-start | bytes 589832 | tf_op jit(solution)/shard_map/ppermute | solution.py:32
  47.2 1.2 %collective-permute-start.16 = (bf16[3,256,128]{2,1,0:T(8,128)(2,1)S(1)}, bf16[3,256,128]{2,1,0:T(8,128)(2,1)S(1)}, u32[]{:S(2)}, u32[]{:S(2)}) collective-permute-start(bf16[3,256,128]{2,1,0:T(8,128)(2,1)S(1)} %constant_dynamic-update-slice_fusion.refs_4_), channel_id=1, source_target_pairs={{0,2},{2,0},{4,6},{6,4},{8,10},{10,8},{12,14},{14,12},{16,18},{18,... | collective-permute-start | bytes 589832 | tf_op jit(solution)/shard_map/ppermute | solution.py:32
  48.5 1.8 %fusion.7.refs_1_ = bf16[2048,128]{1,0:T(8,128)(2,1)S(1)} fusion(bf16[1024,128]{1,0:T(8,128)(2,1)S(1)} %get-tuple-element.100, bf16[1024,2048]{1,0:T(8,128)(2,1)S(1)} %collective-permute-done.7.x_ref, f32[1024]{0:T(1024)S(1)} %add_rsqrt_fusion, f32[2048]{0:T(1024)S(1)} %convert_element_type.73), kind=kOutput, calls=%fused_computation.11 | convolution fusion | flops 545783808 | bytes 4993024 | tf_op jit(solution)/shard_map/dot_general | solution.py:245
  53.2 1.5 %collective-permute-done.17.refs_1_ = bf16[3,256,128]{2,1,0:T(8,128)(2,1)S(1)} collective-permute-done((bf16[3,256,128]{2,1,0:T(8,128)(2,1)S(1)}, bf16[3,256,128]{2,1,0:T(8,128)(2,1)S(1)}, u32[]{:S(2)}, u32[]{:S(2)}) %collective-permute-start.17) | collective-permute-done | bytes 196640 | tf_op jit(solution)/shard_map/ppermute | solution.py:32
  (52 shorter events, 11.4 us)
Async XLA Ops:
  0.6 14.2 %collective-permute-start.7 = (bf16[1024,2048]{1,0:T(8,128)(2,1)}, bf16[1024,2048]{1,0:T(8,128)(2,1)S(1)}, u32[]{:S(2)}, u32[]{:S(2)}) collective-permute-start(bf16[1024,2048]{1,0:T(8,128)(2,1)} %x_ref), channel_id=1, source_target_pairs={{0,1},{1,0},{2,3},{3,2},{4,5},{5,4},{6,7},{7,6},{8,9},{9,8},{10,11... | collective-permute-start | bytes 12582920 | tf_op jit(solution)/shard_map/ppermute | solution.py:32
  2.4 18.4 %copy-start.4 = (bf16[1024,128]{1,0:T(8,128)(2,1)S(1)}, bf16[1024,128]{1,0:T(8,128)(2,1)}, u32[]{:S(2)}) copy-start(bf16[1024,128]{1,0:T(8,128)(2,1)} %grad_ref) | copy-start | bytes 786436
  2.5 10.5 %collective-permute-start = (bf16[2,256,128]{2,1,0:T(8,128)(2,1)S(1)}, bf16[2,256,128]{2,1,0:T(8,128)(2,1)S(1)}, u32[]{:S(2)}, u32[]{:S(2)}) collective-permute-start(bf16[2,256,128]{2,1,0:T(8,128)(2,1)S(1)} %get-tuple-element.76), channel_id=1, source_target_pairs={{0,2},{2,0},{4,6},{6,4},{8,10},{10,8},{12,14},{14,12},{16,18},{18,... | collective-permute-start | bytes 393224 | tf_op jit(solution)/shard_map/ppermute | solution.py:32
  5.1 8.4 %collective-permute-start.1 = (bf16[2,256,128]{2,1,0:T(8,128)(2,1)S(1)}, bf16[2,256,128]{2,1,0:T(8,128)(2,1)S(1)}, u32[]{:S(2)}, u32[]{:S(2)}) collective-permute-start(bf16[2,256,128]{2,1,0:T(8,128)(2,1)S(1)} %get-tuple-element.77), channel_id=1, source_target_pairs={{0,4},{2,6},{4,0},{6,2},{8,12},{10,14},{12,8},{14,10},{16,20},{18,... | collective-permute-start | bytes 393224 | tf_op jit(solution)/shard_map/ppermute | solution.py:32
  6.6 1.6 %collective-permute-start.8 = (bf16[2048]{0:T(1024)(128)(2,1)}, bf16[2048]{0:T(1024)(128)(2,1)S(1)}, u32[]{:S(2)}, u32[]{:S(2)}) collective-permute-start(bf16[2048]{0:T(1024)(128)(2,1)} %param.7), channel_id=1, source_target_pairs={{0,1},{1,0},{2,3},{3,2},{4,5},{5,4},{6,7},{7,6},{8,9},{9,8},{10,11... | collective-permute-start | bytes 12296 | tf_op jit(solution)/shard_map/ppermute | solution.py:32
  6.6 15.7 %collective-permute-start.2 = (bf16[2,256,128]{2,1,0:T(8,128)(2,1)S(1)}, bf16[2,256,128]{2,1,0:T(8,128)(2,1)S(1)}, u32[]{:S(2)}, u32[]{:S(2)}) collective-permute-start(bf16[2,256,128]{2,1,0:T(8,128)(2,1)S(1)} %get-tuple-element.78), channel_id=1, source_target_pairs={{0,8},{2,10},{4,12},{6,14},{8,0},{10,2},{12,4},{14,6},{16,24},{18,... | collective-permute-start | bytes 393224 | tf_op jit(solution)/shard_map/ppermute | solution.py:32
  8.2 14.2 %collective-permute-start.3 = (bf16[2,256,128]{2,1,0:T(8,128)(2,1)S(1)}, bf16[2,256,128]{2,1,0:T(8,128)(2,1)S(1)}, u32[]{:S(2)}, u32[]{:S(2)}) collective-permute-start(bf16[2,256,128]{2,1,0:T(8,128)(2,1)S(1)} %get-tuple-element.79), channel_id=1, source_target_pairs={{0,14},{2,12},{4,10},{6,8},{8,6},{10,4},{12,2},{14,0},{16,30},{18,... | collective-permute-start | bytes 393224 | tf_op jit(solution)/shard_map/ppermute | solution.py:32
  13.0 10.0 %collective-permute-start.4 = (bf16[2,256,128]{2,1,0:T(8,128)(2,1)S(1)}, bf16[2,256,128]{2,1,0:T(8,128)(2,1)S(1)}, u32[]{:S(2)}, u32[]{:S(2)}) collective-permute-start(bf16[2,256,128]{2,1,0:T(8,128)(2,1)S(1)} %get-tuple-element.80), channel_id=1, source_target_pairs={{0,6},{2,4},{4,2},{6,0},{8,14},{10,12},{12,10},{14,8},{16,22},{18,... | collective-permute-start | bytes 393224 | tf_op jit(solution)/shard_map/ppermute | solution.py:32
  13.5 9.6 %collective-permute-start.5 = (bf16[2,256,128]{2,1,0:T(8,128)(2,1)S(1)}, bf16[2,256,128]{2,1,0:T(8,128)(2,1)S(1)}, u32[]{:S(2)}, u32[]{:S(2)}) collective-permute-start(bf16[2,256,128]{2,1,0:T(8,128)(2,1)S(1)} %get-tuple-element.81), channel_id=1, source_target_pairs={{0,10},{2,8},{4,14},{6,12},{8,2},{10,0},{12,6},{14,4},{16,26},{18,... | collective-permute-start | bytes 393224 | tf_op jit(solution)/shard_map/ppermute | solution.py:32
  14.8 9.0 %collective-permute-start.6 = (bf16[2,256,128]{2,1,0:T(8,128)(2,1)S(1)}, bf16[2,256,128]{2,1,0:T(8,128)(2,1)S(1)}, u32[]{:S(2)}, u32[]{:S(2)}) collective-permute-start(bf16[2,256,128]{2,1,0:T(8,128)(2,1)S(1)} %get-tuple-element.82), channel_id=1, source_target_pairs={{0,12},{2,14},{4,8},{6,10},{8,4},{10,6},{12,0},{14,2},{16,28},{18,... | collective-permute-start | bytes 393224 | tf_op jit(solution)/shard_map/ppermute | solution.py:32
  20.7 3.3 %copy-start.7 = (bf16[2048]{0:T(1024)(128)(2,1)S(1)}, bf16[2048]{0:T(1024)(128)(2,1)}, u32[]{:S(2)}) copy-start(bf16[2048]{0:T(1024)(128)(2,1)} %param.7) | copy-start | bytes 12292
  24.0 4.1 %copy-start.3 = (bf16[1024,2048]{1,0:T(8,128)(2,1)S(1)}, bf16[1024,2048]{1,0:T(8,128)(2,1)}, u32[]{:S(2)}) copy-start(bf16[1024,2048]{1,0:T(8,128)(2,1)} %x_ref) | copy-start | bytes 12582916
  24.0 8.7 %collective-permute-start.9 = (f32[256,128]{1,0:T(8,128)S(1)}, f32[256,128]{1,0:T(8,128)S(1)}, u32[]{:S(2)}, u32[]{:S(2)}) collective-permute-start(f32[256,128]{1,0:T(8,128)S(1)} %get-tuple-element.128), channel_id=1, source_target_pairs={{0,16},{2,18},{4,20},{6,22},{8,24},{10,26},{12,28},{14,30},{16,0},... | collective-permute-start | bytes 393224 | tf_op jit(solution)/shard_map/ppermute | solution.py:32
  29.5 3.3 %copy-start.5 = (f32[256,128]{1,0:T(8,128)S(1)}, f32[256,128]{1,0:T(8,128)}, u32[]{:S(2)}) copy-start(f32[256,128]{1,0:T(8,128)} %param.9) | copy-start | bytes 393220
  29.5 3.3 %copy-start.6 = (f32[256,128]{1,0:T(8,128)S(1)}, f32[256,128]{1,0:T(8,128)}, u32[]{:S(2)}) copy-start(f32[256,128]{1,0:T(8,128)} %param.10) | copy-start | bytes 393220
  33.5 7.1 %collective-permute-start.15 = (bf16[1,256,128]{2,1,0:T(8,128)(2,1)S(1)}, bf16[1,256,128]{2,1,0:T(8,128)(2,1)S(1)}, u32[]{:S(2)}, u32[]{:S(2)}) collective-permute-start(bf16[1,256,128]{2,1,0:T(8,128)(2,1)S(1)} %get-tuple-element.112.refs_0_), channel_id=1, source_target_pairs={{0,8},{2,10},{4,12},{6,14},{8,0},{10,2},{12,4},{14,6},{16,24},{18,... | collective-permute-start | bytes 196616 | tf_op jit(solution)/shard_map/ppermute | solution.py:32
  34.2 7.2 %collective-permute-start.14 = (bf16[1,256,128]{2,1,0:T(8,128)(2,1)S(1)}, bf16[1,256,128]{2,1,0:T(8,128)(2,1)S(1)}, u32[]{:S(2)}, u32[]{:S(2)}) collective-permute-start(bf16[1,256,128]{2,1,0:T(8,128)(2,1)S(1)} %get-tuple-element.112.refs_0_), channel_id=1, source_target_pairs={{0,16},{2,18},{4,20},{6,22},{8,24},{10,26},{12,28},{14,30},{16,0},... | collective-permute-start | bytes 196616 | tf_op jit(solution)/shard_map/ppermute | solution.py:32
  36.9 6.1 %collective-permute-start.13 = (bf16[1,256,128]{2,1,0:T(8,128)(2,1)S(1)}, bf16[1,256,128]{2,1,0:T(8,128)(2,1)S(1)}, u32[]{:S(2)}, u32[]{:S(2)}) collective-permute-start(bf16[1,256,128]{2,1,0:T(8,128)(2,1)S(1)} %get-tuple-element.112.refs_0_), channel_id=1, source_target_pairs={{0,24},{2,26},{4,28},{6,30},{8,16},{10,18},{12,20},{14,22},{16,8},... | collective-permute-start | bytes 196616 | tf_op jit(solution)/shard_map/ppermute | solution.py:32
  37.9 5.8 %collective-permute-start.12 = (bf16[1,256,128]{2,1,0:T(8,128)(2,1)S(1)}, bf16[1,256,128]{2,1,0:T(8,128)(2,1)S(1)}, u32[]{:S(2)}, u32[]{:S(2)}) collective-permute-start(bf16[1,256,128]{2,1,0:T(8,128)(2,1)S(1)} %get-tuple-element.112.refs_0_), channel_id=1, source_target_pairs={{0,6},{2,4},{4,2},{6,0},{8,14},{10,12},{12,10},{14,8},{16,22},{18,... | collective-permute-start | bytes 196616 | tf_op jit(solution)/shard_map/ppermute | solution.py:32
  39.4 4.7 %collective-permute-start.11 = (bf16[1,256,128]{2,1,0:T(8,128)(2,1)S(1)}, bf16[1,256,128]{2,1,0:T(8,128)(2,1)S(1)}, u32[]{:S(2)}, u32[]{:S(2)}) collective-permute-start(bf16[1,256,128]{2,1,0:T(8,128)(2,1)S(1)} %get-tuple-element.112.refs_0_), channel_id=1, source_target_pairs={{0,4},{2,6},{4,0},{6,2},{8,12},{10,14},{12,8},{14,10},{16,20},{18,... | collective-permute-start | bytes 196616 | tf_op jit(solution)/shard_map/ppermute | solution.py:32
  40.6 4.3 %collective-permute-start.10 = (bf16[1,256,128]{2,1,0:T(8,128)(2,1)S(1)}, bf16[1,256,128]{2,1,0:T(8,128)(2,1)S(1)}, u32[]{:S(2)}, u32[]{:S(2)}) collective-permute-start(bf16[1,256,128]{2,1,0:T(8,128)(2,1)S(1)} %get-tuple-element.112.refs_0_), channel_id=1, source_target_pairs={{0,2},{2,0},{4,6},{6,4},{8,10},{10,8},{12,14},{14,12},{16,18},{18,... | collective-permute-start | bytes 196616 | tf_op jit(solution)/shard_map/ppermute | solution.py:32
  44.9 8.2 %collective-permute-start.18 = (bf16[3,256,128]{2,1,0:T(8,128)(2,1)S(1)}, bf16[3,256,128]{2,1,0:T(8,128)(2,1)S(1)}, u32[]{:S(2)}, u32[]{:S(2)}) collective-permute-start(bf16[3,256,128]{2,1,0:T(8,128)(2,1)S(1)} %constant_dynamic-update-slice_fusion.refs_4_), channel_id=1, source_target_pairs={{0,6},{2,4},{4,2},{6,0},{8,14},{10,12},{12,10},{14,8},{16,22},{18,... | collective-permute-start | bytes 589832 | tf_op jit(solution)/shard_map/ppermute | solution.py:32
  47.2 7.4 %collective-permute-start.17 = (bf16[3,256,128]{2,1,0:T(8,128)(2,1)S(1)}, bf16[3,256,128]{2,1,0:T(8,128)(2,1)S(1)}, u32[]{:S(2)}, u32[]{:S(2)}) collective-permute-start(bf16[3,256,128]{2,1,0:T(8,128)(2,1)S(1)} %constant_dynamic-update-slice_fusion.refs_4_), channel_id=1, source_target_pairs={{0,4},{2,6},{4,0},{6,2},{8,12},{10,14},{12,8},{14,10},{16,20},{18,... | collective-permute-start | bytes 589832 | tf_op jit(solution)/shard_map/ppermute | solution.py:32
  47.2 7.5 %collective-permute-start.16 = (bf16[3,256,128]{2,1,0:T(8,128)(2,1)S(1)}, bf16[3,256,128]{2,1,0:T(8,128)(2,1)S(1)}, u32[]{:S(2)}, u32[]{:S(2)}) collective-permute-start(bf16[3,256,128]{2,1,0:T(8,128)(2,1)S(1)} %constant_dynamic-update-slice_fusion.refs_4_), channel_id=1, source_target_pairs={{0,2},{2,0},{4,6},{6,4},{8,10},{10,8},{12,14},{14,12},{16,18},{18,... | collective-permute-start | bytes 589832 | tf_op jit(solution)/shard_map/ppermute | solution.py:32
  (3 other events, 5.4 us)

commit v7 on v6

--- a/solution.py
+++ b/solution.py
@@ -10,7 +10,7 @@
 
 HD = 128
 PLANE = 4
-CUBE = 8
+PAIR = 2 * PLANE
 SPAN = 32
 
 
@@ -40,31 +40,32 @@
     return pl.ds(pl.multiple_of(index * rows, rows), rows)
 
 
-def pick_kernel(cores, w_ref, *out_refs):
+def pick_kernel(groups, w_ref, *out_refs):
     me, core = lax.axis_index("rep"), lax.axis_index("tp")
-    far, rows, _ = out_refs[0].shape
-    for c in range(CUBE):
-        for h in range(far):
-            out_refs[c][h] = w_ref[rows_at(me ^ (h * CUBE + c), rows), :]
-    for k, out in enumerate(out_refs[CUBE:]):
+    rows = out_refs[0].shape[1]
+    count = len(groups) * PLANE
+    for out, (offsets, p) in zip(out_refs, [(g, p) for g in groups for p in range(PLANE)]):
+        for i, k in enumerate(offsets):
+            out[i] = w_ref[rows_at(me ^ (k + p), rows), :]
+    for k, out in enumerate(out_refs[count:]):
         out[...] = w_ref[rows_at(core ^ k, out.shape[0]), :]
 
 
-def pick(local_weights, rows):
+def pick(local_weights, rows, groups):
     cores = lax.axis_size("tp")
-    features = local_weights.shape[0]
     kind = local_weights.dtype
-    shapes = [jax.ShapeDtypeStruct((features // (CUBE * rows), rows, HD), kind)] * CUBE
-    shapes += [jax.ShapeDtypeStruct((features // cores, HD), kind)] * cores
+    shapes = [jax.ShapeDtypeStruct((len(g), rows, HD), kind) for g in groups for _ in range(PLANE)]
+    shapes += [jax.ShapeDtypeStruct((local_weights.shape[0] // cores, HD), kind)] * cores
     out = pl.pallas_call(
-        functools.partial(pick_kernel, cores),
+        functools.partial(pick_kernel, groups),
         out_shape=shapes,
         in_specs=[VMEM],
         out_specs=[VMEM] * len(shapes),
         compiler_params=PARAMS,
         cost_estimate=LIGHT,
     )(local_weights)
-    return out[:CUBE], out[CUBE:]
+    count = len(groups) * PLANE
+    return [out[i : i + PLANE] for i in range(0, count, PLANE)], out[count:]
 
 
 def prepare_kernel(grad_ref, cos_ref, sin_ref, out_ref):
@@ -216,29 +217,45 @@
 def body(tokens, norm_gain, local_weights, anchor, momentum, key_grad):
     cores = lax.axis_size("tp")
     replicas = lax.axis_size("rep")
-    far = replicas // PLANE
     rows, part = tokens.shape
     inv_width = 1.0 / math.sqrt(part * cores)
+    far = list(range(PAIR, replicas, PAIR))
+    far_side = far + [k + PLANE for k in far]
+    near_side = [0, PLANE]
+    mates = (1, 2, 3)
+
+    def sum_plane(own, parts):
+        total = own.astype(jnp.float32)
+        for block in parts:
+            total = total + block.astype(jnp.float32)
+        return total
 
     x = [swap(tokens, "tp", k) for k in range(cores)]
+    (first, second), halves = pick(local_weights, anchor.shape[0], [far_side, near_side])
+    first, second, halves, w, own, key_grad = after(
+        first, second, halves, local_weights, tokens, key_grad
+    )
+    x[0] = own
+    first_in = [swap(first[p], "rep", p) for p in mates]
+    second_in = [swap(second[p], "rep", p) for p in mates]
+    cosine, signed, raw_grad = prepare(key_grad)
+    squares = squares_of(own)
+
+    first_in, squares, raw_grad, x, norm_gain = after(first_in, squares, raw_grad, x, norm_gain)
+    total = sum_plane(first[0], first_in)
+    pair = swap(total[len(far) :], "rep", PLANE)
+    for k in range(1, cores):
+        squares = squares + squares_of(x[k])
+
+    pair, squares, x, norm_gain = after(pair, squares, x, norm_gain)
+    total = total[: len(far)] + pair
+    sums = [swap(total[i], "rep", k) for i, k in enumerate(far)]
     gain = [swap(norm_gain, "tp", k) for k in range(cores)]
-    picked, halves = pick(local_weights, anchor.shape[0])
-    picked, halves, w, own, key_grad = after(picked, halves, local_weights, tokens, key_grad)
-    x[0] = own
-    cube = [swap(picked[c], "rep", c) for c in (1, 2, 4, 7, 3, 5, 6)]
-    cosine, signed, raw_grad = prepare(key_grad)
-    squares = sum(squares_of(block) for block in x)
-
-    cube, squares, raw_grad, x, gain = after(cube, squares, raw_grad, x, gain)
-    total = picked[0].astype(jnp.float32)
-    for block in cube:
-        total = total + block.astype(jnp.float32)
-    sums = [swap(total[h], "rep", h * CUBE) if h else total[h] for h in range(replicas // CUBE)]
     scale = lax.rsqrt(squares / (part * cores) + norm_eps)[:, None]
-    raw_keys = 0.0
-    for k in range(cores):
+
+    def key_part(k):
         norm = normalize(x[k], scale, gain[k])
-        raw_keys = raw_keys + jnp.dot(norm, halves[k], preferred_element_type=jnp.float32)
+        return jnp.dot(norm, halves[k], preferred_element_type=jnp.float32)
 
     def weight_rows(k):
         norm = normalize(x[k], scale, gain[k])
@@ -247,30 +264,36 @@
         )
         return (contracted * inv_width).astype(jnp.bfloat16)
 
-    blocks = [weight_rows(0)]
-
-    sums, raw_keys, blocks, x, scale = after(sums, raw_keys, blocks, x, scale)
-    mean_weights = sum(sums) / replicas
+    raw_keys = sum(key_part(k) for k in range(cores))
+
+    second_in, raw_keys, x = after(second_in, raw_keys, x)
+    total = sum_plane(second[0], second_in)
+    sums.append(swap(total[1], "rep", PLANE))
+
+    sums, raw_keys, x, scale, gain = after(sums, raw_keys, x, scale, gain)
+    mean_weights = sum(sums, total[0]) / replicas
     change = anchor - mean_weights
     new_momentum = momentum_rate * momentum + change
     new_anchor = anchor - outer_rate * (change + momentum_rate * new_momentum)
     outgoing = new_anchor.astype(jnp.bfloat16)[None]
 
-    columns = [swap(outgoing, "rep", z * PLANE) for z in range(far - 1, 0, -1)]
-    near = [outgoing] + [swap(outgoing, "rep", p) for p in range(1, PLANE)]
-    near, raw_keys, x, columns = after(near, raw_keys, x, columns)
+    mate = swap(outgoing, "rep", PLANE)
+    column = [swap(outgoing, "rep", k) for k in far]
+    blocks = [weight_rows(0)]
+    mate, blocks = after(mate, blocks)
+    near = jnp.concatenate([outgoing, mate])
+    near = [near] + [swap(near, "rep", p) for p in mates]
+    column = jnp.concatenate(column)
+    pair = swap(column, "rep", PLANE)
+    pair, x, raw_keys = after(pair, x, raw_keys)
+    rest = jnp.concatenate([column, pair])
+    rest = [rest] + [swap(rest, "rep", p) for p in mates]
     blocks += [weight_rows(k) for k in range(1, cores)]
-    block = jnp.concatenate(columns)
-    rest = [block] + [swap(block, "rep", p) for p in range(1, PLANE)]
     key_rows = turn(inv_width, raw_keys, cosine, signed)
     weight_grad = place_blocks(blocks)
-
-    zs = range(far - 1, 0, -1)
-    early = near + rest[:1]
-    merged = merge(w, early, [[p] for p in range(PLANE)] + [[z * PLANE for z in zs]])
-    offsets = [[z * PLANE + p for z in zs] for p in range(1, PLANE)]
-    key_rows, weight_grad, merged, *rest = after(key_rows, weight_grad, merged, *rest[1:])
-    merged = merge(w, rest, offsets, merged)
+    merged = merge(w, near, [[k + p for k in near_side] for p in range(PLANE)])
+    key_rows, weight_grad, merged, *rest = after(key_rows, weight_grad, merged, *rest)
+    merged = merge(w, rest, [[k + p for k in far_side] for p in range(PLANE)], merged)
     return (key_rows, weight_grad, merged, new_anchor, new_momentum)
 
 

time: 55.9 us -> 55.1 us (0.986)
  starting transfers between devices: 29.5 us -> 23 us
  waiting for transfers between devices: 8.02 us -> 12.8 us
  local copies, waits for them, and re-layouts: 3.5 us -> 4.34 us
    ppermute x19 -> x20, starting transfers between devices: 29.5 us -> 23 us  [swap(): return lax.ppermute(value, axis, [(i, i ^ offset) for i in range(size)])]
    ppermute x19 -> x20, waiting for transfers between devices: 8.02 us -> 12.8 us  [swap(): return lax.ppermute(value, axis, [(i, i ^ offset) for i in range(size)])]
    unnamed x18 -> x17, local copies, waits for them, and re-layouts: 3.46 us -> 4.3 us
  transfers between devices with their start and end apart: 19 -> 20, of which waited for: 9 -> 4; matrix products, arithmetic and copies ran while one was open for 11% -> 12% of each run, Pallas kernels for 10% -> 10%
where the time goes in v7:
time: 55.1 us; the launch traced here: 54.9 us
  starting transfers between devices  23 us (42%)
  waiting for transfers between devices  12.8 us (23%)
  Pallas kernels  6.59 us (12%)
  matrix products  6.29 us (11%)
  local copies, waits for them, and re-layouts  4.34 us (8%)
  other arithmetic  0.94 us (2%)
  between operations  0.88 us (2%)
    ppermute x20, starting transfers between devices, swap(): return lax.ppermute(value, axis, [(i, i ^ offset) for i in range(size)])  23 us
    ppermute x20, waiting for transfers between devices, swap(): return lax.ppermute(value, axis, [(i, i ^ offset) for i in range(size)])  12.8 us
    unnamed x17, local copies, waits for them, and re-layouts  4.3 us
    dot_general x2, matrix products, weight_rows(): lax.dot_general(norm, raw_grad, (((0,), (0,)), ((), ())), preferred_eleme...  3.58 us
    dot_general x2, matrix products, key_part(): return jnp.dot(norm, halves[k], preferred_element_type=jnp.float32)  2.71 us
    pallas_call x2, Pallas kernels, squares_of(): pl.pallas_call(squares_kernel, out_shape=jax.ShapeDtypeStruct((1, rows),...  2.29 us
    pallas_call x2, Pallas kernels, merge(): pl.pallas_call(functools.partial(merge_kernel, offsets), out_shape=jax.Sh...  1.81 us
  transfers between devices with their start and end apart: 20, of which 4 were waited for; matrix products, arithmetic and copies ran while one was open for 12% of the time, Pallas kernels for 10%

profile of v7, /device:TPU:0, one launch (start us, length us, event | category | flops | bytes accessed | tf_op | source)
XLA Modules:
  0.0 54.9 jit_solution(16026873452042052492)
XLA Ops:
  1.2 1.2 %copy-done = bf16[4096,128]{1,0:T(8,128)(2,1)S(1)} copy-done((bf16[4096,128]{1,0:T(8,128)(2,1)S(1)}, bf16[4096,128]{1,0:T(8,128)(2,1)}, u32[]{:S(2)}) %copy-start) | copy-done | bytes 1048600
  2.5 2.6 %collective-permute-start.3 = (bf16[2,256,128]{2,1,0:T(8,128)(2,1)S(1)}, bf16[2,256,128]{2,1,0:T(8,128)(2,1)S(1)}, u32[]{:S(2)}, u32[]{:S(2)}) collective-permute-start(bf16[2,256,128]{2,1,0:T(8,128)(2,1)S(1)} %get-tuple-element.85), channel_id=1, source_target_pairs={{0,2},{2,0},{4,6},{6,4},{8,10},{10,8},{12,14},{14,12},{16,18},{18,... | collective-permute-start | bytes 393224 | tf_op jit(solution)/shard_map/ppermute | solution.py:32
  5.1 1.5 %collective-permute-start.4 = (bf16[2,256,128]{2,1,0:T(8,128)(2,1)S(1)}, bf16[2,256,128]{2,1,0:T(8,128)(2,1)S(1)}, u32[]{:S(2)}, u32[]{:S(2)}) collective-permute-start(bf16[2,256,128]{2,1,0:T(8,128)(2,1)S(1)} %get-tuple-element.86), channel_id=1, source_target_pairs={{0,4},{2,6},{4,0},{6,2},{8,12},{10,14},{12,8},{14,10},{16,20},{18,... | collective-permute-start | bytes 393224 | tf_op jit(solution)/shard_map/ppermute | solution.py:32
  6.6 2.2 %copy-done.2 = bf16[1024,2048]{1,0:T(8,128)(2,1)S(1)} copy-done((bf16[1024,2048]{1,0:T(8,128)(2,1)S(1)}, bf16[1024,2048]{1,0:T(8,128)(2,1)}, u32[]{:S(2)}) %copy-start.2) | copy-done | bytes 4194328
  8.8 1.1 %shard_map.102 = f32[1,1024]{1,0:T(1,128)S(1)} custom-call(bf16[1024,2048]{1,0:T(8,128)(2,1)S(1)} %copy-done.2), custom_call_target="tpu_custom_call" | custom-call | flops 1 | bytes 1 | tf_op jit(solution)/shard_map/pallas_call | solution.py:119
  10.4 3.1 %collective-permute-done.4 = bf16[2,256,128]{2,1,0:T(8,128)(2,1)S(1)} collective-permute-done((bf16[2,256,128]{2,1,0:T(8,128)(2,1)S(1)}, bf16[2,256,128]{2,1,0:T(8,128)(2,1)S(1)}, u32[]{:S(2)}, u32[]{:S(2)}) %collective-permute-start.4) | collective-permute-done | bytes 131104 | tf_op jit(solution)/shard_map/ppermute | solution.py:32
  13.6 1.6 %collective-permute-start.7 = (f32[1,256,128]{2,1,0:T(8,128)S(1)}, f32[1,256,128]{2,1,0:T(8,128)S(1)}, u32[]{:S(2)}, u32[]{:S(2)}) collective-permute-start(f32[1,256,128]{2,1,0:T(8,128)S(1)} %slice.16), channel_id=1, source_target_pairs={{0,8},{2,10},{4,12},{6,14},{8,0},{10,2},{12,4},{14,6},{16,24},{18,... | collective-permute-start | bytes 393224 | tf_op jit(solution)/shard_map/ppermute | solution.py:32
  15.2 1.2 %collective-permute-start = (bf16[2,256,128]{2,1,0:T(8,128)(2,1)S(1)}, bf16[2,256,128]{2,1,0:T(8,128)(2,1)S(1)}, u32[]{:S(2)}, u32[]{:S(2)}) collective-permute-start(bf16[2,256,128]{2,1,0:T(8,128)(2,1)S(1)} %get-tuple-element.81), channel_id=1, source_target_pairs={{0,2},{2,0},{4,6},{6,4},{8,10},{10,8},{12,14},{14,12},{16,18},{18,... | collective-permute-start | bytes 393224 | tf_op jit(solution)/shard_map/ppermute | solution.py:32
  17.3 1.4 %collective-permute-start.2 = (bf16[2,256,128]{2,1,0:T(8,128)(2,1)S(1)}, bf16[2,256,128]{2,1,0:T(8,128)(2,1)S(1)}, u32[]{:S(2)}, u32[]{:S(2)}) collective-permute-start(bf16[2,256,128]{2,1,0:T(8,128)(2,1)S(1)} %get-tuple-element.83), channel_id=1, source_target_pairs={{0,6},{2,4},{4,2},{6,0},{8,14},{10,12},{12,10},{14,8},{16,22},{18,... | collective-permute-start | bytes 393224 | tf_op jit(solution)/shard_map/ppermute | solution.py:32
  18.7 1.1 %shard_map.104 = f32[1,1024]{1,0:T(1,128)S(1)} custom-call(bf16[1024,2048]{1,0:T(8,128)(2,1)S(1)} %collective-permute-done.6.x_ref), custom_call_target="tpu_custom_call" | custom-call | flops 1 | bytes 1 | tf_op jit(solution)/shard_map/pallas_call | solution.py:119
  20.0 2.7 %collective-permute-start.9 = (f32[256,128]{1,0:T(8,128)S(1)}, f32[256,128]{1,0:T(8,128)S(1)}, u32[]{:S(2)}, u32[]{:S(2)}) collective-permute-start(f32[256,128]{1,0:T(8,128)S(1)} %fusion.17), channel_id=1, source_target_pairs={{0,16},{2,18},{4,20},{6,22},{8,24},{10,26},{12,28},{14,30},{16,0},... | collective-permute-start | bytes 393224 | tf_op jit(solution)/shard_map/ppermute | solution.py:32
  22.7 1.3 %fusion.1 = f32[1024,128]{1,0:T(8,128)S(1)} fusion(bf16[2048,128]{1,0:T(8,128)(2,1)S(1)} %get-tuple-element.103, bf16[1024,2048]{1,0:T(8,128)(2,1)S(1)} %collective-permute-done.6.x_ref, f32[2048]{0:T(1024)S(1)} %convert_element_type.78, f32[1024]{0:T(1024)S(1)} %add_rsqrt_fusion), kind=kOutput, calls=%fused_computation.5 | convolution fusion | flops 545259520 | bytes 5255168 | tf_op jit(solution)/shard_map/dot_general | solution.py:258
  24.9 1.4 %fusion.16.raw_ref = f32[1024,128]{1,0:T(8,128)S(1)} fusion(f32[1024,128]{1,0:T(8,128)S(1)} %fusion.1, bf16[2048,128]{1,0:T(8,128)(2,1)S(1)} %get-tuple-element.101, bf16[1024,2048]{1,0:T(8,128)(2,1)S(1)} %copy-done.3, f32[2048]{0:T(1024)S(1)} %convert_element_type.75, f32[1024]{0:T(1024)S(1)} %add_rsqrt_fusion), kind=kOutput, calls=%fused_computation.20 | convolution fusion | flops 545390592 | bytes 5779456 | tf_op jit(solution)/shard_map/dot_general | solution.py:258
  26.9 2.6 %collective-permute-done.9 = f32[256,128]{1,0:T(8,128)S(1)} collective-permute-done((f32[256,128]{1,0:T(8,128)S(1)}, f32[256,128]{1,0:T(8,128)S(1)}, u32[]{:S(2)}, u32[]{:S(2)}) %collective-permute-start.9) | collective-permute-done | bytes 131104 | tf_op jit(solution)/shard_map/ppermute | solution.py:32
  29.6 2.8 %collective-permute-done.10 = f32[256,128]{1,0:T(8,128)S(1)} collective-permute-done((f32[256,128]{1,0:T(8,128)S(1)}, f32[256,128]{1,0:T(8,128)S(1)}, u32[]{:S(2)}, u32[]{:S(2)}) %collective-permute-start.10) | collective-permute-done | bytes 131104 | tf_op jit(solution)/shard_map/ppermute | solution.py:32
  33.2 2.8 %collective-permute-start.11 = (bf16[1,256,128]{2,1,0:T(8,128)(2,1)S(1)}, bf16[1,256,128]{2,1,0:T(8,128)(2,1)S(1)}, u32[]{:S(2)}, u32[]{:S(2)}) collective-permute-start(bf16[1,256,128]{2,1,0:T(8,128)(2,1)S(1)} %get-tuple-element.135), channel_id=1, source_target_pairs={{0,16},{2,18},{4,20},{6,22},{8,24},{10,26},{12,28},{14,30},{16,0},... | collective-permute-start | bytes 196616 | tf_op jit(solution)/shard_map/ppermute | solution.py:32
  36.0 1.8 %fusion.14.refs_0_ = bf16[2048,128]{1,0:T(8,128)(2,1)S(1)} fusion(bf16[1024,128]{1,0:T(8,128)(2,1)S(1)} %get-tuple-element.121, bf16[1024,2048]{1,0:T(8,128)(2,1)S(1)} %copy-done.3, f32[2048]{0:T(1024)S(1)} %convert_element_type.85, f32[1024]{0:T(1024)S(1)} %add_rsqrt_fusion), kind=kOutput, calls=%fused_computation.18 | convolution fusion | flops 545783808 | bytes 4993024 | tf_op jit(solution)/shard_map/dot_general | solution.py:262
  37.9 1.6 %collective-permute-start.16 = (bf16[2,256,128]{2,1,0:T(8,128)(2,1)S(1)}, bf16[2,256,128]{2,1,0:T(8,128)(2,1)S(1)}, u32[]{:S(2)}, u32[]{:S(2)}) collective-permute-start(bf16[2,256,128]{2,1,0:T(8,128)(2,1)S(1)} %pad_maximum_fusion.refs_0_), channel_id=1, source_target_pairs={{0,6},{2,4},{4,2},{6,0},{8,14},{10,12},{12,10},{14,8},{16,22},{18,... | collective-permute-start | bytes 393224 | tf_op jit(solution)/shard_map/ppermute | solution.py:32
  39.4 1.2 %collective-permute-start.15 = (bf16[2,256,128]{2,1,0:T(8,128)(2,1)S(1)}, bf16[2,256,128]{2,1,0:T(8,128)(2,1)S(1)}, u32[]{:S(2)}, u32[]{:S(2)}) collective-permute-start(bf16[2,256,128]{2,1,0:T(8,128)(2,1)S(1)} %pad_maximum_fusion.refs_0_), channel_id=1, source_target_pairs={{0,4},{2,6},{4,0},{6,2},{8,12},{10,14},{12,8},{14,10},{16,20},{18,... | collective-permute-start | bytes 393224 | tf_op jit(solution)/shard_map/ppermute | solution.py:32
  41.4 4.3 %collective-permute-done.12 = bf16[1,256,128]{2,1,0:T(8,128)(2,1)S(1)} collective-permute-done((bf16[1,256,128]{2,1,0:T(8,128)(2,1)S(1)}, bf16[1,256,128]{2,1,0:T(8,128)(2,1)S(1)}, u32[]{:S(2)}, u32[]{:S(2)}) %collective-permute-start.12) | collective-permute-done | bytes 65568 | tf_op jit(solution)/shard_map/ppermute | solution.py:32
  45.7 1.6 %collective-permute-start.19 = (bf16[2,256,128]{2,1,0:T(8,128)(2,1)S(1)}, bf16[2,256,128]{2,1,0:T(8,128)(2,1)S(1)}, u32[]{:S(2)}, u32[]{:S(2)}) collective-permute-start(bf16[2,256,128]{2,1,0:T(8,128)(2,1)S(1)} %constant_dynamic-update-slice_fusion.refs_0_), channel_id=1, source_target_pairs={{0,6},{2,4},{4,2},{6,0},{8,14},{10,12},{12,10},{14,8},{16,22},{18,... | collective-permute-start | bytes 393224 | tf_op jit(solution)/shard_map/ppermute | solution.py:32
  47.3 1.2 %collective-permute-start.18 = (bf16[2,256,128]{2,1,0:T(8,128)(2,1)S(1)}, bf16[2,256,128]{2,1,0:T(8,128)(2,1)S(1)}, u32[]{:S(2)}, u32[]{:S(2)}) collective-permute-start(bf16[2,256,128]{2,1,0:T(8,128)(2,1)S(1)} %constant_dynamic-update-slice_fusion.refs_0_), channel_id=1, source_target_pairs={{0,4},{2,6},{4,0},{6,2},{8,12},{10,14},{12,8},{14,10},{16,20},{18,... | collective-permute-start | bytes 393224 | tf_op jit(solution)/shard_map/ppermute | solution.py:32
  49.3 1.8 %fusion.15.refs_1_ = bf16[2048,128]{1,0:T(8,128)(2,1)S(1)} fusion(bf16[1024,128]{1,0:T(8,128)(2,1)S(1)} %get-tuple-element.121, bf16[1024,2048]{1,0:T(8,128)(2,1)S(1)} %collective-permute-done.6.x_ref, f32[2048]{0:T(1024)S(1)} %convert_element_type.89, f32[1024]{0:T(1024)S(1)} %add_rsqrt_fusion), kind=kOutput, calls=%fused_computation.19 | convolution fusion | flops 545783808 | bytes 4993024 | tf_op jit(solution)/shard_map/dot_general | solution.py:262
  51.1 1.0 %shard_map.106 = bf16[4096,128]{1,0:T(8,128)(2,1)} custom-call(bf16[2048,128]{1,0:T(8,128)(2,1)S(1)} %fusion.14.refs_0_, bf16[2048,128]{1,0:T(8,128)(2,1)S(1)} %fusion.15.refs_1_), custom_call_target="tpu_custom_call" | custom-call | flops 1 | bytes 1 | tf_op jit(solution)/shard_map/pallas_call | solution.py:162
  (59 shorter events, 8.9 us)
Async XLA Ops:
  0.6 12.9 %collective-permute-start.6 = (bf16[1024,2048]{1,0:T(8,128)(2,1)}, bf16[1024,2048]{1,0:T(8,128)(2,1)S(1)}, u32[]{:S(2)}, u32[]{:S(2)}) collective-permute-start(bf16[1024,2048]{1,0:T(8,128)(2,1)} %x_ref), channel_id=1, source_target_pairs={{0,1},{1,0},{2,3},{3,2},{4,5},{5,4},{6,7},{7,6},{8,9},{9,8},{10,11... | collective-permute-start | bytes 12582920 | tf_op jit(solution)/shard_map/ppermute | solution.py:32
  2.4 7.6 %copy-start.4 = (bf16[1024,128]{1,0:T(8,128)(2,1)S(1)}, bf16[1024,128]{1,0:T(8,128)(2,1)}, u32[]{:S(2)}) copy-start(bf16[1024,128]{1,0:T(8,128)(2,1)} %grad_ref) | copy-start | bytes 786436
  2.5 7.9 %collective-permute-start.3 = (bf16[2,256,128]{2,1,0:T(8,128)(2,1)S(1)}, bf16[2,256,128]{2,1,0:T(8,128)(2,1)S(1)}, u32[]{:S(2)}, u32[]{:S(2)}) collective-permute-start(bf16[2,256,128]{2,1,0:T(8,128)(2,1)S(1)} %get-tuple-element.85), channel_id=1, source_target_pairs={{0,2},{2,0},{4,6},{6,4},{8,10},{10,8},{12,14},{14,12},{16,18},{18,... | collective-permute-start | bytes 393224 | tf_op jit(solution)/shard_map/ppermute | solution.py:32
  5.1 8.4 %collective-permute-start.4 = (bf16[2,256,128]{2,1,0:T(8,128)(2,1)S(1)}, bf16[2,256,128]{2,1,0:T(8,128)(2,1)S(1)}, u32[]{:S(2)}, u32[]{:S(2)}) collective-permute-start(bf16[2,256,128]{2,1,0:T(8,128)(2,1)S(1)} %get-tuple-element.86), channel_id=1, source_target_pairs={{0,4},{2,6},{4,0},{6,2},{8,12},{10,14},{12,8},{14,10},{16,20},{18,... | collective-permute-start | bytes 393224 | tf_op jit(solution)/shard_map/ppermute | solution.py:32
  6.6 6.9 %collective-permute-start.5 = (bf16[2,256,128]{2,1,0:T(8,128)(2,1)S(1)}, bf16[2,256,128]{2,1,0:T(8,128)(2,1)S(1)}, u32[]{:S(2)}, u32[]{:S(2)}) collective-permute-start(bf16[2,256,128]{2,1,0:T(8,128)(2,1)S(1)} %get-tuple-element.87), channel_id=1, source_target_pairs={{0,6},{2,4},{4,2},{6,0},{8,14},{10,12},{12,10},{14,8},{16,22},{18,... | collective-permute-start | bytes 393224 | tf_op jit(solution)/shard_map/ppermute | solution.py:32
  8.8 11.1 %copy-start.7 = (bf16[2048]{0:T(1024)(128)(2,1)S(1)}, bf16[2048]{0:T(1024)(128)(2,1)}, u32[]{:S(2)}) copy-start(bf16[2048]{0:T(1024)(128)(2,1)} %param.7) | copy-start | bytes 12292
  13.6 6.3 %collective-permute-start.7 = (f32[1,256,128]{2,1,0:T(8,128)S(1)}, f32[1,256,128]{2,1,0:T(8,128)S(1)}, u32[]{:S(2)}, u32[]{:S(2)}) collective-permute-start(f32[1,256,128]{2,1,0:T(8,128)S(1)} %slice.16), channel_id=1, source_target_pairs={{0,8},{2,10},{4,12},{6,14},{8,0},{10,2},{12,4},{14,6},{16,24},{18,... | collective-permute-start | bytes 393224 | tf_op jit(solution)/shard_map/ppermute | solution.py:32
  15.2 11.1 %collective-permute-start = (bf16[2,256,128]{2,1,0:T(8,128)(2,1)S(1)}, bf16[2,256,128]{2,1,0:T(8,128)(2,1)S(1)}, u32[]{:S(2)}, u32[]{:S(2)}) collective-permute-start(bf16[2,256,128]{2,1,0:T(8,128)(2,1)S(1)} %get-tuple-element.81), channel_id=1, source_target_pairs={{0,2},{2,0},{4,6},{6,4},{8,10},{10,8},{12,14},{14,12},{16,18},{18,... | collective-permute-start | bytes 393224 | tf_op jit(solution)/shard_map/ppermute | solution.py:32
  16.5 9.8 %collective-permute-start.1 = (bf16[2,256,128]{2,1,0:T(8,128)(2,1)S(1)}, bf16[2,256,128]{2,1,0:T(8,128)(2,1)S(1)}, u32[]{:S(2)}, u32[]{:S(2)}) collective-permute-start(bf16[2,256,128]{2,1,0:T(8,128)(2,1)S(1)} %get-tuple-element.82), channel_id=1, source_target_pairs={{0,4},{2,6},{4,0},{6,2},{8,12},{10,14},{12,8},{14,10},{16,20},{18,... | collective-permute-start | bytes 393224 | tf_op jit(solution)/shard_map/ppermute | solution.py:32
  17.3 9.0 %collective-permute-start.2 = (bf16[2,256,128]{2,1,0:T(8,128)(2,1)S(1)}, bf16[2,256,128]{2,1,0:T(8,128)(2,1)S(1)}, u32[]{:S(2)}, u32[]{:S(2)}) collective-permute-start(bf16[2,256,128]{2,1,0:T(8,128)(2,1)S(1)} %get-tuple-element.83), channel_id=1, source_target_pairs={{0,6},{2,4},{4,2},{6,0},{8,14},{10,12},{12,10},{14,8},{16,22},{18,... | collective-permute-start | bytes 393224 | tf_op jit(solution)/shard_map/ppermute | solution.py:32
  19.9 2.8 %collective-permute-start.8 = (bf16[2048]{0:T(1024)(128)(2,1)S(1)}, bf16[2048]{0:T(1024)(128)(2,1)S(1)}, u32[]{:S(2)}, u32[]{:S(2)}) collective-permute-start(bf16[2048]{0:T(1024)(128)(2,1)S(1)} %copy-done.7), channel_id=1, source_target_pairs={{0,1},{1,0},{2,3},{3,2},{4,5},{5,4},{6,7},{7,6},{8,9},{9,8},{10,11... | collective-permute-start | bytes 12296 | tf_op jit(solution)/shard_map/ppermute | solution.py:32
  20.0 9.5 %collective-permute-start.9 = (f32[256,128]{1,0:T(8,128)S(1)}, f32[256,128]{1,0:T(8,128)S(1)}, u32[]{:S(2)}, u32[]{:S(2)}) collective-permute-start(f32[256,128]{1,0:T(8,128)S(1)} %fusion.17), channel_id=1, source_target_pairs={{0,16},{2,18},{4,20},{6,22},{8,24},{10,26},{12,28},{14,30},{16,0},... | collective-permute-start | bytes 393224 | tf_op jit(solution)/shard_map/ppermute | solution.py:32
  24.9 7.5 %copy-start.5 = (f32[256,128]{1,0:T(8,128)S(1)}, f32[256,128]{1,0:T(8,128)}, u32[]{:S(2)}) copy-start(f32[256,128]{1,0:T(8,128)} %param.9) | copy-start | bytes 393220
  24.9 7.5 %copy-start.6 = (f32[256,128]{1,0:T(8,128)S(1)}, f32[256,128]{1,0:T(8,128)}, u32[]{:S(2)}) copy-start(f32[256,128]{1,0:T(8,128)} %param.10) | copy-start | bytes 393220
  26.4 5.9 %collective-permute-start.10 = (f32[256,128]{1,0:T(8,128)S(1)}, f32[256,128]{1,0:T(8,128)S(1)}, u32[]{:S(2)}, u32[]{:S(2)}) collective-permute-start(f32[256,128]{1,0:T(8,128)S(1)} %slice_bitcast_fusion), channel_id=1, source_target_pairs={{0,8},{2,10},{4,12},{6,14},{8,0},{10,2},{12,4},{14,6},{16,24},{18,... | collective-permute-start | bytes 393224 | tf_op jit(solution)/shard_map/ppermute | solution.py:32
  33.1 4.7 %collective-permute-start.13 = (bf16[1,256,128]{2,1,0:T(8,128)(2,1)S(1)}, bf16[1,256,128]{2,1,0:T(8,128)(2,1)S(1)}, u32[]{:S(2)}, u32[]{:S(2)}) collective-permute-start(bf16[1,256,128]{2,1,0:T(8,128)(2,1)S(1)} %get-tuple-element.135), channel_id=1, source_target_pairs={{0,8},{2,10},{4,12},{6,14},{8,0},{10,2},{12,4},{14,6},{16,24},{18,... | collective-permute-start | bytes 196616 | tf_op jit(solution)/shard_map/ppermute | solution.py:32
  33.2 8.2 %collective-permute-start.11 = (bf16[1,256,128]{2,1,0:T(8,128)(2,1)S(1)}, bf16[1,256,128]{2,1,0:T(8,128)(2,1)S(1)}, u32[]{:S(2)}, u32[]{:S(2)}) collective-permute-start(bf16[1,256,128]{2,1,0:T(8,128)(2,1)S(1)} %get-tuple-element.135), channel_id=1, source_target_pairs={{0,16},{2,18},{4,20},{6,22},{8,24},{10,26},{12,28},{14,30},{16,0},... | collective-permute-start | bytes 196616 | tf_op jit(solution)/shard_map/ppermute | solution.py:32
  37.9 10.6 %collective-permute-start.16 = (bf16[2,256,128]{2,1,0:T(8,128)(2,1)S(1)}, bf16[2,256,128]{2,1,0:T(8,128)(2,1)S(1)}, u32[]{:S(2)}, u32[]{:S(2)}) collective-permute-start(bf16[2,256,128]{2,1,0:T(8,128)(2,1)S(1)} %pad_maximum_fusion.refs_0_), channel_id=1, source_target_pairs={{0,6},{2,4},{4,2},{6,0},{8,14},{10,12},{12,10},{14,8},{16,22},{18,... | collective-permute-start | bytes 393224 | tf_op jit(solution)/shard_map/ppermute | solution.py:32
  39.4 13.6 %collective-permute-start.15 = (bf16[2,256,128]{2,1,0:T(8,128)(2,1)S(1)}, bf16[2,256,128]{2,1,0:T(8,128)(2,1)S(1)}, u32[]{:S(2)}, u32[]{:S(2)}) collective-permute-start(bf16[2,256,128]{2,1,0:T(8,128)(2,1)S(1)} %pad_maximum_fusion.refs_0_), channel_id=1, source_target_pairs={{0,4},{2,6},{4,0},{6,2},{8,12},{10,14},{12,8},{14,10},{16,20},{18,... | collective-permute-start | bytes 393224 | tf_op jit(solution)/shard_map/ppermute | solution.py:32
  40.6 12.4 %collective-permute-start.14 = (bf16[2,256,128]{2,1,0:T(8,128)(2,1)S(1)}, bf16[2,256,128]{2,1,0:T(8,128)(2,1)S(1)}, u32[]{:S(2)}, u32[]{:S(2)}) collective-permute-start(bf16[2,256,128]{2,1,0:T(8,128)(2,1)S(1)} %pad_maximum_fusion.refs_0_), channel_id=1, source_target_pairs={{0,2},{2,0},{4,6},{6,4},{8,10},{10,8},{12,14},{14,12},{16,18},{18,... | collective-permute-start | bytes 393224 | tf_op jit(solution)/shard_map/ppermute | solution.py:32
  41.4 4.3 %collective-permute-start.12 = (bf16[1,256,128]{2,1,0:T(8,128)(2,1)S(1)}, bf16[1,256,128]{2,1,0:T(8,128)(2,1)S(1)}, u32[]{:S(2)}, u32[]{:S(2)}) collective-permute-start(bf16[1,256,128]{2,1,0:T(8,128)(2,1)S(1)} %collective-permute-done.11), channel_id=1, source_target_pairs={{0,8},{2,10},{4,12},{6,14},{8,0},{10,2},{12,4},{14,6},{16,24},{18,... | collective-permute-start | bytes 196616 | tf_op jit(solution)/shard_map/ppermute | solution.py:32
  45.7 8.3 %collective-permute-start.19 = (bf16[2,256,128]{2,1,0:T(8,128)(2,1)S(1)}, bf16[2,256,128]{2,1,0:T(8,128)(2,1)S(1)}, u32[]{:S(2)}, u32[]{:S(2)}) collective-permute-start(bf16[2,256,128]{2,1,0:T(8,128)(2,1)S(1)} %constant_dynamic-update-slice_fusion.refs_0_), channel_id=1, source_target_pairs={{0,6},{2,4},{4,2},{6,0},{8,14},{10,12},{12,10},{14,8},{16,22},{18,... | collective-permute-start | bytes 393224 | tf_op jit(solution)/shard_map/ppermute | solution.py:32
  47.3 6.7 %collective-permute-start.18 = (bf16[2,256,128]{2,1,0:T(8,128)(2,1)S(1)}, bf16[2,256,128]{2,1,0:T(8,128)(2,1)S(1)}, u32[]{:S(2)}, u32[]{:S(2)}) collective-permute-start(bf16[2,256,128]{2,1,0:T(8,128)(2,1)S(1)} %constant_dynamic-update-slice_fusion.refs_0_), channel_id=1, source_target_pairs={{0,4},{2,6},{4,0},{6,2},{8,12},{10,14},{12,8},{14,10},{16,20},{18,... | collective-permute-start | bytes 393224 | tf_op jit(solution)/shard_map/ppermute | solution.py:32
  48.5 5.5 %collective-permute-start.17 = (bf16[2,256,128]{2,1,0:T(8,128)(2,1)S(1)}, bf16[2,256,128]{2,1,0:T(8,128)(2,1)S(1)}, u32[]{:S(2)}, u32[]{:S(2)}) collective-permute-start(bf16[2,256,128]{2,1,0:T(8,128)(2,1)S(1)} %constant_dynamic-update-slice_fusion.refs_0_), channel_id=1, source_target_pairs={{0,2},{2,0},{4,6},{6,4},{8,10},{10,8},{12,14},{14,12},{16,18},{18,... | collective-permute-start | bytes 393224 | tf_op jit(solution)/shard_map/ppermute | solution.py:32
  (4 other events, 7.6 us)

commit v8 on v7

--- a/solution.py
+++ b/solution.py
@@ -239,14 +239,11 @@
     first_in = [swap(first[p], "rep", p) for p in mates]
     second_in = [swap(second[p], "rep", p) for p in mates]
     cosine, signed, raw_grad = prepare(key_grad)
-    squares = squares_of(own)
+    squares = sum(squares_of(block) for block in x)
 
     first_in, squares, raw_grad, x, norm_gain = after(first_in, squares, raw_grad, x, norm_gain)
     total = sum_plane(first[0], first_in)
     pair = swap(total[len(far) :], "rep", PLANE)
-    for k in range(1, cores):
-        squares = squares + squares_of(x[k])
-
     pair, squares, x, norm_gain = after(pair, squares, x, norm_gain)
     total = total[: len(far)] + pair
     sums = [swap(total[i], "rep", k) for i, k in enumerate(far)]
@@ -270,7 +267,8 @@
     total = sum_plane(second[0], second_in)
     sums.append(swap(total[1], "rep", PLANE))
 
-    sums, raw_keys, x, scale, gain = after(sums, raw_keys, x, scale, gain)
+    key_rows = turn(inv_width, raw_keys, cosine, signed)
+    sums, key_rows, x, scale, gain = after(sums, key_rows, x, scale, gain)
     mean_weights = sum(sums, total[0]) / replicas
     change = anchor - mean_weights
     new_momentum = momentum_rate * momentum + change
@@ -278,18 +276,15 @@
     outgoing = new_anchor.astype(jnp.bfloat16)[None]
 
     mate = swap(outgoing, "rep", PLANE)
-    column = [swap(outgoing, "rep", k) for k in far]
-    blocks = [weight_rows(0)]
-    mate, blocks = after(mate, blocks)
+    column = [swap(outgoing, "rep", k) for k in far_side]
     near = jnp.concatenate([outgoing, mate])
     near = [near] + [swap(near, "rep", p) for p in mates]
-    column = jnp.concatenate(column)
-    pair = swap(column, "rep", PLANE)
-    pair, x, raw_keys = after(pair, x, raw_keys)
-    rest = jnp.concatenate([column, pair])
+    blocks = [weight_rows(0)]
+    column, blocks, x = after(column, blocks, x)
+    rest = jnp.concatenate(column)
     rest = [rest] + [swap(rest, "rep", p) for p in mates]
+    near, x = after(near, x)
     blocks += [weight_rows(k) for k in range(1, cores)]
-    key_rows = turn(inv_width, raw_keys, cosine, signed)
     weight_grad = place_blocks(blocks)
     merged = merge(w, near, [[k + p for k in near_side] for p in range(PLANE)])
     key_rows, weight_grad, merged, *rest = after(key_rows, weight_grad, merged, *rest)

time: 55.1 us -> 54.3 us (0.985)
  waiting for transfers between devices: 12.8 us -> 9.54 us
  starting transfers between devices: 23 us -> 25.5 us
    ppermute x20, waiting for transfers between devices: 12.8 us -> 9.54 us  [swap(): return lax.ppermute(value, axis, [(i, i ^ offset) for i in range(size)])]
    ppermute x20, starting transfers between devices: 23 us -> 25.5 us  [swap(): return lax.ppermute(value, axis, [(i, i ^ offset) for i in range(size)])]
  transfers between devices with their start and end apart: 20 -> 20, of which waited for: 4 -> 6; matrix products, arithmetic and copies ran while one was open for 12% -> 12% of each run, Pallas kernels for 10% -> 11%
where the time goes in v8:
time: 54.3 us; the launch traced here: 54.1 us
  starting transfers between devices  25.5 us (47%)
  waiting for transfers between devices  9.54 us (18%)
  Pallas kernels  6.61 us (12%)
  matrix products  6.3 us (12%)
  local copies, waits for them, and re-layouts  4.33 us (8%)
  other arithmetic  0.93 us (2%)
  between operations  0.88 us (2%)
    ppermute x20, starting transfers between devices, swap(): return lax.ppermute(value, axis, [(i, i ^ offset) for i in range(size)])  25.5 us
    ppermute x20, waiting for transfers between devices, swap(): return lax.ppermute(value, axis, [(i, i ^ offset) for i in range(size)])  9.54 us
    unnamed x17, local copies, waits for them, and re-layouts  4.3 us
    dot_general x2, matrix products, weight_rows(): lax.dot_general(norm, raw_grad, (((0,), (0,)), ((), ())), preferred_eleme...  3.59 us
    dot_general x2, matrix products, key_part(): return jnp.dot(norm, halves[k], preferred_element_type=jnp.float32)  2.72 us
    pallas_call x2, Pallas kernels, squares_of(): pl.pallas_call(squares_kernel, out_shape=jax.ShapeDtypeStruct((1, rows),...  2.31 us
    pallas_call x2, Pallas kernels, merge(): pl.pallas_call(functools.partial(merge_kernel, offsets), out_shape=jax.Sh...  1.8 us
  transfers between devices with their start and end apart: 20, of which 6 were waited for; matrix products, arithmetic and copies ran while one was open for 12% of the time, Pallas kernels for 11%

profile of v8, /device:TPU:0, one launch (start us, length us, event | category | flops | bytes accessed | tf_op | source)
XLA Modules:
  0.0 54.1 jit_solution(6670594465790657427)
XLA Ops:
  1.2 1.2 %copy-done = bf16[4096,128]{1,0:T(8,128)(2,1)S(1)} copy-done((bf16[4096,128]{1,0:T(8,128)(2,1)S(1)}, bf16[4096,128]{1,0:T(8,128)(2,1)}, u32[]{:S(2)}) %copy-start) | copy-done | bytes 1048600
  2.5 2.6 %collective-permute-start = (bf16[2,256,128]{2,1,0:T(8,128)(2,1)S(1)}, bf16[2,256,128]{2,1,0:T(8,128)(2,1)S(1)}, u32[]{:S(2)}, u32[]{:S(2)}) collective-permute-start(bf16[2,256,128]{2,1,0:T(8,128)(2,1)S(1)} %get-tuple-element.85), channel_id=1, source_target_pairs={{0,2},{2,0},{4,6},{6,4},{8,10},{10,8},{12,14},{14,12},{16,18},{18,... | collective-permute-start | bytes 393224 | tf_op jit(solution)/shard_map/ppermute | solution.py:32
  5.1 1.5 %collective-permute-start.1 = (bf16[2,256,128]{2,1,0:T(8,128)(2,1)S(1)}, bf16[2,256,128]{2,1,0:T(8,128)(2,1)S(1)}, u32[]{:S(2)}, u32[]{:S(2)}) collective-permute-start(bf16[2,256,128]{2,1,0:T(8,128)(2,1)S(1)} %get-tuple-element.86), channel_id=1, source_target_pairs={{0,4},{2,6},{4,0},{6,2},{8,12},{10,14},{12,8},{14,10},{16,20},{18,... | collective-permute-start | bytes 393224 | tf_op jit(solution)/shard_map/ppermute | solution.py:32
  6.6 2.2 %copy-done.2 = bf16[1024,2048]{1,0:T(8,128)(2,1)S(1)} copy-done((bf16[1024,2048]{1,0:T(8,128)(2,1)S(1)}, bf16[1024,2048]{1,0:T(8,128)(2,1)}, u32[]{:S(2)}) %copy-start.2) | copy-done | bytes 4194328
  8.8 1.1 %shard_map.102 = f32[1,1024]{1,0:T(1,128)S(1)} custom-call(bf16[1024,2048]{1,0:T(8,128)(2,1)S(1)} %copy-done.2), custom_call_target="tpu_custom_call" | custom-call | flops 1 | bytes 1 | tf_op jit(solution)/shard_map/pallas_call | solution.py:119
  10.4 1.2 %shard_map.103 = f32[1,1024]{1,0:T(1,128)S(1)} custom-call(bf16[1024,2048]{1,0:T(8,128)(2,1)S(1)} %collective-permute-done.3.x_ref), custom_call_target="tpu_custom_call" | custom-call | flops 1 | bytes 1 | tf_op jit(solution)/shard_map/pallas_call | solution.py:119
  11.6 1.9 %collective-permute-done.1 = bf16[2,256,128]{2,1,0:T(8,128)(2,1)S(1)} collective-permute-done((bf16[2,256,128]{2,1,0:T(8,128)(2,1)S(1)}, bf16[2,256,128]{2,1,0:T(8,128)(2,1)S(1)}, u32[]{:S(2)}, u32[]{:S(2)}) %collective-permute-start.1) | collective-permute-done | bytes 131104 | tf_op jit(solution)/shard_map/ppermute | solution.py:32
  13.6 1.6 %collective-permute-start.4 = (f32[1,256,128]{2,1,0:T(8,128)S(1)}, f32[1,256,128]{2,1,0:T(8,128)S(1)}, u32[]{:S(2)}, u32[]{:S(2)}) collective-permute-start(f32[1,256,128]{2,1,0:T(8,128)S(1)} %slice.17), channel_id=1, source_target_pairs={{0,8},{2,10},{4,12},{6,14},{8,0},{10,2},{12,4},{14,6},{16,24},{18,... | collective-permute-start | bytes 393224 | tf_op jit(solution)/shard_map/ppermute | solution.py:32
  15.2 1.2 %collective-permute-start.6 = (bf16[2,256,128]{2,1,0:T(8,128)(2,1)S(1)}, bf16[2,256,128]{2,1,0:T(8,128)(2,1)S(1)}, u32[]{:S(2)}, u32[]{:S(2)}) collective-permute-start(bf16[2,256,128]{2,1,0:T(8,128)(2,1)S(1)} %get-tuple-element.100), channel_id=1, source_target_pairs={{0,2},{2,0},{4,6},{6,4},{8,10},{10,8},{12,14},{14,12},{16,18},{18,... | collective-permute-start | bytes 393224 | tf_op jit(solution)/shard_map/ppermute | solution.py:32
  17.3 1.4 %collective-permute-start.8 = (bf16[2,256,128]{2,1,0:T(8,128)(2,1)S(1)}, bf16[2,256,128]{2,1,0:T(8,128)(2,1)S(1)}, u32[]{:S(2)}, u32[]{:S(2)}) collective-permute-start(bf16[2,256,128]{2,1,0:T(8,128)(2,1)S(1)} %get-tuple-element.102), channel_id=1, source_target_pairs={{0,6},{2,4},{4,2},{6,0},{8,14},{10,12},{12,10},{14,8},{16,22},{18,... | collective-permute-start | bytes 393224 | tf_op jit(solution)/shard_map/ppermute | solution.py:32
  18.9 2.7 %collective-permute-start.5 = (f32[256,128]{1,0:T(8,128)S(1)}, f32[256,128]{1,0:T(8,128)S(1)}, u32[]{:S(2)}, u32[]{:S(2)}) collective-permute-start(f32[256,128]{1,0:T(8,128)S(1)} %fusion.21), channel_id=1, source_target_pairs={{0,16},{2,18},{4,20},{6,22},{8,24},{10,26},{12,28},{14,30},{16,0},... | collective-permute-start | bytes 393224 | tf_op jit(solution)/shard_map/ppermute | solution.py:32
  21.5 1.3 %fusion.1 = f32[1024,128]{1,0:T(8,128)S(1)} fusion(bf16[2048,128]{1,0:T(8,128)(2,1)S(1)} %get-tuple-element.108, bf16[1024,2048]{1,0:T(8,128)(2,1)S(1)} %collective-permute-done.3.x_ref, f32[2048]{0:T(1024)S(1)} %convert_element_type.78, f32[1024]{0:T(1024)S(1)} %add_rsqrt_fusion), kind=kOutput, calls=%fused_computation.5 | convolution fusion | flops 545259520 | bytes 5255168 | tf_op jit(solution)/shard_map/dot_general | solution.py:255
  23.7 1.4 %fusion.16.raw_ref = f32[1024,128]{1,0:T(8,128)S(1)} fusion(f32[1024,128]{1,0:T(8,128)S(1)} %fusion.1, bf16[2048,128]{1,0:T(8,128)(2,1)S(1)} %get-tuple-element.106, bf16[1024,2048]{1,0:T(8,128)(2,1)S(1)} %copy-done.3, f32[2048]{0:T(1024)S(1)} %convert_element_type.75, f32[1024]{0:T(1024)S(1)} %add_rsqrt_fusion), kind=kOutput, calls=%fused_computation.20 | convolution fusion | flops 545390592 | bytes 5779456 | tf_op jit(solution)/shard_map/dot_general | solution.py:255
  25.2 1.5 %collective-permute-start.10 = (f32[256,128]{1,0:T(8,128)S(1)}, f32[256,128]{1,0:T(8,128)S(1)}, u32[]{:S(2)}, u32[]{:S(2)}) collective-permute-start(f32[256,128]{1,0:T(8,128)S(1)} %slice_bitcast_fusion.1), channel_id=1, source_target_pairs={{0,8},{2,10},{4,12},{6,14},{8,0},{10,2},{12,4},{14,6},{16,24},{18,... | collective-permute-start | bytes 393224 | tf_op jit(solution)/shard_map/ppermute | solution.py:32
  28.5 2.8 %collective-permute-done.10 = f32[256,128]{1,0:T(8,128)S(1)} collective-permute-done((f32[256,128]{1,0:T(8,128)S(1)}, f32[256,128]{1,0:T(8,128)S(1)}, u32[]{:S(2)}, u32[]{:S(2)}) %collective-permute-start.10) | collective-permute-done | bytes 131104 | tf_op jit(solution)/shard_map/ppermute | solution.py:32
  33.1 2.4 %collective-permute-start.12 = (bf16[1,256,128]{2,1,0:T(8,128)(2,1)S(1)}, bf16[1,256,128]{2,1,0:T(8,128)(2,1)S(1)}, u32[]{:S(2)}, u32[]{:S(2)}) collective-permute-start(bf16[1,256,128]{2,1,0:T(8,128)(2,1)S(1)} %get-tuple-element.143), channel_id=1, source_target_pairs={{0,24},{2,26},{4,28},{6,30},{8,16},{10,18},{12,20},{14,22},{16,8},... | collective-permute-start | bytes 196616 | tf_op jit(solution)/shard_map/ppermute | solution.py:32
  36.1 1.8 %fusion.14.refs_0_ = bf16[2048,128]{1,0:T(8,128)(2,1)S(1)} fusion(bf16[1024,128]{1,0:T(8,128)(2,1)S(1)} %get-tuple-element.123, bf16[1024,2048]{1,0:T(8,128)(2,1)S(1)} %copy-done.3, f32[2048]{0:T(1024)S(1)} %convert_element_type.85, f32[1024]{0:T(1024)S(1)} %add_rsqrt_fusion), kind=kOutput, calls=%fused_computation.18 | convolution fusion | flops 545783808 | bytes 4993024 | tf_op jit(solution)/shard_map/dot_general | solution.py:259
  37.9 1.6 %collective-permute-start.16 = (bf16[2,256,128]{2,1,0:T(8,128)(2,1)S(1)}, bf16[2,256,128]{2,1,0:T(8,128)(2,1)S(1)}, u32[]{:S(2)}, u32[]{:S(2)}) collective-permute-start(bf16[2,256,128]{2,1,0:T(8,128)(2,1)S(1)} %pad_maximum_fusion.refs_0_), channel_id=1, source_target_pairs={{0,6},{2,4},{4,2},{6,0},{8,14},{10,12},{12,10},{14,8},{16,22},{18,... | collective-permute-start | bytes 393224 | tf_op jit(solution)/shard_map/ppermute | solution.py:32
  39.5 1.2 %collective-permute-start.15 = (bf16[2,256,128]{2,1,0:T(8,128)(2,1)S(1)}, bf16[2,256,128]{2,1,0:T(8,128)(2,1)S(1)}, u32[]{:S(2)}, u32[]{:S(2)}) collective-permute-start(bf16[2,256,128]{2,1,0:T(8,128)(2,1)S(1)} %pad_maximum_fusion.refs_0_), channel_id=1, source_target_pairs={{0,4},{2,6},{4,0},{6,2},{8,12},{10,14},{12,8},{14,10},{16,20},{18,... | collective-permute-start | bytes 393224 | tf_op jit(solution)/shard_map/ppermute | solution.py:32
  42.4 1.6 %collective-permute-start.19 = (bf16[2,256,128]{2,1,0:T(8,128)(2,1)S(1)}, bf16[2,256,128]{2,1,0:T(8,128)(2,1)S(1)}, u32[]{:S(2)}, u32[]{:S(2)}) collective-permute-start(bf16[2,256,128]{2,1,0:T(8,128)(2,1)S(1)} %constant_dynamic-update-slice_fusion.refs_0_), channel_id=1, source_target_pairs={{0,6},{2,4},{4,2},{6,0},{8,14},{10,12},{12,10},{14,8},{16,22},{18,... | collective-permute-start | bytes 393224 | tf_op jit(solution)/shard_map/ppermute | solution.py:32
  43.9 1.2 %collective-permute-start.18 = (bf16[2,256,128]{2,1,0:T(8,128)(2,1)S(1)}, bf16[2,256,128]{2,1,0:T(8,128)(2,1)S(1)}, u32[]{:S(2)}, u32[]{:S(2)}) collective-permute-start(bf16[2,256,128]{2,1,0:T(8,128)(2,1)S(1)} %constant_dynamic-update-slice_fusion.refs_0_), channel_id=1, source_target_pairs={{0,4},{2,6},{4,0},{6,2},{8,12},{10,14},{12,8},{14,10},{16,20},{18,... | collective-permute-start | bytes 393224 | tf_op jit(solution)/shard_map/ppermute | solution.py:32
  45.3 1.1 %collective-permute-start.17 = (bf16[2,256,128]{2,1,0:T(8,128)(2,1)S(1)}, bf16[2,256,128]{2,1,0:T(8,128)(2,1)S(1)}, u32[]{:S(2)}, u32[]{:S(2)}) collective-permute-start(bf16[2,256,128]{2,1,0:T(8,128)(2,1)S(1)} %constant_dynamic-update-slice_fusion.refs_0_), channel_id=1, source_target_pairs={{0,2},{2,0},{4,6},{6,4},{8,10},{10,8},{12,14},{14,12},{16,18},{18,... | collective-permute-start | bytes 393224 | tf_op jit(solution)/shard_map/ppermute | solution.py:32
  46.3 3.1 %collective-permute-done.15.refs_2_ = bf16[2,256,128]{2,1,0:T(8,128)(2,1)S(1)} collective-permute-done((bf16[2,256,128]{2,1,0:T(8,128)(2,1)S(1)}, bf16[2,256,128]{2,1,0:T(8,128)(2,1)S(1)}, u32[]{:S(2)}, u32[]{:S(2)}) %collective-permute-start.15) | collective-permute-done | bytes 131104 | tf_op jit(solution)/shard_map/ppermute | solution.py:32
  49.4 1.8 %fusion.15.refs_1_ = bf16[2048,128]{1,0:T(8,128)(2,1)S(1)} fusion(bf16[1024,128]{1,0:T(8,128)(2,1)S(1)} %get-tuple-element.123, bf16[1024,2048]{1,0:T(8,128)(2,1)S(1)} %collective-permute-done.3.x_ref, f32[2048]{0:T(1024)S(1)} %convert_element_type.89, f32[1024]{0:T(1024)S(1)} %add_rsqrt_fusion), kind=kOutput, calls=%fused_computation.19 | convolution fusion | flops 545783808 | bytes 4993024 | tf_op jit(solution)/shard_map/dot_general | solution.py:259
  (59 shorter events, 11.7 us)
Async XLA Ops:
  0.6 9.7 %collective-permute-start.3 = (bf16[1024,2048]{1,0:T(8,128)(2,1)}, bf16[1024,2048]{1,0:T(8,128)(2,1)S(1)}, u32[]{:S(2)}, u32[]{:S(2)}) collective-permute-start(bf16[1024,2048]{1,0:T(8,128)(2,1)} %x_ref), channel_id=1, source_target_pairs={{0,1},{1,0},{2,3},{3,2},{4,5},{5,4},{6,7},{7,6},{8,9},{9,8},{10,11... | collective-permute-start | bytes 12582920 | tf_op jit(solution)/shard_map/ppermute | solution.py:32
  2.4 7.6 %copy-start.4 = (bf16[1024,128]{1,0:T(8,128)(2,1)S(1)}, bf16[1024,128]{1,0:T(8,128)(2,1)}, u32[]{:S(2)}) copy-start(bf16[1024,128]{1,0:T(8,128)(2,1)} %grad_ref) | copy-start | bytes 786436
  2.5 9.1 %collective-permute-start = (bf16[2,256,128]{2,1,0:T(8,128)(2,1)S(1)}, bf16[2,256,128]{2,1,0:T(8,128)(2,1)S(1)}, u32[]{:S(2)}, u32[]{:S(2)}) collective-permute-start(bf16[2,256,128]{2,1,0:T(8,128)(2,1)S(1)} %get-tuple-element.85), channel_id=1, source_target_pairs={{0,2},{2,0},{4,6},{6,4},{8,10},{10,8},{12,14},{14,12},{16,18},{18,... | collective-permute-start | bytes 393224 | tf_op jit(solution)/shard_map/ppermute | solution.py:32
  5.1 8.4 %collective-permute-start.1 = (bf16[2,256,128]{2,1,0:T(8,128)(2,1)S(1)}, bf16[2,256,128]{2,1,0:T(8,128)(2,1)S(1)}, u32[]{:S(2)}, u32[]{:S(2)}) collective-permute-start(bf16[2,256,128]{2,1,0:T(8,128)(2,1)S(1)} %get-tuple-element.86), channel_id=1, source_target_pairs={{0,4},{2,6},{4,0},{6,2},{8,12},{10,14},{12,8},{14,10},{16,20},{18,... | collective-permute-start | bytes 393224 | tf_op jit(solution)/shard_map/ppermute | solution.py:32
  6.6 6.9 %collective-permute-start.2 = (bf16[2,256,128]{2,1,0:T(8,128)(2,1)S(1)}, bf16[2,256,128]{2,1,0:T(8,128)(2,1)S(1)}, u32[]{:S(2)}, u32[]{:S(2)}) collective-permute-start(bf16[2,256,128]{2,1,0:T(8,128)(2,1)S(1)} %get-tuple-element.87), channel_id=1, source_target_pairs={{0,6},{2,4},{4,2},{6,0},{8,14},{10,12},{12,10},{14,8},{16,22},{18,... | collective-permute-start | bytes 393224 | tf_op jit(solution)/shard_map/ppermute | solution.py:32
  8.8 9.9 %copy-start.7 = (bf16[2048]{0:T(1024)(128)(2,1)S(1)}, bf16[2048]{0:T(1024)(128)(2,1)}, u32[]{:S(2)}) copy-start(bf16[2048]{0:T(1024)(128)(2,1)} %param.7) | copy-start | bytes 12292
  13.6 5.1 %collective-permute-start.4 = (f32[1,256,128]{2,1,0:T(8,128)S(1)}, f32[1,256,128]{2,1,0:T(8,128)S(1)}, u32[]{:S(2)}, u32[]{:S(2)}) collective-permute-start(f32[1,256,128]{2,1,0:T(8,128)S(1)} %slice.17), channel_id=1, source_target_pairs={{0,8},{2,10},{4,12},{6,14},{8,0},{10,2},{12,4},{14,6},{16,24},{18,... | collective-permute-start | bytes 393224 | tf_op jit(solution)/shard_map/ppermute | solution.py:32
  15.2 9.9 %collective-permute-start.6 = (bf16[2,256,128]{2,1,0:T(8,128)(2,1)S(1)}, bf16[2,256,128]{2,1,0:T(8,128)(2,1)S(1)}, u32[]{:S(2)}, u32[]{:S(2)}) collective-permute-start(bf16[2,256,128]{2,1,0:T(8,128)(2,1)S(1)} %get-tuple-element.100), channel_id=1, source_target_pairs={{0,2},{2,0},{4,6},{6,4},{8,10},{10,8},{12,14},{14,12},{16,18},{18,... | collective-permute-start | bytes 393224 | tf_op jit(solution)/shard_map/ppermute | solution.py:32
  16.5 8.7 %collective-permute-start.7 = (bf16[2,256,128]{2,1,0:T(8,128)(2,1)S(1)}, bf16[2,256,128]{2,1,0:T(8,128)(2,1)S(1)}, u32[]{:S(2)}, u32[]{:S(2)}) collective-permute-start(bf16[2,256,128]{2,1,0:T(8,128)(2,1)S(1)} %get-tuple-element.101), channel_id=1, source_target_pairs={{0,4},{2,6},{4,0},{6,2},{8,12},{10,14},{12,8},{14,10},{16,20},{18,... | collective-permute-start | bytes 393224 | tf_op jit(solution)/shard_map/ppermute | solution.py:32
  17.3 7.8 %collective-permute-start.8 = (bf16[2,256,128]{2,1,0:T(8,128)(2,1)S(1)}, bf16[2,256,128]{2,1,0:T(8,128)(2,1)S(1)}, u32[]{:S(2)}, u32[]{:S(2)}) collective-permute-start(bf16[2,256,128]{2,1,0:T(8,128)(2,1)S(1)} %get-tuple-element.102), channel_id=1, source_target_pairs={{0,6},{2,4},{4,2},{6,0},{8,14},{10,12},{12,10},{14,8},{16,22},{18,... | collective-permute-start | bytes 393224 | tf_op jit(solution)/shard_map/ppermute | solution.py:32
  18.8 2.8 %collective-permute-start.9 = (bf16[2048]{0:T(1024)(128)(2,1)S(1)}, bf16[2048]{0:T(1024)(128)(2,1)S(1)}, u32[]{:S(2)}, u32[]{:S(2)}) collective-permute-start(bf16[2048]{0:T(1024)(128)(2,1)S(1)} %copy-done.7), channel_id=1, source_target_pairs={{0,1},{1,0},{2,3},{3,2},{4,5},{5,4},{6,7},{7,6},{8,9},{9,8},{10,11... | collective-permute-start | bytes 12296 | tf_op jit(solution)/shard_map/ppermute | solution.py:32
  18.9 9.7 %collective-permute-start.5 = (f32[256,128]{1,0:T(8,128)S(1)}, f32[256,128]{1,0:T(8,128)S(1)}, u32[]{:S(2)}, u32[]{:S(2)}) collective-permute-start(f32[256,128]{1,0:T(8,128)S(1)} %fusion.21), channel_id=1, source_target_pairs={{0,16},{2,18},{4,20},{6,22},{8,24},{10,26},{12,28},{14,30},{16,0},... | collective-permute-start | bytes 393224 | tf_op jit(solution)/shard_map/ppermute | solution.py:32
  23.7 7.6 %copy-start.6 = (f32[256,128]{1,0:T(8,128)S(1)}, f32[256,128]{1,0:T(8,128)}, u32[]{:S(2)}) copy-start(f32[256,128]{1,0:T(8,128)} %param.10) | copy-start | bytes 393220
  25.2 6.0 %collective-permute-start.10 = (f32[256,128]{1,0:T(8,128)S(1)}, f32[256,128]{1,0:T(8,128)S(1)}, u32[]{:S(2)}, u32[]{:S(2)}) collective-permute-start(f32[256,128]{1,0:T(8,128)S(1)} %slice_bitcast_fusion.1), channel_id=1, source_target_pairs={{0,8},{2,10},{4,12},{6,14},{8,0},{10,2},{12,4},{14,6},{16,24},{18,... | collective-permute-start | bytes 393224 | tf_op jit(solution)/shard_map/ppermute | solution.py:32
  32.0 5.9 %collective-permute-start.13 = (bf16[1,256,128]{2,1,0:T(8,128)(2,1)S(1)}, bf16[1,256,128]{2,1,0:T(8,128)(2,1)S(1)}, u32[]{:S(2)}, u32[]{:S(2)}) collective-permute-start(bf16[1,256,128]{2,1,0:T(8,128)(2,1)S(1)} %get-tuple-element.143), channel_id=1, source_target_pairs={{0,8},{2,10},{4,12},{6,14},{8,0},{10,2},{12,4},{14,6},{16,24},{18,... | collective-permute-start | bytes 196616 | tf_op jit(solution)/shard_map/ppermute | solution.py:32
  33.1 8.4 %collective-permute-start.12 = (bf16[1,256,128]{2,1,0:T(8,128)(2,1)S(1)}, bf16[1,256,128]{2,1,0:T(8,128)(2,1)S(1)}, u32[]{:S(2)}, u32[]{:S(2)}) collective-permute-start(bf16[1,256,128]{2,1,0:T(8,128)(2,1)S(1)} %get-tuple-element.143), channel_id=1, source_target_pairs={{0,24},{2,26},{4,28},{6,30},{8,16},{10,18},{12,20},{14,22},{16,8},... | collective-permute-start | bytes 196616 | tf_op jit(solution)/shard_map/ppermute | solution.py:32
  35.5 6.8 %collective-permute-start.11 = (bf16[1,256,128]{2,1,0:T(8,128)(2,1)S(1)}, bf16[1,256,128]{2,1,0:T(8,128)(2,1)S(1)}, u32[]{:S(2)}, u32[]{:S(2)}) collective-permute-start(bf16[1,256,128]{2,1,0:T(8,128)(2,1)S(1)} %get-tuple-element.143), channel_id=1, source_target_pairs={{0,16},{2,18},{4,20},{6,22},{8,24},{10,26},{12,28},{14,30},{16,0},... | collective-permute-start | bytes 196616 | tf_op jit(solution)/shard_map/ppermute | solution.py:32
  37.9 7.3 %collective-permute-start.16 = (bf16[2,256,128]{2,1,0:T(8,128)(2,1)S(1)}, bf16[2,256,128]{2,1,0:T(8,128)(2,1)S(1)}, u32[]{:S(2)}, u32[]{:S(2)}) collective-permute-start(bf16[2,256,128]{2,1,0:T(8,128)(2,1)S(1)} %pad_maximum_fusion.refs_0_), channel_id=1, source_target_pairs={{0,6},{2,4},{4,2},{6,0},{8,14},{10,12},{12,10},{14,8},{16,22},{18,... | collective-permute-start | bytes 393224 | tf_op jit(solution)/shard_map/ppermute | solution.py:32
  39.5 9.9 %collective-permute-start.15 = (bf16[2,256,128]{2,1,0:T(8,128)(2,1)S(1)}, bf16[2,256,128]{2,1,0:T(8,128)(2,1)S(1)}, u32[]{:S(2)}, u32[]{:S(2)}) collective-permute-start(bf16[2,256,128]{2,1,0:T(8,128)(2,1)S(1)} %pad_maximum_fusion.refs_0_), channel_id=1, source_target_pairs={{0,4},{2,6},{4,0},{6,2},{8,12},{10,14},{12,8},{14,10},{16,20},{18,... | collective-permute-start | bytes 393224 | tf_op jit(solution)/shard_map/ppermute | solution.py:32
  40.7 8.7 %collective-permute-start.14 = (bf16[2,256,128]{2,1,0:T(8,128)(2,1)S(1)}, bf16[2,256,128]{2,1,0:T(8,128)(2,1)S(1)}, u32[]{:S(2)}, u32[]{:S(2)}) collective-permute-start(bf16[2,256,128]{2,1,0:T(8,128)(2,1)S(1)} %pad_maximum_fusion.refs_0_), channel_id=1, source_target_pairs={{0,2},{2,0},{4,6},{6,4},{8,10},{10,8},{12,14},{14,12},{16,18},{18,... | collective-permute-start | bytes 393224 | tf_op jit(solution)/shard_map/ppermute | solution.py:32
  42.4 9.9 %copy-start.1 = (bf16[4096,128]{1,0:T(8,128)(2,1)S(1)}, bf16[4096,128]{1,0:T(8,128)(2,1)}, u32[]{:S(2)}) copy-start(bf16[4096,128]{1,0:T(8,128)(2,1)} %w_ref.3) | copy-start | bytes 3145732
  42.4 10.8 %collective-permute-start.19 = (bf16[2,256,128]{2,1,0:T(8,128)(2,1)S(1)}, bf16[2,256,128]{2,1,0:T(8,128)(2,1)S(1)}, u32[]{:S(2)}, u32[]{:S(2)}) collective-permute-start(bf16[2,256,128]{2,1,0:T(8,128)(2,1)S(1)} %constant_dynamic-update-slice_fusion.refs_0_), channel_id=1, source_target_pairs={{0,6},{2,4},{4,2},{6,0},{8,14},{10,12},{12,10},{14,8},{16,22},{18,... | collective-permute-start | bytes 393224 | tf_op jit(solution)/shard_map/ppermute | solution.py:32
  43.9 9.2 %collective-permute-start.18 = (bf16[2,256,128]{2,1,0:T(8,128)(2,1)S(1)}, bf16[2,256,128]{2,1,0:T(8,128)(2,1)S(1)}, u32[]{:S(2)}, u32[]{:S(2)}) collective-permute-start(bf16[2,256,128]{2,1,0:T(8,128)(2,1)S(1)} %constant_dynamic-update-slice_fusion.refs_0_), channel_id=1, source_target_pairs={{0,4},{2,6},{4,0},{6,2},{8,12},{10,14},{12,8},{14,10},{16,20},{18,... | collective-permute-start | bytes 393224 | tf_op jit(solution)/shard_map/ppermute | solution.py:32
  45.3 7.9 %collective-permute-start.17 = (bf16[2,256,128]{2,1,0:T(8,128)(2,1)S(1)}, bf16[2,256,128]{2,1,0:T(8,128)(2,1)S(1)}, u32[]{:S(2)}, u32[]{:S(2)}) collective-permute-start(bf16[2,256,128]{2,1,0:T(8,128)(2,1)S(1)} %constant_dynamic-update-slice_fusion.refs_0_), channel_id=1, source_target_pairs={{0,2},{2,0},{4,6},{6,4},{8,10},{10,8},{12,14},{14,12},{16,18},{18,... | collective-permute-start | bytes 393224 | tf_op jit(solution)/shard_map/ppermute | solution.py:32
  (4 other events, 13.2 us)

commit v9 on v8

--- a/solution.py
+++ b/solution.py
@@ -268,7 +268,9 @@
     sums.append(swap(total[1], "rep", PLANE))
 
     key_rows = turn(inv_width, raw_keys, cosine, signed)
-    sums, key_rows, x, scale, gain = after(sums, key_rows, x, scale, gain)
+    sums[: len(far)], x, scale = after(sums[: len(far)], x, scale)
+    blocks = [weight_rows(0)]
+    sums, key_rows, blocks, x, scale, gain = after(sums, key_rows, blocks, x, scale, gain)
     mean_weights = sum(sums, total[0]) / replicas
     change = anchor - mean_weights
     new_momentum = momentum_rate * momentum + change
@@ -279,16 +281,16 @@
     column = [swap(outgoing, "rep", k) for k in far_side]
     near = jnp.concatenate([outgoing, mate])
     near = [near] + [swap(near, "rep", p) for p in mates]
-    blocks = [weight_rows(0)]
-    column, blocks, x = after(column, blocks, x)
+    blocks += [weight_rows(k) for k in range(1, cores)]
+    weight_grad = place_blocks(blocks)
+    column, near, weight_grad = after(column, near, weight_grad)
     rest = jnp.concatenate(column)
     rest = [rest] + [swap(rest, "rep", p) for p in mates]
-    near, x = after(near, x)
-    blocks += [weight_rows(k) for k in range(1, cores)]
-    weight_grad = place_blocks(blocks)
     merged = merge(w, near, [[k + p for k in near_side] for p in range(PLANE)])
-    key_rows, weight_grad, merged, *rest = after(key_rows, weight_grad, merged, *rest)
-    merged = merge(w, rest, [[k + p for k in far_side] for p in range(PLANE)], merged)
+    places = [[k + p for k in far_side] for p in range(PLANE)]
+    merged = merge(w, [rest[0], *rest[2:]], [places[0], *places[2:]], merged)
+    last, merged = after(rest[1], merged)
+    merged = merge(w, [last], places[1:2], merged)
     return (key_rows, weight_grad, merged, new_anchor, new_momentum)
 
 

time: 54.3 us -> 55.2 us (1.017)
  waiting for transfers between devices: 9.54 us -> 10.2 us
  Pallas kernels: 6.61 us -> 7.25 us
    pallas_call x2 -> x3, Pallas kernels: 1.8 us -> 2.44 us  [merge(): pl.pallas_call(functools.partial(merge_kernel, offsets), out_shape=jax.Sh...]
    ppermute x20, waiting for transfers between devices: 9.54 us -> 10.2 us  [swap(): return lax.ppermute(value, axis, [(i, i ^ offset) for i in range(size)])]
  transfers between devices with their start and end apart: 20 -> 20, of which waited for: 6 -> 9; matrix products, arithmetic and copies ran while one was open for 12% -> 12% of each run, Pallas kernels for 11% -> 12%
where the time goes in v9:
time: 55.2 us; the launch traced here: 55 us
  starting transfers between devices  25.2 us (46%)
  waiting for transfers between devices  10.2 us (18%)
  Pallas kernels  7.25 us (13%)
  matrix products  6.3 us (11%)
  local copies, waits for them, and re-layouts  4.32 us (8%)
  other arithmetic  0.93 us (2%)
  between operations  0.85 us (2%)
    ppermute x20, starting transfers between devices, swap(): return lax.ppermute(value, axis, [(i, i ^ offset) for i in range(size)])  25.2 us
    ppermute x20, waiting for transfers between devices, swap(): return lax.ppermute(value, axis, [(i, i ^ offset) for i in range(size)])  10.2 us
    unnamed x17, local copies, waits for them, and re-layouts  4.29 us
    dot_general x2, matrix products, weight_rows(): lax.dot_general(norm, raw_grad, (((0,), (0,)), ((), ())), preferred_eleme...  3.59 us
    dot_general x2, matrix products, key_part(): return jnp.dot(norm, halves[k], preferred_element_type=jnp.float32)  2.71 us
    pallas_call x3, Pallas kernels, merge(): pl.pallas_call(functools.partial(merge_kernel, offsets), out_shape=jax.Sh...  2.44 us
    pallas_call x2, Pallas kernels, squares_of(): pl.pallas_call(squares_kernel, out_shape=jax.ShapeDtypeStruct((1, rows),...  2.31 us
  transfers between devices with their start and end apart: 20, of which 9 were waited for; matrix products, arithmetic and copies ran while one was open for 12% of the time, Pallas kernels for 12%

profile of v9, /device:TPU:0, one launch (start us, length us, event | category | flops | bytes accessed | tf_op | source)
XLA Modules:
  0.0 55.0 jit_solution(7799629977830887783)
XLA Ops:
  1.2 1.2 %copy-done = bf16[4096,128]{1,0:T(8,128)(2,1)S(1)} copy-done((bf16[4096,128]{1,0:T(8,128)(2,1)S(1)}, bf16[4096,128]{1,0:T(8,128)(2,1)}, u32[]{:S(2)}) %copy-start) | copy-done | bytes 1048600
  2.5 2.6 %collective-permute-start = (bf16[2,256,128]{2,1,0:T(8,128)(2,1)S(1)}, bf16[2,256,128]{2,1,0:T(8,128)(2,1)S(1)}, u32[]{:S(2)}, u32[]{:S(2)}) collective-permute-start(bf16[2,256,128]{2,1,0:T(8,128)(2,1)S(1)} %get-tuple-element.81), channel_id=1, source_target_pairs={{0,2},{2,0},{4,6},{6,4},{8,10},{10,8},{12,14},{14,12},{16,18},{18,... | collective-permute-start | bytes 393224 | tf_op jit(solution)/shard_map/ppermute | solution.py:32
  5.1 1.5 %collective-permute-start.1 = (bf16[2,256,128]{2,1,0:T(8,128)(2,1)S(1)}, bf16[2,256,128]{2,1,0:T(8,128)(2,1)S(1)}, u32[]{:S(2)}, u32[]{:S(2)}) collective-permute-start(bf16[2,256,128]{2,1,0:T(8,128)(2,1)S(1)} %get-tuple-element.82), channel_id=1, source_target_pairs={{0,4},{2,6},{4,0},{6,2},{8,12},{10,14},{12,8},{14,10},{16,20},{18,... | collective-permute-start | bytes 393224 | tf_op jit(solution)/shard_map/ppermute | solution.py:32
  6.6 2.2 %copy-done.2 = bf16[1024,2048]{1,0:T(8,128)(2,1)S(1)} copy-done((bf16[1024,2048]{1,0:T(8,128)(2,1)S(1)}, bf16[1024,2048]{1,0:T(8,128)(2,1)}, u32[]{:S(2)}) %copy-start.2) | copy-done | bytes 4194328
  8.8 1.1 %shard_map.102 = f32[1,1024]{1,0:T(1,128)S(1)} custom-call(bf16[1024,2048]{1,0:T(8,128)(2,1)S(1)} %copy-done.2), custom_call_target="tpu_custom_call" | custom-call | flops 1 | bytes 1 | tf_op jit(solution)/shard_map/pallas_call | solution.py:119
  10.4 1.2 %shard_map.103 = f32[1,1024]{1,0:T(1,128)S(1)} custom-call(bf16[1024,2048]{1,0:T(8,128)(2,1)S(1)} %collective-permute-done.3.x_ref), custom_call_target="tpu_custom_call" | custom-call | flops 1 | bytes 1 | tf_op jit(solution)/shard_map/pallas_call | solution.py:119
  11.6 1.9 %collective-permute-done.1 = bf16[2,256,128]{2,1,0:T(8,128)(2,1)S(1)} collective-permute-done((bf16[2,256,128]{2,1,0:T(8,128)(2,1)S(1)}, bf16[2,256,128]{2,1,0:T(8,128)(2,1)S(1)}, u32[]{:S(2)}, u32[]{:S(2)}) %collective-permute-start.1) | collective-permute-done | bytes 131104 | tf_op jit(solution)/shard_map/ppermute | solution.py:32
  13.6 1.6 %collective-permute-start.4 = (f32[1,256,128]{2,1,0:T(8,128)S(1)}, f32[1,256,128]{2,1,0:T(8,128)S(1)}, u32[]{:S(2)}, u32[]{:S(2)}) collective-permute-start(f32[1,256,128]{2,1,0:T(8,128)S(1)} %slice.17), channel_id=1, source_target_pairs={{0,8},{2,10},{4,12},{6,14},{8,0},{10,2},{12,4},{14,6},{16,24},{18,... | collective-permute-start | bytes 393224 | tf_op jit(solution)/shard_map/ppermute | solution.py:32
  15.2 1.2 %collective-permute-start.6 = (bf16[2,256,128]{2,1,0:T(8,128)(2,1)S(1)}, bf16[2,256,128]{2,1,0:T(8,128)(2,1)S(1)}, u32[]{:S(2)}, u32[]{:S(2)}) collective-permute-start(bf16[2,256,128]{2,1,0:T(8,128)(2,1)S(1)} %get-tuple-element.95), channel_id=1, source_target_pairs={{0,2},{2,0},{4,6},{6,4},{8,10},{10,8},{12,14},{14,12},{16,18},{18,... | collective-permute-start | bytes 393224 | tf_op jit(solution)/shard_map/ppermute | solution.py:32
  17.3 1.4 %collective-permute-start.8 = (bf16[2,256,128]{2,1,0:T(8,128)(2,1)S(1)}, bf16[2,256,128]{2,1,0:T(8,128)(2,1)S(1)}, u32[]{:S(2)}, u32[]{:S(2)}) collective-permute-start(bf16[2,256,128]{2,1,0:T(8,128)(2,1)S(1)} %get-tuple-element.97), channel_id=1, source_target_pairs={{0,6},{2,4},{4,2},{6,0},{8,14},{10,12},{12,10},{14,8},{16,22},{18,... | collective-permute-start | bytes 393224 | tf_op jit(solution)/shard_map/ppermute | solution.py:32
  18.9 2.7 %collective-permute-start.5 = (f32[256,128]{1,0:T(8,128)S(1)}, f32[256,128]{1,0:T(8,128)S(1)}, u32[]{:S(2)}, u32[]{:S(2)}) collective-permute-start(f32[256,128]{1,0:T(8,128)S(1)} %fusion.21), channel_id=1, source_target_pairs={{0,16},{2,18},{4,20},{6,22},{8,24},{10,26},{12,28},{14,30},{16,0},... | collective-permute-start | bytes 393224 | tf_op jit(solution)/shard_map/ppermute | solution.py:32
  21.5 1.3 %fusion.1 = f32[1024,128]{1,0:T(8,128)S(1)} fusion(bf16[2048,128]{1,0:T(8,128)(2,1)S(1)} %get-tuple-element.103, bf16[1024,2048]{1,0:T(8,128)(2,1)S(1)} %collective-permute-done.3.x_ref, f32[2048]{0:T(1024)S(1)} %convert_element_type.75, f32[1024]{0:T(1024)S(1)} %add_rsqrt_fusion), kind=kOutput, calls=%fused_computation.5 | convolution fusion | flops 545259520 | bytes 5255168 | tf_op jit(solution)/shard_map/dot_general | solution.py:255
  23.7 1.4 %fusion.16.raw_ref = f32[1024,128]{1,0:T(8,128)S(1)} fusion(f32[1024,128]{1,0:T(8,128)S(1)} %fusion.1, bf16[2048,128]{1,0:T(8,128)(2,1)S(1)} %get-tuple-element.101, bf16[1024,2048]{1,0:T(8,128)(2,1)S(1)} %copy-done.3, f32[2048]{0:T(1024)S(1)} %convert_element_type.72, f32[1024]{0:T(1024)S(1)} %add_rsqrt_fusion), kind=kOutput, calls=%fused_computation.20 | convolution fusion | flops 545390592 | bytes 5779456 | tf_op jit(solution)/shard_map/dot_general | solution.py:255
  25.2 1.5 %collective-permute-start.10 = (f32[256,128]{1,0:T(8,128)S(1)}, f32[256,128]{1,0:T(8,128)S(1)}, u32[]{:S(2)}, u32[]{:S(2)}) collective-permute-start(f32[256,128]{1,0:T(8,128)S(1)} %slice_bitcast_fusion.1), channel_id=1, source_target_pairs={{0,8},{2,10},{4,12},{6,14},{8,0},{10,2},{12,4},{14,6},{16,24},{18,... | collective-permute-start | bytes 393224 | tf_op jit(solution)/shard_map/ppermute | solution.py:32
  28.5 1.8 %fusion.14.refs_0_ = bf16[2048,128]{1,0:T(8,128)(2,1)S(1)} fusion(bf16[1024,128]{1,0:T(8,128)(2,1)S(1)} %get-tuple-element.116, bf16[1024,2048]{1,0:T(8,128)(2,1)S(1)} %copy-done.3, f32[1024]{0:T(1024)S(1)} %add_rsqrt_fusion, f32[2048]{0:T(1024)S(1)} %convert_element_type.72), kind=kOutput, calls=%fused_computation.18 | convolution fusion | flops 545783808 | bytes 4993024 | tf_op jit(solution)/shard_map/dot_general | solution.py:259
  33.1 2.5 %collective-permute-start.12 = (bf16[1,256,128]{2,1,0:T(8,128)(2,1)S(1)}, bf16[1,256,128]{2,1,0:T(8,128)(2,1)S(1)}, u32[]{:S(2)}, u32[]{:S(2)}) collective-permute-start(bf16[1,256,128]{2,1,0:T(8,128)(2,1)S(1)} %get-tuple-element.135), channel_id=1, source_target_pairs={{0,24},{2,26},{4,28},{6,30},{8,16},{10,18},{12,20},{14,22},{16,8},... | collective-permute-start | bytes 196616 | tf_op jit(solution)/shard_map/ppermute | solution.py:32
  36.3 1.6 %collective-permute-start.16 = (bf16[2,256,128]{2,1,0:T(8,128)(2,1)S(1)}, bf16[2,256,128]{2,1,0:T(8,128)(2,1)S(1)}, u32[]{:S(2)}, u32[]{:S(2)}) collective-permute-start(bf16[2,256,128]{2,1,0:T(8,128)(2,1)S(1)} %pad_maximum_fusion.refs_0_), channel_id=1, source_target_pairs={{0,6},{2,4},{4,2},{6,0},{8,14},{10,12},{12,10},{14,8},{16,22},{18,... | collective-permute-start | bytes 393224 | tf_op jit(solution)/shard_map/ppermute | solution.py:32
  37.9 1.2 %collective-permute-start.15 = (bf16[2,256,128]{2,1,0:T(8,128)(2,1)S(1)}, bf16[2,256,128]{2,1,0:T(8,128)(2,1)S(1)}, u32[]{:S(2)}, u32[]{:S(2)}) collective-permute-start(bf16[2,256,128]{2,1,0:T(8,128)(2,1)S(1)} %pad_maximum_fusion.refs_0_), channel_id=1, source_target_pairs={{0,4},{2,6},{4,0},{6,2},{8,12},{10,14},{12,8},{14,10},{16,20},{18,... | collective-permute-start | bytes 393224 | tf_op jit(solution)/shard_map/ppermute | solution.py:32
  39.9 1.8 %fusion.15.refs_1_ = bf16[2048,128]{1,0:T(8,128)(2,1)S(1)} fusion(bf16[1024,128]{1,0:T(8,128)(2,1)S(1)} %get-tuple-element.116, bf16[1024,2048]{1,0:T(8,128)(2,1)S(1)} %collective-permute-done.3.x_ref, f32[2048]{0:T(1024)S(1)} %convert_element_type.86, f32[1024]{0:T(1024)S(1)} %add_rsqrt_fusion), kind=kOutput, calls=%fused_computation.19 | convolution fusion | flops 545783808 | bytes 4993024 | tf_op jit(solution)/shard_map/dot_general | solution.py:259
  43.5 1.3 %collective-permute-done.15.refs_2_ = bf16[2,256,128]{2,1,0:T(8,128)(2,1)S(1)} collective-permute-done((bf16[2,256,128]{2,1,0:T(8,128)(2,1)S(1)}, bf16[2,256,128]{2,1,0:T(8,128)(2,1)S(1)}, u32[]{:S(2)}, u32[]{:S(2)}) %collective-permute-start.15) | collective-permute-done | bytes 131104 | tf_op jit(solution)/shard_map/ppermute | solution.py:32
  44.8 1.6 %collective-permute-start.19 = (bf16[2,256,128]{2,1,0:T(8,128)(2,1)S(1)}, bf16[2,256,128]{2,1,0:T(8,128)(2,1)S(1)}, u32[]{:S(2)}, u32[]{:S(2)}) collective-permute-start(bf16[2,256,128]{2,1,0:T(8,128)(2,1)S(1)} %constant_dynamic-update-slice_fusion.refs_0_), channel_id=1, source_target_pairs={{0,6},{2,4},{4,2},{6,0},{8,14},{10,12},{12,10},{14,8},{16,22},{18,... | collective-permute-start | bytes 393224 | tf_op jit(solution)/shard_map/ppermute | solution.py:32
  46.4 1.2 %collective-permute-start.18 = (bf16[2,256,128]{2,1,0:T(8,128)(2,1)S(1)}, bf16[2,256,128]{2,1,0:T(8,128)(2,1)S(1)}, u32[]{:S(2)}, u32[]{:S(2)}) collective-permute-start(bf16[2,256,128]{2,1,0:T(8,128)(2,1)S(1)} %constant_dynamic-update-slice_fusion.refs_0_), channel_id=1, source_target_pairs={{0,4},{2,6},{4,0},{6,2},{8,12},{10,14},{12,8},{14,10},{16,20},{18,... | collective-permute-start | bytes 393224 | tf_op jit(solution)/shard_map/ppermute | solution.py:32
  49.3 2.8 %collective-permute-done.19.refs_2_ = bf16[2,256,128]{2,1,0:T(8,128)(2,1)S(1)} collective-permute-done((bf16[2,256,128]{2,1,0:T(8,128)(2,1)S(1)}, bf16[2,256,128]{2,1,0:T(8,128)(2,1)S(1)}, u32[]{:S(2)}, u32[]{:S(2)}) %collective-permute-start.19) | collective-permute-done | bytes 131104 | tf_op jit(solution)/shard_map/ppermute | solution.py:32
  52.2 1.3 %collective-permute-done.18.refs_1_ = bf16[2,256,128]{2,1,0:T(8,128)(2,1)S(1)} collective-permute-done((bf16[2,256,128]{2,1,0:T(8,128)(2,1)S(1)}, bf16[2,256,128]{2,1,0:T(8,128)(2,1)S(1)}, u32[]{:S(2)}, u32[]{:S(2)}) %collective-permute-start.18) | collective-permute-done | bytes 131104 | tf_op jit(solution)/shard_map/ppermute | solution.py:32
  (59 shorter events, 14.2 us)
Async XLA Ops:
  0.6 9.7 %collective-permute-start.3 = (bf16[1024,2048]{1,0:T(8,128)(2,1)}, bf16[1024,2048]{1,0:T(8,128)(2,1)S(1)}, u32[]{:S(2)}, u32[]{:S(2)}) collective-permute-start(bf16[1024,2048]{1,0:T(8,128)(2,1)} %x_ref), channel_id=1, source_target_pairs={{0,1},{1,0},{2,3},{3,2},{4,5},{5,4},{6,7},{7,6},{8,9},{9,8},{10,11... | collective-permute-start | bytes 12582920 | tf_op jit(solution)/shard_map/ppermute | solution.py:32
  2.4 7.6 %copy-start.4 = (bf16[1024,128]{1,0:T(8,128)(2,1)S(1)}, bf16[1024,128]{1,0:T(8,128)(2,1)}, u32[]{:S(2)}) copy-start(bf16[1024,128]{1,0:T(8,128)(2,1)} %grad_ref) | copy-start | bytes 786436
  2.5 9.1 %collective-permute-start = (bf16[2,256,128]{2,1,0:T(8,128)(2,1)S(1)}, bf16[2,256,128]{2,1,0:T(8,128)(2,1)S(1)}, u32[]{:S(2)}, u32[]{:S(2)}) collective-permute-start(bf16[2,256,128]{2,1,0:T(8,128)(2,1)S(1)} %get-tuple-element.81), channel_id=1, source_target_pairs={{0,2},{2,0},{4,6},{6,4},{8,10},{10,8},{12,14},{14,12},{16,18},{18,... | collective-permute-start | bytes 393224 | tf_op jit(solution)/shard_map/ppermute | solution.py:32
  5.1 8.4 %collective-permute-start.1 = (bf16[2,256,128]{2,1,0:T(8,128)(2,1)S(1)}, bf16[2,256,128]{2,1,0:T(8,128)(2,1)S(1)}, u32[]{:S(2)}, u32[]{:S(2)}) collective-permute-start(bf16[2,256,128]{2,1,0:T(8,128)(2,1)S(1)} %get-tuple-element.82), channel_id=1, source_target_pairs={{0,4},{2,6},{4,0},{6,2},{8,12},{10,14},{12,8},{14,10},{16,20},{18,... | collective-permute-start | bytes 393224 | tf_op jit(solution)/shard_map/ppermute | solution.py:32
  6.6 6.9 %collective-permute-start.2 = (bf16[2,256,128]{2,1,0:T(8,128)(2,1)S(1)}, bf16[2,256,128]{2,1,0:T(8,128)(2,1)S(1)}, u32[]{:S(2)}, u32[]{:S(2)}) collective-permute-start(bf16[2,256,128]{2,1,0:T(8,128)(2,1)S(1)} %get-tuple-element.83), channel_id=1, source_target_pairs={{0,6},{2,4},{4,2},{6,0},{8,14},{10,12},{12,10},{14,8},{16,22},{18,... | collective-permute-start | bytes 393224 | tf_op jit(solution)/shard_map/ppermute | solution.py:32
  8.8 9.9 %copy-start.7 = (bf16[2048]{0:T(1024)(128)(2,1)S(1)}, bf16[2048]{0:T(1024)(128)(2,1)}, u32[]{:S(2)}) copy-start(bf16[2048]{0:T(1024)(128)(2,1)} %param.7) | copy-start | bytes 12292
  13.6 5.1 %collective-permute-start.4 = (f32[1,256,128]{2,1,0:T(8,128)S(1)}, f32[1,256,128]{2,1,0:T(8,128)S(1)}, u32[]{:S(2)}, u32[]{:S(2)}) collective-permute-start(f32[1,256,128]{2,1,0:T(8,128)S(1)} %slice.17), channel_id=1, source_target_pairs={{0,8},{2,10},{4,12},{6,14},{8,0},{10,2},{12,4},{14,6},{16,24},{18,... | collective-permute-start | bytes 393224 | tf_op jit(solution)/shard_map/ppermute | solution.py:32
  15.2 9.9 %collective-permute-start.6 = (bf16[2,256,128]{2,1,0:T(8,128)(2,1)S(1)}, bf16[2,256,128]{2,1,0:T(8,128)(2,1)S(1)}, u32[]{:S(2)}, u32[]{:S(2)}) collective-permute-start(bf16[2,256,128]{2,1,0:T(8,128)(2,1)S(1)} %get-tuple-element.95), channel_id=1, source_target_pairs={{0,2},{2,0},{4,6},{6,4},{8,10},{10,8},{12,14},{14,12},{16,18},{18,... | collective-permute-start | bytes 393224 | tf_op jit(solution)/shard_map/ppermute | solution.py:32
  16.5 8.6 %collective-permute-start.7 = (bf16[2,256,128]{2,1,0:T(8,128)(2,1)S(1)}, bf16[2,256,128]{2,1,0:T(8,128)(2,1)S(1)}, u32[]{:S(2)}, u32[]{:S(2)}) collective-permute-start(bf16[2,256,128]{2,1,0:T(8,128)(2,1)S(1)} %get-tuple-element.96), channel_id=1, source_target_pairs={{0,4},{2,6},{4,0},{6,2},{8,12},{10,14},{12,8},{14,10},{16,20},{18,... | collective-permute-start | bytes 393224 | tf_op jit(solution)/shard_map/ppermute | solution.py:32
  17.3 7.8 %collective-permute-start.8 = (bf16[2,256,128]{2,1,0:T(8,128)(2,1)S(1)}, bf16[2,256,128]{2,1,0:T(8,128)(2,1)S(1)}, u32[]{:S(2)}, u32[]{:S(2)}) collective-permute-start(bf16[2,256,128]{2,1,0:T(8,128)(2,1)S(1)} %get-tuple-element.97), channel_id=1, source_target_pairs={{0,6},{2,4},{4,2},{6,0},{8,14},{10,12},{12,10},{14,8},{16,22},{18,... | collective-permute-start | bytes 393224 | tf_op jit(solution)/shard_map/ppermute | solution.py:32
  18.8 2.8 %collective-permute-start.9 = (bf16[2048]{0:T(1024)(128)(2,1)S(1)}, bf16[2048]{0:T(1024)(128)(2,1)S(1)}, u32[]{:S(2)}, u32[]{:S(2)}) collective-permute-start(bf16[2048]{0:T(1024)(128)(2,1)S(1)} %copy-done.7), channel_id=1, source_target_pairs={{0,1},{1,0},{2,3},{3,2},{4,5},{5,4},{6,7},{7,6},{8,9},{9,8},{10,11... | collective-permute-start | bytes 12296 | tf_op jit(solution)/shard_map/ppermute | solution.py:32
  18.9 9.7 %collective-permute-start.5 = (f32[256,128]{1,0:T(8,128)S(1)}, f32[256,128]{1,0:T(8,128)S(1)}, u32[]{:S(2)}, u32[]{:S(2)}) collective-permute-start(f32[256,128]{1,0:T(8,128)S(1)} %fusion.21), channel_id=1, source_target_pairs={{0,16},{2,18},{4,20},{6,22},{8,24},{10,26},{12,28},{14,30},{16,0},... | collective-permute-start | bytes 393224 | tf_op jit(solution)/shard_map/ppermute | solution.py:32
  25.2 6.1 %collective-permute-start.10 = (f32[256,128]{1,0:T(8,128)S(1)}, f32[256,128]{1,0:T(8,128)S(1)}, u32[]{:S(2)}, u32[]{:S(2)}) collective-permute-start(f32[256,128]{1,0:T(8,128)S(1)} %slice_bitcast_fusion.1), channel_id=1, source_target_pairs={{0,8},{2,10},{4,12},{6,14},{8,0},{10,2},{12,4},{14,6},{16,24},{18,... | collective-permute-start | bytes 393224 | tf_op jit(solution)/shard_map/ppermute | solution.py:32
  28.5 2.8 %copy-start.6 = (f32[256,128]{1,0:T(8,128)S(1)}, f32[256,128]{1,0:T(8,128)}, u32[]{:S(2)}) copy-start(f32[256,128]{1,0:T(8,128)} %param.10) | copy-start | bytes 393220
  32.0 4.3 %collective-permute-start.13 = (bf16[1,256,128]{2,1,0:T(8,128)(2,1)S(1)}, bf16[1,256,128]{2,1,0:T(8,128)(2,1)S(1)}, u32[]{:S(2)}, u32[]{:S(2)}) collective-permute-start(bf16[1,256,128]{2,1,0:T(8,128)(2,1)S(1)} %get-tuple-element.135), channel_id=1, source_target_pairs={{0,8},{2,10},{4,12},{6,14},{8,0},{10,2},{12,4},{14,6},{16,24},{18,... | collective-permute-start | bytes 196616 | tf_op jit(solution)/shard_map/ppermute | solution.py:32
  33.1 9.7 %collective-permute-start.12 = (bf16[1,256,128]{2,1,0:T(8,128)(2,1)S(1)}, bf16[1,256,128]{2,1,0:T(8,128)(2,1)S(1)}, u32[]{:S(2)}, u32[]{:S(2)}) collective-permute-start(bf16[1,256,128]{2,1,0:T(8,128)(2,1)S(1)} %get-tuple-element.135), channel_id=1, source_target_pairs={{0,24},{2,26},{4,28},{6,30},{8,16},{10,18},{12,20},{14,22},{16,8},... | collective-permute-start | bytes 196616 | tf_op jit(solution)/shard_map/ppermute | solution.py:32
  35.5 7.2 %collective-permute-start.11 = (bf16[1,256,128]{2,1,0:T(8,128)(2,1)S(1)}, bf16[1,256,128]{2,1,0:T(8,128)(2,1)S(1)}, u32[]{:S(2)}, u32[]{:S(2)}) collective-permute-start(bf16[1,256,128]{2,1,0:T(8,128)(2,1)S(1)} %get-tuple-element.135), channel_id=1, source_target_pairs={{0,16},{2,18},{4,20},{6,22},{8,24},{10,26},{12,28},{14,30},{16,0},... | collective-permute-start | bytes 196616 | tf_op jit(solution)/shard_map/ppermute | solution.py:32
  36.3 7.2 %collective-permute-start.16 = (bf16[2,256,128]{2,1,0:T(8,128)(2,1)S(1)}, bf16[2,256,128]{2,1,0:T(8,128)(2,1)S(1)}, u32[]{:S(2)}, u32[]{:S(2)}) collective-permute-start(bf16[2,256,128]{2,1,0:T(8,128)(2,1)S(1)} %pad_maximum_fusion.refs_0_), channel_id=1, source_target_pairs={{0,6},{2,4},{4,2},{6,0},{8,14},{10,12},{12,10},{14,8},{16,22},{18,... | collective-permute-start | bytes 393224 | tf_op jit(solution)/shard_map/ppermute | solution.py:32
  37.9 6.9 %collective-permute-start.15 = (bf16[2,256,128]{2,1,0:T(8,128)(2,1)S(1)}, bf16[2,256,128]{2,1,0:T(8,128)(2,1)S(1)}, u32[]{:S(2)}, u32[]{:S(2)}) collective-permute-start(bf16[2,256,128]{2,1,0:T(8,128)(2,1)S(1)} %pad_maximum_fusion.refs_0_), channel_id=1, source_target_pairs={{0,4},{2,6},{4,0},{6,2},{8,12},{10,14},{12,8},{14,10},{16,20},{18,... | collective-permute-start | bytes 393224 | tf_op jit(solution)/shard_map/ppermute | solution.py:32
  39.1 5.7 %collective-permute-start.14 = (bf16[2,256,128]{2,1,0:T(8,128)(2,1)S(1)}, bf16[2,256,128]{2,1,0:T(8,128)(2,1)S(1)}, u32[]{:S(2)}, u32[]{:S(2)}) collective-permute-start(bf16[2,256,128]{2,1,0:T(8,128)(2,1)S(1)} %pad_maximum_fusion.refs_0_), channel_id=1, source_target_pairs={{0,2},{2,0},{4,6},{6,4},{8,10},{10,8},{12,14},{14,12},{16,18},{18,... | collective-permute-start | bytes 393224 | tf_op jit(solution)/shard_map/ppermute | solution.py:32
  39.9 8.5 %copy-start.1 = (bf16[4096,128]{1,0:T(8,128)(2,1)S(1)}, bf16[4096,128]{1,0:T(8,128)(2,1)}, u32[]{:S(2)}) copy-start(bf16[4096,128]{1,0:T(8,128)(2,1)} %w_ref.4) | copy-start | bytes 3145732
  44.8 7.3 %collective-permute-start.19 = (bf16[2,256,128]{2,1,0:T(8,128)(2,1)S(1)}, bf16[2,256,128]{2,1,0:T(8,128)(2,1)S(1)}, u32[]{:S(2)}, u32[]{:S(2)}) collective-permute-start(bf16[2,256,128]{2,1,0:T(8,128)(2,1)S(1)} %constant_dynamic-update-slice_fusion.refs_0_), channel_id=1, source_target_pairs={{0,6},{2,4},{4,2},{6,0},{8,14},{10,12},{12,10},{14,8},{16,22},{18,... | collective-permute-start | bytes 393224 | tf_op jit(solution)/shard_map/ppermute | solution.py:32
  46.4 7.0 %collective-permute-start.18 = (bf16[2,256,128]{2,1,0:T(8,128)(2,1)S(1)}, bf16[2,256,128]{2,1,0:T(8,128)(2,1)S(1)}, u32[]{:S(2)}, u32[]{:S(2)}) collective-permute-start(bf16[2,256,128]{2,1,0:T(8,128)(2,1)S(1)} %constant_dynamic-update-slice_fusion.refs_0_), channel_id=1, source_target_pairs={{0,4},{2,6},{4,0},{6,2},{8,12},{10,14},{12,8},{14,10},{16,20},{18,... | collective-permute-start | bytes 393224 | tf_op jit(solution)/shard_map/ppermute | solution.py:32
  47.6 6.7 %collective-permute-start.17 = (bf16[2,256,128]{2,1,0:T(8,128)(2,1)S(1)}, bf16[2,256,128]{2,1,0:T(8,128)(2,1)S(1)}, u32[]{:S(2)}, u32[]{:S(2)}) collective-permute-start(bf16[2,256,128]{2,1,0:T(8,128)(2,1)S(1)} %constant_dynamic-update-slice_fusion.refs_0_), channel_id=1, source_target_pairs={{0,2},{2,0},{4,6},{6,4},{8,10},{10,8},{12,14},{14,12},{16,18},{18,... | collective-permute-start | bytes 393224 | tf_op jit(solution)/shard_map/ppermute | solution.py:32
  (4 other events, 8.4 us)

commit v10 on v9

--- a/solution.py
+++ b/solution.py
@@ -43,18 +43,17 @@
 def pick_kernel(groups, w_ref, *out_refs):
     me, core = lax.axis_index("rep"), lax.axis_index("tp")
     rows = out_refs[0].shape[1]
-    count = len(groups) * PLANE
-    for out, (offsets, p) in zip(out_refs, [(g, p) for g in groups for p in range(PLANE)]):
+    for offsets, out in zip(groups, out_refs):
         for i, k in enumerate(offsets):
-            out[i] = w_ref[rows_at(me ^ (k + p), rows), :]
-    for k, out in enumerate(out_refs[count:]):
+            out[i] = w_ref[rows_at(me ^ k, rows), :]
+    for k, out in enumerate(out_refs[len(groups) :]):
         out[...] = w_ref[rows_at(core ^ k, out.shape[0]), :]
 
 
 def pick(local_weights, rows, groups):
     cores = lax.axis_size("tp")
     kind = local_weights.dtype
-    shapes = [jax.ShapeDtypeStruct((len(g), rows, HD), kind) for g in groups for _ in range(PLANE)]
+    shapes = [jax.ShapeDtypeStruct((len(g), rows, HD), kind) for g in groups]
     shapes += [jax.ShapeDtypeStruct((local_weights.shape[0] // cores, HD), kind)] * cores
     out = pl.pallas_call(
         functools.partial(pick_kernel, groups),
@@ -64,8 +63,7 @@
         compiler_params=PARAMS,
         cost_estimate=LIGHT,
     )(local_weights)
-    count = len(groups) * PLANE
-    return [out[i : i + PLANE] for i in range(0, count, PLANE)], out[count:]
+    return out[: len(groups)], out[len(groups) :]
 
 
 def prepare_kernel(grad_ref, cos_ref, sin_ref, out_ref):
@@ -222,6 +220,7 @@
     far = list(range(PAIR, replicas, PAIR))
     far_side = far + [k + PLANE for k in far]
     near_side = [0, PLANE]
+
     mates = (1, 2, 3)
 
     def sum_plane(own, parts):
@@ -230,11 +229,14 @@
             total = total + block.astype(jnp.float32)
         return total
 
+    def shifted(side, *steps):
+        return [k + step for step in steps for k in side]
+
     x = [swap(tokens, "tp", k) for k in range(cores)]
-    (first, second), halves = pick(local_weights, anchor.shape[0], [far_side, near_side])
-    first, second, halves, w, own, key_grad = after(
-        first, second, halves, local_weights, tokens, key_grad
-    )
+    groups = [shifted(side, p) for side in (far_side, near_side) for p in range(PLANE)]
+    picked, halves = pick(local_weights, anchor.shape[0], groups)
+    picked, halves, w, own, key_grad = after(picked, halves, local_weights, tokens, key_grad)
+    first, second = picked[:PLANE], picked[PLANE:]
     x[0] = own
     first_in = [swap(first[p], "rep", p) for p in mates]
     second_in = [swap(second[p], "rep", p) for p in mates]
@@ -280,17 +282,23 @@
     mate = swap(outgoing, "rep", PLANE)
     column = [swap(outgoing, "rep", k) for k in far_side]
     near = jnp.concatenate([outgoing, mate])
-    near = [near] + [swap(near, "rep", p) for p in mates]
+    near_in = swap(near, "rep", 2)
+    column = jnp.concatenate(column)
+    near, near_in, column = after(near, near_in, column)
+    column_in = swap(column, "rep", 1)
+    near = jnp.concatenate([near, near_in])
+    near_in = swap(near, "rep", 1)
+    column, column_in, x = after(column, column_in, x)
+    column = jnp.concatenate([column, column_in])
+    column_in = swap(column, "rep", 2)
     blocks += [weight_rows(k) for k in range(1, cores)]
     weight_grad = place_blocks(blocks)
-    column, near, weight_grad = after(column, near, weight_grad)
-    rest = jnp.concatenate(column)
-    rest = [rest] + [swap(rest, "rep", p) for p in mates]
-    merged = merge(w, near, [[k + p for k in near_side] for p in range(PLANE)])
-    places = [[k + p for k in far_side] for p in range(PLANE)]
-    merged = merge(w, [rest[0], *rest[2:]], [places[0], *places[2:]], merged)
-    last, merged = after(rest[1], merged)
-    merged = merge(w, [last], places[1:2], merged)
+    here = [shifted(near_side, 0, 2), shifted(far_side, 0, 1)]
+    merged = merge(w, [near, column], here)
+    weight_grad, merged, column_in = after(weight_grad, merged, column_in)
+    merged = merge(w, [column_in], [shifted(far_side, 2, 3)], merged)
+    near_in, merged = after(near_in, merged)
+    merged = merge(w, [near_in], [shifted(near_side, 1, 3)], merged)
     return (key_rows, weight_grad, merged, new_anchor, new_momentum)
 
 

time: 55.2 us -> 57.1 us (1.034)
  waiting for transfers between devices: 10.2 us -> 13.7 us
  starting transfers between devices: 25.2 us -> 23.4 us
    ppermute x20 -> x18, waiting for transfers between devices: 10.2 us -> 13.7 us  [swap(): return lax.ppermute(value, axis, [(i, i ^ offset) for i in range(size)])]
    ppermute x20 -> x18, starting transfers between devices: 25.2 us -> 23.4 us  [swap(): return lax.ppermute(value, axis, [(i, i ^ offset) for i in range(size)])]
    unnamed x17 -> x18, local copies, waits for them, and re-layouts: 4.29 us -> 4.3 us
  transfers between devices with their start and end apart: 20 -> 18, of which waited for: 9 -> 8; matrix products, arithmetic and copies ran while one was open for 12% -> 11% of each run, Pallas kernels for 12% -> 11%
where the time goes in v10:
time: 57.1 us; the launch traced here: 56.8 us
  starting transfers between devices  23.4 us (41%)
  waiting for transfers between devices  13.7 us (24%)
  Pallas kernels  7.25 us (13%)
  matrix products  6.29 us (11%)
  local copies, waits for them, and re-layouts  4.37 us (8%)
  other arithmetic  0.94 us (2%)
  between operations  0.87 us (2%)
    ppermute x18, starting transfers between devices, swap(): return lax.ppermute(value, axis, [(i, i ^ offset) for i in range(size)])  23.4 us
    ppermute x18, waiting for transfers between devices, swap(): return lax.ppermute(value, axis, [(i, i ^ offset) for i in range(size)])  13.7 us
    unnamed x18, local copies, waits for them, and re-layouts  4.3 us
    dot_general x2, matrix products, weight_rows(): lax.dot_general(norm, raw_grad, (((0,), (0,)), ((), ())), preferred_eleme...  3.59 us
    dot_general x2, matrix products, key_part(): return jnp.dot(norm, halves[k], preferred_element_type=jnp.float32)  2.71 us
    pallas_call x3, Pallas kernels, merge(): pl.pallas_call(functools.partial(merge_kernel, offsets), out_shape=jax.Sh...  2.44 us
    pallas_call x2, Pallas kernels, squares_of(): pl.pallas_call(squares_kernel, out_shape=jax.ShapeDtypeStruct((1, rows),...  2.31 us
  transfers between devices with their start and end apart: 18, of which 8 were waited for; matrix products, arithmetic and copies ran while one was open for 11% of the time, Pallas kernels for 11%

profile of v10, /device:TPU:0, one launch (start us, length us, event | category | flops | bytes accessed | tf_op | source)
XLA Modules:
  0.0 56.8 jit_solution(17905134867832926455)
XLA Ops:
  1.2 1.2 %copy-done = bf16[4096,128]{1,0:T(8,128)(2,1)S(1)} copy-done((bf16[4096,128]{1,0:T(8,128)(2,1)S(1)}, bf16[4096,128]{1,0:T(8,128)(2,1)}, u32[]{:S(2)}) %copy-start) | copy-done | bytes 1048600
  2.5 2.6 %collective-permute-start = (bf16[2,256,128]{2,1,0:T(8,128)(2,1)S(1)}, bf16[2,256,128]{2,1,0:T(8,128)(2,1)S(1)}, u32[]{:S(2)}, u32[]{:S(2)}) collective-permute-start(bf16[2,256,128]{2,1,0:T(8,128)(2,1)S(1)} %get-tuple-element.83), channel_id=1, source_target_pairs={{0,2},{2,0},{4,6},{6,4},{8,10},{10,8},{12,14},{14,12},{16,18},{18,... | collective-permute-start | bytes 393224 | tf_op jit(solution)/shard_map/ppermute | solution.py:32
  5.1 1.5 %collective-permute-start.1 = (bf16[2,256,128]{2,1,0:T(8,128)(2,1)S(1)}, bf16[2,256,128]{2,1,0:T(8,128)(2,1)S(1)}, u32[]{:S(2)}, u32[]{:S(2)}) collective-permute-start(bf16[2,256,128]{2,1,0:T(8,128)(2,1)S(1)} %get-tuple-element.84), channel_id=1, source_target_pairs={{0,4},{2,6},{4,0},{6,2},{8,12},{10,14},{12,8},{14,10},{16,20},{18,... | collective-permute-start | bytes 393224 | tf_op jit(solution)/shard_map/ppermute | solution.py:32
  6.6 2.2 %copy-done.2 = bf16[1024,2048]{1,0:T(8,128)(2,1)S(1)} copy-done((bf16[1024,2048]{1,0:T(8,128)(2,1)S(1)}, bf16[1024,2048]{1,0:T(8,128)(2,1)}, u32[]{:S(2)}) %copy-start.2) | copy-done | bytes 4194328
  8.8 1.1 %shard_map.102 = f32[1,1024]{1,0:T(1,128)S(1)} custom-call(bf16[1024,2048]{1,0:T(8,128)(2,1)S(1)} %copy-done.2), custom_call_target="tpu_custom_call" | custom-call | flops 1 | bytes 1 | tf_op jit(solution)/shard_map/pallas_call | solution.py:117
  10.4 1.2 %shard_map.103 = f32[1,1024]{1,0:T(1,128)S(1)} custom-call(bf16[1024,2048]{1,0:T(8,128)(2,1)S(1)} %collective-permute-done.3.x_ref), custom_call_target="tpu_custom_call" | custom-call | flops 1 | bytes 1 | tf_op jit(solution)/shard_map/pallas_call | solution.py:117
  11.6 1.9 %collective-permute-done.1 = bf16[2,256,128]{2,1,0:T(8,128)(2,1)S(1)} collective-permute-done((bf16[2,256,128]{2,1,0:T(8,128)(2,1)S(1)}, bf16[2,256,128]{2,1,0:T(8,128)(2,1)S(1)}, u32[]{:S(2)}, u32[]{:S(2)}) %collective-permute-start.1) | collective-permute-done | bytes 131104 | tf_op jit(solution)/shard_map/ppermute | solution.py:32
  13.6 1.6 %collective-permute-start.4 = (f32[1,256,128]{2,1,0:T(8,128)S(1)}, f32[1,256,128]{2,1,0:T(8,128)S(1)}, u32[]{:S(2)}, u32[]{:S(2)}) collective-permute-start(f32[1,256,128]{2,1,0:T(8,128)S(1)} %slice.17), channel_id=1, source_target_pairs={{0,8},{2,10},{4,12},{6,14},{8,0},{10,2},{12,4},{14,6},{16,24},{18,... | collective-permute-start | bytes 393224 | tf_op jit(solution)/shard_map/ppermute | solution.py:32
  15.2 1.2 %collective-permute-start.6 = (bf16[2,256,128]{2,1,0:T(8,128)(2,1)S(1)}, bf16[2,256,128]{2,1,0:T(8,128)(2,1)S(1)}, u32[]{:S(2)}, u32[]{:S(2)}) collective-permute-start(bf16[2,256,128]{2,1,0:T(8,128)(2,1)S(1)} %get-tuple-element.97), channel_id=1, source_target_pairs={{0,2},{2,0},{4,6},{6,4},{8,10},{10,8},{12,14},{14,12},{16,18},{18,... | collective-permute-start | bytes 393224 | tf_op jit(solution)/shard_map/ppermute | solution.py:32
  17.3 1.4 %collective-permute-start.8 = (bf16[2,256,128]{2,1,0:T(8,128)(2,1)S(1)}, bf16[2,256,128]{2,1,0:T(8,128)(2,1)S(1)}, u32[]{:S(2)}, u32[]{:S(2)}) collective-permute-start(bf16[2,256,128]{2,1,0:T(8,128)(2,1)S(1)} %get-tuple-element.99), channel_id=1, source_target_pairs={{0,6},{2,4},{4,2},{6,0},{8,14},{10,12},{12,10},{14,8},{16,22},{18,... | collective-permute-start | bytes 393224 | tf_op jit(solution)/shard_map/ppermute | solution.py:32
  18.9 2.7 %collective-permute-start.5 = (f32[256,128]{1,0:T(8,128)S(1)}, f32[256,128]{1,0:T(8,128)S(1)}, u32[]{:S(2)}, u32[]{:S(2)}) collective-permute-start(f32[256,128]{1,0:T(8,128)S(1)} %fusion.21), channel_id=1, source_target_pairs={{0,16},{2,18},{4,20},{6,22},{8,24},{10,26},{12,28},{14,30},{16,0},... | collective-permute-start | bytes 393224 | tf_op jit(solution)/shard_map/ppermute | solution.py:32
  21.5 1.3 %fusion.1 = f32[1024,128]{1,0:T(8,128)S(1)} fusion(bf16[2048,128]{1,0:T(8,128)(2,1)S(1)} %get-tuple-element.105, bf16[1024,2048]{1,0:T(8,128)(2,1)S(1)} %collective-permute-done.3.x_ref, f32[2048]{0:T(1024)S(1)} %convert_element_type.75, f32[1024]{0:T(1024)S(1)} %add_rsqrt_fusion), kind=kOutput, calls=%fused_computation.5 | convolution fusion | flops 545259520 | bytes 5255168 | tf_op jit(solution)/shard_map/dot_general | solution.py:257
  23.7 1.4 %fusion.16.raw_ref = f32[1024,128]{1,0:T(8,128)S(1)} fusion(f32[1024,128]{1,0:T(8,128)S(1)} %fusion.1, bf16[2048,128]{1,0:T(8,128)(2,1)S(1)} %get-tuple-element.103, bf16[1024,2048]{1,0:T(8,128)(2,1)S(1)} %copy-done.3, f32[2048]{0:T(1024)S(1)} %convert_element_type.72, f32[1024]{0:T(1024)S(1)} %add_rsqrt_fusion), kind=kOutput, calls=%fused_computation.20 | convolution fusion | flops 545390592 | bytes 5779456 | tf_op jit(solution)/shard_map/dot_general | solution.py:257
  25.2 1.5 %collective-permute-start.10 = (f32[256,128]{1,0:T(8,128)S(1)}, f32[256,128]{1,0:T(8,128)S(1)}, u32[]{:S(2)}, u32[]{:S(2)}) collective-permute-start(f32[256,128]{1,0:T(8,128)S(1)} %slice_bitcast_fusion.1), channel_id=1, source_target_pairs={{0,8},{2,10},{4,12},{6,14},{8,0},{10,2},{12,4},{14,6},{16,24},{18,... | collective-permute-start | bytes 393224 | tf_op jit(solution)/shard_map/ppermute | solution.py:32
  28.5 1.8 %fusion.14.refs_0_ = bf16[2048,128]{1,0:T(8,128)(2,1)S(1)} fusion(bf16[1024,128]{1,0:T(8,128)(2,1)S(1)} %get-tuple-element.118, bf16[1024,2048]{1,0:T(8,128)(2,1)S(1)} %copy-done.3, f32[1024]{0:T(1024)S(1)} %add_rsqrt_fusion, f32[2048]{0:T(1024)S(1)} %convert_element_type.72), kind=kOutput, calls=%fused_computation.18 | convolution fusion | flops 545783808 | bytes 4993024 | tf_op jit(solution)/shard_map/dot_general | solution.py:261
  33.1 2.5 %collective-permute-start.14 = (bf16[1,256,128]{2,1,0:T(8,128)(2,1)S(1)}, bf16[1,256,128]{2,1,0:T(8,128)(2,1)S(1)}, u32[]{:S(2)}, u32[]{:S(2)}) collective-permute-start(bf16[1,256,128]{2,1,0:T(8,128)(2,1)S(1)} %get-tuple-element.139), channel_id=1, source_target_pairs={{0,24},{2,26},{4,28},{6,30},{8,16},{10,18},{12,20},{14,22},{16,8},... | collective-permute-start | bytes 196616 | tf_op jit(solution)/shard_map/ppermute | solution.py:32
  36.3 1.6 %collective-permute-start.12 = (bf16[2,256,128]{2,1,0:T(8,128)(2,1)S(1)}, bf16[2,256,128]{2,1,0:T(8,128)(2,1)S(1)}, u32[]{:S(2)}, u32[]{:S(2)}) collective-permute-start(bf16[2,256,128]{2,1,0:T(8,128)(2,1)S(1)} %pad_maximum_fusion), channel_id=1, source_target_pairs={{0,4},{2,6},{4,0},{6,2},{8,12},{10,14},{12,8},{14,10},{16,20},{18,... | collective-permute-start | bytes 393224 | tf_op jit(solution)/shard_map/ppermute | solution.py:32
  37.9 1.6 %collective-permute-done.14 = bf16[1,256,128]{2,1,0:T(8,128)(2,1)S(1)} collective-permute-done((bf16[1,256,128]{2,1,0:T(8,128)(2,1)S(1)}, bf16[1,256,128]{2,1,0:T(8,128)(2,1)S(1)}, u32[]{:S(2)}, u32[]{:S(2)}) %collective-permute-start.14) | collective-permute-done | bytes 65568 | tf_op jit(solution)/shard_map/ppermute | solution.py:32
  39.5 2.8 %collective-permute-done.13 = bf16[1,256,128]{2,1,0:T(8,128)(2,1)S(1)} collective-permute-done((bf16[1,256,128]{2,1,0:T(8,128)(2,1)S(1)}, bf16[1,256,128]{2,1,0:T(8,128)(2,1)S(1)}, u32[]{:S(2)}, u32[]{:S(2)}) %collective-permute-start.13) | collective-permute-done | bytes 65568 | tf_op jit(solution)/shard_map/ppermute | solution.py:32
  42.4 1.3 %collective-permute-start.15 = (bf16[2,256,128]{2,1,0:T(8,128)(2,1)S(1)}, bf16[2,256,128]{2,1,0:T(8,128)(2,1)S(1)}, u32[]{:S(2)}, u32[]{:S(2)}) collective-permute-start(bf16[2,256,128]{2,1,0:T(8,128)(2,1)S(1)} %pad_maximum_fusion.1), channel_id=1, source_target_pairs={{0,2},{2,0},{4,6},{6,4},{8,10},{10,8},{12,14},{14,12},{16,18},{18,... | collective-permute-start | bytes 393224 | tf_op jit(solution)/shard_map/ppermute | solution.py:32
  44.6 4.2 %collective-permute-done.15 = bf16[2,256,128]{2,1,0:T(8,128)(2,1)S(1)} collective-permute-done((bf16[2,256,128]{2,1,0:T(8,128)(2,1)S(1)}, bf16[2,256,128]{2,1,0:T(8,128)(2,1)S(1)}, u32[]{:S(2)}, u32[]{:S(2)}) %collective-permute-start.15) | collective-permute-done | bytes 131104 | tf_op jit(solution)/shard_map/ppermute | solution.py:32
  48.8 1.6 %collective-permute-start.16 = (bf16[4,256,128]{2,1,0:T(8,128)(2,1)S(1)}, bf16[4,256,128]{2,1,0:T(8,128)(2,1)S(1)}, u32[]{:S(2)}, u32[]{:S(2)}) collective-permute-start(bf16[4,256,128]{2,1,0:T(8,128)(2,1)S(1)} %constant_dynamic-update-slice_fusion.2.refs_1_), channel_id=1, source_target_pairs={{0,4},{2,6},{4,0},{6,2},{8,12},{10,14},{12,8},{14,10},{16,20},{18,... | collective-permute-start | bytes 786440 | tf_op jit(solution)/shard_map/ppermute | solution.py:32
  51.3 1.8 %fusion.15.refs_1_ = bf16[2048,128]{1,0:T(8,128)(2,1)S(1)} fusion(bf16[1024,128]{1,0:T(8,128)(2,1)S(1)} %get-tuple-element.118, bf16[1024,2048]{1,0:T(8,128)(2,1)S(1)} %collective-permute-done.3.x_ref, f32[2048]{0:T(1024)S(1)} %convert_element_type.86, f32[1024]{0:T(1024)S(1)} %add_rsqrt_fusion), kind=kOutput, calls=%fused_computation.19 | convolution fusion | flops 545783808 | bytes 4993024 | tf_op jit(solution)/shard_map/dot_general | solution.py:261
  54.2 1.1 %collective-permute-done.16.refs_0_ = bf16[4,256,128]{2,1,0:T(8,128)(2,1)S(1)} collective-permute-done((bf16[4,256,128]{2,1,0:T(8,128)(2,1)S(1)}, bf16[4,256,128]{2,1,0:T(8,128)(2,1)S(1)}, u32[]{:S(2)}, u32[]{:S(2)}) %collective-permute-start.16) | collective-permute-done | bytes 262176 | tf_op jit(solution)/shard_map/ppermute | solution.py:32
  (58 shorter events, 12.7 us)
Async XLA Ops:
  0.6 9.7 %collective-permute-start.3 = (bf16[1024,2048]{1,0:T(8,128)(2,1)}, bf16[1024,2048]{1,0:T(8,128)(2,1)S(1)}, u32[]{:S(2)}, u32[]{:S(2)}) collective-permute-start(bf16[1024,2048]{1,0:T(8,128)(2,1)} %x_ref), channel_id=1, source_target_pairs={{0,1},{1,0},{2,3},{3,2},{4,5},{5,4},{6,7},{7,6},{8,9},{9,8},{10,11... | collective-permute-start | bytes 12582920 | tf_op jit(solution)/shard_map/ppermute | solution.py:32
  2.4 7.6 %copy-start.4 = (bf16[1024,128]{1,0:T(8,128)(2,1)S(1)}, bf16[1024,128]{1,0:T(8,128)(2,1)}, u32[]{:S(2)}) copy-start(bf16[1024,128]{1,0:T(8,128)(2,1)} %grad_ref) | copy-start | bytes 786436
  2.5 9.1 %collective-permute-start = (bf16[2,256,128]{2,1,0:T(8,128)(2,1)S(1)}, bf16[2,256,128]{2,1,0:T(8,128)(2,1)S(1)}, u32[]{:S(2)}, u32[]{:S(2)}) collective-permute-start(bf16[2,256,128]{2,1,0:T(8,128)(2,1)S(1)} %get-tuple-element.83), channel_id=1, source_target_pairs={{0,2},{2,0},{4,6},{6,4},{8,10},{10,8},{12,14},{14,12},{16,18},{18,... | collective-permute-start | bytes 393224 | tf_op jit(solution)/shard_map/ppermute | solution.py:32
  5.1 8.4 %collective-permute-start.1 = (bf16[2,256,128]{2,1,0:T(8,128)(2,1)S(1)}, bf16[2,256,128]{2,1,0:T(8,128)(2,1)S(1)}, u32[]{:S(2)}, u32[]{:S(2)}) collective-permute-start(bf16[2,256,128]{2,1,0:T(8,128)(2,1)S(1)} %get-tuple-element.84), channel_id=1, source_target_pairs={{0,4},{2,6},{4,0},{6,2},{8,12},{10,14},{12,8},{14,10},{16,20},{18,... | collective-permute-start | bytes 393224 | tf_op jit(solution)/shard_map/ppermute | solution.py:32
  6.6 6.9 %collective-permute-start.2 = (bf16[2,256,128]{2,1,0:T(8,128)(2,1)S(1)}, bf16[2,256,128]{2,1,0:T(8,128)(2,1)S(1)}, u32[]{:S(2)}, u32[]{:S(2)}) collective-permute-start(bf16[2,256,128]{2,1,0:T(8,128)(2,1)S(1)} %get-tuple-element.85), channel_id=1, source_target_pairs={{0,6},{2,4},{4,2},{6,0},{8,14},{10,12},{12,10},{14,8},{16,22},{18,... | collective-permute-start | bytes 393224 | tf_op jit(solution)/shard_map/ppermute | solution.py:32
  8.8 9.9 %copy-start.7 = (bf16[2048]{0:T(1024)(128)(2,1)S(1)}, bf16[2048]{0:T(1024)(128)(2,1)}, u32[]{:S(2)}) copy-start(bf16[2048]{0:T(1024)(128)(2,1)} %param.7) | copy-start | bytes 12292
  13.6 5.1 %collective-permute-start.4 = (f32[1,256,128]{2,1,0:T(8,128)S(1)}, f32[1,256,128]{2,1,0:T(8,128)S(1)}, u32[]{:S(2)}, u32[]{:S(2)}) collective-permute-start(f32[1,256,128]{2,1,0:T(8,128)S(1)} %slice.17), channel_id=1, source_target_pairs={{0,8},{2,10},{4,12},{6,14},{8,0},{10,2},{12,4},{14,6},{16,24},{18,... | collective-permute-start | bytes 393224 | tf_op jit(solution)/shard_map/ppermute | solution.py:32
  15.2 9.9 %collective-permute-start.6 = (bf16[2,256,128]{2,1,0:T(8,128)(2,1)S(1)}, bf16[2,256,128]{2,1,0:T(8,128)(2,1)S(1)}, u32[]{:S(2)}, u32[]{:S(2)}) collective-permute-start(bf16[2,256,128]{2,1,0:T(8,128)(2,1)S(1)} %get-tuple-element.97), channel_id=1, source_target_pairs={{0,2},{2,0},{4,6},{6,4},{8,10},{10,8},{12,14},{14,12},{16,18},{18,... | collective-permute-start | bytes 393224 | tf_op jit(solution)/shard_map/ppermute | solution.py:32
  16.5 8.6 %collective-permute-start.7 = (bf16[2,256,128]{2,1,0:T(8,128)(2,1)S(1)}, bf16[2,256,128]{2,1,0:T(8,128)(2,1)S(1)}, u32[]{:S(2)}, u32[]{:S(2)}) collective-permute-start(bf16[2,256,128]{2,1,0:T(8,128)(2,1)S(1)} %get-tuple-element.98), channel_id=1, source_target_pairs={{0,4},{2,6},{4,0},{6,2},{8,12},{10,14},{12,8},{14,10},{16,20},{18,... | collective-permute-start | bytes 393224 | tf_op jit(solution)/shard_map/ppermute | solution.py:32
  17.3 7.8 %collective-permute-start.8 = (bf16[2,256,128]{2,1,0:T(8,128)(2,1)S(1)}, bf16[2,256,128]{2,1,0:T(8,128)(2,1)S(1)}, u32[]{:S(2)}, u32[]{:S(2)}) collective-permute-start(bf16[2,256,128]{2,1,0:T(8,128)(2,1)S(1)} %get-tuple-element.99), channel_id=1, source_target_pairs={{0,6},{2,4},{4,2},{6,0},{8,14},{10,12},{12,10},{14,8},{16,22},{18,... | collective-permute-start | bytes 393224 | tf_op jit(solution)/shard_map/ppermute | solution.py:32
  18.8 2.8 %collective-permute-start.9 = (bf16[2048]{0:T(1024)(128)(2,1)S(1)}, bf16[2048]{0:T(1024)(128)(2,1)S(1)}, u32[]{:S(2)}, u32[]{:S(2)}) collective-permute-start(bf16[2048]{0:T(1024)(128)(2,1)S(1)} %copy-done.7), channel_id=1, source_target_pairs={{0,1},{1,0},{2,3},{3,2},{4,5},{5,4},{6,7},{7,6},{8,9},{9,8},{10,11... | collective-permute-start | bytes 12296 | tf_op jit(solution)/shard_map/ppermute | solution.py:32
  18.9 9.7 %collective-permute-start.5 = (f32[256,128]{1,0:T(8,128)S(1)}, f32[256,128]{1,0:T(8,128)S(1)}, u32[]{:S(2)}, u32[]{:S(2)}) collective-permute-start(f32[256,128]{1,0:T(8,128)S(1)} %fusion.21), channel_id=1, source_target_pairs={{0,16},{2,18},{4,20},{6,22},{8,24},{10,26},{12,28},{14,30},{16,0},... | collective-permute-start | bytes 393224 | tf_op jit(solution)/shard_map/ppermute | solution.py:32
  21.5 2.2 %copy-start.3 = (bf16[1024,2048]{1,0:T(8,128)(2,1)S(1)}, bf16[1024,2048]{1,0:T(8,128)(2,1)}, u32[]{:S(2)}) copy-start(bf16[1024,2048]{1,0:T(8,128)(2,1)} %x_ref) | copy-start | bytes 12582916
  25.2 6.1 %collective-permute-start.10 = (f32[256,128]{1,0:T(8,128)S(1)}, f32[256,128]{1,0:T(8,128)S(1)}, u32[]{:S(2)}, u32[]{:S(2)}) collective-permute-start(f32[256,128]{1,0:T(8,128)S(1)} %slice_bitcast_fusion.1), channel_id=1, source_target_pairs={{0,8},{2,10},{4,12},{6,14},{8,0},{10,2},{12,4},{14,6},{16,24},{18,... | collective-permute-start | bytes 393224 | tf_op jit(solution)/shard_map/ppermute | solution.py:32
  28.5 2.8 %copy-start.5 = (f32[256,128]{1,0:T(8,128)S(1)}, f32[256,128]{1,0:T(8,128)}, u32[]{:S(2)}) copy-start(f32[256,128]{1,0:T(8,128)} %param.9) | copy-start | bytes 393220
  28.5 2.8 %copy-start.6 = (f32[256,128]{1,0:T(8,128)S(1)}, f32[256,128]{1,0:T(8,128)}, u32[]{:S(2)}) copy-start(f32[256,128]{1,0:T(8,128)} %param.10) | copy-start | bytes 393220
  28.5 21.9 %copy-start.1 = (bf16[4096,128]{1,0:T(8,128)(2,1)S(1)}, bf16[4096,128]{1,0:T(8,128)(2,1)}, u32[]{:S(2)}) copy-start(bf16[4096,128]{1,0:T(8,128)(2,1)} %w_ref.4) | copy-start | bytes 3145732
  32.0 4.3 %collective-permute-start.11 = (bf16[1,256,128]{2,1,0:T(8,128)(2,1)S(1)}, bf16[1,256,128]{2,1,0:T(8,128)(2,1)S(1)}, u32[]{:S(2)}, u32[]{:S(2)}) collective-permute-start(bf16[1,256,128]{2,1,0:T(8,128)(2,1)S(1)} %get-tuple-element.139), channel_id=1, source_target_pairs={{0,8},{2,10},{4,12},{6,14},{8,0},{10,2},{12,4},{14,6},{16,24},{18,... | collective-permute-start | bytes 196616 | tf_op jit(solution)/shard_map/ppermute | solution.py:32
  33.1 6.5 %collective-permute-start.14 = (bf16[1,256,128]{2,1,0:T(8,128)(2,1)S(1)}, bf16[1,256,128]{2,1,0:T(8,128)(2,1)S(1)}, u32[]{:S(2)}, u32[]{:S(2)}) collective-permute-start(bf16[1,256,128]{2,1,0:T(8,128)(2,1)S(1)} %get-tuple-element.139), channel_id=1, source_target_pairs={{0,24},{2,26},{4,28},{6,30},{8,16},{10,18},{12,20},{14,22},{16,8},... | collective-permute-start | bytes 196616 | tf_op jit(solution)/shard_map/ppermute | solution.py:32
  35.5 6.8 %collective-permute-start.13 = (bf16[1,256,128]{2,1,0:T(8,128)(2,1)S(1)}, bf16[1,256,128]{2,1,0:T(8,128)(2,1)S(1)}, u32[]{:S(2)}, u32[]{:S(2)}) collective-permute-start(bf16[1,256,128]{2,1,0:T(8,128)(2,1)S(1)} %get-tuple-element.139), channel_id=1, source_target_pairs={{0,16},{2,18},{4,20},{6,22},{8,24},{10,26},{12,28},{14,30},{16,0},... | collective-permute-start | bytes 196616 | tf_op jit(solution)/shard_map/ppermute | solution.py:32
  36.3 6.0 %collective-permute-start.12 = (bf16[2,256,128]{2,1,0:T(8,128)(2,1)S(1)}, bf16[2,256,128]{2,1,0:T(8,128)(2,1)S(1)}, u32[]{:S(2)}, u32[]{:S(2)}) collective-permute-start(bf16[2,256,128]{2,1,0:T(8,128)(2,1)S(1)} %pad_maximum_fusion), channel_id=1, source_target_pairs={{0,4},{2,6},{4,0},{6,2},{8,12},{10,14},{12,8},{14,10},{16,20},{18,... | collective-permute-start | bytes 393224 | tf_op jit(solution)/shard_map/ppermute | solution.py:32
  42.4 6.4 %collective-permute-start.15 = (bf16[2,256,128]{2,1,0:T(8,128)(2,1)S(1)}, bf16[2,256,128]{2,1,0:T(8,128)(2,1)S(1)}, u32[]{:S(2)}, u32[]{:S(2)}) collective-permute-start(bf16[2,256,128]{2,1,0:T(8,128)(2,1)S(1)} %pad_maximum_fusion.1), channel_id=1, source_target_pairs={{0,2},{2,0},{4,6},{6,4},{8,10},{10,8},{12,14},{14,12},{16,18},{18,... | collective-permute-start | bytes 393224 | tf_op jit(solution)/shard_map/ppermute | solution.py:32
  43.7 12.3 %collective-permute-start.17 = (bf16[4,256,128]{2,1,0:T(8,128)(2,1)S(1)}, bf16[4,256,128]{2,1,0:T(8,128)(2,1)S(1)}, u32[]{:S(2)}, u32[]{:S(2)}) collective-permute-start(bf16[4,256,128]{2,1,0:T(8,128)(2,1)S(1)} %constant_dynamic-update-slice_fusion.refs_0_), channel_id=1, source_target_pairs={{0,2},{2,0},{4,6},{6,4},{8,10},{10,8},{12,14},{14,12},{16,18},{18,... | collective-permute-start | bytes 786440 | tf_op jit(solution)/shard_map/ppermute | solution.py:32
  48.8 6.4 %collective-permute-start.16 = (bf16[4,256,128]{2,1,0:T(8,128)(2,1)S(1)}, bf16[4,256,128]{2,1,0:T(8,128)(2,1)S(1)}, u32[]{:S(2)}, u32[]{:S(2)}) collective-permute-start(bf16[4,256,128]{2,1,0:T(8,128)(2,1)S(1)} %constant_dynamic-update-slice_fusion.2.refs_1_), channel_id=1, source_target_pairs={{0,4},{2,6},{4,0},{6,2},{8,12},{10,14},{12,8},{14,10},{16,20},{18,... | collective-permute-start | bytes 786440 | tf_op jit(solution)/shard_map/ppermute | solution.py:32
  (2 other events, 3.4 us)

commit v11 on v9

--- a/solution.py
+++ b/solution.py
@@ -279,15 +279,18 @@
 
     mate = swap(outgoing, "rep", PLANE)
     column = [swap(outgoing, "rep", k) for k in far_side]
+    mate, x = after(mate, x)
     near = jnp.concatenate([outgoing, mate])
     near = [near] + [swap(near, "rep", p) for p in mates]
     blocks += [weight_rows(k) for k in range(1, cores)]
-    weight_grad = place_blocks(blocks)
-    column, near, weight_grad = after(column, near, weight_grad)
+    column, blocks = after(column, blocks)
     rest = jnp.concatenate(column)
     rest = [rest] + [swap(rest, "rep", p) for p in mates]
+    weight_grad = place_blocks(blocks)
+    near, weight_grad = after(near, weight_grad)
     merged = merge(w, near, [[k + p for k in near_side] for p in range(PLANE)])
     places = [[k + p for k in far_side] for p in range(PLANE)]
+    rest[2:], merged, weight_grad = after(rest[2:], merged, weight_grad)
     merged = merge(w, [rest[0], *rest[2:]], [places[0], *places[2:]], merged)
     last, merged = after(rest[1], merged)
     merged = merge(w, [last], places[1:2], merged)

time: 55.2 us -> 53.2 us (0.964)
  waiting for transfers between devices: 10.2 us -> 8.18 us
    ppermute x20, waiting for transfers between devices: 10.2 us -> 8.18 us  [swap(): return lax.ppermute(value, axis, [(i, i ^ offset) for i in range(size)])]
  transfers between devices with their start and end apart: 20 -> 20, of which waited for: 9 -> 7; matrix products, arithmetic and copies ran while one was open for 12% -> 12% of each run, Pallas kernels for 12% -> 12%
where the time goes in v11:
time: 53.2 us; the launch traced here: 53 us
  starting transfers between devices  25.2 us (47%)
  waiting for transfers between devices  8.18 us (15%)
  Pallas kernels  7.25 us (14%)
  matrix products  6.3 us (12%)
  local copies, waits for them, and re-layouts  4.32 us (8%)
  other arithmetic  0.93 us (2%)
  between operations  0.86 us (2%)
    ppermute x20, starting transfers between devices, swap(): return lax.ppermute(value, axis, [(i, i ^ offset) for i in range(size)])  25.2 us
    ppermute x20, waiting for transfers between devices, swap(): return lax.ppermute(value, axis, [(i, i ^ offset) for i in range(size)])  8.18 us
    unnamed x17, local copies, waits for them, and re-layouts  4.29 us
    dot_general x2, matrix products, weight_rows(): lax.dot_general(norm, raw_grad, (((0,), (0,)), ((), ())), preferred_eleme...  3.59 us
    dot_general x2, matrix products, key_part(): return jnp.dot(norm, halves[k], preferred_element_type=jnp.float32)  2.71 us
    pallas_call x3, Pallas kernels, merge(): pl.pallas_call(functools.partial(merge_kernel, offsets), out_shape=jax.Sh...  2.45 us
    pallas_call x2, Pallas kernels, squares_of(): pl.pallas_call(squares_kernel, out_shape=jax.ShapeDtypeStruct((1, rows),...  2.31 us
  transfers between devices with their start and end apart: 20, of which 7 were waited for; matrix products, arithmetic and copies ran while one was open for 12% of the time, Pallas kernels for 12%

profile of v11, /device:TPU:0, one launch (start us, length us, event | category | flops | bytes accessed | tf_op | source)
XLA Modules:
  0.0 53.0 jit_solution(5951303002289906936)
XLA Ops:
  1.2 1.2 %copy-done = bf16[4096,128]{1,0:T(8,128)(2,1)S(1)} copy-done((bf16[4096,128]{1,0:T(8,128)(2,1)S(1)}, bf16[4096,128]{1,0:T(8,128)(2,1)}, u32[]{:S(2)}) %copy-start) | copy-done | bytes 1048600
  2.5 2.6 %collective-permute-start = (bf16[2,256,128]{2,1,0:T(8,128)(2,1)S(1)}, bf16[2,256,128]{2,1,0:T(8,128)(2,1)S(1)}, u32[]{:S(2)}, u32[]{:S(2)}) collective-permute-start(bf16[2,256,128]{2,1,0:T(8,128)(2,1)S(1)} %get-tuple-element.89), channel_id=1, source_target_pairs={{0,2},{2,0},{4,6},{6,4},{8,10},{10,8},{12,14},{14,12},{16,18},{18,... | collective-permute-start | bytes 393224 | tf_op jit(solution)/shard_map/ppermute | solution.py:32
  5.1 1.5 %collective-permute-start.1 = (bf16[2,256,128]{2,1,0:T(8,128)(2,1)S(1)}, bf16[2,256,128]{2,1,0:T(8,128)(2,1)S(1)}, u32[]{:S(2)}, u32[]{:S(2)}) collective-permute-start(bf16[2,256,128]{2,1,0:T(8,128)(2,1)S(1)} %get-tuple-element.90), channel_id=1, source_target_pairs={{0,4},{2,6},{4,0},{6,2},{8,12},{10,14},{12,8},{14,10},{16,20},{18,... | collective-permute-start | bytes 393224 | tf_op jit(solution)/shard_map/ppermute | solution.py:32
  6.6 2.2 %copy-done.2 = bf16[1024,2048]{1,0:T(8,128)(2,1)S(1)} copy-done((bf16[1024,2048]{1,0:T(8,128)(2,1)S(1)}, bf16[1024,2048]{1,0:T(8,128)(2,1)}, u32[]{:S(2)}) %copy-start.2) | copy-done | bytes 4194328
  8.8 1.1 %shard_map.102 = f32[1,1024]{1,0:T(1,128)S(1)} custom-call(bf16[1024,2048]{1,0:T(8,128)(2,1)S(1)} %copy-done.2), custom_call_target="tpu_custom_call" | custom-call | flops 1 | bytes 1 | tf_op jit(solution)/shard_map/pallas_call | solution.py:119
  10.4 1.2 %shard_map.103 = f32[1,1024]{1,0:T(1,128)S(1)} custom-call(bf16[1024,2048]{1,0:T(8,128)(2,1)S(1)} %collective-permute-done.3.x_ref), custom_call_target="tpu_custom_call" | custom-call | flops 1 | bytes 1 | tf_op jit(solution)/shard_map/pallas_call | solution.py:119
  11.6 1.9 %collective-permute-done.1 = bf16[2,256,128]{2,1,0:T(8,128)(2,1)S(1)} collective-permute-done((bf16[2,256,128]{2,1,0:T(8,128)(2,1)S(1)}, bf16[2,256,128]{2,1,0:T(8,128)(2,1)S(1)}, u32[]{:S(2)}, u32[]{:S(2)}) %collective-permute-start.1) | collective-permute-done | bytes 131104 | tf_op jit(solution)/shard_map/ppermute | solution.py:32
  13.6 1.6 %collective-permute-start.4 = (f32[1,256,128]{2,1,0:T(8,128)S(1)}, f32[1,256,128]{2,1,0:T(8,128)S(1)}, u32[]{:S(2)}, u32[]{:S(2)}) collective-permute-start(f32[1,256,128]{2,1,0:T(8,128)S(1)} %slice.17), channel_id=1, source_target_pairs={{0,8},{2,10},{4,12},{6,14},{8,0},{10,2},{12,4},{14,6},{16,24},{18,... | collective-permute-start | bytes 393224 | tf_op jit(solution)/shard_map/ppermute | solution.py:32
  15.2 1.2 %collective-permute-start.6 = (bf16[2,256,128]{2,1,0:T(8,128)(2,1)S(1)}, bf16[2,256,128]{2,1,0:T(8,128)(2,1)S(1)}, u32[]{:S(2)}, u32[]{:S(2)}) collective-permute-start(bf16[2,256,128]{2,1,0:T(8,128)(2,1)S(1)} %get-tuple-element.103), channel_id=1, source_target_pairs={{0,2},{2,0},{4,6},{6,4},{8,10},{10,8},{12,14},{14,12},{16,18},{18,... | collective-permute-start | bytes 393224 | tf_op jit(solution)/shard_map/ppermute | solution.py:32
  17.3 1.4 %collective-permute-start.8 = (bf16[2,256,128]{2,1,0:T(8,128)(2,1)S(1)}, bf16[2,256,128]{2,1,0:T(8,128)(2,1)S(1)}, u32[]{:S(2)}, u32[]{:S(2)}) collective-permute-start(bf16[2,256,128]{2,1,0:T(8,128)(2,1)S(1)} %get-tuple-element.105), channel_id=1, source_target_pairs={{0,6},{2,4},{4,2},{6,0},{8,14},{10,12},{12,10},{14,8},{16,22},{18,... | collective-permute-start | bytes 393224 | tf_op jit(solution)/shard_map/ppermute | solution.py:32
  18.9 2.7 %collective-permute-start.5 = (f32[256,128]{1,0:T(8,128)S(1)}, f32[256,128]{1,0:T(8,128)S(1)}, u32[]{:S(2)}, u32[]{:S(2)}) collective-permute-start(f32[256,128]{1,0:T(8,128)S(1)} %fusion.21), channel_id=1, source_target_pairs={{0,16},{2,18},{4,20},{6,22},{8,24},{10,26},{12,28},{14,30},{16,0},... | collective-permute-start | bytes 393224 | tf_op jit(solution)/shard_map/ppermute | solution.py:32
  21.5 1.3 %fusion.1 = f32[1024,128]{1,0:T(8,128)S(1)} fusion(bf16[2048,128]{1,0:T(8,128)(2,1)S(1)} %get-tuple-element.111, bf16[1024,2048]{1,0:T(8,128)(2,1)S(1)} %collective-permute-done.3.x_ref, f32[2048]{0:T(1024)S(1)} %convert_element_type.75, f32[1024]{0:T(1024)S(1)} %add_rsqrt_fusion), kind=kOutput, calls=%fused_computation.5 | convolution fusion | flops 545259520 | bytes 5255168 | tf_op jit(solution)/shard_map/dot_general | solution.py:255
  23.7 1.4 %fusion.16.raw_ref = f32[1024,128]{1,0:T(8,128)S(1)} fusion(f32[1024,128]{1,0:T(8,128)S(1)} %fusion.1, bf16[2048,128]{1,0:T(8,128)(2,1)S(1)} %get-tuple-element.109, bf16[1024,2048]{1,0:T(8,128)(2,1)S(1)} %copy-done.3, f32[2048]{0:T(1024)S(1)} %convert_element_type.72, f32[1024]{0:T(1024)S(1)} %add_rsqrt_fusion), kind=kOutput, calls=%fused_computation.20 | convolution fusion | flops 545390592 | bytes 5779456 | tf_op jit(solution)/shard_map/dot_general | solution.py:255
  25.2 1.5 %collective-permute-start.10 = (f32[256,128]{1,0:T(8,128)S(1)}, f32[256,128]{1,0:T(8,128)S(1)}, u32[]{:S(2)}, u32[]{:S(2)}) collective-permute-start(f32[256,128]{1,0:T(8,128)S(1)} %slice_bitcast_fusion.1), channel_id=1, source_target_pairs={{0,8},{2,10},{4,12},{6,14},{8,0},{10,2},{12,4},{14,6},{16,24},{18,... | collective-permute-start | bytes 393224 | tf_op jit(solution)/shard_map/ppermute | solution.py:32
  28.5 1.8 %fusion.14.refs_0_ = bf16[2048,128]{1,0:T(8,128)(2,1)S(1)} fusion(bf16[1024,128]{1,0:T(8,128)(2,1)S(1)} %get-tuple-element.124, bf16[1024,2048]{1,0:T(8,128)(2,1)S(1)} %copy-done.3, f32[1024]{0:T(1024)S(1)} %add_rsqrt_fusion, f32[2048]{0:T(1024)S(1)} %convert_element_type.72), kind=kOutput, calls=%fused_computation.18 | convolution fusion | flops 545783808 | bytes 4993024 | tf_op jit(solution)/shard_map/dot_general | solution.py:259
  33.1 2.5 %collective-permute-start.12 = (bf16[1,256,128]{2,1,0:T(8,128)(2,1)S(1)}, bf16[1,256,128]{2,1,0:T(8,128)(2,1)S(1)}, u32[]{:S(2)}, u32[]{:S(2)}) collective-permute-start(bf16[1,256,128]{2,1,0:T(8,128)(2,1)S(1)} %get-tuple-element.151), channel_id=1, source_target_pairs={{0,24},{2,26},{4,28},{6,30},{8,16},{10,18},{12,20},{14,22},{16,8},... | collective-permute-start | bytes 196616 | tf_op jit(solution)/shard_map/ppermute | solution.py:32
  36.3 1.6 %collective-permute-start.18 = (bf16[2,256,128]{2,1,0:T(8,128)(2,1)S(1)}, bf16[2,256,128]{2,1,0:T(8,128)(2,1)S(1)}, u32[]{:S(2)}, u32[]{:S(2)}) collective-permute-start(bf16[2,256,128]{2,1,0:T(8,128)(2,1)S(1)} %pad_maximum_fusion.refs_0_), channel_id=1, source_target_pairs={{0,6},{2,4},{4,2},{6,0},{8,14},{10,12},{12,10},{14,8},{16,22},{18,... | collective-permute-start | bytes 393224 | tf_op jit(solution)/shard_map/ppermute | solution.py:32
  37.9 1.2 %collective-permute-start.17 = (bf16[2,256,128]{2,1,0:T(8,128)(2,1)S(1)}, bf16[2,256,128]{2,1,0:T(8,128)(2,1)S(1)}, u32[]{:S(2)}, u32[]{:S(2)}) collective-permute-start(bf16[2,256,128]{2,1,0:T(8,128)(2,1)S(1)} %pad_maximum_fusion.refs_0_), channel_id=1, source_target_pairs={{0,4},{2,6},{4,0},{6,2},{8,12},{10,14},{12,8},{14,10},{16,20},{18,... | collective-permute-start | bytes 393224 | tf_op jit(solution)/shard_map/ppermute | solution.py:32
  39.9 1.8 %fusion.15.refs_1_ = bf16[2048,128]{1,0:T(8,128)(2,1)S(1)} fusion(bf16[1024,128]{1,0:T(8,128)(2,1)S(1)} %get-tuple-element.124, bf16[1024,2048]{1,0:T(8,128)(2,1)S(1)} %collective-permute-done.3.x_ref, f32[2048]{0:T(1024)S(1)} %convert_element_type.86, f32[1024]{0:T(1024)S(1)} %add_rsqrt_fusion), kind=kOutput, calls=%fused_computation.19 | convolution fusion | flops 545783808 | bytes 4993024 | tf_op jit(solution)/shard_map/dot_general | solution.py:259
  42.4 1.6 %collective-permute-start.15 = (bf16[2,256,128]{2,1,0:T(8,128)(2,1)S(1)}, bf16[2,256,128]{2,1,0:T(8,128)(2,1)S(1)}, u32[]{:S(2)}, u32[]{:S(2)}) collective-permute-start(bf16[2,256,128]{2,1,0:T(8,128)(2,1)S(1)} %constant_dynamic-update-slice_fusion.refs_0_), channel_id=1, source_target_pairs={{0,6},{2,4},{4,2},{6,0},{8,14},{10,12},{12,10},{14,8},{16,22},{18,... | collective-permute-start | bytes 393224 | tf_op jit(solution)/shard_map/ppermute | solution.py:32
  43.9 1.2 %collective-permute-start.14 = (bf16[2,256,128]{2,1,0:T(8,128)(2,1)S(1)}, bf16[2,256,128]{2,1,0:T(8,128)(2,1)S(1)}, u32[]{:S(2)}, u32[]{:S(2)}) collective-permute-start(bf16[2,256,128]{2,1,0:T(8,128)(2,1)S(1)} %constant_dynamic-update-slice_fusion.refs_0_), channel_id=1, source_target_pairs={{0,4},{2,6},{4,0},{6,2},{8,12},{10,14},{12,8},{14,10},{16,20},{18,... | collective-permute-start | bytes 393224 | tf_op jit(solution)/shard_map/ppermute | solution.py:32
  45.9 1.0 %shard_map.106 = bf16[4096,128]{1,0:T(8,128)(2,1)} custom-call(bf16[2048,128]{1,0:T(8,128)(2,1)S(1)} %fusion.14.refs_0_, bf16[2048,128]{1,0:T(8,128)(2,1)S(1)} %fusion.15.refs_1_), custom_call_target="tpu_custom_call" | custom-call | flops 1 | bytes 1 | tf_op jit(solution)/shard_map/pallas_call | solution.py:162
  47.9 1.8 %collective-permute-done.15.refs_2_ = bf16[2,256,128]{2,1,0:T(8,128)(2,1)S(1)} collective-permute-done((bf16[2,256,128]{2,1,0:T(8,128)(2,1)S(1)}, bf16[2,256,128]{2,1,0:T(8,128)(2,1)S(1)}, u32[]{:S(2)}, u32[]{:S(2)}) %collective-permute-start.15) | collective-permute-done | bytes 131104 | tf_op jit(solution)/shard_map/ppermute | solution.py:32
  49.7 1.8 %collective-permute-done.14.refs_1_ = bf16[2,256,128]{2,1,0:T(8,128)(2,1)S(1)} collective-permute-done((bf16[2,256,128]{2,1,0:T(8,128)(2,1)S(1)}, bf16[2,256,128]{2,1,0:T(8,128)(2,1)S(1)}, u32[]{:S(2)}, u32[]{:S(2)}) %collective-permute-start.14) | collective-permute-done | bytes 131104 | tf_op jit(solution)/shard_map/ppermute | solution.py:32
  (59 shorter events, 13.0 us)
Async XLA Ops:
  0.6 9.7 %collective-permute-start.3 = (bf16[1024,2048]{1,0:T(8,128)(2,1)}, bf16[1024,2048]{1,0:T(8,128)(2,1)S(1)}, u32[]{:S(2)}, u32[]{:S(2)}) collective-permute-start(bf16[1024,2048]{1,0:T(8,128)(2,1)} %x_ref), channel_id=1, source_target_pairs={{0,1},{1,0},{2,3},{3,2},{4,5},{5,4},{6,7},{7,6},{8,9},{9,8},{10,11... | collective-permute-start | bytes 12582920 | tf_op jit(solution)/shard_map/ppermute | solution.py:32
  2.4 7.6 %copy-start.4 = (bf16[1024,128]{1,0:T(8,128)(2,1)S(1)}, bf16[1024,128]{1,0:T(8,128)(2,1)}, u32[]{:S(2)}) copy-start(bf16[1024,128]{1,0:T(8,128)(2,1)} %grad_ref) | copy-start | bytes 786436
  2.5 9.1 %collective-permute-start = (bf16[2,256,128]{2,1,0:T(8,128)(2,1)S(1)}, bf16[2,256,128]{2,1,0:T(8,128)(2,1)S(1)}, u32[]{:S(2)}, u32[]{:S(2)}) collective-permute-start(bf16[2,256,128]{2,1,0:T(8,128)(2,1)S(1)} %get-tuple-element.89), channel_id=1, source_target_pairs={{0,2},{2,0},{4,6},{6,4},{8,10},{10,8},{12,14},{14,12},{16,18},{18,... | collective-permute-start | bytes 393224 | tf_op jit(solution)/shard_map/ppermute | solution.py:32
  5.1 8.4 %collective-permute-start.1 = (bf16[2,256,128]{2,1,0:T(8,128)(2,1)S(1)}, bf16[2,256,128]{2,1,0:T(8,128)(2,1)S(1)}, u32[]{:S(2)}, u32[]{:S(2)}) collective-permute-start(bf16[2,256,128]{2,1,0:T(8,128)(2,1)S(1)} %get-tuple-element.90), channel_id=1, source_target_pairs={{0,4},{2,6},{4,0},{6,2},{8,12},{10,14},{12,8},{14,10},{16,20},{18,... | collective-permute-start | bytes 393224 | tf_op jit(solution)/shard_map/ppermute | solution.py:32
  6.6 6.9 %collective-permute-start.2 = (bf16[2,256,128]{2,1,0:T(8,128)(2,1)S(1)}, bf16[2,256,128]{2,1,0:T(8,128)(2,1)S(1)}, u32[]{:S(2)}, u32[]{:S(2)}) collective-permute-start(bf16[2,256,128]{2,1,0:T(8,128)(2,1)S(1)} %get-tuple-element.91), channel_id=1, source_target_pairs={{0,6},{2,4},{4,2},{6,0},{8,14},{10,12},{12,10},{14,8},{16,22},{18,... | collective-permute-start | bytes 393224 | tf_op jit(solution)/shard_map/ppermute | solution.py:32
  8.8 9.9 %copy-start.7 = (bf16[2048]{0:T(1024)(128)(2,1)S(1)}, bf16[2048]{0:T(1024)(128)(2,1)}, u32[]{:S(2)}) copy-start(bf16[2048]{0:T(1024)(128)(2,1)} %param.7) | copy-start | bytes 12292
  13.6 5.1 %collective-permute-start.4 = (f32[1,256,128]{2,1,0:T(8,128)S(1)}, f32[1,256,128]{2,1,0:T(8,128)S(1)}, u32[]{:S(2)}, u32[]{:S(2)}) collective-permute-start(f32[1,256,128]{2,1,0:T(8,128)S(1)} %slice.17), channel_id=1, source_target_pairs={{0,8},{2,10},{4,12},{6,14},{8,0},{10,2},{12,4},{14,6},{16,24},{18,... | collective-permute-start | bytes 393224 | tf_op jit(solution)/shard_map/ppermute | solution.py:32
  15.2 9.9 %collective-permute-start.6 = (bf16[2,256,128]{2,1,0:T(8,128)(2,1)S(1)}, bf16[2,256,128]{2,1,0:T(8,128)(2,1)S(1)}, u32[]{:S(2)}, u32[]{:S(2)}) collective-permute-start(bf16[2,256,128]{2,1,0:T(8,128)(2,1)S(1)} %get-tuple-element.103), channel_id=1, source_target_pairs={{0,2},{2,0},{4,6},{6,4},{8,10},{10,8},{12,14},{14,12},{16,18},{18,... | collective-permute-start | bytes 393224 | tf_op jit(solution)/shard_map/ppermute | solution.py:32
  16.5 8.6 %collective-permute-start.7 = (bf16[2,256,128]{2,1,0:T(8,128)(2,1)S(1)}, bf16[2,256,128]{2,1,0:T(8,128)(2,1)S(1)}, u32[]{:S(2)}, u32[]{:S(2)}) collective-permute-start(bf16[2,256,128]{2,1,0:T(8,128)(2,1)S(1)} %get-tuple-element.104), channel_id=1, source_target_pairs={{0,4},{2,6},{4,0},{6,2},{8,12},{10,14},{12,8},{14,10},{16,20},{18,... | collective-permute-start | bytes 393224 | tf_op jit(solution)/shard_map/ppermute | solution.py:32
  17.3 7.8 %collective-permute-start.8 = (bf16[2,256,128]{2,1,0:T(8,128)(2,1)S(1)}, bf16[2,256,128]{2,1,0:T(8,128)(2,1)S(1)}, u32[]{:S(2)}, u32[]{:S(2)}) collective-permute-start(bf16[2,256,128]{2,1,0:T(8,128)(2,1)S(1)} %get-tuple-element.105), channel_id=1, source_target_pairs={{0,6},{2,4},{4,2},{6,0},{8,14},{10,12},{12,10},{14,8},{16,22},{18,... | collective-permute-start | bytes 393224 | tf_op jit(solution)/shard_map/ppermute | solution.py:32
  18.8 2.8 %collective-permute-start.9 = (bf16[2048]{0:T(1024)(128)(2,1)S(1)}, bf16[2048]{0:T(1024)(128)(2,1)S(1)}, u32[]{:S(2)}, u32[]{:S(2)}) collective-permute-start(bf16[2048]{0:T(1024)(128)(2,1)S(1)} %copy-done.7), channel_id=1, source_target_pairs={{0,1},{1,0},{2,3},{3,2},{4,5},{5,4},{6,7},{7,6},{8,9},{9,8},{10,11... | collective-permute-start | bytes 12296 | tf_op jit(solution)/shard_map/ppermute | solution.py:32
  18.9 9.7 %collective-permute-start.5 = (f32[256,128]{1,0:T(8,128)S(1)}, f32[256,128]{1,0:T(8,128)S(1)}, u32[]{:S(2)}, u32[]{:S(2)}) collective-permute-start(f32[256,128]{1,0:T(8,128)S(1)} %fusion.21), channel_id=1, source_target_pairs={{0,16},{2,18},{4,20},{6,22},{8,24},{10,26},{12,28},{14,30},{16,0},... | collective-permute-start | bytes 393224 | tf_op jit(solution)/shard_map/ppermute | solution.py:32
  25.2 6.1 %collective-permute-start.10 = (f32[256,128]{1,0:T(8,128)S(1)}, f32[256,128]{1,0:T(8,128)S(1)}, u32[]{:S(2)}, u32[]{:S(2)}) collective-permute-start(f32[256,128]{1,0:T(8,128)S(1)} %slice_bitcast_fusion.1), channel_id=1, source_target_pairs={{0,8},{2,10},{4,12},{6,14},{8,0},{10,2},{12,4},{14,6},{16,24},{18,... | collective-permute-start | bytes 393224 | tf_op jit(solution)/shard_map/ppermute | solution.py:32
  28.5 2.8 %copy-start.6 = (f32[256,128]{1,0:T(8,128)S(1)}, f32[256,128]{1,0:T(8,128)}, u32[]{:S(2)}) copy-start(f32[256,128]{1,0:T(8,128)} %param.10) | copy-start | bytes 393220
  32.0 4.3 %collective-permute-start.13 = (bf16[1,256,128]{2,1,0:T(8,128)(2,1)S(1)}, bf16[1,256,128]{2,1,0:T(8,128)(2,1)S(1)}, u32[]{:S(2)}, u32[]{:S(2)}) collective-permute-start(bf16[1,256,128]{2,1,0:T(8,128)(2,1)S(1)} %get-tuple-element.151), channel_id=1, source_target_pairs={{0,8},{2,10},{4,12},{6,14},{8,0},{10,2},{12,4},{14,6},{16,24},{18,... | collective-permute-start | bytes 196616 | tf_op jit(solution)/shard_map/ppermute | solution.py:32
  33.1 8.6 %collective-permute-start.12 = (bf16[1,256,128]{2,1,0:T(8,128)(2,1)S(1)}, bf16[1,256,128]{2,1,0:T(8,128)(2,1)S(1)}, u32[]{:S(2)}, u32[]{:S(2)}) collective-permute-start(bf16[1,256,128]{2,1,0:T(8,128)(2,1)S(1)} %get-tuple-element.151), channel_id=1, source_target_pairs={{0,24},{2,26},{4,28},{6,30},{8,16},{10,18},{12,20},{14,22},{16,8},... | collective-permute-start | bytes 196616 | tf_op jit(solution)/shard_map/ppermute | solution.py:32
  35.5 6.8 %collective-permute-start.11 = (bf16[1,256,128]{2,1,0:T(8,128)(2,1)S(1)}, bf16[1,256,128]{2,1,0:T(8,128)(2,1)S(1)}, u32[]{:S(2)}, u32[]{:S(2)}) collective-permute-start(bf16[1,256,128]{2,1,0:T(8,128)(2,1)S(1)} %get-tuple-element.151), channel_id=1, source_target_pairs={{0,16},{2,18},{4,20},{6,22},{8,24},{10,26},{12,28},{14,30},{16,0},... | collective-permute-start | bytes 196616 | tf_op jit(solution)/shard_map/ppermute | solution.py:32
  36.3 8.8 %collective-permute-start.18 = (bf16[2,256,128]{2,1,0:T(8,128)(2,1)S(1)}, bf16[2,256,128]{2,1,0:T(8,128)(2,1)S(1)}, u32[]{:S(2)}, u32[]{:S(2)}) collective-permute-start(bf16[2,256,128]{2,1,0:T(8,128)(2,1)S(1)} %pad_maximum_fusion.refs_0_), channel_id=1, source_target_pairs={{0,6},{2,4},{4,2},{6,0},{8,14},{10,12},{12,10},{14,8},{16,22},{18,... | collective-permute-start | bytes 393224 | tf_op jit(solution)/shard_map/ppermute | solution.py:32
  37.9 9.1 %collective-permute-start.17 = (bf16[2,256,128]{2,1,0:T(8,128)(2,1)S(1)}, bf16[2,256,128]{2,1,0:T(8,128)(2,1)S(1)}, u32[]{:S(2)}, u32[]{:S(2)}) collective-permute-start(bf16[2,256,128]{2,1,0:T(8,128)(2,1)S(1)} %pad_maximum_fusion.refs_0_), channel_id=1, source_target_pairs={{0,4},{2,6},{4,0},{6,2},{8,12},{10,14},{12,8},{14,10},{16,20},{18,... | collective-permute-start | bytes 393224 | tf_op jit(solution)/shard_map/ppermute | solution.py:32
  39.1 7.8 %collective-permute-start.16 = (bf16[2,256,128]{2,1,0:T(8,128)(2,1)S(1)}, bf16[2,256,128]{2,1,0:T(8,128)(2,1)S(1)}, u32[]{:S(2)}, u32[]{:S(2)}) collective-permute-start(bf16[2,256,128]{2,1,0:T(8,128)(2,1)S(1)} %pad_maximum_fusion.refs_0_), channel_id=1, source_target_pairs={{0,2},{2,0},{4,6},{6,4},{8,10},{10,8},{12,14},{14,12},{16,18},{18,... | collective-permute-start | bytes 393224 | tf_op jit(solution)/shard_map/ppermute | solution.py:32
  39.9 7.1 %copy-start.1 = (bf16[4096,128]{1,0:T(8,128)(2,1)S(1)}, bf16[4096,128]{1,0:T(8,128)(2,1)}, u32[]{:S(2)}) copy-start(bf16[4096,128]{1,0:T(8,128)(2,1)} %w_ref.4) | copy-start | bytes 3145732
  42.4 7.3 %collective-permute-start.15 = (bf16[2,256,128]{2,1,0:T(8,128)(2,1)S(1)}, bf16[2,256,128]{2,1,0:T(8,128)(2,1)S(1)}, u32[]{:S(2)}, u32[]{:S(2)}) collective-permute-start(bf16[2,256,128]{2,1,0:T(8,128)(2,1)S(1)} %constant_dynamic-update-slice_fusion.refs_0_), channel_id=1, source_target_pairs={{0,6},{2,4},{4,2},{6,0},{8,14},{10,12},{12,10},{14,8},{16,22},{18,... | collective-permute-start | bytes 393224 | tf_op jit(solution)/shard_map/ppermute | solution.py:32
  43.9 7.5 %collective-permute-start.14 = (bf16[2,256,128]{2,1,0:T(8,128)(2,1)S(1)}, bf16[2,256,128]{2,1,0:T(8,128)(2,1)S(1)}, u32[]{:S(2)}, u32[]{:S(2)}) collective-permute-start(bf16[2,256,128]{2,1,0:T(8,128)(2,1)S(1)} %constant_dynamic-update-slice_fusion.refs_0_), channel_id=1, source_target_pairs={{0,4},{2,6},{4,0},{6,2},{8,12},{10,14},{12,8},{14,10},{16,20},{18,... | collective-permute-start | bytes 393224 | tf_op jit(solution)/shard_map/ppermute | solution.py:32
  45.2 7.1 %collective-permute-start.19 = (bf16[2,256,128]{2,1,0:T(8,128)(2,1)S(1)}, bf16[2,256,128]{2,1,0:T(8,128)(2,1)S(1)}, u32[]{:S(2)}, u32[]{:S(2)}) collective-permute-start(bf16[2,256,128]{2,1,0:T(8,128)(2,1)S(1)} %constant_dynamic-update-slice_fusion.refs_0_), channel_id=1, source_target_pairs={{0,2},{2,0},{4,6},{6,4},{8,10},{10,8},{12,14},{14,12},{16,18},{18,... | collective-permute-start | bytes 393224 | tf_op jit(solution)/shard_map/ppermute | solution.py:32
  (4 other events, 8.4 us)

commit v12 on v11

--- a/solution.py
+++ b/solution.py
@@ -271,15 +271,19 @@
     sums[: len(far)], x, scale = after(sums[: len(far)], x, scale)
     blocks = [weight_rows(0)]
     sums, key_rows, blocks, x, scale, gain = after(sums, key_rows, blocks, x, scale, gain)
-    mean_weights = sum(sums, total[0]) / replicas
-    change = anchor - mean_weights
-    new_momentum = momentum_rate * momentum + change
-    new_anchor = anchor - outer_rate * (change + momentum_rate * new_momentum)
-    outgoing = new_anchor.astype(jnp.bfloat16)[None]
+
+    def update(parts, anchor, momentum):
+        change = anchor - sum(parts) / replicas
+        new_momentum = momentum_rate * momentum + change
+        new_anchor = anchor - outer_rate * (change + momentum_rate * new_momentum)
+        return new_anchor, new_momentum
+
+    parts = [total[0], *sums]
+    outgoing = update(parts, anchor, momentum)[0].astype(jnp.bfloat16)[None]
 
     mate = swap(outgoing, "rep", PLANE)
     column = [swap(outgoing, "rep", k) for k in far_side]
-    mate, x = after(mate, x)
+    mate, x, parts, anchor, momentum = after(mate, x, parts, anchor, momentum)
     near = jnp.concatenate([outgoing, mate])
     near = [near] + [swap(near, "rep", p) for p in mates]
     blocks += [weight_rows(k) for k in range(1, cores)]
@@ -287,13 +291,12 @@
     rest = jnp.concatenate(column)
     rest = [rest] + [swap(rest, "rep", p) for p in mates]
     weight_grad = place_blocks(blocks)
-    near, weight_grad = after(near, weight_grad)
+    outer = update(parts, anchor, momentum)
+    near, weight_grad, (new_anchor, new_momentum) = after(near, weight_grad, outer)
     merged = merge(w, near, [[k + p for k in near_side] for p in range(PLANE)])
     places = [[k + p for k in far_side] for p in range(PLANE)]
-    rest[2:], merged, weight_grad = after(rest[2:], merged, weight_grad)
-    merged = merge(w, [rest[0], *rest[2:]], [places[0], *places[2:]], merged)
-    last, merged = after(rest[1], merged)
-    merged = merge(w, [last], places[1:2], merged)
+    weight_grad, merged, *rest = after(weight_grad, merged, *rest)
+    merged = merge(w, rest, places, merged)
     return (key_rows, weight_grad, merged, new_anchor, new_momentum)
 
 

time: 53.2 us -> 52.1 us (0.979)
  Pallas kernels: 7.25 us -> 6.6 us
  waiting for transfers between devices: 8.18 us -> 7.54 us
    add x0 -> x1, other arithmetic: none -> 0.74 us  [update(): new_momentum = momentum_rate * momentum + change]
    broadcast_in_dim x1, other arithmetic: 0.75 us -> 0.05 us  [body(): outgoing = update(parts, anchor, momentum)[0].astype(jnp.bfloat16)[None]]
    pallas_call x3 -> x2, Pallas kernels: 2.45 us -> 1.8 us  [merge(): pl.pallas_call(functools.partial(merge_kernel, offsets), out_shape=jax.Sh...]
    ppermute x20, waiting for transfers between devices: 8.18 us -> 7.54 us  [swap(): return lax.ppermute(value, axis, [(i, i ^ offset) for i in range(size)])]
  transfers between devices with their start and end apart: 20 -> 20, of which waited for: 7 -> 8; matrix products, arithmetic and copies ran while one was open for 12% -> 14% of each run, Pallas kernels for 12% -> 11%
where the time goes in v12:
time: 52.1 us; the launch traced here: 51.8 us
  starting transfers between devices  25.2 us (48%)
  waiting for transfers between devices  7.54 us (14%)
  Pallas kernels  6.6 us (13%)
  matrix products  6.29 us (12%)
  local copies, waits for them, and re-layouts  4.33 us (8%)
  other arithmetic  0.98 us (2%)
  between operations  0.84 us (2%)
    ppermute x20, starting transfers between devices, swap(): return lax.ppermute(value, axis, [(i, i ^ offset) for i in range(size)])  25.2 us
    ppermute x20, waiting for transfers between devices, swap(): return lax.ppermute(value, axis, [(i, i ^ offset) for i in range(size)])  7.54 us
    unnamed x17, local copies, waits for them, and re-layouts  4.29 us
    dot_general x2, matrix products, weight_rows(): lax.dot_general(norm, raw_grad, (((0,), (0,)), ((), ())), preferred_eleme...  3.59 us
    dot_general x2, matrix products, key_part(): return jnp.dot(norm, halves[k], preferred_element_type=jnp.float32)  2.71 us
    pallas_call x2, Pallas kernels, squares_of(): pl.pallas_call(squares_kernel, out_shape=jax.ShapeDtypeStruct((1, rows),...  2.31 us
    pallas_call x2, Pallas kernels, merge(): pl.pallas_call(functools.partial(merge_kernel, offsets), out_shape=jax.Sh...  1.8 us
    pallas_call x1, Pallas kernels, place_blocks(): pl.pallas_call(place_kernel, out_shape=jax.ShapeDtypeStruct((len(blocks)...  1.05 us
  transfers between devices with their start and end apart: 20, of which 8 were waited for; matrix products, arithmetic and copies ran while one was open for 14% of the time, Pallas kernels for 11%

profile of v12, /device:TPU:0, one launch (start us, length us, event | category | flops | bytes accessed | tf_op | source)
XLA Modules:
  0.0 51.8 jit_solution(14325826076105988568)
XLA Ops:
  1.2 1.2 %copy-done = bf16[4096,128]{1,0:T(8,128)(2,1)S(1)} copy-done((bf16[4096,128]{1,0:T(8,128)(2,1)S(1)}, bf16[4096,128]{1,0:T(8,128)(2,1)}, u32[]{:S(2)}) %copy-start) | copy-done | bytes 1048600
  2.5 2.6 %collective-permute-start = (bf16[2,256,128]{2,1,0:T(8,128)(2,1)S(1)}, bf16[2,256,128]{2,1,0:T(8,128)(2,1)S(1)}, u32[]{:S(2)}, u32[]{:S(2)}) collective-permute-start(bf16[2,256,128]{2,1,0:T(8,128)(2,1)S(1)} %get-tuple-element.96), channel_id=1, source_target_pairs={{0,2},{2,0},{4,6},{6,4},{8,10},{10,8},{12,14},{14,12},{16,18},{18,... | collective-permute-start | bytes 393224 | tf_op jit(solution)/shard_map/ppermute | solution.py:32
  5.1 1.5 %collective-permute-start.1 = (bf16[2,256,128]{2,1,0:T(8,128)(2,1)S(1)}, bf16[2,256,128]{2,1,0:T(8,128)(2,1)S(1)}, u32[]{:S(2)}, u32[]{:S(2)}) collective-permute-start(bf16[2,256,128]{2,1,0:T(8,128)(2,1)S(1)} %get-tuple-element.97), channel_id=1, source_target_pairs={{0,4},{2,6},{4,0},{6,2},{8,12},{10,14},{12,8},{14,10},{16,20},{18,... | collective-permute-start | bytes 393224 | tf_op jit(solution)/shard_map/ppermute | solution.py:32
  6.6 2.2 %copy-done.2 = bf16[1024,2048]{1,0:T(8,128)(2,1)S(1)} copy-done((bf16[1024,2048]{1,0:T(8,128)(2,1)S(1)}, bf16[1024,2048]{1,0:T(8,128)(2,1)}, u32[]{:S(2)}) %copy-start.2) | copy-done | bytes 4194328
  8.8 1.1 %shard_map.102 = f32[1,1024]{1,0:T(1,128)S(1)} custom-call(bf16[1024,2048]{1,0:T(8,128)(2,1)S(1)} %copy-done.2), custom_call_target="tpu_custom_call" | custom-call | flops 1 | bytes 1 | tf_op jit(solution)/shard_map/pallas_call | solution.py:119
  10.4 1.2 %shard_map.103 = f32[1,1024]{1,0:T(1,128)S(1)} custom-call(bf16[1024,2048]{1,0:T(8,128)(2,1)S(1)} %collective-permute-done.3.x_ref), custom_call_target="tpu_custom_call" | custom-call | flops 1 | bytes 1 | tf_op jit(solution)/shard_map/pallas_call | solution.py:119
  11.6 1.9 %collective-permute-done.1 = bf16[2,256,128]{2,1,0:T(8,128)(2,1)S(1)} collective-permute-done((bf16[2,256,128]{2,1,0:T(8,128)(2,1)S(1)}, bf16[2,256,128]{2,1,0:T(8,128)(2,1)S(1)}, u32[]{:S(2)}, u32[]{:S(2)}) %collective-permute-start.1) | collective-permute-done | bytes 131104 | tf_op jit(solution)/shard_map/ppermute | solution.py:32
  13.6 1.6 %collective-permute-start.4 = (f32[1,256,128]{2,1,0:T(8,128)S(1)}, f32[1,256,128]{2,1,0:T(8,128)S(1)}, u32[]{:S(2)}, u32[]{:S(2)}) collective-permute-start(f32[1,256,128]{2,1,0:T(8,128)S(1)} %slice.17), channel_id=1, source_target_pairs={{0,8},{2,10},{4,12},{6,14},{8,0},{10,2},{12,4},{14,6},{16,24},{18,... | collective-permute-start | bytes 393224 | tf_op jit(solution)/shard_map/ppermute | solution.py:32
  15.2 1.2 %collective-permute-start.6 = (bf16[2,256,128]{2,1,0:T(8,128)(2,1)S(1)}, bf16[2,256,128]{2,1,0:T(8,128)(2,1)S(1)}, u32[]{:S(2)}, u32[]{:S(2)}) collective-permute-start(bf16[2,256,128]{2,1,0:T(8,128)(2,1)S(1)} %get-tuple-element.110), channel_id=1, source_target_pairs={{0,2},{2,0},{4,6},{6,4},{8,10},{10,8},{12,14},{14,12},{16,18},{18,... | collective-permute-start | bytes 393224 | tf_op jit(solution)/shard_map/ppermute | solution.py:32
  17.3 1.4 %collective-permute-start.8 = (bf16[2,256,128]{2,1,0:T(8,128)(2,1)S(1)}, bf16[2,256,128]{2,1,0:T(8,128)(2,1)S(1)}, u32[]{:S(2)}, u32[]{:S(2)}) collective-permute-start(bf16[2,256,128]{2,1,0:T(8,128)(2,1)S(1)} %get-tuple-element.112), channel_id=1, source_target_pairs={{0,6},{2,4},{4,2},{6,0},{8,14},{10,12},{12,10},{14,8},{16,22},{18,... | collective-permute-start | bytes 393224 | tf_op jit(solution)/shard_map/ppermute | solution.py:32
  18.9 2.7 %collective-permute-start.5 = (f32[256,128]{1,0:T(8,128)S(1)}, f32[256,128]{1,0:T(8,128)S(1)}, u32[]{:S(2)}, u32[]{:S(2)}) collective-permute-start(f32[256,128]{1,0:T(8,128)S(1)} %fusion.17), channel_id=1, source_target_pairs={{0,16},{2,18},{4,20},{6,22},{8,24},{10,26},{12,28},{14,30},{16,0},... | collective-permute-start | bytes 393224 | tf_op jit(solution)/shard_map/ppermute | solution.py:32
  21.5 1.3 %fusion.1 = f32[1024,128]{1,0:T(8,128)S(1)} fusion(bf16[2048,128]{1,0:T(8,128)(2,1)S(1)} %get-tuple-element.118, bf16[1024,2048]{1,0:T(8,128)(2,1)S(1)} %collective-permute-done.3.x_ref, f32[2048]{0:T(1024)S(1)} %convert_element_type.75, f32[1024]{0:T(1024)S(1)} %add_rsqrt_fusion), kind=kOutput, calls=%fused_computation.5 | convolution fusion | flops 545259520 | bytes 5255168 | tf_op jit(solution)/shard_map/dot_general | solution.py:255
  23.7 1.4 %fusion.16.raw_ref = f32[1024,128]{1,0:T(8,128)S(1)} fusion(f32[1024,128]{1,0:T(8,128)S(1)} %fusion.1, bf16[2048,128]{1,0:T(8,128)(2,1)S(1)} %get-tuple-element.116, bf16[1024,2048]{1,0:T(8,128)(2,1)S(1)} %copy-done.3, f32[2048]{0:T(1024)S(1)} %convert_element_type.72, f32[1024]{0:T(1024)S(1)} %add_rsqrt_fusion), kind=kOutput, calls=%fused_computation.20 | convolution fusion | flops 545390592 | bytes 5779456 | tf_op jit(solution)/shard_map/dot_general | solution.py:255
  25.2 1.5 %collective-permute-start.10 = (f32[256,128]{1,0:T(8,128)S(1)}, f32[256,128]{1,0:T(8,128)S(1)}, u32[]{:S(2)}, u32[]{:S(2)}) collective-permute-start(f32[256,128]{1,0:T(8,128)S(1)} %get-tuple-element.168), channel_id=1, source_target_pairs={{0,8},{2,10},{4,12},{6,14},{8,0},{10,2},{12,4},{14,6},{16,24},{18,... | collective-permute-start | bytes 393224 | tf_op jit(solution)/shard_map/ppermute | solution.py:32
  28.5 1.8 %fusion.14.refs_0_ = bf16[2048,128]{1,0:T(8,128)(2,1)S(1)} fusion(bf16[1024,128]{1,0:T(8,128)(2,1)S(1)} %get-tuple-element.131, bf16[1024,2048]{1,0:T(8,128)(2,1)S(1)} %copy-done.3, f32[1024]{0:T(1024)S(1)} %add_rsqrt_fusion, f32[2048]{0:T(1024)S(1)} %convert_element_type.72), kind=kOutput, calls=%fused_computation.18 | convolution fusion | flops 545783808 | bytes 4993024 | tf_op jit(solution)/shard_map/dot_general | solution.py:259
  31.3 1.1 %collective-permute-start.11 = (bf16[1,256,128]{2,1,0:T(8,128)(2,1)S(1)}, bf16[1,256,128]{2,1,0:T(8,128)(2,1)S(1)}, u32[]{:S(2)}, u32[]{:S(2)}) collective-permute-start(bf16[1,256,128]{2,1,0:T(8,128)(2,1)S(1)} %fusion.18), channel_id=1, source_target_pairs={{0,8},{2,10},{4,12},{6,14},{8,0},{10,2},{12,4},{14,6},{16,24},{18,... | collective-permute-start | bytes 196616 | tf_op jit(solution)/shard_map/ppermute | solution.py:32
  32.5 2.5 %collective-permute-start.16 = (bf16[1,256,128]{2,1,0:T(8,128)(2,1)S(1)}, bf16[1,256,128]{2,1,0:T(8,128)(2,1)S(1)}, u32[]{:S(2)}, u32[]{:S(2)}) collective-permute-start(bf16[1,256,128]{2,1,0:T(8,128)(2,1)S(1)} %fusion.18), channel_id=1, source_target_pairs={{0,24},{2,26},{4,28},{6,30},{8,16},{10,18},{12,20},{14,22},{16,8},... | collective-permute-start | bytes 196616 | tf_op jit(solution)/shard_map/ppermute | solution.py:32
  35.7 1.6 %collective-permute-start.14 = (bf16[2,256,128]{2,1,0:T(8,128)(2,1)S(1)}, bf16[2,256,128]{2,1,0:T(8,128)(2,1)S(1)}, u32[]{:S(2)}, u32[]{:S(2)}) collective-permute-start(bf16[2,256,128]{2,1,0:T(8,128)(2,1)S(1)} %pad_maximum_fusion.refs_0_), channel_id=1, source_target_pairs={{0,6},{2,4},{4,2},{6,0},{8,14},{10,12},{12,10},{14,8},{16,22},{18,... | collective-permute-start | bytes 393224 | tf_op jit(solution)/shard_map/ppermute | solution.py:32
  37.3 1.2 %collective-permute-start.13 = (bf16[2,256,128]{2,1,0:T(8,128)(2,1)S(1)}, bf16[2,256,128]{2,1,0:T(8,128)(2,1)S(1)}, u32[]{:S(2)}, u32[]{:S(2)}) collective-permute-start(bf16[2,256,128]{2,1,0:T(8,128)(2,1)S(1)} %pad_maximum_fusion.refs_0_), channel_id=1, source_target_pairs={{0,4},{2,6},{4,0},{6,2},{8,12},{10,14},{12,8},{14,10},{16,20},{18,... | collective-permute-start | bytes 393224 | tf_op jit(solution)/shard_map/ppermute | solution.py:32
  39.3 1.8 %fusion.15.refs_1_ = bf16[2048,128]{1,0:T(8,128)(2,1)S(1)} fusion(bf16[1024,128]{1,0:T(8,128)(2,1)S(1)} %get-tuple-element.131, bf16[1024,2048]{1,0:T(8,128)(2,1)S(1)} %collective-permute-done.3.x_ref, f32[2048]{0:T(1024)S(1)} %convert_element_type.86, f32[1024]{0:T(1024)S(1)} %add_rsqrt_fusion), kind=kOutput, calls=%fused_computation.19 | convolution fusion | flops 545783808 | bytes 4993024 | tf_op jit(solution)/shard_map/dot_general | solution.py:259
  41.7 1.6 %collective-permute-start.19 = (bf16[2,256,128]{2,1,0:T(8,128)(2,1)S(1)}, bf16[2,256,128]{2,1,0:T(8,128)(2,1)S(1)}, u32[]{:S(2)}, u32[]{:S(2)}) collective-permute-start(bf16[2,256,128]{2,1,0:T(8,128)(2,1)S(1)} %constant_dynamic-update-slice_fusion.refs_0_), channel_id=1, source_target_pairs={{0,6},{2,4},{4,2},{6,0},{8,14},{10,12},{12,10},{14,8},{16,22},{18,... | collective-permute-start | bytes 393224 | tf_op jit(solution)/shard_map/ppermute | solution.py:32
  43.3 1.2 %collective-permute-start.18 = (bf16[2,256,128]{2,1,0:T(8,128)(2,1)S(1)}, bf16[2,256,128]{2,1,0:T(8,128)(2,1)S(1)}, u32[]{:S(2)}, u32[]{:S(2)}) collective-permute-start(bf16[2,256,128]{2,1,0:T(8,128)(2,1)S(1)} %constant_dynamic-update-slice_fusion.refs_0_), channel_id=1, source_target_pairs={{0,4},{2,6},{4,0},{6,2},{8,12},{10,14},{12,8},{14,10},{16,20},{18,... | collective-permute-start | bytes 393224 | tf_op jit(solution)/shard_map/ppermute | solution.py:32
  44.5 1.0 %shard_map.106 = bf16[4096,128]{1,0:T(8,128)(2,1)} custom-call(bf16[2048,128]{1,0:T(8,128)(2,1)S(1)} %fusion.14.refs_0_, bf16[2048,128]{1,0:T(8,128)(2,1)S(1)} %fusion.15.refs_1_), custom_call_target="tpu_custom_call" | custom-call | flops 1 | bytes 1 | tf_op jit(solution)/shard_map/pallas_call | solution.py:162
  48.3 2.5 %collective-permute-done.18.refs_2_ = bf16[2,256,128]{2,1,0:T(8,128)(2,1)S(1)} collective-permute-done((bf16[2,256,128]{2,1,0:T(8,128)(2,1)S(1)}, bf16[2,256,128]{2,1,0:T(8,128)(2,1)S(1)}, u32[]{:S(2)}, u32[]{:S(2)}) %collective-permute-start.18) | collective-permute-done | bytes 131104 | tf_op jit(solution)/shard_map/ppermute | solution.py:32
  (59 shorter events, 11.7 us)
Async XLA Ops:
  0.6 9.7 %collective-permute-start.3 = (bf16[1024,2048]{1,0:T(8,128)(2,1)}, bf16[1024,2048]{1,0:T(8,128)(2,1)S(1)}, u32[]{:S(2)}, u32[]{:S(2)}) collective-permute-start(bf16[1024,2048]{1,0:T(8,128)(2,1)} %x_ref), channel_id=1, source_target_pairs={{0,1},{1,0},{2,3},{3,2},{4,5},{5,4},{6,7},{7,6},{8,9},{9,8},{10,11... | collective-permute-start | bytes 12582920 | tf_op jit(solution)/shard_map/ppermute | solution.py:32
  2.4 7.6 %copy-start.4 = (bf16[1024,128]{1,0:T(8,128)(2,1)S(1)}, bf16[1024,128]{1,0:T(8,128)(2,1)}, u32[]{:S(2)}) copy-start(bf16[1024,128]{1,0:T(8,128)(2,1)} %grad_ref) | copy-start | bytes 786436
  2.5 9.1 %collective-permute-start = (bf16[2,256,128]{2,1,0:T(8,128)(2,1)S(1)}, bf16[2,256,128]{2,1,0:T(8,128)(2,1)S(1)}, u32[]{:S(2)}, u32[]{:S(2)}) collective-permute-start(bf16[2,256,128]{2,1,0:T(8,128)(2,1)S(1)} %get-tuple-element.96), channel_id=1, source_target_pairs={{0,2},{2,0},{4,6},{6,4},{8,10},{10,8},{12,14},{14,12},{16,18},{18,... | collective-permute-start | bytes 393224 | tf_op jit(solution)/shard_map/ppermute | solution.py:32
  5.1 8.4 %collective-permute-start.1 = (bf16[2,256,128]{2,1,0:T(8,128)(2,1)S(1)}, bf16[2,256,128]{2,1,0:T(8,128)(2,1)S(1)}, u32[]{:S(2)}, u32[]{:S(2)}) collective-permute-start(bf16[2,256,128]{2,1,0:T(8,128)(2,1)S(1)} %get-tuple-element.97), channel_id=1, source_target_pairs={{0,4},{2,6},{4,0},{6,2},{8,12},{10,14},{12,8},{14,10},{16,20},{18,... | collective-permute-start | bytes 393224 | tf_op jit(solution)/shard_map/ppermute | solution.py:32
  6.6 6.9 %collective-permute-start.2 = (bf16[2,256,128]{2,1,0:T(8,128)(2,1)S(1)}, bf16[2,256,128]{2,1,0:T(8,128)(2,1)S(1)}, u32[]{:S(2)}, u32[]{:S(2)}) collective-permute-start(bf16[2,256,128]{2,1,0:T(8,128)(2,1)S(1)} %get-tuple-element.98), channel_id=1, source_target_pairs={{0,6},{2,4},{4,2},{6,0},{8,14},{10,12},{12,10},{14,8},{16,22},{18,... | collective-permute-start | bytes 393224 | tf_op jit(solution)/shard_map/ppermute | solution.py:32
  8.8 9.9 %copy-start.7 = (bf16[2048]{0:T(1024)(128)(2,1)S(1)}, bf16[2048]{0:T(1024)(128)(2,1)}, u32[]{:S(2)}) copy-start(bf16[2048]{0:T(1024)(128)(2,1)} %param.7) | copy-start | bytes 12292
  13.6 5.1 %collective-permute-start.4 = (f32[1,256,128]{2,1,0:T(8,128)S(1)}, f32[1,256,128]{2,1,0:T(8,128)S(1)}, u32[]{:S(2)}, u32[]{:S(2)}) collective-permute-start(f32[1,256,128]{2,1,0:T(8,128)S(1)} %slice.17), channel_id=1, source_target_pairs={{0,8},{2,10},{4,12},{6,14},{8,0},{10,2},{12,4},{14,6},{16,24},{18,... | collective-permute-start | bytes 393224 | tf_op jit(solution)/shard_map/ppermute | solution.py:32
  15.2 9.9 %collective-permute-start.6 = (bf16[2,256,128]{2,1,0:T(8,128)(2,1)S(1)}, bf16[2,256,128]{2,1,0:T(8,128)(2,1)S(1)}, u32[]{:S(2)}, u32[]{:S(2)}) collective-permute-start(bf16[2,256,128]{2,1,0:T(8,128)(2,1)S(1)} %get-tuple-element.110), channel_id=1, source_target_pairs={{0,2},{2,0},{4,6},{6,4},{8,10},{10,8},{12,14},{14,12},{16,18},{18,... | collective-permute-start | bytes 393224 | tf_op jit(solution)/shard_map/ppermute | solution.py:32
  16.5 8.6 %collective-permute-start.7 = (bf16[2,256,128]{2,1,0:T(8,128)(2,1)S(1)}, bf16[2,256,128]{2,1,0:T(8,128)(2,1)S(1)}, u32[]{:S(2)}, u32[]{:S(2)}) collective-permute-start(bf16[2,256,128]{2,1,0:T(8,128)(2,1)S(1)} %get-tuple-element.111), channel_id=1, source_target_pairs={{0,4},{2,6},{4,0},{6,2},{8,12},{10,14},{12,8},{14,10},{16,20},{18,... | collective-permute-start | bytes 393224 | tf_op jit(solution)/shard_map/ppermute | solution.py:32
  17.3 7.8 %collective-permute-start.8 = (bf16[2,256,128]{2,1,0:T(8,128)(2,1)S(1)}, bf16[2,256,128]{2,1,0:T(8,128)(2,1)S(1)}, u32[]{:S(2)}, u32[]{:S(2)}) collective-permute-start(bf16[2,256,128]{2,1,0:T(8,128)(2,1)S(1)} %get-tuple-element.112), channel_id=1, source_target_pairs={{0,6},{2,4},{4,2},{6,0},{8,14},{10,12},{12,10},{14,8},{16,22},{18,... | collective-permute-start | bytes 393224 | tf_op jit(solution)/shard_map/ppermute | solution.py:32
  18.8 2.8 %collective-permute-start.9 = (bf16[2048]{0:T(1024)(128)(2,1)S(1)}, bf16[2048]{0:T(1024)(128)(2,1)S(1)}, u32[]{:S(2)}, u32[]{:S(2)}) collective-permute-start(bf16[2048]{0:T(1024)(128)(2,1)S(1)} %copy-done.7), channel_id=1, source_target_pairs={{0,1},{1,0},{2,3},{3,2},{4,5},{5,4},{6,7},{7,6},{8,9},{9,8},{10,11... | collective-permute-start | bytes 12296 | tf_op jit(solution)/shard_map/ppermute | solution.py:32
  18.9 9.7 %collective-permute-start.5 = (f32[256,128]{1,0:T(8,128)S(1)}, f32[256,128]{1,0:T(8,128)S(1)}, u32[]{:S(2)}, u32[]{:S(2)}) collective-permute-start(f32[256,128]{1,0:T(8,128)S(1)} %fusion.17), channel_id=1, source_target_pairs={{0,16},{2,18},{4,20},{6,22},{8,24},{10,26},{12,28},{14,30},{16,0},... | collective-permute-start | bytes 393224 | tf_op jit(solution)/shard_map/ppermute | solution.py:32
  25.2 6.1 %collective-permute-start.10 = (f32[256,128]{1,0:T(8,128)S(1)}, f32[256,128]{1,0:T(8,128)S(1)}, u32[]{:S(2)}, u32[]{:S(2)}) collective-permute-start(f32[256,128]{1,0:T(8,128)S(1)} %get-tuple-element.168), channel_id=1, source_target_pairs={{0,8},{2,10},{4,12},{6,14},{8,0},{10,2},{12,4},{14,6},{16,24},{18,... | collective-permute-start | bytes 393224 | tf_op jit(solution)/shard_map/ppermute | solution.py:32
  28.5 2.8 %copy-start.6 = (f32[256,128]{1,0:T(8,128)S(1)}, f32[256,128]{1,0:T(8,128)}, u32[]{:S(2)}) copy-start(f32[256,128]{1,0:T(8,128)} %param.10) | copy-start | bytes 393220
  31.3 4.3 %collective-permute-start.11 = (bf16[1,256,128]{2,1,0:T(8,128)(2,1)S(1)}, bf16[1,256,128]{2,1,0:T(8,128)(2,1)S(1)}, u32[]{:S(2)}, u32[]{:S(2)}) collective-permute-start(bf16[1,256,128]{2,1,0:T(8,128)(2,1)S(1)} %fusion.18), channel_id=1, source_target_pairs={{0,8},{2,10},{4,12},{6,14},{8,0},{10,2},{12,4},{14,6},{16,24},{18,... | collective-permute-start | bytes 196616 | tf_op jit(solution)/shard_map/ppermute | solution.py:32
  32.5 8.6 %collective-permute-start.16 = (bf16[1,256,128]{2,1,0:T(8,128)(2,1)S(1)}, bf16[1,256,128]{2,1,0:T(8,128)(2,1)S(1)}, u32[]{:S(2)}, u32[]{:S(2)}) collective-permute-start(bf16[1,256,128]{2,1,0:T(8,128)(2,1)S(1)} %fusion.18), channel_id=1, source_target_pairs={{0,24},{2,26},{4,28},{6,30},{8,16},{10,18},{12,20},{14,22},{16,8},... | collective-permute-start | bytes 196616 | tf_op jit(solution)/shard_map/ppermute | solution.py:32
  35.0 6.7 %collective-permute-start.15 = (bf16[1,256,128]{2,1,0:T(8,128)(2,1)S(1)}, bf16[1,256,128]{2,1,0:T(8,128)(2,1)S(1)}, u32[]{:S(2)}, u32[]{:S(2)}) collective-permute-start(bf16[1,256,128]{2,1,0:T(8,128)(2,1)S(1)} %fusion.18), channel_id=1, source_target_pairs={{0,16},{2,18},{4,20},{6,22},{8,24},{10,26},{12,28},{14,30},{16,0},... | collective-permute-start | bytes 196616 | tf_op jit(solution)/shard_map/ppermute | solution.py:32
  35.7 9.9 %collective-permute-start.14 = (bf16[2,256,128]{2,1,0:T(8,128)(2,1)S(1)}, bf16[2,256,128]{2,1,0:T(8,128)(2,1)S(1)}, u32[]{:S(2)}, u32[]{:S(2)}) collective-permute-start(bf16[2,256,128]{2,1,0:T(8,128)(2,1)S(1)} %pad_maximum_fusion.refs_0_), channel_id=1, source_target_pairs={{0,6},{2,4},{4,2},{6,0},{8,14},{10,12},{12,10},{14,8},{16,22},{18,... | collective-permute-start | bytes 393224 | tf_op jit(solution)/shard_map/ppermute | solution.py:32
  37.3 9.8 %collective-permute-start.13 = (bf16[2,256,128]{2,1,0:T(8,128)(2,1)S(1)}, bf16[2,256,128]{2,1,0:T(8,128)(2,1)S(1)}, u32[]{:S(2)}, u32[]{:S(2)}) collective-permute-start(bf16[2,256,128]{2,1,0:T(8,128)(2,1)S(1)} %pad_maximum_fusion.refs_0_), channel_id=1, source_target_pairs={{0,4},{2,6},{4,0},{6,2},{8,12},{10,14},{12,8},{14,10},{16,20},{18,... | collective-permute-start | bytes 393224 | tf_op jit(solution)/shard_map/ppermute | solution.py:32
  38.5 8.6 %collective-permute-start.12 = (bf16[2,256,128]{2,1,0:T(8,128)(2,1)S(1)}, bf16[2,256,128]{2,1,0:T(8,128)(2,1)S(1)}, u32[]{:S(2)}, u32[]{:S(2)}) collective-permute-start(bf16[2,256,128]{2,1,0:T(8,128)(2,1)S(1)} %pad_maximum_fusion.refs_0_), channel_id=1, source_target_pairs={{0,2},{2,0},{4,6},{6,4},{8,10},{10,8},{12,14},{14,12},{16,18},{18,... | collective-permute-start | bytes 393224 | tf_op jit(solution)/shard_map/ppermute | solution.py:32
  39.2 7.8 %copy-start.1 = (bf16[4096,128]{1,0:T(8,128)(2,1)S(1)}, bf16[4096,128]{1,0:T(8,128)(2,1)}, u32[]{:S(2)}) copy-start(bf16[4096,128]{1,0:T(8,128)(2,1)} %w_ref.3) | copy-start | bytes 3145732
  41.7 6.6 %collective-permute-start.19 = (bf16[2,256,128]{2,1,0:T(8,128)(2,1)S(1)}, bf16[2,256,128]{2,1,0:T(8,128)(2,1)S(1)}, u32[]{:S(2)}, u32[]{:S(2)}) collective-permute-start(bf16[2,256,128]{2,1,0:T(8,128)(2,1)S(1)} %constant_dynamic-update-slice_fusion.refs_0_), channel_id=1, source_target_pairs={{0,6},{2,4},{4,2},{6,0},{8,14},{10,12},{12,10},{14,8},{16,22},{18,... | collective-permute-start | bytes 393224 | tf_op jit(solution)/shard_map/ppermute | solution.py:32
  43.3 7.5 %collective-permute-start.18 = (bf16[2,256,128]{2,1,0:T(8,128)(2,1)S(1)}, bf16[2,256,128]{2,1,0:T(8,128)(2,1)S(1)}, u32[]{:S(2)}, u32[]{:S(2)}) collective-permute-start(bf16[2,256,128]{2,1,0:T(8,128)(2,1)S(1)} %constant_dynamic-update-slice_fusion.refs_0_), channel_id=1, source_target_pairs={{0,4},{2,6},{4,0},{6,2},{8,12},{10,14},{12,8},{14,10},{16,20},{18,... | collective-permute-start | bytes 393224 | tf_op jit(solution)/shard_map/ppermute | solution.py:32
  45.6 5.4 %collective-permute-start.17 = (bf16[2,256,128]{2,1,0:T(8,128)(2,1)S(1)}, bf16[2,256,128]{2,1,0:T(8,128)(2,1)S(1)}, u32[]{:S(2)}, u32[]{:S(2)}) collective-permute-start(bf16[2,256,128]{2,1,0:T(8,128)(2,1)S(1)} %constant_dynamic-update-slice_fusion.refs_0_), channel_id=1, source_target_pairs={{0,2},{2,0},{4,6},{6,4},{8,10},{10,8},{12,14},{14,12},{16,18},{18,... | collective-permute-start | bytes 393224 | tf_op jit(solution)/shard_map/ppermute | solution.py:32
  (4 other events, 8.4 us)

commit v13 on v12

--- a/solution.py
+++ b/solution.py
@@ -236,8 +236,8 @@
         first, second, halves, local_weights, tokens, key_grad
     )
     x[0] = own
-    first_in = [swap(first[p], "rep", p) for p in mates]
-    second_in = [swap(second[p], "rep", p) for p in mates]
+    first_in = [swap(first[p], "rep", p) for p in reversed(mates)]
+    second_in = [swap(second[p], "rep", p) for p in reversed(mates)]
     cosine, signed, raw_grad = prepare(key_grad)
     squares = sum(squares_of(block) for block in x)
 

time: 52.1 us -> 52.1 us (level)
  transfers between devices with their start and end apart: 20 -> 20, of which waited for: 8 -> 10; matrix products, arithmetic and copies ran while one was open for 14% -> 14% of each run, Pallas kernels for 11% -> 11%
where the time goes in v13:
time: 52.1 us; the launch traced here: 51.9 us
  starting transfers between devices  25.6 us (49%)
  waiting for transfers between devices  7.22 us (14%)
  Pallas kernels  6.6 us (13%)
  matrix products  6.29 us (12%)
  local copies, waits for them, and re-layouts  4.34 us (8%)
  other arithmetic  0.98 us (2%)
  between operations  0.84 us (2%)
    ppermute x20, starting transfers between devices, swap(): return lax.ppermute(value, axis, [(i, i ^ offset) for i in range(size)])  25.6 us
    ppermute x20, waiting for transfers between devices, swap(): return lax.ppermute(value, axis, [(i, i ^ offset) for i in range(size)])  7.22 us
    unnamed x17, local copies, waits for them, and re-layouts  4.3 us
    dot_general x2, matrix products, weight_rows(): lax.dot_general(norm, raw_grad, (((0,), (0,)), ((), ())), preferred_eleme...  3.59 us
    dot_general x2, matrix products, key_part(): return jnp.dot(norm, halves[k], preferred_element_type=jnp.float32)  2.7 us
    pallas_call x2, Pallas kernels, squares_of(): pl.pallas_call(squares_kernel, out_shape=jax.ShapeDtypeStruct((1, rows),...  2.31 us
    pallas_call x2, Pallas kernels, merge(): pl.pallas_call(functools.partial(merge_kernel, offsets), out_shape=jax.Sh...  1.8 us
    pallas_call x1, Pallas kernels, place_blocks(): pl.pallas_call(place_kernel, out_shape=jax.ShapeDtypeStruct((len(blocks)...  1.05 us
  transfers between devices with their start and end apart: 20, of which 10 were waited for; matrix products, arithmetic and copies ran while one was open for 14% of the time, Pallas kernels for 11%

profile of v13, /device:TPU:0, one launch (start us, length us, event | category | flops | bytes accessed | tf_op | source)
XLA Modules:
  0.0 51.9 jit_solution(2706839516698759999)
XLA Ops:
  1.2 1.2 %copy-done = bf16[4096,128]{1,0:T(8,128)(2,1)S(1)} copy-done((bf16[4096,128]{1,0:T(8,128)(2,1)S(1)}, bf16[4096,128]{1,0:T(8,128)(2,1)}, u32[]{:S(2)}) %copy-start) | copy-done | bytes 1048600
  2.5 3.5 %collective-permute-start = (bf16[2,256,128]{2,1,0:T(8,128)(2,1)S(1)}, bf16[2,256,128]{2,1,0:T(8,128)(2,1)S(1)}, u32[]{:S(2)}, u32[]{:S(2)}) collective-permute-start(bf16[2,256,128]{2,1,0:T(8,128)(2,1)S(1)} %get-tuple-element.96), channel_id=1, source_target_pairs={{0,6},{2,4},{4,2},{6,0},{8,14},{10,12},{12,10},{14,8},{16,22},{18,... | collective-permute-start | bytes 393224 | tf_op jit(solution)/shard_map/ppermute | solution.py:32
  6.7 2.2 %copy-done.2 = bf16[1024,2048]{1,0:T(8,128)(2,1)S(1)} copy-done((bf16[1024,2048]{1,0:T(8,128)(2,1)S(1)}, bf16[1024,2048]{1,0:T(8,128)(2,1)}, u32[]{:S(2)}) %copy-start.2) | copy-done | bytes 4194328
  8.9 1.1 %shard_map.102 = f32[1,1024]{1,0:T(1,128)S(1)} custom-call(bf16[1024,2048]{1,0:T(8,128)(2,1)S(1)} %copy-done.2), custom_call_target="tpu_custom_call" | custom-call | flops 1 | bytes 1 | tf_op jit(solution)/shard_map/pallas_call | solution.py:119
  10.4 1.2 %shard_map.103 = f32[1,1024]{1,0:T(1,128)S(1)} custom-call(bf16[1024,2048]{1,0:T(8,128)(2,1)S(1)} %collective-permute-done.3.x_ref), custom_call_target="tpu_custom_call" | custom-call | flops 1 | bytes 1 | tf_op jit(solution)/shard_map/pallas_call | solution.py:119
  11.6 1.4 %collective-permute-done.1 = bf16[2,256,128]{2,1,0:T(8,128)(2,1)S(1)} collective-permute-done((bf16[2,256,128]{2,1,0:T(8,128)(2,1)S(1)}, bf16[2,256,128]{2,1,0:T(8,128)(2,1)S(1)}, u32[]{:S(2)}, u32[]{:S(2)}) %collective-permute-start.1) | collective-permute-done | bytes 131104 | tf_op jit(solution)/shard_map/ppermute | solution.py:32
  13.4 1.6 %collective-permute-start.4 = (f32[1,256,128]{2,1,0:T(8,128)S(1)}, f32[1,256,128]{2,1,0:T(8,128)S(1)}, u32[]{:S(2)}, u32[]{:S(2)}) collective-permute-start(f32[1,256,128]{2,1,0:T(8,128)S(1)} %slice.17), channel_id=1, source_target_pairs={{0,8},{2,10},{4,12},{6,14},{8,0},{10,2},{12,4},{14,6},{16,24},{18,... | collective-permute-start | bytes 393224 | tf_op jit(solution)/shard_map/ppermute | solution.py:32
  15.0 1.6 %collective-permute-start.6 = (bf16[2,256,128]{2,1,0:T(8,128)(2,1)S(1)}, bf16[2,256,128]{2,1,0:T(8,128)(2,1)S(1)}, u32[]{:S(2)}, u32[]{:S(2)}) collective-permute-start(bf16[2,256,128]{2,1,0:T(8,128)(2,1)S(1)} %get-tuple-element.110), channel_id=1, source_target_pairs={{0,6},{2,4},{4,2},{6,0},{8,14},{10,12},{12,10},{14,8},{16,22},{18,... | collective-permute-start | bytes 393224 | tf_op jit(solution)/shard_map/ppermute | solution.py:32
  16.7 1.3 %collective-permute-start.7 = (bf16[2,256,128]{2,1,0:T(8,128)(2,1)S(1)}, bf16[2,256,128]{2,1,0:T(8,128)(2,1)S(1)}, u32[]{:S(2)}, u32[]{:S(2)}) collective-permute-start(bf16[2,256,128]{2,1,0:T(8,128)(2,1)S(1)} %get-tuple-element.111), channel_id=1, source_target_pairs={{0,4},{2,6},{4,0},{6,2},{8,12},{10,14},{12,8},{14,10},{16,20},{18,... | collective-permute-start | bytes 393224 | tf_op jit(solution)/shard_map/ppermute | solution.py:32
  18.8 2.8 %collective-permute-start.5 = (f32[256,128]{1,0:T(8,128)S(1)}, f32[256,128]{1,0:T(8,128)S(1)}, u32[]{:S(2)}, u32[]{:S(2)}) collective-permute-start(f32[256,128]{1,0:T(8,128)S(1)} %fusion.17), channel_id=1, source_target_pairs={{0,16},{2,18},{4,20},{6,22},{8,24},{10,26},{12,28},{14,30},{16,0},... | collective-permute-start | bytes 393224 | tf_op jit(solution)/shard_map/ppermute | solution.py:32
  21.6 1.3 %fusion.1 = f32[1024,128]{1,0:T(8,128)S(1)} fusion(bf16[2048,128]{1,0:T(8,128)(2,1)S(1)} %get-tuple-element.118, bf16[1024,2048]{1,0:T(8,128)(2,1)S(1)} %collective-permute-done.3.x_ref, f32[2048]{0:T(1024)S(1)} %convert_element_type.75, f32[1024]{0:T(1024)S(1)} %add_rsqrt_fusion), kind=kOutput, calls=%fused_computation.5 | convolution fusion | flops 545259520 | bytes 5255168 | tf_op jit(solution)/shard_map/dot_general | solution.py:255
  23.8 1.4 %fusion.16.raw_ref = f32[1024,128]{1,0:T(8,128)S(1)} fusion(f32[1024,128]{1,0:T(8,128)S(1)} %fusion.1, bf16[2048,128]{1,0:T(8,128)(2,1)S(1)} %get-tuple-element.116, bf16[1024,2048]{1,0:T(8,128)(2,1)S(1)} %copy-done.3, f32[2048]{0:T(1024)S(1)} %convert_element_type.72, f32[1024]{0:T(1024)S(1)} %add_rsqrt_fusion), kind=kOutput, calls=%fused_computation.20 | convolution fusion | flops 545390592 | bytes 5779456 | tf_op jit(solution)/shard_map/dot_general | solution.py:255
  25.3 1.6 %collective-permute-start.10 = (f32[256,128]{1,0:T(8,128)S(1)}, f32[256,128]{1,0:T(8,128)S(1)}, u32[]{:S(2)}, u32[]{:S(2)}) collective-permute-start(f32[256,128]{1,0:T(8,128)S(1)} %get-tuple-element.168), channel_id=1, source_target_pairs={{0,8},{2,10},{4,12},{6,14},{8,0},{10,2},{12,4},{14,6},{16,24},{18,... | collective-permute-start | bytes 393224 | tf_op jit(solution)/shard_map/ppermute | solution.py:32
  28.5 1.8 %fusion.14.refs_0_ = bf16[2048,128]{1,0:T(8,128)(2,1)S(1)} fusion(bf16[1024,128]{1,0:T(8,128)(2,1)S(1)} %get-tuple-element.131, bf16[1024,2048]{1,0:T(8,128)(2,1)S(1)} %copy-done.3, f32[1024]{0:T(1024)S(1)} %add_rsqrt_fusion, f32[2048]{0:T(1024)S(1)} %convert_element_type.72), kind=kOutput, calls=%fused_computation.18 | convolution fusion | flops 545783808 | bytes 4993024 | tf_op jit(solution)/shard_map/dot_general | solution.py:259
  30.3 1.0 %collective-permute-done.10 = f32[256,128]{1,0:T(8,128)S(1)} collective-permute-done((f32[256,128]{1,0:T(8,128)S(1)}, f32[256,128]{1,0:T(8,128)S(1)}, u32[]{:S(2)}, u32[]{:S(2)}) %collective-permute-start.10) | collective-permute-done | bytes 131104 | tf_op jit(solution)/shard_map/ppermute | solution.py:32
  31.3 1.3 %collective-permute-start.11 = (bf16[1,256,128]{2,1,0:T(8,128)(2,1)S(1)}, bf16[1,256,128]{2,1,0:T(8,128)(2,1)S(1)}, u32[]{:S(2)}, u32[]{:S(2)}) collective-permute-start(bf16[1,256,128]{2,1,0:T(8,128)(2,1)S(1)} %fusion.18), channel_id=1, source_target_pairs={{0,8},{2,10},{4,12},{6,14},{8,0},{10,2},{12,4},{14,6},{16,24},{18,... | collective-permute-start | bytes 196616 | tf_op jit(solution)/shard_map/ppermute | solution.py:32
  32.6 2.4 %collective-permute-start.16 = (bf16[1,256,128]{2,1,0:T(8,128)(2,1)S(1)}, bf16[1,256,128]{2,1,0:T(8,128)(2,1)S(1)}, u32[]{:S(2)}, u32[]{:S(2)}) collective-permute-start(bf16[1,256,128]{2,1,0:T(8,128)(2,1)S(1)} %fusion.18), channel_id=1, source_target_pairs={{0,24},{2,26},{4,28},{6,30},{8,16},{10,18},{12,20},{14,22},{16,8},... | collective-permute-start | bytes 196616 | tf_op jit(solution)/shard_map/ppermute | solution.py:32
  35.7 1.5 %collective-permute-start.14 = (bf16[2,256,128]{2,1,0:T(8,128)(2,1)S(1)}, bf16[2,256,128]{2,1,0:T(8,128)(2,1)S(1)}, u32[]{:S(2)}, u32[]{:S(2)}) collective-permute-start(bf16[2,256,128]{2,1,0:T(8,128)(2,1)S(1)} %pad_maximum_fusion.refs_0_), channel_id=1, source_target_pairs={{0,6},{2,4},{4,2},{6,0},{8,14},{10,12},{12,10},{14,8},{16,22},{18,... | collective-permute-start | bytes 393224 | tf_op jit(solution)/shard_map/ppermute | solution.py:32
  37.2 1.6 %collective-permute-start.13 = (bf16[2,256,128]{2,1,0:T(8,128)(2,1)S(1)}, bf16[2,256,128]{2,1,0:T(8,128)(2,1)S(1)}, u32[]{:S(2)}, u32[]{:S(2)}) collective-permute-start(bf16[2,256,128]{2,1,0:T(8,128)(2,1)S(1)} %pad_maximum_fusion.refs_0_), channel_id=1, source_target_pairs={{0,4},{2,6},{4,0},{6,2},{8,12},{10,14},{12,8},{14,10},{16,20},{18,... | collective-permute-start | bytes 393224 | tf_op jit(solution)/shard_map/ppermute | solution.py:32
  39.2 1.8 %fusion.15.refs_1_ = bf16[2048,128]{1,0:T(8,128)(2,1)S(1)} fusion(bf16[1024,128]{1,0:T(8,128)(2,1)S(1)} %get-tuple-element.131, bf16[1024,2048]{1,0:T(8,128)(2,1)S(1)} %collective-permute-done.3.x_ref, f32[2048]{0:T(1024)S(1)} %convert_element_type.86, f32[1024]{0:T(1024)S(1)} %add_rsqrt_fusion), kind=kOutput, calls=%fused_computation.19 | convolution fusion | flops 545783808 | bytes 4993024 | tf_op jit(solution)/shard_map/dot_general | solution.py:259
  41.8 1.4 %collective-permute-start.19 = (bf16[2,256,128]{2,1,0:T(8,128)(2,1)S(1)}, bf16[2,256,128]{2,1,0:T(8,128)(2,1)S(1)}, u32[]{:S(2)}, u32[]{:S(2)}) collective-permute-start(bf16[2,256,128]{2,1,0:T(8,128)(2,1)S(1)} %constant_dynamic-update-slice_fusion.refs_0_), channel_id=1, source_target_pairs={{0,6},{2,4},{4,2},{6,0},{8,14},{10,12},{12,10},{14,8},{16,22},{18,... | collective-permute-start | bytes 393224 | tf_op jit(solution)/shard_map/ppermute | solution.py:32
  43.2 1.6 %collective-permute-start.18 = (bf16[2,256,128]{2,1,0:T(8,128)(2,1)S(1)}, bf16[2,256,128]{2,1,0:T(8,128)(2,1)S(1)}, u32[]{:S(2)}, u32[]{:S(2)}) collective-permute-start(bf16[2,256,128]{2,1,0:T(8,128)(2,1)S(1)} %constant_dynamic-update-slice_fusion.refs_0_), channel_id=1, source_target_pairs={{0,4},{2,6},{4,0},{6,2},{8,12},{10,14},{12,8},{14,10},{16,20},{18,... | collective-permute-start | bytes 393224 | tf_op jit(solution)/shard_map/ppermute | solution.py:32
  44.8 1.0 %shard_map.106 = bf16[4096,128]{1,0:T(8,128)(2,1)} custom-call(bf16[2048,128]{1,0:T(8,128)(2,1)S(1)} %fusion.14.refs_0_, bf16[2048,128]{1,0:T(8,128)(2,1)S(1)} %fusion.15.refs_1_), custom_call_target="tpu_custom_call" | custom-call | flops 1 | bytes 1 | tf_op jit(solution)/shard_map/pallas_call | solution.py:162
  48.5 2.4 %collective-permute-done.18.refs_2_ = bf16[2,256,128]{2,1,0:T(8,128)(2,1)S(1)} collective-permute-done((bf16[2,256,128]{2,1,0:T(8,128)(2,1)S(1)}, bf16[2,256,128]{2,1,0:T(8,128)(2,1)S(1)}, u32[]{:S(2)}, u32[]{:S(2)}) %collective-permute-start.18) | collective-permute-done | bytes 131104 | tf_op jit(solution)/shard_map/ppermute | solution.py:32
  (59 shorter events, 10.9 us)
Async XLA Ops:
  0.6 9.8 %collective-permute-start.3 = (bf16[1024,2048]{1,0:T(8,128)(2,1)}, bf16[1024,2048]{1,0:T(8,128)(2,1)S(1)}, u32[]{:S(2)}, u32[]{:S(2)}) collective-permute-start(bf16[1024,2048]{1,0:T(8,128)(2,1)} %x_ref), channel_id=1, source_target_pairs={{0,1},{1,0},{2,3},{3,2},{4,5},{5,4},{6,7},{7,6},{8,9},{9,8},{10,11... | collective-permute-start | bytes 12582920 | tf_op jit(solution)/shard_map/ppermute | solution.py:32
  2.4 7.7 %copy-start.4 = (bf16[1024,128]{1,0:T(8,128)(2,1)S(1)}, bf16[1024,128]{1,0:T(8,128)(2,1)}, u32[]{:S(2)}) copy-start(bf16[1024,128]{1,0:T(8,128)(2,1)} %grad_ref) | copy-start | bytes 786436
  2.5 9.1 %collective-permute-start = (bf16[2,256,128]{2,1,0:T(8,128)(2,1)S(1)}, bf16[2,256,128]{2,1,0:T(8,128)(2,1)S(1)}, u32[]{:S(2)}, u32[]{:S(2)}) collective-permute-start(bf16[2,256,128]{2,1,0:T(8,128)(2,1)S(1)} %get-tuple-element.96), channel_id=1, source_target_pairs={{0,6},{2,4},{4,2},{6,0},{8,14},{10,12},{12,10},{14,8},{16,22},{18,... | collective-permute-start | bytes 393224 | tf_op jit(solution)/shard_map/ppermute | solution.py:32
  6.0 7.0 %collective-permute-start.1 = (bf16[2,256,128]{2,1,0:T(8,128)(2,1)S(1)}, bf16[2,256,128]{2,1,0:T(8,128)(2,1)S(1)}, u32[]{:S(2)}, u32[]{:S(2)}) collective-permute-start(bf16[2,256,128]{2,1,0:T(8,128)(2,1)S(1)} %get-tuple-element.97), channel_id=1, source_target_pairs={{0,4},{2,6},{4,0},{6,2},{8,12},{10,14},{12,8},{14,10},{16,20},{18,... | collective-permute-start | bytes 393224 | tf_op jit(solution)/shard_map/ppermute | solution.py:32
  6.5 6.7 %collective-permute-start.2 = (bf16[2,256,128]{2,1,0:T(8,128)(2,1)S(1)}, bf16[2,256,128]{2,1,0:T(8,128)(2,1)S(1)}, u32[]{:S(2)}, u32[]{:S(2)}) collective-permute-start(bf16[2,256,128]{2,1,0:T(8,128)(2,1)S(1)} %get-tuple-element.98), channel_id=1, source_target_pairs={{0,2},{2,0},{4,6},{6,4},{8,10},{10,8},{12,14},{14,12},{16,18},{18,... | collective-permute-start | bytes 393224 | tf_op jit(solution)/shard_map/ppermute | solution.py:32
  8.9 9.8 %copy-start.7 = (bf16[2048]{0:T(1024)(128)(2,1)S(1)}, bf16[2048]{0:T(1024)(128)(2,1)}, u32[]{:S(2)}) copy-start(bf16[2048]{0:T(1024)(128)(2,1)} %param.7) | copy-start | bytes 12292
  13.4 5.3 %collective-permute-start.4 = (f32[1,256,128]{2,1,0:T(8,128)S(1)}, f32[1,256,128]{2,1,0:T(8,128)S(1)}, u32[]{:S(2)}, u32[]{:S(2)}) collective-permute-start(f32[1,256,128]{2,1,0:T(8,128)S(1)} %slice.17), channel_id=1, source_target_pairs={{0,8},{2,10},{4,12},{6,14},{8,0},{10,2},{12,4},{14,6},{16,24},{18,... | collective-permute-start | bytes 393224 | tf_op jit(solution)/shard_map/ppermute | solution.py:32
  15.0 10.1 %collective-permute-start.6 = (bf16[2,256,128]{2,1,0:T(8,128)(2,1)S(1)}, bf16[2,256,128]{2,1,0:T(8,128)(2,1)S(1)}, u32[]{:S(2)}, u32[]{:S(2)}) collective-permute-start(bf16[2,256,128]{2,1,0:T(8,128)(2,1)S(1)} %get-tuple-element.110), channel_id=1, source_target_pairs={{0,6},{2,4},{4,2},{6,0},{8,14},{10,12},{12,10},{14,8},{16,22},{18,... | collective-permute-start | bytes 393224 | tf_op jit(solution)/shard_map/ppermute | solution.py:32
  16.7 8.5 %collective-permute-start.7 = (bf16[2,256,128]{2,1,0:T(8,128)(2,1)S(1)}, bf16[2,256,128]{2,1,0:T(8,128)(2,1)S(1)}, u32[]{:S(2)}, u32[]{:S(2)}) collective-permute-start(bf16[2,256,128]{2,1,0:T(8,128)(2,1)S(1)} %get-tuple-element.111), channel_id=1, source_target_pairs={{0,4},{2,6},{4,0},{6,2},{8,12},{10,14},{12,8},{14,10},{16,20},{18,... | collective-permute-start | bytes 393224 | tf_op jit(solution)/shard_map/ppermute | solution.py:32
  18.0 7.2 %collective-permute-start.8 = (bf16[2,256,128]{2,1,0:T(8,128)(2,1)S(1)}, bf16[2,256,128]{2,1,0:T(8,128)(2,1)S(1)}, u32[]{:S(2)}, u32[]{:S(2)}) collective-permute-start(bf16[2,256,128]{2,1,0:T(8,128)(2,1)S(1)} %get-tuple-element.112), channel_id=1, source_target_pairs={{0,2},{2,0},{4,6},{6,4},{8,10},{10,8},{12,14},{14,12},{16,18},{18,... | collective-permute-start | bytes 393224 | tf_op jit(solution)/shard_map/ppermute | solution.py:32
  18.7 2.9 %collective-permute-start.9 = (bf16[2048]{0:T(1024)(128)(2,1)S(1)}, bf16[2048]{0:T(1024)(128)(2,1)S(1)}, u32[]{:S(2)}, u32[]{:S(2)}) collective-permute-start(bf16[2048]{0:T(1024)(128)(2,1)S(1)} %copy-done.7), channel_id=1, source_target_pairs={{0,1},{1,0},{2,3},{3,2},{4,5},{5,4},{6,7},{7,6},{8,9},{9,8},{10,11... | collective-permute-start | bytes 12296 | tf_op jit(solution)/shard_map/ppermute | solution.py:32
  18.8 9.7 %collective-permute-start.5 = (f32[256,128]{1,0:T(8,128)S(1)}, f32[256,128]{1,0:T(8,128)S(1)}, u32[]{:S(2)}, u32[]{:S(2)}) collective-permute-start(f32[256,128]{1,0:T(8,128)S(1)} %fusion.17), channel_id=1, source_target_pairs={{0,16},{2,18},{4,20},{6,22},{8,24},{10,26},{12,28},{14,30},{16,0},... | collective-permute-start | bytes 393224 | tf_op jit(solution)/shard_map/ppermute | solution.py:32
  25.3 6.0 %collective-permute-start.10 = (f32[256,128]{1,0:T(8,128)S(1)}, f32[256,128]{1,0:T(8,128)S(1)}, u32[]{:S(2)}, u32[]{:S(2)}) collective-permute-start(f32[256,128]{1,0:T(8,128)S(1)} %get-tuple-element.168), channel_id=1, source_target_pairs={{0,8},{2,10},{4,12},{6,14},{8,0},{10,2},{12,4},{14,6},{16,24},{18,... | collective-permute-start | bytes 393224 | tf_op jit(solution)/shard_map/ppermute | solution.py:32
  28.5 2.8 %copy-start.6 = (f32[256,128]{1,0:T(8,128)S(1)}, f32[256,128]{1,0:T(8,128)}, u32[]{:S(2)}) copy-start(f32[256,128]{1,0:T(8,128)} %param.10) | copy-start | bytes 393220
  31.3 4.3 %collective-permute-start.11 = (bf16[1,256,128]{2,1,0:T(8,128)(2,1)S(1)}, bf16[1,256,128]{2,1,0:T(8,128)(2,1)S(1)}, u32[]{:S(2)}, u32[]{:S(2)}) collective-permute-start(bf16[1,256,128]{2,1,0:T(8,128)(2,1)S(1)} %fusion.18), channel_id=1, source_target_pairs={{0,8},{2,10},{4,12},{6,14},{8,0},{10,2},{12,4},{14,6},{16,24},{18,... | collective-permute-start | bytes 196616 | tf_op jit(solution)/shard_map/ppermute | solution.py:32
  32.6 8.4 %collective-permute-start.16 = (bf16[1,256,128]{2,1,0:T(8,128)(2,1)S(1)}, bf16[1,256,128]{2,1,0:T(8,128)(2,1)S(1)}, u32[]{:S(2)}, u32[]{:S(2)}) collective-permute-start(bf16[1,256,128]{2,1,0:T(8,128)(2,1)S(1)} %fusion.18), channel_id=1, source_target_pairs={{0,24},{2,26},{4,28},{6,30},{8,16},{10,18},{12,20},{14,22},{16,8},... | collective-permute-start | bytes 196616 | tf_op jit(solution)/shard_map/ppermute | solution.py:32
  35.0 6.7 %collective-permute-start.15 = (bf16[1,256,128]{2,1,0:T(8,128)(2,1)S(1)}, bf16[1,256,128]{2,1,0:T(8,128)(2,1)S(1)}, u32[]{:S(2)}, u32[]{:S(2)}) collective-permute-start(bf16[1,256,128]{2,1,0:T(8,128)(2,1)S(1)} %fusion.18), channel_id=1, source_target_pairs={{0,16},{2,18},{4,20},{6,22},{8,24},{10,26},{12,28},{14,30},{16,0},... | collective-permute-start | bytes 196616 | tf_op jit(solution)/shard_map/ppermute | solution.py:32
  35.7 10.2 %collective-permute-start.14 = (bf16[2,256,128]{2,1,0:T(8,128)(2,1)S(1)}, bf16[2,256,128]{2,1,0:T(8,128)(2,1)S(1)}, u32[]{:S(2)}, u32[]{:S(2)}) collective-permute-start(bf16[2,256,128]{2,1,0:T(8,128)(2,1)S(1)} %pad_maximum_fusion.refs_0_), channel_id=1, source_target_pairs={{0,6},{2,4},{4,2},{6,0},{8,14},{10,12},{12,10},{14,8},{16,22},{18,... | collective-permute-start | bytes 393224 | tf_op jit(solution)/shard_map/ppermute | solution.py:32
  37.2 10.0 %collective-permute-start.13 = (bf16[2,256,128]{2,1,0:T(8,128)(2,1)S(1)}, bf16[2,256,128]{2,1,0:T(8,128)(2,1)S(1)}, u32[]{:S(2)}, u32[]{:S(2)}) collective-permute-start(bf16[2,256,128]{2,1,0:T(8,128)(2,1)S(1)} %pad_maximum_fusion.refs_0_), channel_id=1, source_target_pairs={{0,4},{2,6},{4,0},{6,2},{8,12},{10,14},{12,8},{14,10},{16,20},{18,... | collective-permute-start | bytes 393224 | tf_op jit(solution)/shard_map/ppermute | solution.py:32
  38.8 8.4 %collective-permute-start.12 = (bf16[2,256,128]{2,1,0:T(8,128)(2,1)S(1)}, bf16[2,256,128]{2,1,0:T(8,128)(2,1)S(1)}, u32[]{:S(2)}, u32[]{:S(2)}) collective-permute-start(bf16[2,256,128]{2,1,0:T(8,128)(2,1)S(1)} %pad_maximum_fusion.refs_0_), channel_id=1, source_target_pairs={{0,2},{2,0},{4,6},{6,4},{8,10},{10,8},{12,14},{14,12},{16,18},{18,... | collective-permute-start | bytes 393224 | tf_op jit(solution)/shard_map/ppermute | solution.py:32
  39.2 7.9 %copy-start.1 = (bf16[4096,128]{1,0:T(8,128)(2,1)S(1)}, bf16[4096,128]{1,0:T(8,128)(2,1)}, u32[]{:S(2)}) copy-start(bf16[4096,128]{1,0:T(8,128)(2,1)} %w_ref.3) | copy-start | bytes 3145732
  41.8 6.7 %collective-permute-start.19 = (bf16[2,256,128]{2,1,0:T(8,128)(2,1)S(1)}, bf16[2,256,128]{2,1,0:T(8,128)(2,1)S(1)}, u32[]{:S(2)}, u32[]{:S(2)}) collective-permute-start(bf16[2,256,128]{2,1,0:T(8,128)(2,1)S(1)} %constant_dynamic-update-slice_fusion.refs_0_), channel_id=1, source_target_pairs={{0,6},{2,4},{4,2},{6,0},{8,14},{10,12},{12,10},{14,8},{16,22},{18,... | collective-permute-start | bytes 393224 | tf_op jit(solution)/shard_map/ppermute | solution.py:32
  43.2 7.7 %collective-permute-start.18 = (bf16[2,256,128]{2,1,0:T(8,128)(2,1)S(1)}, bf16[2,256,128]{2,1,0:T(8,128)(2,1)S(1)}, u32[]{:S(2)}, u32[]{:S(2)}) collective-permute-start(bf16[2,256,128]{2,1,0:T(8,128)(2,1)S(1)} %constant_dynamic-update-slice_fusion.refs_0_), channel_id=1, source_target_pairs={{0,4},{2,6},{4,0},{6,2},{8,12},{10,14},{12,8},{14,10},{16,20},{18,... | collective-permute-start | bytes 393224 | tf_op jit(solution)/shard_map/ppermute | solution.py:32
  45.9 5.1 %collective-permute-start.17 = (bf16[2,256,128]{2,1,0:T(8,128)(2,1)S(1)}, bf16[2,256,128]{2,1,0:T(8,128)(2,1)S(1)}, u32[]{:S(2)}, u32[]{:S(2)}) collective-permute-start(bf16[2,256,128]{2,1,0:T(8,128)(2,1)S(1)} %constant_dynamic-update-slice_fusion.refs_0_), channel_id=1, source_target_pairs={{0,2},{2,0},{4,6},{6,4},{8,10},{10,8},{12,14},{14,12},{16,18},{18,... | collective-permute-start | bytes 393224 | tf_op jit(solution)/shard_map/ppermute | solution.py:32
  (4 other events, 8.4 us)
